TPU v7x, 32 devices: a whole 2x2x4 slice. The times are simulated.
32 devices in a mesh: slab: 4 (over y, x), ctrl: 8 (over z, core).
Axes of the slice: x: 2, y: 2, z: 4, core: 2. Of those that a mesh axis runs over, the one named last changes fastest.
Arguments:
- value: float32 [64, 128, 128], P('slab'), may hold values from -6 to 6
- speed: float32 [64, 128, 128], P('slab'), may hold values from 0.25 to 1
- reward: bfloat16 [16, 64, 128, 128], P('ctrl', 'slab'), may hold values from -0.8984375 to 0.8984375
- ctrl_set: int32 [16], P('ctrl'), may hold values from 0 to 15, as said below
- drift_sets: float32 [16, 3], replicated, may hold values from -0.08 to 0.08
- diffusion_sets: float32 [16, 3], replicated, may hold values from 0.03 to 0.12
Outputs:
- value_out: float32 [64, 128, 128], P('slab')
Inputs may be any that keep to these rules, and one draw needn't show every extreme that they name: `ctrl_set`: each of the 16 sets is named by exactly 1 controls.
All inputs are finite; a program needn't handle non-finite values.
Results may differ from a plain program's by a relative error of at most 0.0014.
Values may be sent and summed in bfloat16 or wider, within the bound.
No kernel may reach another device: no remote copies, remote signals or barrier semaphores. Data moves between devices by JAX's collectives and lax.ppermute only.
A program may use at most 64 MiB of HBM per device.

v0:
```python
import jax
import jax.numpy as jnp
from jax import lax
from jax.sharding import PartitionSpec as P

SUBSTEPS = 3
OUTER = 2


def with_halo(cells, sides, width):
    for axis, dim in sides:
        count = lax.axis_size(axis)
        ends = count - 1
        head = lax.slice_in_dim(cells, 0, width, axis=dim)
        tail = lax.slice_in_dim(cells, cells.shape[dim] - width, cells.shape[dim], axis=dim)
        cells = jnp.concatenate(
            [
                lax.ppermute(tail, axis, [(i, (i + 1) % count) for i in range(ends)]),
                cells,
                lax.ppermute(head, axis, [((i + 1) % count, i) for i in range(ends)]),
            ],
            axis=dim,
        )
    return cells


def upshift(field, axis):
    widths = [(0, 0)] * 4
    widths[axis] = (0, 1)
    padded = jnp.pad(field, widths)
    return lax.slice_in_dim(padded, 1, padded.shape[axis], axis=axis)


def downshift(field, axis):
    widths = [(0, 0)] * 4
    widths[axis] = (1, 0)
    padded = jnp.pad(field, widths)
    return lax.slice_in_dim(padded, 0, padded.shape[axis] - 1, axis=axis)


def advance(padded, speed_part, reward_part, diffusion, drift):
    center = padded[:, 1:-1]
    ahead = [padded[:, 2:], upshift(center, 2), upshift(center, 3)]
    behind = [padded[:, :-2], downshift(center, 2), downshift(center, 3)]
    total = center + reward_part
    for axis_num in range(3):
        rate = diffusion[:, axis_num][:, None, None, None]
        flow = drift[:, axis_num][:, None, None, None] * speed_part[None]
        forward = ahead[axis_num] - center
        backward = center - behind[axis_num]
        total = (
            total
            + rate * (forward - backward)
            + jnp.maximum(flow, 0.0) * forward
            + jnp.minimum(flow, 0.0) * backward
        )
    return total


def merge_controls(fields):
    local_best = jnp.max(fields, axis=0)
    return lax.pmax(local_best, "ctrl")


def body(value, speed, reward, ctrl_set, drift_sets, diffusion_sets):
    set_count = drift_sets.shape[0]
    onehot = (ctrl_set[:, None] == jnp.arange(set_count, dtype=jnp.int32)[None, :]).astype(
        jnp.float32
    )
    diffusion = jnp.dot(onehot, diffusion_sets, precision=lax.Precision.HIGHEST)
    drift = jnp.dot(onehot, drift_sets, precision=lax.Precision.HIGHEST)
    local_count = reward.shape[0]
    cells = value.shape[0]
    current = value
    depth = SUBSTEPS
    speed_wide = with_halo(speed.astype(jnp.bfloat16), (("slab", 0),), depth).astype(speed.dtype)
    reward_wide = with_halo(reward, (("slab", 1),), depth).astype(jnp.float32)
    total_rows = cells * lax.axis_size("slab")
    anchor = lax.axis_index("slab") * cells - depth
    for outer_round in range(OUTER):
        wide = with_halo(current.astype(jnp.bfloat16), (("slab", 0),), depth).astype(current.dtype)
        fields = jnp.broadcast_to(wide[None], (local_count,) + wide.shape)
        for substep in range(SUBSTEPS):
            extent = cells + 2 * (depth - 1 - substep)
            lower = substep + 1
            speed_part = lax.slice_in_dim(speed_wide, lower, lower + extent, axis=0)
            reward_part = lax.slice_in_dim(reward_wide, lower, lower + extent, axis=1)
            fields = advance(fields, speed_part, reward_part, diffusion, drift)
            positions = anchor + lower + jnp.arange(extent, dtype=jnp.int32)
            inside = (positions >= 0) & (positions < total_rows)
            fields = jnp.where(inside[None, :, None, None], fields, jnp.zeros_like(fields))
        current = merge_controls(fields)
    return current


def solution(mesh):
    in_specs = (
        P("slab", None, None),
        P("slab", None, None),
        P("ctrl", "slab", None, None),
        P("ctrl"),
        P(),
        P(),
    )
    out_specs = P("slab", None, None)
    return jax.shard_map(body, mesh=mesh, in_specs=in_specs, out_specs=out_specs, check_vma=False)
```

profile of v0, /device:TPU:5, one launch (start us, length us, event | category | flops | bytes accessed | tf_op | source)
XLA Modules:
  0.0 199.3 jit_solution(4716262314056734996)
XLA Ops:
  6.5 1.4 convert_element_type.74
  8.0 0.7 fusion.137
  8.7 3.1 %collective-permute-start = (bf16[3,128,128]{2,1,0:T(8,128)(2,1)}, bf16[3,128,128]{2,1,0:T(8,128)(2,1)S(1)}, u32[]{:S(2)}, u32[]{:S(2)}) collective-permute-start(bf16[3,128,128]{2,1,0:T(8,128)(2,1)} %get-tuple-element.23), channel_id=1, source_target_pairs={{0,8},{8,16},{16,24},{1,9},{9,17},{17,25},{2,10},{10,18},{18,26},{... | collective-permute-start | bytes 294920 | tf_op jit(solution)/shard_map/ppermute | solution.py:18
  11.8 3.1 %collective-permute-start.1 = (bf16[3,128,128]{2,1,0:T(8,128)(2,1)}, bf16[3,128,128]{2,1,0:T(8,128)(2,1)S(1)}, u32[]{:S(2)}, u32[]{:S(2)}) collective-permute-start(bf16[3,128,128]{2,1,0:T(8,128)(2,1)} %get-tuple-element.24), channel_id=1, source_target_pairs={{8,0},{16,8},{24,16},{9,1},{17,9},{25,17},{10,2},{18,10},{26,18},{... | collective-permute-start | bytes 294920 | tf_op jit(solution)/shard_map/ppermute | solution.py:20
  14.8 1.3 convert_element_type.77
  16.2 0.7 fusion.136
  16.8 2.2 %collective-permute-start.4 = (bf16[3,128,128]{2,1,0:T(8,128)(2,1)}, bf16[3,128,128]{2,1,0:T(8,128)(2,1)}, u32[]{:S(2)}, u32[]{:S(2)}) collective-permute-start(bf16[3,128,128]{2,1,0:T(8,128)(2,1)} %get-tuple-element.21), channel_id=1, source_target_pairs={{0,8},{8,16},{16,24},{1,9},{9,17},{17,25},{2,10},{10,18},{18,26},{... | collective-permute-start | bytes 294920 | tf_op jit(solution)/shard_map/ppermute | solution.py:18
  19.1 4.0 %collective-permute-start.5 = (bf16[3,128,128]{2,1,0:T(8,128)(2,1)}, bf16[3,128,128]{2,1,0:T(8,128)(2,1)}, u32[]{:S(2)}, u32[]{:S(2)}) collective-permute-start(bf16[3,128,128]{2,1,0:T(8,128)(2,1)} %get-tuple-element.22), channel_id=1, source_target_pairs={{8,0},{16,8},{24,16},{9,1},{17,9},{25,17},{10,2},{18,10},{26,18},{... | collective-permute-start | bytes 294920 | tf_op jit(solution)/shard_map/ppermute | solution.py:20
  23.0 1.1 fusion.134
  24.1 1.9 collective-permute-start.2
  26.0 0.1 convert_bitcast_fusion
  26.2 0.2 fusion.126
  26.4 0.2 fusion.127
  26.6 0.3 slice_reduce_fusion.4
  26.8 4.2 %collective-permute-start.3 = (bf16[2,3,128,128]{3,2,1,0:T(8,128)(2,1)S(1)}, bf16[2,3,128,128]{3,2,1,0:T(8,128)(2,1)S(1)}, u32[]{:S(2)}, u32[]{:S(2)}) collective-permute-start(bf16[2,3,128,128]{3,2,1,0:T(8,128)(2,1)S(1)} %get-tuple-element.18), channel_id=1, source_target_pairs={{8,0},{16,8},{24,16},{9,1},{17,9},{25,17},{10,2},{18,10},{26,18},{... | collective-permute-start | bytes 589832 | tf_op jit(solution)/shard_map/ppermute | solution.py:20
  31.1 1.1 maximum_convert_fusion.2
  32.2 0.1 slice.321
  32.3 0.1 slice.326
  32.5 0.1 maximum_convert_fusion.1
  32.6 0.5 fusion.132
  33.1 0.1 slice_bitcast_fusion.3
  33.2 0.5 collective-permute-done.3
  33.7 1.0 copy-done.8
  34.7 0.2 maximum_convert_fusion
  34.9 0.3 broadcast_in_dim.86
  35.2 3.9 %fusion.45 = f32[2,20,128,128]{3,2,1,0:T(8,128)S(1)} fusion(f32[2,20,128,128]{3,2,1,0:T(8,128)S(1)} %broadcast_in_dim.86, f32[2,22,128,128]{3,2,1,0:T(8,128)S(1)} %maximum_convert_fusion, f32[2]{0:T(128)S(1)} %get-tuple-element.9, f32[2]{0:T(128)S(1)} %get-tuple-element.26, f32[2]{0:T(128)S(1)} %get-tuple-element.10, f32[2]{0:T(128)S(1)} %get-tuple-element.25, ...), kind=kLoop, calls=%fused_computation.79 | loop fusion | flops 22937600 | bytes 13107268 | tf_op jit(solution)/shard_map/jit(_where)/select_n | solution.py:91
  39.1 0.2 slice.322
  39.3 3.7 %fusion.75 = f32[2,18,128,128]{3,2,1,0:T(8,128)S(1)} fusion(f32[2,18,128,128]{3,2,1,0:T(8,128)S(1)} %slice.322, f32[2,20,128,128]{3,2,1,0:T(8,128)S(1)} %fusion.45, f32[2,22,128,128]{3,2,1,0:T(8,128)S(1)} %maximum_convert_fusion, f32[2]{0:T(128)S(1)} %get-tuple-element.9, f32[2]{0:T(128)S(1)} %get-tuple-element.26, f32[2]{0:T(128)S(1)} %get-tuple-element.10, ...), kind=kLoop, calls=%fused_computation.113 | loop fusion | flops 22413312 | bytes 12976194 | tf_op jit(solution)/shard_map/jit(_where)/select_n | solution.py:91
  43.1 0.2 slice.327
  43.3 4.4 %fusion.102 = f32[16,128,128]{2,1,0:T(8,128)} fusion(f32[2,16,128,128]{3,2,1,0:T(8,128)S(1)} %slice.327, f32[2,18,128,128]{3,2,1,0:T(8,128)S(1)} %fusion.75, f32[2,22,128,128]{3,2,1,0:T(8,128)S(1)} %maximum_convert_fusion, f32[2]{0:T(128)S(1)} %get-tuple-element.9, f32[2]{0:T(128)S(1)} %get-tuple-element.26, f32[2]{0:T(128)S(1)} %get-tuple-element.10, ...), kind=kLoop, calls=%fused_computation.148 | loop fusion | flops 20185088 | bytes 10485824 | tf_op jit(solution)/shard_map/reduce_max | solution.py:61
  47.7 58.3 %all-reduce.28 = bf16[16,128,128]{2,1,0:T(8,128)(2,1)S(1)} all-reduce(f32[16,128,128]{2,1,0:T(8,128)} %fusion.102), channel_id=1, replica_groups=mesh['slab'=4,'ctrl'=8] {'ctrl'}, use_global_device_ids=true, to_apply=%region_1.2 | all-reduce | flops 262144 | bytes 1572864 | tf_op jit(solution)/shard_map/pmax | solution.py:62
  106.0 1.9 collective-permute-start.6
  107.9 4.8 %collective-permute-start.7 = (bf16[3,128,128]{2,1,0:T(8,128)(2,1)S(1)}, bf16[3,128,128]{2,1,0:T(8,128)(2,1)S(1)}, u32[]{:S(2)}, u32[]{:S(2)}) collective-permute-start(bf16[3,128,128]{2,1,0:T(8,128)(2,1)S(1)} %get-tuple-element.20), channel_id=1, source_target_pairs={{8,0},{16,8},{24,16},{9,1},{17,9},{25,17},{10,2},{18,10},{26,18},{... | collective-permute-start | bytes 294920 | tf_op jit(solution)/shard_map/ppermute | solution.py:20
  112.8 1.4 collective-permute-done.7
  114.2 0.1 maximum_convert_fusion.3
  114.3 0.1 slice_bitcast_fusion.1
  114.5 0.5 fusion.130
  115.0 0.3 broadcast_in_dim.90
  115.3 1.0 copy-done.2
  116.3 3.8 %fusion.56 = f32[2,20,128,128]{3,2,1,0:T(8,128)S(1)} fusion(f32[2,20,128,128]{3,2,1,0:T(8,128)S(1)} %broadcast_in_dim.90, f32[2,22,128,128]{3,2,1,0:T(8,128)S(1)} %maximum_convert_fusion, f32[20,128,128]{2,1,0:T(8,128)S(1)} %get-tuple-element.13, f32[20,128,128]{2,1,0:T(8,128)S(1)} %get-tuple-element.12, f32[20,128,128]{2,1,0:T(8,128)S(1)} %get-tuple-element.11, ...), kind=kLoop, calls=%fused_computation.90 | loop fusion | flops 22937600 | bytes 13107268 | tf_op jit(solution)/shard_map/jit(_where)/select_n | solution.py:91
  120.1 0.2 slice.336
  120.4 1.0 copy-done.4
  121.4 3.7 %fusion.77 = f32[2,18,128,128]{3,2,1,0:T(8,128)S(1)} fusion(f32[2,18,128,128]{3,2,1,0:T(8,128)S(1)} %slice.336, f32[2,20,128,128]{3,2,1,0:T(8,128)S(1)} %fusion.56, f32[2,22,128,128]{3,2,1,0:T(8,128)S(1)} %maximum_convert_fusion, f32[2]{0:T(128)S(1)} %get-tuple-element.9, f32[2]{0:T(128)S(1)} %get-tuple-element.26, f32[2]{0:T(128)S(1)} %get-tuple-element.10, ...), kind=kLoop, calls=%fused_computation.115 | loop fusion | flops 22413312 | bytes 12976194 | tf_op jit(solution)/shard_map/jit(_where)/select_n | solution.py:91
  125.0 0.2 slice.339
  125.3 1.0 copy-done.6
  126.3 4.4 %fusion.105 = f32[16,128,128]{2,1,0:T(8,128)} fusion(f32[2,16,128,128]{3,2,1,0:T(8,128)S(1)} %slice.339, f32[2,18,128,128]{3,2,1,0:T(8,128)S(1)} %fusion.77, f32[2,22,128,128]{3,2,1,0:T(8,128)S(1)} %maximum_convert_fusion, f32[2]{0:T(128)S(1)} %get-tuple-element.9, f32[2]{0:T(128)S(1)} %get-tuple-element.26, f32[2]{0:T(128)S(1)} %get-tuple-element.10, ...), kind=kLoop, calls=%fused_computation.151 | loop fusion | flops 20185088 | bytes 10485824 | tf_op jit(solution)/shard_map/reduce_max | solution.py:61
  130.7 59.4 %all-reduce.27.cloned.1.call-done = f32[16,128,128]{2,1,0:T(8,128)} async-done(((f32[16,128,128]{2,1,0:T(8,128)}), f32[16,128,128]{2,1,0:T(8,128)}) %all-reduce.27.cloned.1.call-update) | async-done | bytes 1048592 | tf_op jit(solution)/shard_map/pmax | solution.py:62
  190.1 2.3 %copy.10 = f32[16,128,128]{2,1,0:T(8,128)} copy(f32[16,128,128]{2,1,0:T(8,128)} %all-reduce.27.cloned.1.call-done) | data formatting | bytes 2097152
  (31 shorter events, 0.2 us)
Async XLA Ops:
  6.5 19.6 %copy-start = (f32[16,3]{0,1:T(4,128)S(1)}, f32[16,3]{0,1:T(4,128)}, u32[]{:S(2)}) copy-start(f32[16,3]{0,1:T(4,128)} %param.10) | copy-start | bytes 580
  6.5 19.5 %copy-start.7 = (f32[16,128,128]{2,1,0:T(8,128)S(1)}, f32[16,128,128]{2,1,0:T(8,128)}, u32[]{:S(2)}) copy-start(f32[16,128,128]{2,1,0:T(8,128)} %param.6) | copy-start | bytes 3145732
  6.5 183.6 %all-reduce.27.cloned.1.call-start = ((), (), s32[]{:S(2)}) async-start(), calls=%async_computation | async-start | bytes 2097152 | tf_op jit(solution)/shard_map/pmax | solution.py:62
  8.0 18.2 %copy-start.10 = (s32[2]{0:T(128)S(1)}, s32[2]{0:T(128)}, u32[]{:S(2)}) copy-start(s32[2]{0:T(128)} %param.9) | copy-start | bytes 28
  8.0 18.4 %copy-start.9 = (f32[16,3]{0,1:T(4,128)S(1)}, f32[16,3]{0,1:T(4,128)}, u32[]{:S(2)}) copy-start(f32[16,3]{0,1:T(4,128)} %param.11) | copy-start | bytes 580
  8.7 23.8 %collective-permute-start = (bf16[3,128,128]{2,1,0:T(8,128)(2,1)}, bf16[3,128,128]{2,1,0:T(8,128)(2,1)S(1)}, u32[]{:S(2)}, u32[]{:S(2)}) collective-permute-start(bf16[3,128,128]{2,1,0:T(8,128)(2,1)} %get-tuple-element.23), channel_id=1, source_target_pairs={{0,8},{8,16},{16,24},{1,9},{9,17},{17,25},{2,10},{10,18},{18,26},{... | collective-permute-start | bytes 294920 | tf_op jit(solution)/shard_map/ppermute | solution.py:18
  11.8 20.7 %collective-permute-start.1 = (bf16[3,128,128]{2,1,0:T(8,128)(2,1)}, bf16[3,128,128]{2,1,0:T(8,128)(2,1)S(1)}, u32[]{:S(2)}, u32[]{:S(2)}) collective-permute-start(bf16[3,128,128]{2,1,0:T(8,128)(2,1)} %get-tuple-element.24), channel_id=1, source_target_pairs={{8,0},{16,8},{24,16},{9,1},{17,9},{25,17},{10,2},{18,10},{26,18},{... | collective-permute-start | bytes 294920 | tf_op jit(solution)/shard_map/ppermute | solution.py:20
  16.8 10.0 %collective-permute-start.4 = (bf16[3,128,128]{2,1,0:T(8,128)(2,1)}, bf16[3,128,128]{2,1,0:T(8,128)(2,1)}, u32[]{:S(2)}, u32[]{:S(2)}) collective-permute-start(bf16[3,128,128]{2,1,0:T(8,128)(2,1)} %get-tuple-element.21), channel_id=1, source_target_pairs={{0,8},{8,16},{16,24},{1,9},{9,17},{17,25},{2,10},{10,18},{18,26},{... | collective-permute-start | bytes 294920 | tf_op jit(solution)/shard_map/ppermute | solution.py:18
  19.1 12.0 %collective-permute-start.5 = (bf16[3,128,128]{2,1,0:T(8,128)(2,1)}, bf16[3,128,128]{2,1,0:T(8,128)(2,1)}, u32[]{:S(2)}, u32[]{:S(2)}) collective-permute-start(bf16[3,128,128]{2,1,0:T(8,128)(2,1)} %get-tuple-element.22), channel_id=1, source_target_pairs={{8,0},{16,8},{24,16},{9,1},{17,9},{25,17},{10,2},{18,10},{26,18},{... | collective-permute-start | bytes 294920 | tf_op jit(solution)/shard_map/ppermute | solution.py:20
  24.1 9.1 %collective-permute-start.2 = (bf16[2,3,128,128]{3,2,1,0:T(8,128)(2,1)S(1)}, bf16[2,3,128,128]{3,2,1,0:T(8,128)(2,1)S(1)}, u32[]{:S(2)}, u32[]{:S(2)}) collective-permute-start(bf16[2,3,128,128]{3,2,1,0:T(8,128)(2,1)S(1)} %get-tuple-element.17), channel_id=1, source_target_pairs={{0,8},{8,16},{16,24},{1,9},{9,17},{17,25},{2,10},{10,18},{18,26},{... | collective-permute-start | bytes 589832 | tf_op jit(solution)/shard_map/ppermute | solution.py:18
  26.8 6.8 %collective-permute-start.3 = (bf16[2,3,128,128]{3,2,1,0:T(8,128)(2,1)S(1)}, bf16[2,3,128,128]{3,2,1,0:T(8,128)(2,1)S(1)}, u32[]{:S(2)}, u32[]{:S(2)}) collective-permute-start(bf16[2,3,128,128]{3,2,1,0:T(8,128)(2,1)S(1)} %get-tuple-element.18), channel_id=1, source_target_pairs={{8,0},{16,8},{24,16},{9,1},{17,9},{25,17},{10,2},{18,10},{26,18},{... | collective-permute-start | bytes 589832 | tf_op jit(solution)/shard_map/ppermute | solution.py:20
  32.3 3.0 %copy-start.1 = (f32[20,128,128]{2,1,0:T(8,128)}, f32[20,128,128]{2,1,0:T(8,128)S(1)}, u32[]{:S(2)}) copy-start(f32[20,128,128]{2,1,0:T(8,128)S(1)} %slice.321) | copy-start | bytes 3932164
  32.4 7.0 %copy-start.3 = (f32[18,128,128]{2,1,0:T(8,128)}, f32[18,128,128]{2,1,0:T(8,128)S(1)}, u32[]{:S(2)}) copy-start(f32[18,128,128]{2,1,0:T(8,128)S(1)} %slice.326) | copy-start | bytes 3538948
  32.4 10.8 %copy-start.5 = (f32[16,128,128]{2,1,0:T(8,128)}, f32[16,128,128]{2,1,0:T(8,128)S(1)}, u32[]{:S(2)}) copy-start(f32[16,128,128]{2,1,0:T(8,128)S(1)} %slice.331) | copy-start | bytes 3145732
  33.1 1.6 copy-start.8
  106.0 6.8 %collective-permute-start.6 = (bf16[3,128,128]{2,1,0:T(8,128)(2,1)S(1)}, bf16[3,128,128]{2,1,0:T(8,128)(2,1)S(1)}, u32[]{:S(2)}, u32[]{:S(2)}) collective-permute-start(bf16[3,128,128]{2,1,0:T(8,128)(2,1)S(1)} %get-tuple-element.19), channel_id=1, source_target_pairs={{0,8},{8,16},{16,24},{1,9},{9,17},{17,25},{2,10},{10,18},{18,26},{... | collective-permute-start | bytes 294920 | tf_op jit(solution)/shard_map/ppermute | solution.py:18
  107.9 6.3 %collective-permute-start.7 = (bf16[3,128,128]{2,1,0:T(8,128)(2,1)S(1)}, bf16[3,128,128]{2,1,0:T(8,128)(2,1)S(1)}, u32[]{:S(2)}, u32[]{:S(2)}) collective-permute-start(bf16[3,128,128]{2,1,0:T(8,128)(2,1)S(1)} %get-tuple-element.20), channel_id=1, source_target_pairs={{8,0},{16,8},{24,16},{9,1},{17,9},{25,17},{10,2},{18,10},{26,18},{... | collective-permute-start | bytes 294920 | tf_op jit(solution)/shard_map/ppermute | solution.py:20
  114.9 1.3 copy-start.2
  120.1 1.3 copy-start.4
  125.0 1.2 copy-start.6
Sparse Core Ops, SparseCore 0:
  130.8 59.2 all-reduce.26
where the time goes:
time: 203 us; the launch traced here: 199 us
  waiting for transfers between devices  61.3 us (30%)
  blocking collectives  58.3 us (29%)
  other arithmetic  29.1 us (14%)
  starting transfers between devices  25.3 us (12%)
  between operations  13.8 us (7%)
  local copies, waits for them, and re-layouts  11 us (5%)
    pmax x1, waiting for transfers between devices, merge_controls(): return lax.pmax(local_best, 'ctrl')  59.4 us
    pmax x1, blocking collectives, merge_controls(): return lax.pmax(local_best, 'ctrl')  58.3 us
    ppermute x4, starting transfers between devices, with_halo(): lax.ppermute(head, axis, [((i + 1) % count, i) for i in range(ends)])  16.1 us
    select_n x4, other arithmetic, body(): jnp.where(inside[None, :, None, None], fields, jnp.zeros_like(fields))  15 us
    ppermute x4, starting transfers between devices, with_halo(): lax.ppermute(tail, axis, [(i, (i + 1) % count) for i in range(ends)])  9.18 us
    reduce_max x2, other arithmetic, merge_controls(): local_best = jnp.max(fields, axis=0)  8.81 us
    unnamed x23, local copies, waits for them, and re-layouts  6.36 us
  transfers between devices with their start and end apart: 9, of which 3 were waited for; matrix products, arithmetic and copies ran while one was open for 3% of the time, Pallas kernels for 0%

commit v1 on v0

v1 whole, which is shorter than its diff:
```python
import functools

import jax
import jax.numpy as jnp
from jax import lax
from jax.experimental import pallas as pl
from jax.experimental.pallas import tpu as pltpu
from jax.sharding import PartitionSpec as P

SUBSTEPS = 3
OUTER = 2
PAD = 8
LOWEST = -3.0e38
COEFS = 12


def mate(chip, step, chips):
    if chips & (chips - 1) == 0:
        return chip ^ step
    return (chip + step) % chips


def shift_rows(rows, count, start):
    return lax.dynamic_slice_in_dim(rows, start, count, axis=0)


def stencil(coef, ctrl, src, row, first, size, speed, reward, fixed):
    lines = pl.ds(PAD + first, size)
    center = src[row, lines, :]
    y_ahead = src[row, pl.ds(PAD + first + 1, size), :]
    y_behind = src[row, pl.ds(PAD + first - 1, size), :]
    x_sum = src[row + 1, lines, :] + src[row - 1, lines, :]
    x_wind = src[row + fixed["x_step"], lines, :]
    depth = center.shape[1]
    lane = lax.broadcasted_iota(jnp.int32, center.shape, 1)
    z_ahead = jnp.where(lane == depth - 1, 0.0, pltpu.roll(center, depth - 1, 1))
    z_behind = jnp.where(lane == 0, 0.0, pltpu.roll(center, 1, 1))
    y_wind = jnp.where(fixed["y_up"], y_ahead, y_behind)
    z_wind = jnp.where(fixed["z_up"], z_ahead, z_behind)
    still = reward + coef[ctrl, 6] * center + coef[ctrl, 0] * x_sum
    still = still + coef[ctrl, 1] * (y_ahead + y_behind) + coef[ctrl, 2] * (z_ahead + z_behind)
    wind = coef[ctrl, 3] * x_wind + coef[ctrl, 4] * y_wind + coef[ctrl, 5] * z_wind
    return still + speed * (wind - coef[ctrl, 7] * center)


def march(place, coef, block, speed, reward, out, mid, late, chips, half, ny):
    lines = out.shape[1]
    chunk = min(lines, ny)
    count = reward.shape[0]
    chip = place[0]
    low = place[1].astype(jnp.float32)
    high = place[2].astype(jnp.float32)
    for shard in range(chips):
        out[shard] = jnp.full(out.shape[1:], LOWEST, out.dtype)

    def one(ctrl, carry):
        fixed = {
            "x_step": jnp.where(coef[ctrl, 8] > 0.0, 1, -1),
            "y_up": coef[ctrl, 9] > 0.0,
            "z_up": coef[ctrl, 10] > 0.0,
        }
        fields = [block, mid, late]
        for substep in range(SUBSTEPS):
            last = substep == SUBSTEPS - 1
            for row in range(substep + 1, half + 2 * SUBSTEPS - 1 - substep):
                for first in range(0, ny, chunk):
                    part = pl.ds(first, chunk)
                    new = stencil(
                        coef,
                        ctrl,
                        fields[substep],
                        row,
                        first,
                        chunk,
                        speed[row - 1, part, :],
                        reward[ctrl, row - 1, part, :],
                        fixed,
                    )
                    if last:
                        line = (row - SUBSTEPS) * ny + first
                        shard = mate(chip, line // lines, chips)
                        spot = pl.ds(line % lines, chunk)
                        out[shard, spot, :] = jnp.maximum(out[shard, spot, :], new)
                    else:
                        if row < SUBSTEPS:
                            new = new * low
                        if row >= SUBSTEPS + half:
                            new = new * high
                        fields[substep + 1][row, pl.ds(PAD + first, chunk), :] = new
        return carry

    lax.fori_loop(0, count, one, 0)


def clear_pads(fields, ny):
    for field in fields:
        zero = jnp.zeros((PAD, field.shape[2]), field.dtype)
        for row in range(field.shape[0]):
            field[row, 0:PAD, :] = zero
            field[row, PAD + ny : 2 * PAD + ny, :] = zero


def lay_out(place, speed, reward, other, edge, edge_own, speed_ext, reward_ext, half):
    core = place[3]
    margin = SUBSTEPS - 1
    own = reward.shape[0]
    inner = half + margin
    head = margin * (1 - core)
    tail = inner * core
    start = (half - margin) * core
    for row in range(inner):
        speed_ext[row + head] = speed[row + start]
        for ctrl in range(own):
            reward_ext[ctrl, row + head] = reward[ctrl, row + start].astype(jnp.float32)
            reward_ext[own + ctrl, row + head] = other[ctrl, row].astype(jnp.float32)
    for row in range(margin):
        speed_ext[row + tail] = edge[SUBSTEPS + row].astype(jnp.float32)
        for ctrl in range(own):
            reward_ext[ctrl, row + tail] = edge_own[ctrl * margin + row].astype(jnp.float32)
            reward_ext[own + ctrl, row + tail] = edge[
                SUBSTEPS + margin + ctrl * margin + row
            ].astype(jnp.float32)


def first_kernel(
    place, coef, value, speed, reward, other, edge, edge_own, out, block, mid, late, speed_ext, reward_ext, *, chips
):
    half = speed_ext.shape[0] - 2 * (SUBSTEPS - 1)
    ny = value.shape[1]
    core = place[3]
    clear_pads((block, mid, late), ny)
    middle = pl.ds(PAD, ny)
    inner = half + SUBSTEPS
    for row in range(inner):
        block[row + SUBSTEPS * (1 - core), middle, :] = value[row + (half - SUBSTEPS) * core]
    for row in range(SUBSTEPS):
        block[row + inner * core, middle, :] = edge[row].astype(jnp.float32)
    lay_out(place, speed, reward, other, edge, edge_own, speed_ext, reward_ext, half)
    march(place, coef, block, speed_ext, reward_ext, out, mid, late, chips, half, ny)


def second_kernel(
    place, coef, current, below, above, speed, reward, other, edge, edge_own, out, block, mid, late, speed_ext, reward_ext, *, chips
):
    half = speed_ext.shape[0] - 2 * (SUBSTEPS - 1)
    ny = below.shape[1]
    lines = current.shape[1]
    chunk = min(lines, ny)
    clear_pads((block, mid, late), ny)
    middle = pl.ds(PAD, ny)
    for row in range(SUBSTEPS):
        block[row, middle, :] = below[row]
        block[SUBSTEPS + half + row, middle, :] = above[row]
    for line in range(0, half * ny, chunk):
        row, first = line // ny, line % ny
        block[SUBSTEPS + row, pl.ds(PAD + first, chunk), :] = current[
            mate(place[0], line // lines, chips), pl.ds(line % lines, chunk), :
        ]
    lay_out(place, speed, reward, other, edge, edge_own, speed_ext, reward_ext, half)
    march(place, coef, block, speed_ext, reward_ext, out, mid, late, chips, half, ny)


def run_kernel(kernel, chips, half, count, ny, nz, place, coef, arrays):
    lines = half * ny // chips
    padded = pltpu.VMEM((half + 2 * SUBSTEPS, ny + 2 * PAD, nz), jnp.float32)
    inner = half + 2 * (SUBSTEPS - 1)
    cells = count * nz * ny * (3 * half + SUBSTEPS * (SUBSTEPS - 1))
    return pl.pallas_call(
        functools.partial(kernel, chips=chips),
        out_shape=jax.ShapeDtypeStruct((chips, lines, nz), jnp.float32),
        in_specs=[pl.BlockSpec(memory_space=pltpu.SMEM)] * 2
        + [pl.BlockSpec(memory_space=pltpu.VMEM)] * len(arrays),
        out_specs=pl.BlockSpec(memory_space=pltpu.VMEM),
        scratch_shapes=[
            padded,
            padded,
            padded,
            pltpu.VMEM((inner, ny, nz), jnp.float32),
            pltpu.VMEM((count, inner, ny, nz), jnp.float32),
        ],
        compiler_params=pltpu.CompilerParams(vmem_limit_bytes=32 * 2**20),
        cost_estimate=pl.CostEstimate(flops=25 * cells, bytes_accessed=4 * 2**20, transcendentals=0),
    )(place, coef, *arrays)


def body(value, speed, reward, ctrl_set, drift_sets, diffusion_sets):
    own, cells, ny, nz = reward.shape
    slabs, members = lax.axis_size("slab"), lax.axis_size("ctrl")
    chips, half = members // 2, cells // 2
    slab, member = lax.axis_index("slab"), lax.axis_index("ctrl")
    chip, core = member // 2, member % 2
    margin = SUBSTEPS - 1
    narrow = jnp.bfloat16

    def device(s, z, c):
        return s * members + 2 * z + c

    partners = [(i, i ^ 1) for i in range(members)]
    across, along = [], []
    for s in range(slabs - 1):
        for z in range(chips):
            across += [(device(s, z, 1), device(s + 1, z, 0)), (device(s + 1, z, 0), device(s, z, 1))]
            along += [(device(s, z, 0), device(s + 1, z, 0)), (device(s + 1, z, 1), device(s, z, 1))]

    other_set = lax.ppermute(ctrl_set, "ctrl", partners)
    other = lax.ppermute(
        lax.dynamic_slice_in_dim(reward, (half - margin) * (1 - core), half + margin, axis=1), "ctrl", partners
    )
    near = core * (cells - margin)
    rim = jnp.concatenate(
        [
            shift_rows(value, SUBSTEPS, core * (cells - SUBSTEPS)).astype(narrow),
            shift_rows(speed, margin, near).astype(narrow),
            lax.dynamic_slice_in_dim(reward, near, margin, axis=1).reshape(own * margin, ny, nz),
        ],
        axis=0,
    )
    edge = lax.ppermute(rim, ("slab", "ctrl"), across)
    far = lax.dynamic_slice_in_dim(reward, (1 - core) * (cells - margin), margin, axis=1)
    edge_own = lax.ppermute(far.reshape(own * margin, ny, nz), ("slab", "ctrl"), along)

    sets = jnp.concatenate([ctrl_set, other_set])
    picked = sets[:, None] == jnp.arange(drift_sets.shape[0], dtype=jnp.int32)[None, :]
    diffusion = jnp.sum(jnp.where(picked[:, :, None], diffusion_sets[None], 0.0), axis=1)
    drift = jnp.sum(jnp.where(picked[:, :, None], drift_sets[None], 0.0), axis=1)
    size = jnp.abs(drift)
    coef = jnp.concatenate(
        [
            diffusion,
            size,
            1.0 - 2.0 * jnp.sum(diffusion, axis=1, keepdims=True),
            jnp.sum(size, axis=1, keepdims=True),
            drift,
            jnp.zeros((2 * own, 1), jnp.float32),
        ],
        axis=1,
    )
    place = jnp.stack(
        [
            chip,
            jnp.where((slab == 0) & (core == 0), 0, 1),
            jnp.where((slab == slabs - 1) & (core == 1), 0, 1),
            core,
        ]
    ).astype(jnp.int32)
    run = functools.partial(run_kernel, chips=chips, half=half, count=2 * own, ny=ny, nz=nz, place=place, coef=coef)
    shared = (speed, reward, other, edge, edge_own)

    def merge(best):
        wire = best.astype(jnp.float16)
        mine = wire[0]
        for step in range(1, chips):
            pairs = [(2 * z + c, 2 * mate(z, step, chips) + c) for z in range(chips) for c in range(2)]
            mine = jnp.maximum(mine, lax.ppermute(wire[step], "ctrl", pairs))
        pieces = [mine]
        for step in range(1, chips):
            pairs = [(2 * mate(z, step, chips) + c, 2 * z + c) for z in range(chips) for c in range(2)]
            pieces.append(lax.ppermute(mine, "ctrl", pairs))
        return pieces

    def in_order(pieces):
        stacked = jnp.stack(pieces)
        return jnp.concatenate(
            [lax.dynamic_index_in_dim(stacked, mate(chip, shard, chips), 0, keepdims=False) for shard in range(chips)]
            if chips & (chips - 1) == 0
            else [
                lax.dynamic_index_in_dim(stacked, (shard - chip) % chips, 0, keepdims=False) for shard in range(chips)
            ]
        ).reshape(half, ny, nz)

    pieces = merge(run(first_kernel, arrays=(value,) + shared))
    for _ in range(1, OUTER):
        rows = in_order(pieces)
        bottom, top = rows[:SUBSTEPS], rows[half - SUBSTEPS :]
        from_core = lax.ppermute(jnp.where(core == 0, top, bottom), "ctrl", partners).astype(jnp.float32)
        from_slab = lax.ppermute(jnp.where(core == 0, bottom, top), ("slab", "ctrl"), across).astype(jnp.float32)
        below = jnp.where(core == 0, from_slab, from_core)
        above = jnp.where(core == 0, from_core, from_slab)
        current = jnp.stack(pieces).astype(jnp.float32)
        pieces = merge(run(second_kernel, arrays=(current, below, above) + shared))
    rows = in_order(pieces)
    partner_rows = lax.ppermute(rows, "ctrl", partners)
    lower = jnp.where(core == 0, rows, partner_rows).astype(jnp.float32)
    upper = jnp.where(core == 0, partner_rows, rows).astype(jnp.float32)
    return jnp.concatenate([lower, upper], axis=0)


def solution(mesh):
    in_specs = (
        P("slab", None, None),
        P("slab", None, None),
        P("ctrl", "slab", None, None),
        P("ctrl"),
        P(),
        P(),
    )
    out_specs = P("slab", None, None)
    return jax.shard_map(body, mesh=mesh, in_specs=in_specs, out_specs=out_specs, check_vma=False)
```

time: 203 us -> 84 us (0.41); the launches traced: 199 us -> 83.7 us
  blocking collectives: 58.3 us -> 0 us
  waiting for transfers between devices: 61.3 us -> 28.2 us
  other arithmetic: 29.1 us -> 2.26 us
  Pallas kernels: 0 us -> 15.9 us
  between operations: 13.8 us -> 0.22 us
  starting transfers between devices: 25.3 us -> 30.3 us
  local copies, waits for them, and re-layouts: 11 us -> 6.89 us
    pmax x1 -> x0, waiting for transfers between devices: 59.4 us -> none  [merge_controls(): return lax.pmax(local_best, 'ctrl')]
    pmax x1 -> x0, blocking collectives: 58.3 us -> none  [merge_controls(): return lax.pmax(local_best, 'ctrl')]
    ppermute x8 -> x19, waiting for transfers between devices: 1.9 us -> 28.2 us  [the longest x6 11.4 us: merge(): mine = jnp.maximum(mine, lax.ppermute(wire[step], 'ctrl', pairs))]
    pallas_call x0 -> x2, Pallas kernels: none -> 15.9 us  [run_kernel(): pl.pallas_call(functools.partial(kernel, chips=chips), out_shape=jax.Shap...]
    select_n x4 -> x3, other arithmetic: 15 us -> 0.25 us  [the longest x1 0.15 us: body(): lower = jnp.where(core == 0, rows, partner_rows).astype(jnp.float32)]
    reduce_max x2 -> x0, other arithmetic: 8.81 us -> none  [merge_controls(): local_best = jnp.max(fields, axis=0)]
    ppermute x8 -> x19, starting transfers between devices: 25.3 us -> 30.3 us  [the longest x1 7.72 us: body(): lax.ppermute(jnp.where(core == 0, top, bottom), 'ctrl', partners)]
    unnamed x23 -> x12, local copies, waits for them, and re-layouts: 6.36 us -> 1.81 us
  transfers between devices with their start and end apart: 9 -> 19, of which waited for: 3 -> 12; matrix products, arithmetic and copies ran while one was open for 3% -> 6% of each run, Pallas kernels for 0% -> 0%
where the time goes in v1:
time: 84 us; the launch traced here: 83.7 us
  starting transfers between devices  30.3 us (36%)
  waiting for transfers between devices  28.2 us (34%)
  Pallas kernels  15.9 us (19%)
  local copies, waits for them, and re-layouts  6.89 us (8%)
  other arithmetic  2.26 us (3%)
    pallas_call x2, Pallas kernels, run_kernel(): pl.pallas_call(functools.partial(kernel, chips=chips), out_shape=jax.Shap...  15.9 us
    ppermute x6, waiting for transfers between devices, merge(): mine = jnp.maximum(mine, lax.ppermute(wire[step], 'ctrl', pairs))  11.4 us
    ppermute x6, waiting for transfers between devices, merge(): pieces.append(lax.ppermute(mine, 'ctrl', pairs))  7.85 us
    ppermute x1, starting transfers between devices, body(): lax.ppermute(jnp.where(core == 0, top, bottom), 'ctrl', partners)  7.72 us
    ppermute x6, starting transfers between devices, merge(): pieces.append(lax.ppermute(mine, 'ctrl', pairs))  7.23 us
    ppermute x6, starting transfers between devices, merge(): mine = jnp.maximum(mine, lax.ppermute(wire[step], 'ctrl', pairs))  6.67 us
    ppermute x1, waiting for transfers between devices, body(): lax.ppermute(jnp.where(core == 0, bottom, top), ('slab', 'ctrl'), across)  4.29 us
    ppermute x1, waiting for transfers between devices, body(): edge = lax.ppermute(rim, ('slab', 'ctrl'), across)  3.52 us
  transfers between devices with their start and end apart: 19, of which 12 were waited for; matrix products, arithmetic and copies ran while one was open for 6% of the time, Pallas kernels for 0%

profile of v1, /device:TPU:5, one launch (start us, length us, event | category | flops | bytes accessed | tf_op | source)
XLA Modules:
  0.0 83.7 jit_solution(12951909303517594836)
XLA Ops:
  0.0 0.7 collective-permute-start
  0.7 1.6 %constant_dynamic-slice_fusion = (bf16[2,2,128,128]{3,2,1,0:T(8,128)(2,1)}, bf16[2,2,128,128]{3,2,1,0:T(8,128)(2,1)S(1)}) fusion(bf16[2,16,128,128]{3,2,1,0:T(8,128)(2,1)} %reward.3, s32[]{:T(128)S(6)} %select_n.107, s32[]{:T(128)S(6)} %select_n.106), kind=kLoop, calls=%fused_computation.40 | loop fusion | bytes 524296 | tf_op jit(solution)/shard_map/dynamic_slice | solution.py:219
  2.3 3.0 %collective-permute-start.3 = (bf16[4,128,128]{2,1,0:T(8,128)(2,1)}, bf16[4,128,128]{2,1,0:T(8,128)(2,1)S(1)}, u32[]{:S(2)}, u32[]{:S(2)}) collective-permute-start(bf16[4,128,128]{2,1,0:T(8,128)(2,1)} %bitcast.7), channel_id=1, source_target_pairs={{0,8},{9,1},{2,10},{11,3},{4,12},{13,5},{6,14},{15,7},{8,16},{17,9... | collective-permute-start | bytes 393224 | tf_op jit(solution)/shard_map/ppermute | solution.py:220
  5.4 0.9 %dynamic-slice_convert_fusion.1 = bf16[2,128,128]{2,1,0:T(8,128)(2,1)S(1)} fusion(f32[16,128,128]{2,1,0:T(8,128)} %speed.3, s32[]{:T(128)S(6)} %select_n.106), kind=kLoop, calls=%fused_computation.10 | loop fusion | bytes 131076 | tf_op jit(solution)/shard_map/convert_element_type | solution.py:213
  6.3 0.9 %dynamic-slice_convert_fusion = bf16[3,128,128]{2,1,0:T(8,128)(2,1)S(1)} fusion(f32[16,128,128]{2,1,0:T(8,128)} %value.1, s32[]{:T(128)S(6)} %select_n.105), kind=kLoop, calls=%fused_computation.9 | loop fusion | bytes 196612 | tf_op jit(solution)/shard_map/convert_element_type | solution.py:212
  7.3 2.1 %collective-permute-start.2 = (bf16[9,128,128]{2,1,0:T(8,128)(2,1)S(1)}, bf16[9,128,128]{2,1,0:T(8,128)(2,1)S(1)}, u32[]{:S(2)}, u32[]{:S(2)}) collective-permute-start(bf16[9,128,128]{2,1,0:T(8,128)(2,1)S(1)} %pad_maximum_fusion), channel_id=1, source_target_pairs={{1,8},{8,1},{3,10},{10,3},{5,12},{12,5},{7,14},{14,7},{9,16},{16,9... | collective-permute-start | bytes 884744 | tf_op jit(solution)/shard_map/ppermute | solution.py:218
  9.4 0.9 %constant_dynamic-slice_fusion.2 = bf16[2,10,128,128]{3,2,1,0:T(8,128)(2,1)} fusion(bf16[2,16,128,128]{3,2,1,0:T(8,128)(2,1)S(1)} %copy-done, s32[]{:T(128)S(6)} %select_n.104), kind=kLoop, calls=%fused_computation.42 | loop fusion | bytes 1310724 | tf_op jit(solution)/shard_map/dynamic_slice | solution.py:207
  10.3 0.4 collective-permute-start.1
  10.8 0.6 copy-done.5
  11.5 0.1 select_reduce_fusion
  11.7 0.1 copy.13
  11.8 0.1 copy.11
  11.8 0.1 copy.12
  11.9 0.1 abs_reduce_fusion
  12.1 0.1 copy.14
  12.1 0.1 concatenate.26.coef
  12.3 3.5 %collective-permute-done.2.edge = bf16[9,128,128]{2,1,0:T(8,128)(2,1)S(1)} collective-permute-done((bf16[9,128,128]{2,1,0:T(8,128)(2,1)S(1)}, bf16[9,128,128]{2,1,0:T(8,128)(2,1)S(1)}, u32[]{:S(2)}, u32[]{:S(2)}) %collective-permute-start.2) | collective-permute-done | bytes 294944 | tf_op jit(solution)/shard_map/ppermute | solution.py:218
  15.8 1.2 %copy-done.2 = f32[16,128,128]{2,1,0:T(8,128)S(1)} copy-done((f32[16,128,128]{2,1,0:T(8,128)S(1)}, f32[16,128,128]{2,1,0:T(8,128)}, u32[]{:S(2)}) %copy-start.2) | copy-done | bytes 1048600
  17.0 7.9 %shard_map.64 = f32[4,256,128]{2,1,0:T(8,128)S(1)} custom-call(s32[4]{0:T(128)S(1)} %pad_add_fusion.place, f32[4,12]{1,0:T(4,128)S(1)} %concatenate.26.coef, f32[16,128,128]{2,1,0:T(8,128)S(1)} %copy-done.2, f32[16,128,128]{2,1,0:T(8,128)S(1)} %copy-done.1, bf16[2,16,128,128]{3,2,1,0:T(8,128)(2,1)S(1)} %copy-done, ...), custom_call_target="tpu_custom_call" | custom-call | flops 49152000 | bytes 4194304 | tf_op jit(solution)/shard_map/pallas_call | solution.py:168
  25.1 1.4 %collective-permute-start.4 = (f16[256,128]{1,0:T(8,128)(2,1)S(1)}, f16[256,128]{1,0:T(8,128)(2,1)S(1)}, u32[]{:S(2)}, u32[]{:S(2)}) collective-permute-start(f16[256,128]{1,0:T(8,128)(2,1)S(1)} %get-tuple-element.27), channel_id=1, source_target_pairs={{0,2},{1,3},{2,0},{3,1},{4,6},{5,7},{6,4},{7,5},{8,10},{9,11},{10,... | collective-permute-start | bytes 196616 | tf_op jit(solution)/shard_map/ppermute | solution.py:254
  26.4 2.2 %collective-permute-start.6 = (f16[256,128]{1,0:T(8,128)(2,1)S(1)}, f16[256,128]{1,0:T(8,128)(2,1)S(1)}, u32[]{:S(2)}, u32[]{:S(2)}) collective-permute-start(f16[256,128]{1,0:T(8,128)(2,1)S(1)} %get-tuple-element.28), channel_id=1, source_target_pairs={{0,6},{1,7},{2,4},{3,5},{4,2},{5,3},{6,0},{7,1},{8,14},{9,15},{10,... | collective-permute-start | bytes 196616 | tf_op jit(solution)/shard_map/ppermute | solution.py:254
  28.6 0.1 collective-permute-start.5
  28.7 2.6 %collective-permute-done.6 = f16[256,128]{1,0:T(8,128)(2,1)S(1)} collective-permute-done((f16[256,128]{1,0:T(8,128)(2,1)S(1)}, f16[256,128]{1,0:T(8,128)(2,1)S(1)}, u32[]{:S(2)}, u32[]{:S(2)}) %collective-permute-start.6) | collective-permute-done | bytes 65568 | tf_op jit(solution)/shard_map/ppermute | solution.py:254
  31.3 2.0 %collective-permute-done.5 = f16[256,128]{1,0:T(8,128)(2,1)S(1)} collective-permute-done((f16[256,128]{1,0:T(8,128)(2,1)S(1)}, f16[256,128]{1,0:T(8,128)(2,1)S(1)}, u32[]{:S(2)}, u32[]{:S(2)}) %collective-permute-start.5) | collective-permute-done | bytes 65568 | tf_op jit(solution)/shard_map/ppermute | solution.py:254
  33.4 1.7 %collective-permute-start.9 = (f16[256,128]{1,0:T(8,128)(2,1)S(1)}, f16[256,128]{1,0:T(8,128)(2,1)S(1)}, u32[]{:S(2)}, u32[]{:S(2)}) collective-permute-start(f16[256,128]{1,0:T(8,128)(2,1)S(1)} %fusion.5), channel_id=1, source_target_pairs={{6,0},{7,1},{4,2},{5,3},{2,4},{3,5},{0,6},{1,7},{14,8},{15,9},{12,... | collective-permute-start | bytes 196616 | tf_op jit(solution)/shard_map/ppermute | solution.py:258
  35.1 1.9 %collective-permute-start.7 = (f16[256,128]{1,0:T(8,128)(2,1)S(1)}, f16[256,128]{1,0:T(8,128)(2,1)S(1)}, u32[]{:S(2)}, u32[]{:S(2)}) collective-permute-start(f16[256,128]{1,0:T(8,128)(2,1)S(1)} %fusion.5), channel_id=1, source_target_pairs={{2,0},{3,1},{0,2},{1,3},{6,4},{7,5},{4,6},{5,7},{10,8},{11,9},{8,1... | collective-permute-start | bytes 196616 | tf_op jit(solution)/shard_map/ppermute | solution.py:258
  37.0 1.4 %collective-permute-done.9 = f16[256,128]{1,0:T(8,128)(2,1)S(1)} collective-permute-done((f16[256,128]{1,0:T(8,128)(2,1)S(1)}, f16[256,128]{1,0:T(8,128)(2,1)S(1)}, u32[]{:S(2)}, u32[]{:S(2)}) %collective-permute-start.9) | collective-permute-done | bytes 65568 | tf_op jit(solution)/shard_map/ppermute | solution.py:258
  38.4 1.4 %collective-permute-done.8 = f16[256,128]{1,0:T(8,128)(2,1)S(1)} collective-permute-done((f16[256,128]{1,0:T(8,128)(2,1)S(1)}, f16[256,128]{1,0:T(8,128)(2,1)S(1)}, u32[]{:S(2)}, u32[]{:S(2)}) %collective-permute-start.8) | collective-permute-done | bytes 65568 | tf_op jit(solution)/shard_map/ppermute | solution.py:258
  39.8 0.1 pad_maximum_fusion.1
  40.0 7.7 %collective-permute-start.11 = (f16[3,128,128]{2,1,0:T(8,128)(2,1)S(1)}, f16[3,128,128]{2,1,0:T(8,128)(2,1)S(1)}, u32[]{:S(2)}, u32[]{:S(2)}) collective-permute-start(f16[3,128,128]{2,1,0:T(8,128)(2,1)S(1)} %bitcast.70), channel_id=1, source_target_pairs={{0,1},{1,0},{2,3},{3,2},{4,5},{5,4},{6,7},{7,6},{8,9},{9,8},{10,11... | collective-permute-start | bytes 294920 | tf_op jit(solution)/shard_map/ppermute | solution.py:275
  47.7 1.9 %collective-permute-start.10 = (f16[3,128,128]{2,1,0:T(8,128)(2,1)S(1)}, f16[3,128,128]{2,1,0:T(8,128)(2,1)S(1)}, u32[]{:S(2)}, u32[]{:S(2)}) collective-permute-start(f16[3,128,128]{2,1,0:T(8,128)(2,1)S(1)} %bitcast.69), channel_id=1, source_target_pairs={{1,8},{8,1},{3,10},{10,3},{5,12},{12,5},{7,14},{14,7},{9,16},{16,9... | collective-permute-start | bytes 294920 | tf_op jit(solution)/shard_map/ppermute | solution.py:276
  49.7 4.3 %collective-permute-done.10 = f16[3,128,128]{2,1,0:T(8,128)(2,1)S(1)} collective-permute-done((f16[3,128,128]{2,1,0:T(8,128)(2,1)S(1)}, f16[3,128,128]{2,1,0:T(8,128)(2,1)S(1)}, u32[]{:S(2)}, u32[]{:S(2)}) %collective-permute-start.10) | collective-permute-done | bytes 98336 | tf_op jit(solution)/shard_map/ppermute | solution.py:276
  54.0 7.9 %shard_map.65 = f32[4,256,128]{2,1,0:T(8,128)S(1)} custom-call(s32[4]{0:T(128)S(1)} %pad_add_fusion.place, f32[4,12]{1,0:T(4,128)S(1)} %concatenate.26.coef, f32[4,256,128]{2,1,0:T(8,128)S(1)} %get-tuple-element.26.current, f32[3,128,128]{2,1,0:T(8,128)S(1)} %get-tuple-element.31.below, f32[3,128,128]{2,1,0:T(8,128)S(1)} %get-tuple-element.30.above, ...), custom_call_target="tpu_custom_call" | custom-call | flops 49152000 | bytes 4194304 | tf_op jit(solution)/shard_map/pallas_call | solution.py:168
  62.0 0.3 collective-permute-start.12
  62.3 2.7 %collective-permute-start.14 = (f16[256,128]{1,0:T(8,128)(2,1)S(1)}, f16[256,128]{1,0:T(8,128)(2,1)S(1)}, u32[]{:S(2)}, u32[]{:S(2)}) collective-permute-start(f16[256,128]{1,0:T(8,128)(2,1)S(1)} %get-tuple-element.17), channel_id=1, source_target_pairs={{0,6},{1,7},{2,4},{3,5},{4,2},{5,3},{6,0},{7,1},{8,14},{9,15},{10,... | collective-permute-start | bytes 196616 | tf_op jit(solution)/shard_map/ppermute | solution.py:254
  65.0 0.2 collective-permute-done.12
  65.2 2.5 %collective-permute-done.14 = f16[256,128]{1,0:T(8,128)(2,1)S(1)} collective-permute-done((f16[256,128]{1,0:T(8,128)(2,1)S(1)}, f16[256,128]{1,0:T(8,128)(2,1)S(1)}, u32[]{:S(2)}, u32[]{:S(2)}) %collective-permute-start.14) | collective-permute-done | bytes 65568 | tf_op jit(solution)/shard_map/ppermute | solution.py:254
  67.7 4.1 %collective-permute-done.13 = f16[256,128]{1,0:T(8,128)(2,1)S(1)} collective-permute-done((f16[256,128]{1,0:T(8,128)(2,1)S(1)}, f16[256,128]{1,0:T(8,128)(2,1)S(1)}, u32[]{:S(2)}, u32[]{:S(2)}) %collective-permute-start.13) | collective-permute-done | bytes 65568 | tf_op jit(solution)/shard_map/ppermute | solution.py:254
  71.8 1.6 %collective-permute-start.17 = (f16[256,128]{1,0:T(8,128)(2,1)S(1)}, f16[256,128]{1,0:T(8,128)(2,1)S(1)}, u32[]{:S(2)}, u32[]{:S(2)}) collective-permute-start(f16[256,128]{1,0:T(8,128)(2,1)S(1)} %fusion.2), channel_id=1, source_target_pairs={{6,0},{7,1},{4,2},{5,3},{2,4},{3,5},{0,6},{1,7},{14,8},{15,9},{12,... | collective-permute-start | bytes 196616 | tf_op jit(solution)/shard_map/ppermute | solution.py:258
  73.4 2.0 %collective-permute-start.15 = (f16[256,128]{1,0:T(8,128)(2,1)S(1)}, f16[256,128]{1,0:T(8,128)(2,1)S(1)}, u32[]{:S(2)}, u32[]{:S(2)}) collective-permute-start(f16[256,128]{1,0:T(8,128)(2,1)S(1)} %fusion.2), channel_id=1, source_target_pairs={{2,0},{3,1},{0,2},{1,3},{6,4},{7,5},{4,6},{5,7},{10,8},{11,9},{8,1... | collective-permute-start | bytes 196616 | tf_op jit(solution)/shard_map/ppermute | solution.py:258
  75.4 1.4 %collective-permute-done.17 = f16[256,128]{1,0:T(8,128)(2,1)S(1)} collective-permute-done((f16[256,128]{1,0:T(8,128)(2,1)S(1)}, f16[256,128]{1,0:T(8,128)(2,1)S(1)}, u32[]{:S(2)}, u32[]{:S(2)}) %collective-permute-start.17) | collective-permute-done | bytes 65568 | tf_op jit(solution)/shard_map/ppermute | solution.py:258
  76.8 3.7 %collective-permute-done.16 = f16[256,128]{1,0:T(8,128)(2,1)S(1)} collective-permute-done((f16[256,128]{1,0:T(8,128)(2,1)S(1)}, f16[256,128]{1,0:T(8,128)(2,1)S(1)}, u32[]{:S(2)}, u32[]{:S(2)}) %collective-permute-start.16) | collective-permute-done | bytes 65568 | tf_op jit(solution)/shard_map/ppermute | solution.py:258
  80.5 0.1 pad_maximum_fusion.2
  80.7 0.1 pad_maximum_fusion.3
  80.8 0.6 collective-permute-start.18
  81.3 1.2 %collective-permute-done.18 = f16[8,128,128]{2,1,0:T(8,128)(2,1)S(1)} collective-permute-done((f16[8,128,128]{2,1,0:T(8,128)(2,1)S(1)}, f16[8,128,128]{2,1,0:T(8,128)(2,1)S(1)}, u32[]{:S(2)}, u32[]{:S(2)}) %collective-permute-start.18) | collective-permute-done | bytes 262176 | tf_op jit(solution)/shard_map/ppermute | solution.py:282
  82.5 0.1 broadcast_select_fusion.1
  82.7 1.1 %maximum_convert_fusion = f32[16,128,128]{2,1,0:T(8,128)} fusion(f16[8,128,128]{2,1,0:T(8,128)(2,1)S(1)} %get-tuple-element.11, f16[8,128,128]{2,1,0:T(8,128)(2,1)S(1)} %get-tuple-element.10), kind=kLoop, calls=%fused_computation | loop fusion | flops 524288 | bytes 1572864 | tf_op jit(solution)/shard_map/concatenate | solution.py:285
  (36 shorter events, 0.8 us)
Async XLA Ops:
  0.0 9.4 %copy-start = (bf16[2,16,128,128]{3,2,1,0:T(8,128)(2,1)S(1)}, bf16[2,16,128,128]{3,2,1,0:T(8,128)(2,1)}, u32[]{:S(2)}) copy-start(bf16[2,16,128,128]{3,2,1,0:T(8,128)(2,1)} %reward.3) | copy-start | bytes 3145732
  0.0 10.8 %collective-permute-start = (s32[2]{0:T(128)}, s32[2]{0:T(128)S(1)}, u32[]{:S(2)}, u32[]{:S(2)}) collective-permute-start(s32[2]{0:T(128)} %param.9), channel_id=1, source_target_pairs={{0,1},{1,0},{2,3},{3,2},{4,5},{5,4},{6,7},{7,6},{8,9},{9,8},{10,11... | collective-permute-start | bytes 32 | tf_op jit(solution)/shard_map/ppermute | solution.py:205
  2.3 9.9 %collective-permute-start.3 = (bf16[4,128,128]{2,1,0:T(8,128)(2,1)}, bf16[4,128,128]{2,1,0:T(8,128)(2,1)S(1)}, u32[]{:S(2)}, u32[]{:S(2)}) collective-permute-start(bf16[4,128,128]{2,1,0:T(8,128)(2,1)} %bitcast.7), channel_id=1, source_target_pairs={{0,8},{9,1},{2,10},{11,3},{4,12},{13,5},{6,14},{15,7},{8,16},{17,9... | collective-permute-start | bytes 393224 | tf_op jit(solution)/shard_map/ppermute | solution.py:220
  7.2 8.5 %copy-start.1 = (f32[16,128,128]{2,1,0:T(8,128)S(1)}, f32[16,128,128]{2,1,0:T(8,128)}, u32[]{:S(2)}) copy-start(f32[16,128,128]{2,1,0:T(8,128)} %speed.3) | copy-start | bytes 3145732
  7.3 8.5 %collective-permute-start.2 = (bf16[9,128,128]{2,1,0:T(8,128)(2,1)S(1)}, bf16[9,128,128]{2,1,0:T(8,128)(2,1)S(1)}, u32[]{:S(2)}, u32[]{:S(2)}) collective-permute-start(bf16[9,128,128]{2,1,0:T(8,128)(2,1)S(1)} %pad_maximum_fusion), channel_id=1, source_target_pairs={{1,8},{8,1},{3,10},{10,3},{5,12},{12,5},{7,14},{14,7},{9,16},{16,9... | collective-permute-start | bytes 884744 | tf_op jit(solution)/shard_map/ppermute | solution.py:218
  10.3 5.5 %collective-permute-start.1 = (bf16[2,10,128,128]{3,2,1,0:T(8,128)(2,1)}, bf16[2,10,128,128]{3,2,1,0:T(8,128)(2,1)S(1)}, u32[]{:S(2)}, u32[]{:S(2)}) collective-permute-start(bf16[2,10,128,128]{3,2,1,0:T(8,128)(2,1)} %constant_dynamic-slice_fusion.2), channel_id=1, source_target_pairs={{0,1},{1,0},{2,3},{3,2},{4,5},{5,4},{6,7},{7,6},{8,9},{9,8},{10,11... | collective-permute-start | bytes 1966088 | tf_op jit(solution)/shard_map/ppermute | solution.py:206
  10.7 0.7 copy-start.5
  10.7 0.8 copy-start.4
  10.8 0.7 copy-start.3
  15.8 1.2 %copy-start.2 = (f32[16,128,128]{2,1,0:T(8,128)S(1)}, f32[16,128,128]{2,1,0:T(8,128)}, u32[]{:S(2)}) copy-start(f32[16,128,128]{2,1,0:T(8,128)} %value.1) | copy-start | bytes 3145732
  25.1 3.7 %collective-permute-start.4 = (f16[256,128]{1,0:T(8,128)(2,1)S(1)}, f16[256,128]{1,0:T(8,128)(2,1)S(1)}, u32[]{:S(2)}, u32[]{:S(2)}) collective-permute-start(f16[256,128]{1,0:T(8,128)(2,1)S(1)} %get-tuple-element.27), channel_id=1, source_target_pairs={{0,2},{1,3},{2,0},{3,1},{4,6},{5,7},{6,4},{7,5},{8,10},{9,11},{10,... | collective-permute-start | bytes 196616 | tf_op jit(solution)/shard_map/ppermute | solution.py:254
  26.4 4.9 %collective-permute-start.6 = (f16[256,128]{1,0:T(8,128)(2,1)S(1)}, f16[256,128]{1,0:T(8,128)(2,1)S(1)}, u32[]{:S(2)}, u32[]{:S(2)}) collective-permute-start(f16[256,128]{1,0:T(8,128)(2,1)S(1)} %get-tuple-element.28), channel_id=1, source_target_pairs={{0,6},{1,7},{2,4},{3,5},{4,2},{5,3},{6,0},{7,1},{8,14},{9,15},{10,... | collective-permute-start | bytes 196616 | tf_op jit(solution)/shard_map/ppermute | solution.py:254
  28.6 4.7 %collective-permute-start.5 = (f16[256,128]{1,0:T(8,128)(2,1)S(1)}, f16[256,128]{1,0:T(8,128)(2,1)S(1)}, u32[]{:S(2)}, u32[]{:S(2)}) collective-permute-start(f16[256,128]{1,0:T(8,128)(2,1)S(1)} %get-tuple-element.29), channel_id=1, source_target_pairs={{0,4},{1,5},{2,6},{3,7},{4,0},{5,1},{6,2},{7,3},{8,12},{9,13},{10,... | collective-permute-start | bytes 196616 | tf_op jit(solution)/shard_map/ppermute | solution.py:254
  33.4 5.0 %collective-permute-start.9 = (f16[256,128]{1,0:T(8,128)(2,1)S(1)}, f16[256,128]{1,0:T(8,128)(2,1)S(1)}, u32[]{:S(2)}, u32[]{:S(2)}) collective-permute-start(f16[256,128]{1,0:T(8,128)(2,1)S(1)} %fusion.5), channel_id=1, source_target_pairs={{6,0},{7,1},{4,2},{5,3},{2,4},{3,5},{0,6},{1,7},{14,8},{15,9},{12,... | collective-permute-start | bytes 196616 | tf_op jit(solution)/shard_map/ppermute | solution.py:258
  35.1 4.7 %collective-permute-start.8 = (f16[256,128]{1,0:T(8,128)(2,1)S(1)}, f16[256,128]{1,0:T(8,128)(2,1)S(1)}, u32[]{:S(2)}, u32[]{:S(2)}) collective-permute-start(f16[256,128]{1,0:T(8,128)(2,1)S(1)} %fusion.5), channel_id=1, source_target_pairs={{4,0},{5,1},{6,2},{7,3},{0,4},{1,5},{2,6},{3,7},{12,8},{13,9},{14,... | collective-permute-start | bytes 196616 | tf_op jit(solution)/shard_map/ppermute | solution.py:258
  35.1 4.7 %collective-permute-start.7 = (f16[256,128]{1,0:T(8,128)(2,1)S(1)}, f16[256,128]{1,0:T(8,128)(2,1)S(1)}, u32[]{:S(2)}, u32[]{:S(2)}) collective-permute-start(f16[256,128]{1,0:T(8,128)(2,1)S(1)} %fusion.5), channel_id=1, source_target_pairs={{2,0},{3,1},{0,2},{1,3},{6,4},{7,5},{4,6},{5,7},{10,8},{11,9},{8,1... | collective-permute-start | bytes 196616 | tf_op jit(solution)/shard_map/ppermute | solution.py:258
  40.0 9.6 %collective-permute-start.11 = (f16[3,128,128]{2,1,0:T(8,128)(2,1)S(1)}, f16[3,128,128]{2,1,0:T(8,128)(2,1)S(1)}, u32[]{:S(2)}, u32[]{:S(2)}) collective-permute-start(f16[3,128,128]{2,1,0:T(8,128)(2,1)S(1)} %bitcast.70), channel_id=1, source_target_pairs={{0,1},{1,0},{2,3},{3,2},{4,5},{5,4},{6,7},{7,6},{8,9},{9,8},{10,11... | collective-permute-start | bytes 294920 | tf_op jit(solution)/shard_map/ppermute | solution.py:275
  47.7 6.2 %collective-permute-start.10 = (f16[3,128,128]{2,1,0:T(8,128)(2,1)S(1)}, f16[3,128,128]{2,1,0:T(8,128)(2,1)S(1)}, u32[]{:S(2)}, u32[]{:S(2)}) collective-permute-start(f16[3,128,128]{2,1,0:T(8,128)(2,1)S(1)} %bitcast.69), channel_id=1, source_target_pairs={{1,8},{8,1},{3,10},{10,3},{5,12},{12,5},{7,14},{14,7},{9,16},{16,9... | collective-permute-start | bytes 294920 | tf_op jit(solution)/shard_map/ppermute | solution.py:276
  62.0 3.2 %collective-permute-start.12 = (f16[256,128]{1,0:T(8,128)(2,1)S(1)}, f16[256,128]{1,0:T(8,128)(2,1)S(1)}, u32[]{:S(2)}, u32[]{:S(2)}) collective-permute-start(f16[256,128]{1,0:T(8,128)(2,1)S(1)} %get-tuple-element.16), channel_id=1, source_target_pairs={{0,2},{1,3},{2,0},{3,1},{4,6},{5,7},{6,4},{7,5},{8,10},{9,11},{10,... | collective-permute-start | bytes 196616 | tf_op jit(solution)/shard_map/ppermute | solution.py:254
  62.3 5.4 %collective-permute-start.14 = (f16[256,128]{1,0:T(8,128)(2,1)S(1)}, f16[256,128]{1,0:T(8,128)(2,1)S(1)}, u32[]{:S(2)}, u32[]{:S(2)}) collective-permute-start(f16[256,128]{1,0:T(8,128)(2,1)S(1)} %get-tuple-element.17), channel_id=1, source_target_pairs={{0,6},{1,7},{2,4},{3,5},{4,2},{5,3},{6,0},{7,1},{8,14},{9,15},{10,... | collective-permute-start | bytes 196616 | tf_op jit(solution)/shard_map/ppermute | solution.py:254
  65.0 6.8 %collective-permute-start.13 = (f16[256,128]{1,0:T(8,128)(2,1)S(1)}, f16[256,128]{1,0:T(8,128)(2,1)S(1)}, u32[]{:S(2)}, u32[]{:S(2)}) collective-permute-start(f16[256,128]{1,0:T(8,128)(2,1)S(1)} %get-tuple-element.18), channel_id=1, source_target_pairs={{0,4},{1,5},{2,6},{3,7},{4,0},{5,1},{6,2},{7,3},{8,12},{9,13},{10,... | collective-permute-start | bytes 196616 | tf_op jit(solution)/shard_map/ppermute | solution.py:254
  71.8 5.0 %collective-permute-start.17 = (f16[256,128]{1,0:T(8,128)(2,1)S(1)}, f16[256,128]{1,0:T(8,128)(2,1)S(1)}, u32[]{:S(2)}, u32[]{:S(2)}) collective-permute-start(f16[256,128]{1,0:T(8,128)(2,1)S(1)} %fusion.2), channel_id=1, source_target_pairs={{6,0},{7,1},{4,2},{5,3},{2,4},{3,5},{0,6},{1,7},{14,8},{15,9},{12,... | collective-permute-start | bytes 196616 | tf_op jit(solution)/shard_map/ppermute | solution.py:258
  73.4 7.1 %collective-permute-start.16 = (f16[256,128]{1,0:T(8,128)(2,1)S(1)}, f16[256,128]{1,0:T(8,128)(2,1)S(1)}, u32[]{:S(2)}, u32[]{:S(2)}) collective-permute-start(f16[256,128]{1,0:T(8,128)(2,1)S(1)} %fusion.2), channel_id=1, source_target_pairs={{4,0},{5,1},{6,2},{7,3},{0,4},{1,5},{2,6},{3,7},{12,8},{13,9},{14,... | collective-permute-start | bytes 196616 | tf_op jit(solution)/shard_map/ppermute | solution.py:258
  73.4 7.1 %collective-permute-start.15 = (f16[256,128]{1,0:T(8,128)(2,1)S(1)}, f16[256,128]{1,0:T(8,128)(2,1)S(1)}, u32[]{:S(2)}, u32[]{:S(2)}) collective-permute-start(f16[256,128]{1,0:T(8,128)(2,1)S(1)} %fusion.2), channel_id=1, source_target_pairs={{2,0},{3,1},{0,2},{1,3},{6,4},{7,5},{4,6},{5,7},{10,8},{11,9},{8,1... | collective-permute-start | bytes 196616 | tf_op jit(solution)/shard_map/ppermute | solution.py:258
  80.8 1.7 %collective-permute-start.18 = (f16[8,128,128]{2,1,0:T(8,128)(2,1)S(1)}, f16[8,128,128]{2,1,0:T(8,128)(2,1)S(1)}, u32[]{:S(2)}, u32[]{:S(2)}) collective-permute-start(f16[8,128,128]{2,1,0:T(8,128)(2,1)S(1)} %bitcast.64), channel_id=1, source_target_pairs={{0,1},{1,0},{2,3},{3,2},{4,5},{5,4},{6,7},{7,6},{8,9},{9,8},{10,11... | collective-permute-start | bytes 786440 | tf_op jit(solution)/shard_map/ppermute | solution.py:282

commit v2 on v0

v2 whole, which is shorter than its diff:
```python
import functools

import jax
import jax.numpy as jnp
from jax import lax
from jax.experimental import pallas as pl
from jax.experimental.pallas import tpu as pltpu
from jax.sharding import PartitionSpec as P

SUBSTEPS = 3
PAD = 8
LOWEST = -3.0e38


def mate(chip, step, chips):
    if chips & (chips - 1) == 0:
        return chip ^ step
    return (chip + step) % chips


def mate_step(chip, other, chips):
    if chips & (chips - 1) == 0:
        return chip ^ other
    return (other - chip) % chips


def stencil(coef, ctrl, src, row, speed, reward, winds):
    ny = src.shape[1] - 2 * PAD
    lines = pl.ds(PAD, ny)
    center = src[row, lines, :]
    y_ahead = src[row, pl.ds(PAD + 1, ny), :]
    y_behind = src[row, pl.ds(PAD - 1, ny), :]
    x_sum = src[row + 1, lines, :] + src[row - 1, lines, :]
    x_wind = src[row + winds[0], lines, :]
    nz = center.shape[1]
    lane = lax.broadcasted_iota(jnp.int32, center.shape, 1)
    z_ahead = jnp.where(lane == nz - 1, 0.0, pltpu.roll(center, nz - 1, 1))
    z_behind = jnp.where(lane == 0, 0.0, pltpu.roll(center, 1, 1))
    y_wind = jnp.where(winds[1], y_ahead, y_behind)
    z_wind = jnp.where(winds[2], z_ahead, z_behind)
    still = reward + coef[ctrl, 6] * center + coef[ctrl, 0] * x_sum
    still = still + coef[ctrl, 1] * (y_ahead + y_behind) + coef[ctrl, 2] * (z_ahead + z_behind)
    wind = coef[ctrl, 3] * x_wind + coef[ctrl, 4] * y_wind + coef[ctrl, 5] * z_wind
    return still + speed * (wind - coef[ctrl, 7] * center)


def winds_of(place, coef, ctrl):
    step = jnp.where(coef[ctrl, 8] > 0.0, 1, -1)
    return jnp.where(place[1] == 0, step, -step), coef[ctrl, 9] > 0.0, coef[ctrl, 10] > 0.0


def put_max(place, out, index, new):
    chips, width = out.shape[0], out.shape[2]
    for shard in range(chips):
        spot = mate_step(place[0], shard, chips)
        out[spot, index] = jnp.maximum(out[spot, index], new[shard * width : (shard + 1) * width])


def start_max(out):
    for shard in range(out.shape[0]):
        for row in range(out.shape[1]):
            out[shard, row] = jnp.full(out.shape[2:], LOWEST, out.dtype)


def clear_pads(field, ny):
    zero = jnp.zeros((PAD, field.shape[2]), field.dtype)
    for row in range(field.shape[0]):
        field[row, 0:PAD, :] = zero
        field[row, PAD + ny : 2 * PAD + ny, :] = zero


def lay_own(place, first, last, base, speed, reward, other, speed_rows, reward_rows):
    cells = speed.shape[0]
    own = reward.shape[0]
    for row in range(first, last):
        real = jnp.where(place[1] == 0, row, cells - 1 - row)
        speed_rows[row - base] = speed[real]
        for ctrl in range(own):
            reward_rows[ctrl, row - base] = reward[ctrl, real].astype(jnp.float32)
            reward_rows[own + ctrl, row - base] = other[ctrl, real].astype(jnp.float32)


def lay_edge(base, edge, edge_own, speed_rows, reward_rows):
    margin = SUBSTEPS - 1
    own = edge_own.shape[0] // margin
    for row in range(margin):
        spot = -1 - row - base
        speed_rows[spot] = edge[SUBSTEPS + row].astype(jnp.float32)
        for ctrl in range(own):
            reward_rows[ctrl, spot] = edge_own[ctrl * margin + row].astype(jnp.float32)
            far = edge[SUBSTEPS + margin + ctrl * margin + row]
            reward_rows[own + ctrl, spot] = far.astype(jnp.float32)


def spread(place, pieces, index, field, row):
    chips, width = pieces.shape[0], pieces.shape[2]
    for shard in range(chips):
        piece = pieces[mate_step(place[0], shard, chips), index]
        field[row, pl.ds(PAD + shard * width, width), :] = piece.astype(field.dtype)


def early_march(place, coef, known, half, block, speed_rows, reward_rows, out, keeps, fields):
    ny = block.shape[1] - 2 * PAD
    start_max(out)

    def one(ctrl, carry):
        winds = winds_of(place, coef, ctrl)
        source = block
        for substep in range(SUBSTEPS):
            for q in range(known + 1 + substep, half + SUBSTEPS - 1 - substep):
                row = q - known
                new = stencil(coef, ctrl, source, row, speed_rows[row], reward_rows[ctrl, row], winds)
                if substep == SUBSTEPS - 1:
                    put_max(place, out, q - known - SUBSTEPS, new)
                    continue
                fields[substep][row, pl.ds(PAD, ny), :] = new
                if row < substep + 3:
                    keeps[substep][ctrl, row - substep - 1] = new
            if substep < SUBSTEPS - 1:
                source = fields[substep]
        return carry

    lax.fori_loop(0, reward_rows.shape[0], one, 0)


def rest_march(place, coef, known, block, speed_rows, reward_rows, out, keeps, fields):
    ny = block.shape[1] - 2 * PAD
    inside = place[2].astype(jnp.float32)
    start_max(out)

    def one(ctrl, carry):
        winds = winds_of(place, coef, ctrl)
        source = block
        for substep in range(SUBSTEPS):
            for q in range(substep + 1 - SUBSTEPS, known + 1 + substep):
                given = q + SUBSTEPS - 1
                new = stencil(
                    coef, ctrl, source, q + SUBSTEPS, speed_rows[given], reward_rows[ctrl, given], winds
                )
                if substep == SUBSTEPS - 1:
                    put_max(place, out, q, new)
                    continue
                if q < 0:
                    new = new * inside
                fields[substep][q + SUBSTEPS, pl.ds(PAD, ny), :] = new
            if substep < SUBSTEPS - 1:
                source = fields[substep]
                for kept in range(2):
                    row = known + 1 + substep + kept + SUBSTEPS
                    source[row, pl.ds(PAD, ny), :] = keeps[substep][ctrl, kept]
        return carry

    lax.fori_loop(0, reward_rows.shape[0], one, 0)


def pack_kernel(place, value, speed, reward, edge, far):
    cells = value.shape[0]
    own = reward.shape[0]
    margin = SUBSTEPS - 1
    for row in range(SUBSTEPS):
        near = jnp.where(place[1] == 0, row, cells - 1 - row)
        away = jnp.where(place[1] == 0, cells - 1 - row, row)
        edge[row] = value[near].astype(edge.dtype)
        if row < margin:
            edge[SUBSTEPS + row] = speed[near].astype(edge.dtype)
            for ctrl in range(own):
                edge[SUBSTEPS + margin + ctrl * margin + row] = reward[ctrl, near]
                far[ctrl * margin + row] = reward[ctrl, away]


def early_first(place, coef, value, speed, reward, other, out, *refs, half):
    keeps, fields, (block, speed_rows, reward_rows) = refs[:2], refs[2:4], refs[4:]
    cells, ny = value.shape[:2]
    for field in (block, *fields):
        clear_pads(field, ny)
    for q in range(half + SUBSTEPS):
        block[q, pl.ds(PAD, ny), :] = value[jnp.where(place[1] == 0, q, cells - 1 - q)]
    lay_own(place, 1, half + SUBSTEPS - 1, 0, speed, reward, other, speed_rows, reward_rows)
    early_march(place, coef, 0, half, block, speed_rows, reward_rows, out, keeps, fields)


def rest_first(place, coef, value, speed, reward, other, edge, edge_own, *refs, half):
    keeps, out, fields, (block, speed_rows, reward_rows) = refs[:2], refs[2], refs[3:5], refs[5:]
    cells, ny = value.shape[:2]
    for field in (block, *fields):
        clear_pads(field, ny)
    for q in range(-SUBSTEPS, 2):
        if q < 0:
            block[q + SUBSTEPS, pl.ds(PAD, ny), :] = edge[-1 - q].astype(jnp.float32)
        else:
            block[q + SUBSTEPS, pl.ds(PAD, ny), :] = value[jnp.where(place[1] == 0, q, cells - 1 - q)]
    lay_edge(1 - SUBSTEPS, edge, edge_own, speed_rows, reward_rows)
    lay_own(place, 0, SUBSTEPS, 1 - SUBSTEPS, speed, reward, other, speed_rows, reward_rows)
    rest_march(place, coef, 0, block, speed_rows, reward_rows, out, keeps, fields)


def early_later(place, coef, inner, across, speed, reward, other, out, *refs, half):
    keeps, fields, (block, speed_rows, reward_rows) = refs[:2], refs[2:4], refs[4:]
    ny = speed.shape[1]
    for field in (block, *fields):
        clear_pads(field, ny)
    for q in range(SUBSTEPS, half):
        spread(place, inner, q - SUBSTEPS, block, q - SUBSTEPS)
    for row in range(SUBSTEPS):
        spread(place, across, SUBSTEPS - 1 - row, block, half + row - SUBSTEPS)
    lay_own(place, SUBSTEPS + 1, half + SUBSTEPS - 1, SUBSTEPS, speed, reward, other, speed_rows, reward_rows)
    early_march(place, coef, SUBSTEPS, half, block, speed_rows, reward_rows, out, keeps, fields)


def rest_later(place, coef, inner, outer, beyond, speed, reward, other, edge, edge_own, *refs, half):
    keeps, out, fields, (block, speed_rows, reward_rows) = refs[:2], refs[2], refs[3:5], refs[5:]
    ny = speed.shape[1]
    for field in (block, *fields):
        clear_pads(field, ny)
    for row in range(SUBSTEPS):
        spread(place, beyond, row, block, SUBSTEPS - 1 - row)
        spread(place, outer, row, block, SUBSTEPS + row)
    for row in range(2):
        spread(place, inner, row, block, 2 * SUBSTEPS + row)
    lay_edge(1 - SUBSTEPS, edge, edge_own, speed_rows, reward_rows)
    lay_own(place, 0, 2 * SUBSTEPS, 1 - SUBSTEPS, speed, reward, other, speed_rows, reward_rows)
    rest_march(place, coef, SUBSTEPS, block, speed_rows, reward_rows, out, keeps, fields)


def body(value, speed, reward, ctrl_set, drift_sets, diffusion_sets):
    own, cells, ny, nz = reward.shape
    count = 2 * own
    slabs, members = lax.axis_size("slab"), lax.axis_size("ctrl")
    chips, half = members // 2, cells // 2
    width = ny // chips
    slab, member = lax.axis_index("slab"), lax.axis_index("ctrl")
    chip, core = member // 2, member % 2
    margin = SUBSTEPS - 1
    narrow, wire = jnp.bfloat16, jnp.float16
    both = ("slab", "ctrl")

    def device(s, z, c):
        return s * members + 2 * z + c

    partners = [(i, i ^ 1) for i in range(members)]

    def facing(step):
        pairs = []
        for s in range(slabs - 1):
            for z in range(chips):
                to = mate(z, step, chips)
                pairs += [(device(s, to, 1), device(s + 1, z, 0)), (device(s + 1, to, 0), device(s, z, 1))]
        return pairs

    along = []
    for s in range(slabs - 1):
        for z in range(chips):
            along += [(device(s, z, 0), device(s + 1, z, 0)), (device(s + 1, z, 1), device(s, z, 1))]

    whole = pl.BlockSpec(memory_space=pltpu.VMEM)
    scalars = pl.BlockSpec(memory_space=pltpu.SMEM)
    place = jnp.stack(
        [
            chip,
            core,
            jnp.where(slab == jnp.where(core == 0, 0, slabs - 1), 0, 1),
        ]
    ).astype(jnp.int32)

    def shape(*dims, kind=jnp.float32):
        return jax.ShapeDtypeStruct(dims, kind)

    def call(kernel, rows, first, arrays, outs):
        field = pltpu.VMEM((rows, ny + 2 * PAD, nz), jnp.float32)
        return pl.pallas_call(
            functools.partial(kernel, half=half),
            out_shape=outs,
            in_specs=[scalars] * 2 + [whole] * len(arrays),
            out_specs=jax.tree.map(lambda _: whole, outs),
            scratch_shapes=[
                field,
                field,
                field,
                pltpu.VMEM((rows, ny, nz), jnp.float32),
                pltpu.VMEM((count, rows, ny, nz), jnp.float32),
            ],
            compiler_params=pltpu.CompilerParams(vmem_limit_bytes=32 * 2**20),
            cost_estimate=pl.CostEstimate(
                flops=25 * count * first * ny * nz, bytes_accessed=2**20, transcendentals=0
            ),
        )(place, coef, *arrays)

    keeps = [shape(count, 2, ny, nz)] * (SUBSTEPS - 1)

    other_set = lax.ppermute(ctrl_set, "ctrl", partners)
    other = lax.ppermute(reward, "ctrl", partners)
    edge_rows = SUBSTEPS + margin + own * margin
    packed, far = pl.pallas_call(
        pack_kernel,
        out_shape=[shape(edge_rows, ny, nz, kind=narrow), shape(own * margin, ny, nz, kind=narrow)],
        in_specs=[scalars] + [whole] * 3,
        out_specs=[whole] * 2,
    )(place, value, speed, reward)
    edge = lax.ppermute(packed, both, facing(0))
    edge_own = lax.ppermute(far, both, along)

    sets = jnp.concatenate([ctrl_set, other_set])
    picked = sets[:, None] == jnp.arange(drift_sets.shape[0], dtype=jnp.int32)[None, :]
    diffusion = jnp.sum(jnp.where(picked[:, :, None], diffusion_sets[None], 0.0), axis=1)
    drift = jnp.sum(jnp.where(picked[:, :, None], drift_sets[None], 0.0), axis=1)
    size = jnp.abs(drift)
    coef = jnp.concatenate(
        [
            diffusion,
            size,
            1.0 - 2.0 * jnp.sum(diffusion, axis=1, keepdims=True),
            jnp.sum(size, axis=1, keepdims=True),
            drift,
            jnp.zeros((count, 1), jnp.float32),
        ],
        axis=1,
    )

    def reduce(best):
        parts = best.astype(wire)
        mine = parts[0]
        for step in range(1, chips):
            pairs = [(2 * z + c, 2 * mate(z, step, chips) + c) for z in range(chips) for c in range(2)]
            mine = jnp.maximum(mine, lax.ppermute(parts[step], "ctrl", pairs))
        return mine

    def gather(mine):
        pieces = [mine]
        for step in range(1, chips):
            pairs = [(2 * mate(z, step, chips) + c, 2 * z + c) for z in range(chips) for c in range(2)]
            pieces.append(lax.ppermute(mine, "ctrl", pairs))
        return jnp.stack(pieces)

    steps = sum(half + SUBSTEPS - 2 - 2 * k for k in range(SUBSTEPS))
    best, *kept = call(
        early_first,
        half + SUBSTEPS,
        steps,
        (value, speed, reward, other),
        [shape(chips, half - SUBSTEPS, width, nz)] + keeps,
    )
    inner_mine = reduce(best)
    best = call(
        rest_first,
        2 * SUBSTEPS + 2,
        SUBSTEPS * SUBSTEPS,
        (value, speed, reward, other, edge, edge_own, *kept),
        shape(chips, SUBSTEPS, width, nz),
    )
    inner = gather(inner_mine)
    across = lax.ppermute(inner[:, -SUBSTEPS:], "ctrl", partners)
    outer_mine = reduce(best)
    outer = gather(outer_mine)
    beyond = jnp.stack([lax.ppermute(outer_mine, both, facing(step)) for step in range(chips)])

    inner_full = inner.astype(jnp.float32)
    best_early, *kept = call(
        early_later,
        half,
        steps - SUBSTEPS * SUBSTEPS,
        (inner_full, across.astype(jnp.float32), speed, reward, other),
        [shape(chips, half - 2 * SUBSTEPS, width, nz)] + keeps,
    )
    best_rest = call(
        rest_later,
        3 * SUBSTEPS + 2,
        2 * SUBSTEPS * SUBSTEPS,
        (
            inner_full,
            outer.astype(jnp.float32),
            beyond.astype(jnp.float32),
            speed,
            reward,
            other,
            edge,
            edge_own,
            *kept,
        ),
        shape(chips, 2 * SUBSTEPS, width, nz),
    )
    pieces = gather(reduce(jnp.concatenate([best_rest, best_early], axis=1)))

    from_partner = lax.ppermute(pieces, "ctrl", partners)
    lower = jnp.where(core == 0, pieces, from_partner)
    upper = jnp.where(core == 0, from_partner, pieces)[:, ::-1]
    slab_pieces = jnp.concatenate([lower, upper], axis=1)
    ordered = [
        lax.dynamic_index_in_dim(slab_pieces, mate_step(chip, shard, chips), 0, keepdims=False)
        for shard in range(chips)
    ]
    return jnp.concatenate(ordered, axis=1).astype(jnp.float32)


def solution(mesh):
    in_specs = (
        P("slab", None, None),
        P("slab", None, None),
        P("ctrl", "slab", None, None),
        P("ctrl"),
        P(),
        P(),
    )
    out_specs = P("slab", None, None)
    return jax.shard_map(body, mesh=mesh, in_specs=in_specs, out_specs=out_specs, check_vma=False)
```

time: 203 us -> 89.3 us (0.44); the launches traced: 199 us -> 88.5 us
  blocking collectives: 58.3 us -> 0 us
  waiting for transfers between devices: 61.3 us -> 13.9 us
  other arithmetic: 29.1 us -> 2.93 us
  starting transfers between devices: 25.3 us -> 48 us
  Pallas kernels: 0 us -> 20.9 us
  between operations: 13.8 us -> 0.33 us
  local copies, waits for them, and re-layouts: 11 us -> 2.36 us
    pmax x1 -> x0, waiting for transfers between devices: 59.4 us -> none  [merge_controls(): return lax.pmax(local_best, 'ctrl')]
    pmax x1 -> x0, blocking collectives: 58.3 us -> none  [merge_controls(): return lax.pmax(local_best, 'ctrl')]
    ppermute x8 -> x28, starting transfers between devices: 25.3 us -> 48 us  [the longest x4 15.3 us: body(): lax.ppermute(outer_mine, both, facing(step))]
    pallas_call x0 -> x5, Pallas kernels: none -> 20.9 us  [the longest x4 18.1 us: call(): pl.pallas_call(functools.partial(kernel, half=half), out_shape=outs, in_s...]
    select_n x4 -> x1, other arithmetic: 15 us -> 0.18 us  [body(): upper = jnp.where(core == 0, from_partner, pieces)[:, ::-1]]
    ppermute x8 -> x28, waiting for transfers between devices: 1.9 us -> 13.9 us  [the longest x9 6.69 us: gather(): pieces.append(lax.ppermute(mine, 'ctrl', pairs))]
    reduce_max x2 -> x0, other arithmetic: 8.81 us -> none  [merge_controls(): local_best = jnp.max(fields, axis=0)]
    unnamed x23 -> x14, local copies, waits for them, and re-layouts: 6.36 us -> 1.76 us
  transfers between devices with their start and end apart: 9 -> 28, of which waited for: 3 -> 8; matrix products, arithmetic and copies ran while one was open for 3% -> 2% of each run, Pallas kernels for 0% -> 10%
where the time goes in v2:
time: 89.3 us; the launch traced here: 88.5 us
  starting transfers between devices  48 us (54%)
  Pallas kernels  20.9 us (23%)
  waiting for transfers between devices  13.9 us (16%)
  other arithmetic  2.93 us (3%)
  local copies, waits for them, and re-layouts  2.36 us (3%)
    pallas_call x4, Pallas kernels, call(): pl.pallas_call(functools.partial(kernel, half=half), out_shape=outs, in_s...  18.1 us
    ppermute x4, starting transfers between devices, body(): lax.ppermute(outer_mine, both, facing(step))  15.3 us
    ppermute x9, starting transfers between devices, reduce(): mine = jnp.maximum(mine, lax.ppermute(parts[step], 'ctrl', pairs))  11 us
    ppermute x9, starting transfers between devices, gather(): pieces.append(lax.ppermute(mine, 'ctrl', pairs))  10.8 us
    ppermute x9, waiting for transfers between devices, gather(): pieces.append(lax.ppermute(mine, 'ctrl', pairs))  6.69 us
    ppermute x9, waiting for transfers between devices, reduce(): mine = jnp.maximum(mine, lax.ppermute(parts[step], 'ctrl', pairs))  5.09 us
    ppermute x1, starting transfers between devices, body(): edge = lax.ppermute(packed, both, facing(0))  3.63 us
    ppermute x1, starting transfers between devices, body(): edge_own = lax.ppermute(far, both, along)  3.06 us
  transfers between devices with their start and end apart: 28, of which 8 were waited for; matrix products, arithmetic and copies ran while one was open for 2% of the time, Pallas kernels for 10%

profile of v2, /device:TPU:5, one launch (start us, length us, event | category | flops | bytes accessed | tf_op | source)
XLA Modules:
  0.0 88.5 jit_solution(17879958891718316133)
XLA Ops:
  0.0 0.7 collective-permute-start.1
  0.7 0.6 pad_add_fusion.place
  1.3 2.8 %shard_map.65 = (bf16[9,128,128]{2,1,0:T(8,128)(2,1)}, bf16[4,128,128]{2,1,0:T(8,128)(2,1)}) custom-call(s32[3]{0:T(128)} %pad_add_fusion.place, f32[16,128,128]{2,1,0:T(8,128)} %value.5, f32[16,128,128]{2,1,0:T(8,128)} %speed.9, bf16[2,16,128,128]{3,2,1,0:T(8,128)(2,1)} %reward.9), custom_call_target="tpu_custom_call" | custom-call | tf_op jit(solution)/shard_map/pallas_call | solution.py:293
  4.1 3.6 %collective-permute-start.8 = (bf16[9,128,128]{2,1,0:T(8,128)(2,1)}, bf16[9,128,128]{2,1,0:T(8,128)(2,1)S(1)}, u32[]{:S(2)}, u32[]{:S(2)}) collective-permute-start(bf16[9,128,128]{2,1,0:T(8,128)(2,1)} %get-tuple-element.14), channel_id=1, source_target_pairs={{1,8},{8,1},{3,10},{10,3},{5,12},{12,5},{7,14},{14,7},{9,16},{16,9... | collective-permute-start | bytes 884744 | tf_op jit(solution)/shard_map/ppermute | solution.py:299
  7.8 3.1 %collective-permute-start.9 = (bf16[4,128,128]{2,1,0:T(8,128)(2,1)}, bf16[4,128,128]{2,1,0:T(8,128)(2,1)}, u32[]{:S(2)}, u32[]{:S(2)}) collective-permute-start(bf16[4,128,128]{2,1,0:T(8,128)(2,1)} %get-tuple-element.15), channel_id=1, source_target_pairs={{0,8},{9,1},{2,10},{11,3},{4,12},{13,5},{6,14},{15,7},{8,16},{17,9... | collective-permute-start | bytes 393224 | tf_op jit(solution)/shard_map/ppermute | solution.py:300
  11.0 0.1 select_reduce_fusion
  11.2 0.1 copy.12
  11.3 0.1 copy.11
  11.3 0.1 copy.13
  11.4 0.1 abs_reduce_fusion
  11.6 0.1 copy.14
  11.7 0.1 concatenate.17.coef
  11.8 0.5 copy-done.3
  12.3 1.2 %copy-done.2 = f32[16,128,128]{2,1,0:T(8,128)S(1)} copy-done((f32[16,128,128]{2,1,0:T(8,128)S(1)}, f32[16,128,128]{2,1,0:T(8,128)}, u32[]{:S(2)}) %copy-start.2) | copy-done | bytes 1048600
  13.5 5.8 %shard_map.64 = (f32[4,5,32,128]{3,2,1,0:T(8,128)S(1)}, f32[4,2,128,128]{3,2,1,0:T(8,128)S(1)}, f32[4,2,128,128]{3,2,1,0:T(8,128)S(1)}) custom-call(s32[3]{0:T(128)S(1)} %copy-done.3, f32[4,12]{1,0:T(4,128)S(1)} %concatenate.17.coef, f32[16,128,128]{2,1,0:T(8,128)S(1)} %copy-done.2, f32[16,128,128]{2,1,0:T(8,128)S(1)} %copy-done, ...), custom_call_target="tpu_custom_call" | custom-call | flops 34406400 | bytes 1048576 | tf_op jit(solution)/shard_map/pallas_call | solution.py:270
  19.3 3.3 %shard_map.66 = f32[4,3,32,128]{3,2,1,0:T(8,128)S(1)} custom-call(s32[3]{0:T(128)S(1)} %copy-done.3, f32[4,12]{1,0:T(4,128)S(1)} %concatenate.17.coef, f32[16,128,128]{2,1,0:T(8,128)S(1)} %copy-done.2, f32[16,128,128]{2,1,0:T(8,128)S(1)} %copy-done, bf16[2,16,128,128]{3,2,1,0:T(8,128)(2,1)S(1)} %copy-done.1, ...), custom_call_target="tpu_custom_call" | custom-call | flops 14745600 | bytes 1048576 | tf_op jit(solution)/shard_map/pallas_call | solution.py:270
  22.7 3.4 %collective-permute-start.12 = (f16[3,32,128]{2,1,0:T(8,128)(2,1)S(1)}, f16[3,32,128]{2,1,0:T(8,128)(2,1)S(1)}, u32[]{:S(2)}, u32[]{:S(2)}) collective-permute-start(f16[3,32,128]{2,1,0:T(8,128)(2,1)S(1)} %get-tuple-element.39), channel_id=1, source_target_pairs={{0,6},{1,7},{2,4},{3,5},{4,2},{5,3},{6,0},{7,1},{8,14},{9,15},{10,... | collective-permute-start | bytes 73736 | tf_op jit(solution)/shard_map/ppermute | solution.py:324
  26.1 0.4 collective-permute-start.10
  26.5 3.2 %collective-permute-start.4 = (f16[5,32,128]{2,1,0:T(8,128)(2,1)S(1)}, f16[5,32,128]{2,1,0:T(8,128)(2,1)S(1)}, u32[]{:S(2)}, u32[]{:S(2)}) collective-permute-start(f16[5,32,128]{2,1,0:T(8,128)(2,1)S(1)} %get-tuple-element.36), channel_id=1, source_target_pairs={{0,6},{1,7},{2,4},{3,5},{4,2},{5,3},{6,0},{7,1},{8,14},{9,15},{10,... | collective-permute-start | bytes 122888 | tf_op jit(solution)/shard_map/ppermute | solution.py:324
  29.8 0.4 collective-permute-start.2
  30.2 3.2 %collective-permute-start.15 = (f16[3,32,128]{2,1,0:T(8,128)(2,1)S(1)}, f16[3,32,128]{2,1,0:T(8,128)(2,1)S(1)}, u32[]{:S(2)}, u32[]{:S(2)}) collective-permute-start(f16[3,32,128]{2,1,0:T(8,128)(2,1)S(1)} %fusion.23), channel_id=1, source_target_pairs={{6,0},{7,1},{4,2},{5,3},{2,4},{3,5},{0,6},{1,7},{14,8},{15,9},{12,... | collective-permute-start | bytes 73736 | tf_op jit(solution)/shard_map/ppermute | solution.py:331
  33.4 0.4 collective-permute-start.13
  33.8 8.1 %collective-permute-start.19 = (f16[3,32,128]{2,1,0:T(8,128)(2,1)S(1)}, f16[3,32,128]{2,1,0:T(8,128)(2,1)S(1)}, u32[]{:S(2)}, u32[]{:S(2)}) collective-permute-start(f16[3,32,128]{2,1,0:T(8,128)(2,1)S(1)} %fusion.23), channel_id=1, source_target_pairs={{7,8},{14,1},{5,10},{12,3},{3,12},{10,5},{1,14},{8,7},{15,16},{22,... | collective-permute-start | bytes 73736 | tf_op jit(solution)/shard_map/ppermute | solution.py:354
  41.9 1.9 %collective-permute-start.18 = (f16[3,32,128]{2,1,0:T(8,128)(2,1)S(1)}, f16[3,32,128]{2,1,0:T(8,128)(2,1)S(1)}, u32[]{:S(2)}, u32[]{:S(2)}) collective-permute-start(f16[3,32,128]{2,1,0:T(8,128)(2,1)S(1)} %fusion.23), channel_id=1, source_target_pairs={{5,8},{12,1},{7,10},{14,3},{1,12},{8,5},{3,14},{10,7},{13,16},{20,... | collective-permute-start | bytes 73736 | tf_op jit(solution)/shard_map/ppermute | solution.py:354
  44.0 1.4 %collective-permute-start.6 = (f16[5,32,128]{2,1,0:T(8,128)(2,1)S(1)}, f16[5,32,128]{2,1,0:T(8,128)(2,1)S(1)}, u32[]{:S(2)}, u32[]{:S(2)}) collective-permute-start(f16[5,32,128]{2,1,0:T(8,128)(2,1)S(1)} %fusion.20), channel_id=1, source_target_pairs={{4,0},{5,1},{6,2},{7,3},{0,4},{1,5},{2,6},{3,7},{12,8},{13,9},{14,... | collective-permute-start | bytes 122888 | tf_op jit(solution)/shard_map/ppermute | solution.py:331
  45.4 2.1 %collective-permute-start.5 = (f16[5,32,128]{2,1,0:T(8,128)(2,1)S(1)}, f16[5,32,128]{2,1,0:T(8,128)(2,1)S(1)}, u32[]{:S(2)}, u32[]{:S(2)}) collective-permute-start(f16[5,32,128]{2,1,0:T(8,128)(2,1)S(1)} %fusion.20), channel_id=1, source_target_pairs={{2,0},{3,1},{0,2},{1,3},{6,4},{7,5},{4,6},{5,7},{10,8},{11,9},{8,1... | collective-permute-start | bytes 122888 | tf_op jit(solution)/shard_map/ppermute | solution.py:331
  47.6 1.6 %collective-permute-done.7 = f16[5,32,128]{2,1,0:T(8,128)(2,1)S(1)} collective-permute-done((f16[5,32,128]{2,1,0:T(8,128)(2,1)S(1)}, f16[5,32,128]{2,1,0:T(8,128)(2,1)S(1)}, u32[]{:S(2)}, u32[]{:S(2)}) %collective-permute-start.7) | collective-permute-done | bytes 40992 | tf_op jit(solution)/shard_map/ppermute | solution.py:331
  49.2 3.3 %collective-permute-start.17 = (f16[3,32,128]{2,1,0:T(8,128)(2,1)S(1)}, f16[3,32,128]{2,1,0:T(8,128)(2,1)S(1)}, u32[]{:S(2)}, u32[]{:S(2)}) collective-permute-start(f16[3,32,128]{2,1,0:T(8,128)(2,1)S(1)} %fusion.23), channel_id=1, source_target_pairs={{3,8},{10,1},{1,10},{8,3},{7,12},{14,5},{5,14},{12,7},{11,16},{18,... | collective-permute-start | bytes 73736 | tf_op jit(solution)/shard_map/ppermute | solution.py:354
  52.5 1.9 %collective-permute-start.16 = (f16[3,32,128]{2,1,0:T(8,128)(2,1)S(1)}, f16[3,32,128]{2,1,0:T(8,128)(2,1)S(1)}, u32[]{:S(2)}, u32[]{:S(2)}) collective-permute-start(f16[3,32,128]{2,1,0:T(8,128)(2,1)S(1)} %fusion.23), channel_id=1, source_target_pairs={{1,8},{8,1},{3,10},{10,3},{5,12},{12,5},{7,14},{14,7},{9,16},{16,9... | collective-permute-start | bytes 73736 | tf_op jit(solution)/shard_map/ppermute | solution.py:354
  54.6 3.0 %collective-permute-start.20 = (f16[4,3,32,128]{3,2,1,0:T(8,128)(2,1)S(1)}, f16[4,3,32,128]{3,2,1,0:T(8,128)(2,1)S(1)}, u32[]{:S(2)}, u32[]{:S(2)}) collective-permute-start(f16[4,3,32,128]{3,2,1,0:T(8,128)(2,1)S(1)} %slice.60), channel_id=1, source_target_pairs={{0,1},{1,0},{2,3},{3,2},{4,5},{5,4},{6,7},{7,6},{8,9},{9,8},{10,11... | collective-permute-start | bytes 294920 | tf_op jit(solution)/shard_map/ppermute | solution.py:351
  57.6 0.1 collective-permute-done.16
  57.7 0.8 collective-permute-done.20
  58.5 3.6 %shard_map.67 = (f32[4,2,32,128]{3,2,1,0:T(8,128)S(1)}, f32[4,2,128,128]{3,2,1,0:T(8,128)S(1)}, f32[4,2,128,128]{3,2,1,0:T(8,128)S(1)}) custom-call(s32[3]{0:T(128)S(1)} %copy-done.3, f32[4,12]{1,0:T(4,128)S(1)} %concatenate.17.coef, f32[4,5,32,128]{3,2,1,0:T(8,128)S(1)} %get-tuple-element.34.inner, f32[4,3,32,128]{3,2,1,0:T(8,128)S(1)} %convert_element_type.27.across, ...), custom_call_target="tpu_custom_call" | custom-call | flops 19660800 | bytes 1048576 | tf_op jit(solution)/shard_map/pallas_call | solution.py:270
  62.1 5.5 %shard_map.68 = f32[4,6,32,128]{3,2,1,0:T(8,128)S(1)} custom-call(s32[3]{0:T(128)S(1)} %copy-done.3, f32[4,12]{1,0:T(4,128)S(1)} %concatenate.17.coef, f32[4,5,32,128]{3,2,1,0:T(8,128)S(1)} %get-tuple-element.34.inner, f32[4,3,32,128]{3,2,1,0:T(8,128)S(1)} %maximum_convert_fusion.1.outer, f32[4,3,32,128]{3,2,1,0:T(8,128)S(1)} %maximum_convert_fusion.2.beyond, ...), custom_call_target="tpu_custom_call" | custom-call | flops 29491200 | bytes 1048576 | tf_op jit(solution)/shard_map/pallas_call | solution.py:270
  67.7 1.7 %collective-permute-start.23 = (f16[8,32,128]{2,1,0:T(8,128)(2,1)S(1)}, f16[8,32,128]{2,1,0:T(8,128)(2,1)S(1)}, u32[]{:S(2)}, u32[]{:S(2)}) collective-permute-start(f16[8,32,128]{2,1,0:T(8,128)(2,1)S(1)} %get-tuple-element.31), channel_id=1, source_target_pairs={{0,6},{1,7},{2,4},{3,5},{4,2},{5,3},{6,0},{7,1},{8,14},{9,15},{10,... | collective-permute-start | bytes 196616 | tf_op jit(solution)/shard_map/ppermute | solution.py:324
  69.4 1.9 %collective-permute-start.21 = (f16[8,32,128]{2,1,0:T(8,128)(2,1)S(1)}, f16[8,32,128]{2,1,0:T(8,128)(2,1)S(1)}, u32[]{:S(2)}, u32[]{:S(2)}) collective-permute-start(f16[8,32,128]{2,1,0:T(8,128)(2,1)S(1)} %get-tuple-element.30), channel_id=1, source_target_pairs={{0,2},{1,3},{2,0},{3,1},{4,6},{5,7},{6,4},{7,5},{8,10},{9,11},{10,... | collective-permute-start | bytes 196616 | tf_op jit(solution)/shard_map/ppermute | solution.py:324
  71.3 1.4 %collective-permute-done.23 = f16[8,32,128]{2,1,0:T(8,128)(2,1)S(1)} collective-permute-done((f16[8,32,128]{2,1,0:T(8,128)(2,1)S(1)}, f16[8,32,128]{2,1,0:T(8,128)(2,1)S(1)}, u32[]{:S(2)}, u32[]{:S(2)}) %collective-permute-start.23) | collective-permute-done | bytes 65568 | tf_op jit(solution)/shard_map/ppermute | solution.py:324
  72.7 3.7 %collective-permute-done.22 = f16[8,32,128]{2,1,0:T(8,128)(2,1)S(1)} collective-permute-done((f16[8,32,128]{2,1,0:T(8,128)(2,1)S(1)}, f16[8,32,128]{2,1,0:T(8,128)(2,1)S(1)}, u32[]{:S(2)}, u32[]{:S(2)}) %collective-permute-start.22) | collective-permute-done | bytes 65568 | tf_op jit(solution)/shard_map/ppermute | solution.py:324
  76.4 1.7 %collective-permute-start.26 = (f16[8,32,128]{2,1,0:T(8,128)(2,1)S(1)}, f16[8,32,128]{2,1,0:T(8,128)(2,1)S(1)}, u32[]{:S(2)}, u32[]{:S(2)}) collective-permute-start(f16[8,32,128]{2,1,0:T(8,128)(2,1)S(1)} %fusion.14), channel_id=1, source_target_pairs={{6,0},{7,1},{4,2},{5,3},{2,4},{3,5},{0,6},{1,7},{14,8},{15,9},{12,... | collective-permute-start | bytes 196616 | tf_op jit(solution)/shard_map/ppermute | solution.py:331
  78.1 1.9 %collective-permute-start.24 = (f16[8,32,128]{2,1,0:T(8,128)(2,1)S(1)}, f16[8,32,128]{2,1,0:T(8,128)(2,1)S(1)}, u32[]{:S(2)}, u32[]{:S(2)}) collective-permute-start(f16[8,32,128]{2,1,0:T(8,128)(2,1)S(1)} %fusion.14), channel_id=1, source_target_pairs={{2,0},{3,1},{0,2},{1,3},{6,4},{7,5},{4,6},{5,7},{10,8},{11,9},{8,1... | collective-permute-start | bytes 196616 | tf_op jit(solution)/shard_map/ppermute | solution.py:331
  80.0 1.4 %collective-permute-done.26 = f16[8,32,128]{2,1,0:T(8,128)(2,1)S(1)} collective-permute-done((f16[8,32,128]{2,1,0:T(8,128)(2,1)S(1)}, f16[8,32,128]{2,1,0:T(8,128)(2,1)S(1)}, u32[]{:S(2)}, u32[]{:S(2)}) %collective-permute-start.26) | collective-permute-done | bytes 65568 | tf_op jit(solution)/shard_map/ppermute | solution.py:331
  81.5 3.7 %collective-permute-done.25 = f16[8,32,128]{2,1,0:T(8,128)(2,1)S(1)} collective-permute-done((f16[8,32,128]{2,1,0:T(8,128)(2,1)S(1)}, f16[8,32,128]{2,1,0:T(8,128)(2,1)S(1)}, u32[]{:S(2)}, u32[]{:S(2)}) %collective-permute-start.25) | collective-permute-done | bytes 65568 | tf_op jit(solution)/shard_map/ppermute | solution.py:331
  85.1 0.1 pad_maximum_fusion
  85.2 0.6 collective-permute-start.27
  85.8 1.2 %collective-permute-done.27 = f16[4,8,32,128]{3,2,1,0:T(8,128)(2,1)S(1)} collective-permute-done((f16[4,8,32,128]{3,2,1,0:T(8,128)(2,1)S(1)}, f16[4,8,32,128]{3,2,1,0:T(8,128)(2,1)S(1)}, u32[]{:S(2)}, u32[]{:S(2)}) %collective-permute-start.27) | collective-permute-done | bytes 262176 | tf_op jit(solution)/shard_map/ppermute | solution.py:383
  86.9 0.2 broadcast_select_fusion
  87.2 0.2 fusion.3
  87.3 1.1 %maximum_convert_fusion = f32[16,128,128]{2,1,0:T(8,128)} fusion(f16[16,32,128]{2,1,0:T(8,128)(2,1)S(1)} %get-tuple-element.27, f16[16,32,128]{2,1,0:T(8,128)(2,1)S(1)} %get-tuple-element.26, f16[16,32,128]{2,1,0:T(8,128)(2,1)S(1)} %get-tuple-element.25, f16[16,32,128]{2,1,0:T(8,128)(2,1)S(1)} %get-tuple-element.24), kind=kLoop, calls=%fused_computation.8 | loop fusion | flops 1048576 | bytes 1572864 | tf_op jit(solution)/shard_map/convert_element_type | solution.py:391
  (59 shorter events, 0.8 us)
Async XLA Ops:
  0.0 11.8 %collective-permute-start.1 = (bf16[2,16,128,128]{3,2,1,0:T(8,128)(2,1)}, bf16[2,16,128,128]{3,2,1,0:T(8,128)(2,1)S(1)}, u32[]{:S(2)}, u32[]{:S(2)}) collective-permute-start(bf16[2,16,128,128]{3,2,1,0:T(8,128)(2,1)} %reward.9), channel_id=1, source_target_pairs={{0,1},{1,0},{2,3},{3,2},{4,5},{5,4},{6,7},{7,6},{8,9},{9,8},{10,11... | collective-permute-start | bytes 3145736 | tf_op jit(solution)/shard_map/ppermute | solution.py:291
  0.7 10.2 %collective-permute-start = (s32[2]{0:T(128)}, s32[2]{0:T(128)S(1)}, u32[]{:S(2)}, u32[]{:S(2)}) collective-permute-start(s32[2]{0:T(128)} %param.9), channel_id=1, source_target_pairs={{0,1},{1,0},{2,3},{3,2},{4,5},{5,4},{6,7},{7,6},{8,9},{9,8},{10,11... | collective-permute-start | bytes 32 | tf_op jit(solution)/shard_map/ppermute | solution.py:290
  1.3 10.5 %copy-start = (f32[16,128,128]{2,1,0:T(8,128)S(1)}, f32[16,128,128]{2,1,0:T(8,128)}, u32[]{:S(2)}) copy-start(f32[16,128,128]{2,1,0:T(8,128)} %speed.9) | copy-start | bytes 3145732
  1.3 10.5 %copy-start.1 = (bf16[2,16,128,128]{3,2,1,0:T(8,128)(2,1)S(1)}, bf16[2,16,128,128]{3,2,1,0:T(8,128)(2,1)}, u32[]{:S(2)}) copy-start(bf16[2,16,128,128]{3,2,1,0:T(8,128)(2,1)} %reward.9) | copy-start | bytes 3145732
  4.1 6.7 %copy-start.6 = (s32[2]{0:T(128)S(1)}, s32[2]{0:T(128)}, u32[]{:S(2)}) copy-start(s32[2]{0:T(128)} %param.9) | copy-start | bytes 28
  4.1 15.2 %collective-permute-start.8 = (bf16[9,128,128]{2,1,0:T(8,128)(2,1)}, bf16[9,128,128]{2,1,0:T(8,128)(2,1)S(1)}, u32[]{:S(2)}, u32[]{:S(2)}) collective-permute-start(bf16[9,128,128]{2,1,0:T(8,128)(2,1)} %get-tuple-element.14), channel_id=1, source_target_pairs={{1,8},{8,1},{3,10},{10,3},{5,12},{12,5},{7,14},{14,7},{9,16},{16,9... | collective-permute-start | bytes 884744 | tf_op jit(solution)/shard_map/ppermute | solution.py:299
  7.7 3.3 %copy-start.5 = (f32[16,3]{0,1:T(4,128)S(1)}, f32[16,3]{0,1:T(4,128)}, u32[]{:S(2)}) copy-start(f32[16,3]{0,1:T(4,128)} %param.10) | copy-start | bytes 580
  7.8 3.3 %copy-start.4 = (f32[16,3]{0,1:T(4,128)S(1)}, f32[16,3]{0,1:T(4,128)}, u32[]{:S(2)}) copy-start(f32[16,3]{0,1:T(4,128)} %param.11) | copy-start | bytes 580
  7.8 11.5 %collective-permute-start.9 = (bf16[4,128,128]{2,1,0:T(8,128)(2,1)}, bf16[4,128,128]{2,1,0:T(8,128)(2,1)}, u32[]{:S(2)}, u32[]{:S(2)}) collective-permute-start(bf16[4,128,128]{2,1,0:T(8,128)(2,1)} %get-tuple-element.15), channel_id=1, source_target_pairs={{0,8},{9,1},{2,10},{11,3},{4,12},{13,5},{6,14},{15,7},{8,16},{17,9... | collective-permute-start | bytes 393224 | tf_op jit(solution)/shard_map/ppermute | solution.py:300
  11.7 0.6 copy-start.3
  12.3 1.2 %copy-start.2 = (f32[16,128,128]{2,1,0:T(8,128)S(1)}, f32[16,128,128]{2,1,0:T(8,128)}, u32[]{:S(2)}) copy-start(f32[16,128,128]{2,1,0:T(8,128)} %value.5) | copy-start | bytes 3145732
  22.7 7.0 %collective-permute-start.12 = (f16[3,32,128]{2,1,0:T(8,128)(2,1)S(1)}, f16[3,32,128]{2,1,0:T(8,128)(2,1)S(1)}, u32[]{:S(2)}, u32[]{:S(2)}) collective-permute-start(f16[3,32,128]{2,1,0:T(8,128)(2,1)S(1)} %get-tuple-element.39), channel_id=1, source_target_pairs={{0,6},{1,7},{2,4},{3,5},{4,2},{5,3},{6,0},{7,1},{8,14},{9,15},{10,... | collective-permute-start | bytes 73736 | tf_op jit(solution)/shard_map/ppermute | solution.py:324
  26.1 4.0 %collective-permute-start.11 = (f16[3,32,128]{2,1,0:T(8,128)(2,1)S(1)}, f16[3,32,128]{2,1,0:T(8,128)(2,1)S(1)}, u32[]{:S(2)}, u32[]{:S(2)}) collective-permute-start(f16[3,32,128]{2,1,0:T(8,128)(2,1)S(1)} %get-tuple-element.40), channel_id=1, source_target_pairs={{0,4},{1,5},{2,6},{3,7},{4,0},{5,1},{6,2},{7,3},{8,12},{9,13},{10,... | collective-permute-start | bytes 73736 | tf_op jit(solution)/shard_map/ppermute | solution.py:324
  26.1 4.0 %collective-permute-start.10 = (f16[3,32,128]{2,1,0:T(8,128)(2,1)S(1)}, f16[3,32,128]{2,1,0:T(8,128)(2,1)S(1)}, u32[]{:S(2)}, u32[]{:S(2)}) collective-permute-start(f16[3,32,128]{2,1,0:T(8,128)(2,1)S(1)} %get-tuple-element.38), channel_id=1, source_target_pairs={{0,2},{1,3},{2,0},{3,1},{4,6},{5,7},{6,4},{7,5},{8,10},{9,11},{10,... | collective-permute-start | bytes 73736 | tf_op jit(solution)/shard_map/ppermute | solution.py:324
  26.5 6.9 %collective-permute-start.4 = (f16[5,32,128]{2,1,0:T(8,128)(2,1)S(1)}, f16[5,32,128]{2,1,0:T(8,128)(2,1)S(1)}, u32[]{:S(2)}, u32[]{:S(2)}) collective-permute-start(f16[5,32,128]{2,1,0:T(8,128)(2,1)S(1)} %get-tuple-element.36), channel_id=1, source_target_pairs={{0,6},{1,7},{2,4},{3,5},{4,2},{5,3},{6,0},{7,1},{8,14},{9,15},{10,... | collective-permute-start | bytes 122888 | tf_op jit(solution)/shard_map/ppermute | solution.py:324
  29.7 4.0 %collective-permute-start.3 = (f16[5,32,128]{2,1,0:T(8,128)(2,1)S(1)}, f16[5,32,128]{2,1,0:T(8,128)(2,1)S(1)}, u32[]{:S(2)}, u32[]{:S(2)}) collective-permute-start(f16[5,32,128]{2,1,0:T(8,128)(2,1)S(1)} %get-tuple-element.37), channel_id=1, source_target_pairs={{0,4},{1,5},{2,6},{3,7},{4,0},{5,1},{6,2},{7,3},{8,12},{9,13},{10,... | collective-permute-start | bytes 122888 | tf_op jit(solution)/shard_map/ppermute | solution.py:324
  29.8 12.2 %collective-permute-start.2 = (f16[5,32,128]{2,1,0:T(8,128)(2,1)S(1)}, f16[5,32,128]{2,1,0:T(8,128)(2,1)S(1)}, u32[]{:S(2)}, u32[]{:S(2)}) collective-permute-start(f16[5,32,128]{2,1,0:T(8,128)(2,1)S(1)} %get-tuple-element.35), channel_id=1, source_target_pairs={{0,2},{1,3},{2,0},{3,1},{4,6},{5,7},{6,4},{7,5},{8,10},{9,11},{10,... | collective-permute-start | bytes 122888 | tf_op jit(solution)/shard_map/ppermute | solution.py:324
  30.2 13.7 %collective-permute-start.15 = (f16[3,32,128]{2,1,0:T(8,128)(2,1)S(1)}, f16[3,32,128]{2,1,0:T(8,128)(2,1)S(1)}, u32[]{:S(2)}, u32[]{:S(2)}) collective-permute-start(f16[3,32,128]{2,1,0:T(8,128)(2,1)S(1)} %fusion.23), channel_id=1, source_target_pairs={{6,0},{7,1},{4,2},{5,3},{2,4},{3,5},{0,6},{1,7},{14,8},{15,9},{12,... | collective-permute-start | bytes 73736 | tf_op jit(solution)/shard_map/ppermute | solution.py:331
  33.4 10.6 %collective-permute-start.14 = (f16[3,32,128]{2,1,0:T(8,128)(2,1)S(1)}, f16[3,32,128]{2,1,0:T(8,128)(2,1)S(1)}, u32[]{:S(2)}, u32[]{:S(2)}) collective-permute-start(f16[3,32,128]{2,1,0:T(8,128)(2,1)S(1)} %fusion.23), channel_id=1, source_target_pairs={{4,0},{5,1},{6,2},{7,3},{0,4},{1,5},{2,6},{3,7},{12,8},{13,9},{14,... | collective-permute-start | bytes 73736 | tf_op jit(solution)/shard_map/ppermute | solution.py:331
  33.4 12.0 %collective-permute-start.13 = (f16[3,32,128]{2,1,0:T(8,128)(2,1)S(1)}, f16[3,32,128]{2,1,0:T(8,128)(2,1)S(1)}, u32[]{:S(2)}, u32[]{:S(2)}) collective-permute-start(f16[3,32,128]{2,1,0:T(8,128)(2,1)S(1)} %fusion.23), channel_id=1, source_target_pairs={{2,0},{3,1},{0,2},{1,3},{6,4},{7,5},{4,6},{5,7},{10,8},{11,9},{8,1... | collective-permute-start | bytes 73736 | tf_op jit(solution)/shard_map/ppermute | solution.py:331
  33.8 23.8 %collective-permute-start.19 = (f16[3,32,128]{2,1,0:T(8,128)(2,1)S(1)}, f16[3,32,128]{2,1,0:T(8,128)(2,1)S(1)}, u32[]{:S(2)}, u32[]{:S(2)}) collective-permute-start(f16[3,32,128]{2,1,0:T(8,128)(2,1)S(1)} %fusion.23), channel_id=1, source_target_pairs={{7,8},{14,1},{5,10},{12,3},{3,12},{10,5},{1,14},{8,7},{15,16},{22,... | collective-permute-start | bytes 73736 | tf_op jit(solution)/shard_map/ppermute | solution.py:354
  41.9 15.6 %collective-permute-start.18 = (f16[3,32,128]{2,1,0:T(8,128)(2,1)S(1)}, f16[3,32,128]{2,1,0:T(8,128)(2,1)S(1)}, u32[]{:S(2)}, u32[]{:S(2)}) collective-permute-start(f16[3,32,128]{2,1,0:T(8,128)(2,1)S(1)} %fusion.23), channel_id=1, source_target_pairs={{5,8},{12,1},{7,10},{14,3},{1,12},{8,5},{3,14},{10,7},{13,16},{20,... | collective-permute-start | bytes 73736 | tf_op jit(solution)/shard_map/ppermute | solution.py:354
  43.9 5.3 %collective-permute-start.7 = (f16[5,32,128]{2,1,0:T(8,128)(2,1)S(1)}, f16[5,32,128]{2,1,0:T(8,128)(2,1)S(1)}, u32[]{:S(2)}, u32[]{:S(2)}) collective-permute-start(f16[5,32,128]{2,1,0:T(8,128)(2,1)S(1)} %fusion.20), channel_id=1, source_target_pairs={{6,0},{7,1},{4,2},{5,3},{2,4},{3,5},{0,6},{1,7},{14,8},{15,9},{12,... | collective-permute-start | bytes 122888 | tf_op jit(solution)/shard_map/ppermute | solution.py:331
  44.0 8.5 %collective-permute-start.6 = (f16[5,32,128]{2,1,0:T(8,128)(2,1)S(1)}, f16[5,32,128]{2,1,0:T(8,128)(2,1)S(1)}, u32[]{:S(2)}, u32[]{:S(2)}) collective-permute-start(f16[5,32,128]{2,1,0:T(8,128)(2,1)S(1)} %fusion.20), channel_id=1, source_target_pairs={{4,0},{5,1},{6,2},{7,3},{0,4},{1,5},{2,6},{3,7},{12,8},{13,9},{14,... | collective-permute-start | bytes 122888 | tf_op jit(solution)/shard_map/ppermute | solution.py:331
  45.4 9.0 %collective-permute-start.5 = (f16[5,32,128]{2,1,0:T(8,128)(2,1)S(1)}, f16[5,32,128]{2,1,0:T(8,128)(2,1)S(1)}, u32[]{:S(2)}, u32[]{:S(2)}) collective-permute-start(f16[5,32,128]{2,1,0:T(8,128)(2,1)S(1)} %fusion.20), channel_id=1, source_target_pairs={{2,0},{3,1},{0,2},{1,3},{6,4},{7,5},{4,6},{5,7},{10,8},{11,9},{8,1... | collective-permute-start | bytes 122888 | tf_op jit(solution)/shard_map/ppermute | solution.py:331
  49.2 8.4 %collective-permute-start.17 = (f16[3,32,128]{2,1,0:T(8,128)(2,1)S(1)}, f16[3,32,128]{2,1,0:T(8,128)(2,1)S(1)}, u32[]{:S(2)}, u32[]{:S(2)}) collective-permute-start(f16[3,32,128]{2,1,0:T(8,128)(2,1)S(1)} %fusion.23), channel_id=1, source_target_pairs={{3,8},{10,1},{1,10},{8,3},{7,12},{14,5},{5,14},{12,7},{11,16},{18,... | collective-permute-start | bytes 73736 | tf_op jit(solution)/shard_map/ppermute | solution.py:354
  52.5 5.1 %collective-permute-start.16 = (f16[3,32,128]{2,1,0:T(8,128)(2,1)S(1)}, f16[3,32,128]{2,1,0:T(8,128)(2,1)S(1)}, u32[]{:S(2)}, u32[]{:S(2)}) collective-permute-start(f16[3,32,128]{2,1,0:T(8,128)(2,1)S(1)} %fusion.23), channel_id=1, source_target_pairs={{1,8},{8,1},{3,10},{10,3},{5,12},{12,5},{7,14},{14,7},{9,16},{16,9... | collective-permute-start | bytes 73736 | tf_op jit(solution)/shard_map/ppermute | solution.py:354
  54.6 3.9 %collective-permute-start.20 = (f16[4,3,32,128]{3,2,1,0:T(8,128)(2,1)S(1)}, f16[4,3,32,128]{3,2,1,0:T(8,128)(2,1)S(1)}, u32[]{:S(2)}, u32[]{:S(2)}) collective-permute-start(f16[4,3,32,128]{3,2,1,0:T(8,128)(2,1)S(1)} %slice.60), channel_id=1, source_target_pairs={{0,1},{1,0},{2,3},{3,2},{4,5},{5,4},{6,7},{7,6},{8,9},{9,8},{10,11... | collective-permute-start | bytes 294920 | tf_op jit(solution)/shard_map/ppermute | solution.py:351
  67.7 5.0 %collective-permute-start.23 = (f16[8,32,128]{2,1,0:T(8,128)(2,1)S(1)}, f16[8,32,128]{2,1,0:T(8,128)(2,1)S(1)}, u32[]{:S(2)}, u32[]{:S(2)}) collective-permute-start(f16[8,32,128]{2,1,0:T(8,128)(2,1)S(1)} %get-tuple-element.31), channel_id=1, source_target_pairs={{0,6},{1,7},{2,4},{3,5},{4,2},{5,3},{6,0},{7,1},{8,14},{9,15},{10,... | collective-permute-start | bytes 196616 | tf_op jit(solution)/shard_map/ppermute | solution.py:324
  69.3 7.0 %collective-permute-start.22 = (f16[8,32,128]{2,1,0:T(8,128)(2,1)S(1)}, f16[8,32,128]{2,1,0:T(8,128)(2,1)S(1)}, u32[]{:S(2)}, u32[]{:S(2)}) collective-permute-start(f16[8,32,128]{2,1,0:T(8,128)(2,1)S(1)} %get-tuple-element.32), channel_id=1, source_target_pairs={{0,4},{1,5},{2,6},{3,7},{4,0},{5,1},{6,2},{7,3},{8,12},{9,13},{10,... | collective-permute-start | bytes 196616 | tf_op jit(solution)/shard_map/ppermute | solution.py:324
  69.4 7.0 %collective-permute-start.21 = (f16[8,32,128]{2,1,0:T(8,128)(2,1)S(1)}, f16[8,32,128]{2,1,0:T(8,128)(2,1)S(1)}, u32[]{:S(2)}, u32[]{:S(2)}) collective-permute-start(f16[8,32,128]{2,1,0:T(8,128)(2,1)S(1)} %get-tuple-element.30), channel_id=1, source_target_pairs={{0,2},{1,3},{2,0},{3,1},{4,6},{5,7},{6,4},{7,5},{8,10},{9,11},{10,... | collective-permute-start | bytes 196616 | tf_op jit(solution)/shard_map/ppermute | solution.py:324
  76.4 5.0 %collective-permute-start.26 = (f16[8,32,128]{2,1,0:T(8,128)(2,1)S(1)}, f16[8,32,128]{2,1,0:T(8,128)(2,1)S(1)}, u32[]{:S(2)}, u32[]{:S(2)}) collective-permute-start(f16[8,32,128]{2,1,0:T(8,128)(2,1)S(1)} %fusion.14), channel_id=1, source_target_pairs={{6,0},{7,1},{4,2},{5,3},{2,4},{3,5},{0,6},{1,7},{14,8},{15,9},{12,... | collective-permute-start | bytes 196616 | tf_op jit(solution)/shard_map/ppermute | solution.py:331
  78.1 7.0 %collective-permute-start.25 = (f16[8,32,128]{2,1,0:T(8,128)(2,1)S(1)}, f16[8,32,128]{2,1,0:T(8,128)(2,1)S(1)}, u32[]{:S(2)}, u32[]{:S(2)}) collective-permute-start(f16[8,32,128]{2,1,0:T(8,128)(2,1)S(1)} %fusion.14), channel_id=1, source_target_pairs={{4,0},{5,1},{6,2},{7,3},{0,4},{1,5},{2,6},{3,7},{12,8},{13,9},{14,... | collective-permute-start | bytes 196616 | tf_op jit(solution)/shard_map/ppermute | solution.py:331
  78.1 7.0 %collective-permute-start.24 = (f16[8,32,128]{2,1,0:T(8,128)(2,1)S(1)}, f16[8,32,128]{2,1,0:T(8,128)(2,1)S(1)}, u32[]{:S(2)}, u32[]{:S(2)}) collective-permute-start(f16[8,32,128]{2,1,0:T(8,128)(2,1)S(1)} %fusion.14), channel_id=1, source_target_pairs={{2,0},{3,1},{0,2},{1,3},{6,4},{7,5},{4,6},{5,7},{10,8},{11,9},{8,1... | collective-permute-start | bytes 196616 | tf_op jit(solution)/shard_map/ppermute | solution.py:331
  85.2 1.7 %collective-permute-start.27 = (f16[4,8,32,128]{3,2,1,0:T(8,128)(2,1)S(1)}, f16[4,8,32,128]{3,2,1,0:T(8,128)(2,1)S(1)}, u32[]{:S(2)}, u32[]{:S(2)}) collective-permute-start(f16[4,8,32,128]{3,2,1,0:T(8,128)(2,1)S(1)} %pad_maximum_fusion), channel_id=1, source_target_pairs={{0,1},{1,0},{2,3},{3,2},{4,5},{5,4},{6,7},{7,6},{8,9},{9,8},{10,11... | collective-permute-start | bytes 786440 | tf_op jit(solution)/shard_map/ppermute | solution.py:383

commit v3 on v2

--- a/solution.py
+++ b/solution.py
@@ -153,19 +153,32 @@
     lax.fori_loop(0, reward_rows.shape[0], one, 0)
 
 
-def pack_kernel(place, value, speed, reward, edge, far):
+def pack_kernel(place, value, speed, reward, edge, far, value_rows, speed_rows, value_sem, speed_sem, near_sem, far_sem):
     cells = value.shape[0]
     own = reward.shape[0]
     margin = SUBSTEPS - 1
+    copies, later = [], []
     for row in range(SUBSTEPS):
         near = jnp.where(place[1] == 0, row, cells - 1 - row)
         away = jnp.where(place[1] == 0, cells - 1 - row, row)
-        edge[row] = value[near].astype(edge.dtype)
+        copies.append(pltpu.make_async_copy(value.at[near], value_rows.at[row], value_sem.at[row]))
         if row < margin:
-            edge[SUBSTEPS + row] = speed[near].astype(edge.dtype)
+            copies.append(pltpu.make_async_copy(speed.at[near], speed_rows.at[row], speed_sem.at[row]))
             for ctrl in range(own):
-                edge[SUBSTEPS + margin + ctrl * margin + row] = reward[ctrl, near]
-                far[ctrl * margin + row] = reward[ctrl, away]
+                spot = ctrl * margin + row
+                place_near = edge.at[SUBSTEPS + margin + spot]
+                later.append(pltpu.make_async_copy(reward.at[ctrl, near], place_near, near_sem.at[spot]))
+                later.append(pltpu.make_async_copy(reward.at[ctrl, away], far.at[spot], far_sem.at[spot]))
+    for copy in copies + later:
+        copy.start()
+    for copy in copies:
+        copy.wait()
+    for row in range(SUBSTEPS):
+        edge[row] = value_rows[row].astype(edge.dtype)
+    for row in range(margin):
+        edge[SUBSTEPS + row] = speed_rows[row].astype(edge.dtype)
+    for copy in later:
+        copy.wait()
 
 
 def early_first(place, coef, value, speed, reward, other, out, *refs, half):
@@ -194,32 +207,31 @@
     rest_march(place, coef, 0, block, speed_rows, reward_rows, out, keeps, fields)
 
 
-def early_later(place, coef, inner, across, speed, reward, other, out, *refs, half):
+def early_later(place, coef, current, across, speed, reward, other, out, *refs, half):
     keeps, fields, (block, speed_rows, reward_rows) = refs[:2], refs[2:4], refs[4:]
     ny = speed.shape[1]
     for field in (block, *fields):
         clear_pads(field, ny)
-    for q in range(SUBSTEPS, half):
-        spread(place, inner, q - SUBSTEPS, block, q - SUBSTEPS)
+    for q in range(half):
+        spread(place, current, q, block, q)
     for row in range(SUBSTEPS):
-        spread(place, across, SUBSTEPS - 1 - row, block, half + row - SUBSTEPS)
-    lay_own(place, SUBSTEPS + 1, half + SUBSTEPS - 1, SUBSTEPS, speed, reward, other, speed_rows, reward_rows)
-    early_march(place, coef, SUBSTEPS, half, block, speed_rows, reward_rows, out, keeps, fields)
-
-
-def rest_later(place, coef, inner, outer, beyond, speed, reward, other, edge, edge_own, *refs, half):
+        spread(place, across, SUBSTEPS - 1 - row, block, half + row)
+    lay_own(place, 1, half + SUBSTEPS - 1, 0, speed, reward, other, speed_rows, reward_rows)
+    early_march(place, coef, 0, half, block, speed_rows, reward_rows, out, keeps, fields)
+
+
+def rest_later(place, coef, current, beyond, speed, reward, other, edge, edge_own, *refs, half):
     keeps, out, fields, (block, speed_rows, reward_rows) = refs[:2], refs[2], refs[3:5], refs[5:]
     ny = speed.shape[1]
     for field in (block, *fields):
         clear_pads(field, ny)
     for row in range(SUBSTEPS):
         spread(place, beyond, row, block, SUBSTEPS - 1 - row)
-        spread(place, outer, row, block, SUBSTEPS + row)
     for row in range(2):
-        spread(place, inner, row, block, 2 * SUBSTEPS + row)
+        spread(place, current, row, block, SUBSTEPS + row)
     lay_edge(1 - SUBSTEPS, edge, edge_own, speed_rows, reward_rows)
-    lay_own(place, 0, 2 * SUBSTEPS, 1 - SUBSTEPS, speed, reward, other, speed_rows, reward_rows)
-    rest_march(place, coef, SUBSTEPS, block, speed_rows, reward_rows, out, keeps, fields)
+    lay_own(place, 0, SUBSTEPS, 1 - SUBSTEPS, speed, reward, other, speed_rows, reward_rows)
+    rest_march(place, coef, 0, block, speed_rows, reward_rows, out, keeps, fields)
 
 
 def body(value, speed, reward, ctrl_set, drift_sets, diffusion_sets):
@@ -290,11 +302,20 @@
     other_set = lax.ppermute(ctrl_set, "ctrl", partners)
     other = lax.ppermute(reward, "ctrl", partners)
     edge_rows = SUBSTEPS + margin + own * margin
+    dma = pltpu.SemaphoreType.DMA
     packed, far = pl.pallas_call(
         pack_kernel,
         out_shape=[shape(edge_rows, ny, nz, kind=narrow), shape(own * margin, ny, nz, kind=narrow)],
-        in_specs=[scalars] + [whole] * 3,
+        in_specs=[scalars] + [pl.BlockSpec(memory_space=pl.ANY)] * 3,
         out_specs=[whole] * 2,
+        scratch_shapes=[
+            pltpu.VMEM((SUBSTEPS, ny, nz), jnp.float32),
+            pltpu.VMEM((margin, ny, nz), jnp.float32),
+            dma((SUBSTEPS,)),
+            dma((margin,)),
+            dma((own * margin,)),
+            dma((own * margin,)),
+        ],
     )(place, value, speed, reward)
     edge = lax.ppermute(packed, both, facing(0))
     edge_own = lax.ppermute(far, both, along)
@@ -339,46 +360,33 @@
         (value, speed, reward, other),
         [shape(chips, half - SUBSTEPS, width, nz)] + keeps,
     )
-    inner_mine = reduce(best)
-    best = call(
+    best_rest = call(
         rest_first,
         2 * SUBSTEPS + 2,
         SUBSTEPS * SUBSTEPS,
         (value, speed, reward, other, edge, edge_own, *kept),
         shape(chips, SUBSTEPS, width, nz),
     )
-    inner = gather(inner_mine)
-    across = lax.ppermute(inner[:, -SUBSTEPS:], "ctrl", partners)
-    outer_mine = reduce(best)
-    outer = gather(outer_mine)
-    beyond = jnp.stack([lax.ppermute(outer_mine, both, facing(step)) for step in range(chips)])
-
-    inner_full = inner.astype(jnp.float32)
-    best_early, *kept = call(
+    pieces = gather(reduce(jnp.concatenate([best_rest, best], axis=1)))
+
+    across = lax.ppermute(pieces[:, -SUBSTEPS:], "ctrl", partners)
+    beyond = lax.ppermute(pieces[:, :SUBSTEPS], both, facing(0))
+    current = pieces.astype(jnp.float32)
+    best, *kept = call(
         early_later,
-        half,
-        steps - SUBSTEPS * SUBSTEPS,
-        (inner_full, across.astype(jnp.float32), speed, reward, other),
-        [shape(chips, half - 2 * SUBSTEPS, width, nz)] + keeps,
+        half + SUBSTEPS,
+        steps,
+        (current, across.astype(jnp.float32), speed, reward, other),
+        [shape(chips, half - SUBSTEPS, width, nz)] + keeps,
     )
     best_rest = call(
         rest_later,
-        3 * SUBSTEPS + 2,
-        2 * SUBSTEPS * SUBSTEPS,
-        (
-            inner_full,
-            outer.astype(jnp.float32),
-            beyond.astype(jnp.float32),
-            speed,
-            reward,
-            other,
-            edge,
-            edge_own,
-            *kept,
-        ),
-        shape(chips, 2 * SUBSTEPS, width, nz),
-    )
-    pieces = gather(reduce(jnp.concatenate([best_rest, best_early], axis=1)))
+        2 * SUBSTEPS + 2,
+        SUBSTEPS * SUBSTEPS,
+        (current, beyond.astype(jnp.float32), speed, reward, other, edge, edge_own, *kept),
+        shape(chips, SUBSTEPS, width, nz),
+    )
+    pieces = gather(reduce(jnp.concatenate([best_rest, best], axis=1)))
 
     from_partner = lax.ppermute(pieces, "ctrl", partners)
     lower = jnp.where(core == 0, pieces, from_partner)

time: 89.3 us -> 74.9 us (0.84)
  starting transfers between devices: 48 us -> 26.1 us
  waiting for transfers between devices: 13.9 us -> 22 us
    ppermute x5 -> x2, starting transfers between devices: 18.3 us -> 3.68 us  [the longest x1 2.96 us: body(): beyond = lax.ppermute(pieces[:, :SUBSTEPS], both, facing(0))]
    ppermute x9 -> x6, waiting for transfers between devices: 5.09 us -> 10.4 us  [reduce(): mine = jnp.maximum(mine, lax.ppermute(parts[step], 'ctrl', pairs))]
    ppermute x9 -> x6, waiting for transfers between devices: 6.69 us -> 10.4 us  [gather(): pieces.append(lax.ppermute(mine, 'ctrl', pairs))]
    ppermute x9 -> x6, starting transfers between devices: 11 us -> 7.36 us  [reduce(): mine = jnp.maximum(mine, lax.ppermute(parts[step], 'ctrl', pairs))]
    ppermute x9 -> x6, starting transfers between devices: 10.8 us -> 7.23 us  [gather(): pieces.append(lax.ppermute(mine, 'ctrl', pairs))]
    ppermute x5 -> x2, waiting for transfers between devices: 0.91 us -> 0.01 us  [the longest x1 0.01 us: body(): across = lax.ppermute(pieces[:, -SUBSTEPS:], 'ctrl', partners)]
  transfers between devices with their start and end apart: 28 -> 19, of which waited for: 8 -> 9; matrix products, arithmetic and copies ran while one was open for 2% -> 2% of each run, Pallas kernels for 10% -> 19%
where the time goes in v3:
time: 74.9 us; the launch traced here: 74.6 us
  starting transfers between devices  26.1 us (35%)
  waiting for transfers between devices  22 us (29%)
  Pallas kernels  20.9 us (28%)
  other arithmetic  2.97 us (4%)
  local copies, waits for them, and re-layouts  2.33 us (3%)
    pallas_call x4, Pallas kernels, call(): pl.pallas_call(functools.partial(kernel, half=half), out_shape=outs, in_s...  18.2 us
    ppermute x6, waiting for transfers between devices, reduce(): mine = jnp.maximum(mine, lax.ppermute(parts[step], 'ctrl', pairs))  10.4 us
    ppermute x6, waiting for transfers between devices, gather(): pieces.append(lax.ppermute(mine, 'ctrl', pairs))  10.4 us
    ppermute x6, starting transfers between devices, reduce(): mine = jnp.maximum(mine, lax.ppermute(parts[step], 'ctrl', pairs))  7.36 us
    ppermute x6, starting transfers between devices, gather(): pieces.append(lax.ppermute(mine, 'ctrl', pairs))  7.23 us
    ppermute x1, starting transfers between devices, body(): edge = lax.ppermute(packed, both, facing(0))  3.51 us
    ppermute x1, starting transfers between devices, body(): edge_own = lax.ppermute(far, both, along)  3.06 us
    ppermute x1, starting transfers between devices, body(): beyond = lax.ppermute(pieces[:, :SUBSTEPS], both, facing(0))  2.96 us
  transfers between devices with their start and end apart: 19, of which 9 were waited for; matrix products, arithmetic and copies ran while one was open for 2% of the time, Pallas kernels for 19%

profile of v3, /device:TPU:5, one launch (start us, length us, event | category | flops | bytes accessed | tf_op | source)
XLA Modules:
  0.0 74.6 jit_solution(795449902141132604)
XLA Ops:
  0.0 0.7 collective-permute-start.1
  0.7 0.6 pad_add_fusion.place
  1.3 2.8 %shard_map.64 = (bf16[9,128,128]{2,1,0:T(8,128)(2,1)}, bf16[4,128,128]{2,1,0:T(8,128)(2,1)}) custom-call(s32[3]{0:T(128)} %pad_add_fusion.place, f32[16,128,128]{2,1,0:T(8,128)} %value.5, f32[16,128,128]{2,1,0:T(8,128)} %speed.9, bf16[2,16,128,128]{3,2,1,0:T(8,128)(2,1)} %reward.9), custom_call_target="tpu_custom_call" | custom-call | tf_op jit(solution)/shard_map/pallas_call | solution.py:306
  4.0 3.5 %collective-permute-start.2 = (bf16[9,128,128]{2,1,0:T(8,128)(2,1)}, bf16[9,128,128]{2,1,0:T(8,128)(2,1)S(1)}, u32[]{:S(2)}, u32[]{:S(2)}) collective-permute-start(bf16[9,128,128]{2,1,0:T(8,128)(2,1)} %get-tuple-element.13), channel_id=1, source_target_pairs={{1,8},{8,1},{3,10},{10,3},{5,12},{12,5},{7,14},{14,7},{9,16},{16,9... | collective-permute-start | bytes 884744 | tf_op jit(solution)/shard_map/ppermute | solution.py:320
  7.6 3.1 %collective-permute-start.3 = (bf16[4,128,128]{2,1,0:T(8,128)(2,1)}, bf16[4,128,128]{2,1,0:T(8,128)(2,1)}, u32[]{:S(2)}, u32[]{:S(2)}) collective-permute-start(bf16[4,128,128]{2,1,0:T(8,128)(2,1)} %get-tuple-element.14), channel_id=1, source_target_pairs={{0,8},{9,1},{2,10},{11,3},{4,12},{13,5},{6,14},{15,7},{8,16},{17,9... | collective-permute-start | bytes 393224 | tf_op jit(solution)/shard_map/ppermute | solution.py:321
  10.7 0.1 pad_add_fusion.1
  10.8 0.1 iota_compare_fusion
  10.8 0.1 select_reduce_fusion
  11.0 0.1 copy.12
  11.1 0.1 copy.11
  11.2 0.1 copy.13
  11.3 0.1 abs_reduce_fusion
  11.4 0.1 copy.14
  11.5 0.1 concatenate.21.coef
  11.6 0.5 copy-done.3
  12.1 1.2 %copy-done.2 = f32[16,128,128]{2,1,0:T(8,128)S(1)} copy-done((f32[16,128,128]{2,1,0:T(8,128)S(1)}, f32[16,128,128]{2,1,0:T(8,128)}, u32[]{:S(2)}) %copy-start.2) | copy-done | bytes 1048600
  13.3 5.8 %shard_map.65 = (f32[4,5,32,128]{3,2,1,0:T(8,128)S(1)}, f32[4,2,128,128]{3,2,1,0:T(8,128)S(1)}, f32[4,2,128,128]{3,2,1,0:T(8,128)S(1)}) custom-call(s32[3]{0:T(128)S(1)} %copy-done.3, f32[4,12]{1,0:T(4,128)S(1)} %concatenate.21.coef, f32[16,128,128]{2,1,0:T(8,128)S(1)} %copy-done.2, f32[16,128,128]{2,1,0:T(8,128)S(1)} %copy-done, ...), custom_call_target="tpu_custom_call" | custom-call | flops 34406400 | bytes 1048576 | tf_op jit(solution)/shard_map/pallas_call | solution.py:282
  19.1 3.3 %shard_map.66 = f32[4,3,32,128]{3,2,1,0:T(8,128)S(1)} custom-call(s32[3]{0:T(128)S(1)} %copy-done.3, f32[4,12]{1,0:T(4,128)S(1)} %concatenate.21.coef, f32[16,128,128]{2,1,0:T(8,128)S(1)} %copy-done.2, f32[16,128,128]{2,1,0:T(8,128)S(1)} %copy-done, bf16[2,16,128,128]{3,2,1,0:T(8,128)(2,1)S(1)} %copy-done.1, ...), custom_call_target="tpu_custom_call" | custom-call | flops 14745600 | bytes 1048576 | tf_op jit(solution)/shard_map/pallas_call | solution.py:282
  22.5 0.1 fusion.25
  22.6 3.4 %collective-permute-start.6 = (f16[8,32,128]{2,1,0:T(8,128)(2,1)S(1)}, f16[8,32,128]{2,1,0:T(8,128)(2,1)S(1)}, u32[]{:S(2)}, u32[]{:S(2)}) collective-permute-start(f16[8,32,128]{2,1,0:T(8,128)(2,1)S(1)} %get-tuple-element.38), channel_id=1, source_target_pairs={{0,6},{1,7},{2,4},{3,5},{4,2},{5,3},{6,0},{7,1},{8,14},{9,15},{10,... | collective-permute-start | bytes 196616 | tf_op jit(solution)/shard_map/ppermute | solution.py:345
  26.0 0.4 collective-permute-start.4
  26.3 1.9 %collective-permute-done.6 = f16[8,32,128]{2,1,0:T(8,128)(2,1)S(1)} collective-permute-done((f16[8,32,128]{2,1,0:T(8,128)(2,1)S(1)}, f16[8,32,128]{2,1,0:T(8,128)(2,1)S(1)}, u32[]{:S(2)}, u32[]{:S(2)}) %collective-permute-start.6) | collective-permute-done | bytes 65568 | tf_op jit(solution)/shard_map/ppermute | solution.py:345
  28.2 3.4 %collective-permute-done.5 = f16[8,32,128]{2,1,0:T(8,128)(2,1)S(1)} collective-permute-done((f16[8,32,128]{2,1,0:T(8,128)(2,1)S(1)}, f16[8,32,128]{2,1,0:T(8,128)(2,1)S(1)}, u32[]{:S(2)}, u32[]{:S(2)}) %collective-permute-start.5) | collective-permute-done | bytes 65568 | tf_op jit(solution)/shard_map/ppermute | solution.py:345
  31.7 2.3 %collective-permute-start.9 = (f16[8,32,128]{2,1,0:T(8,128)(2,1)S(1)}, f16[8,32,128]{2,1,0:T(8,128)(2,1)S(1)}, u32[]{:S(2)}, u32[]{:S(2)}) collective-permute-start(f16[8,32,128]{2,1,0:T(8,128)(2,1)S(1)} %fusion.23), channel_id=1, source_target_pairs={{6,0},{7,1},{4,2},{5,3},{2,4},{3,5},{0,6},{1,7},{14,8},{15,9},{12,... | collective-permute-start | bytes 196616 | tf_op jit(solution)/shard_map/ppermute | solution.py:352
  34.0 1.3 %collective-permute-start.7 = (f16[8,32,128]{2,1,0:T(8,128)(2,1)S(1)}, f16[8,32,128]{2,1,0:T(8,128)(2,1)S(1)}, u32[]{:S(2)}, u32[]{:S(2)}) collective-permute-start(f16[8,32,128]{2,1,0:T(8,128)(2,1)S(1)} %fusion.23), channel_id=1, source_target_pairs={{2,0},{3,1},{0,2},{1,3},{6,4},{7,5},{4,6},{5,7},{10,8},{11,9},{8,1... | collective-permute-start | bytes 196616 | tf_op jit(solution)/shard_map/ppermute | solution.py:352
  35.3 1.5 %collective-permute-done.9 = f16[8,32,128]{2,1,0:T(8,128)(2,1)S(1)} collective-permute-done((f16[8,32,128]{2,1,0:T(8,128)(2,1)S(1)}, f16[8,32,128]{2,1,0:T(8,128)(2,1)S(1)}, u32[]{:S(2)}, u32[]{:S(2)}) %collective-permute-start.9) | collective-permute-done | bytes 65568 | tf_op jit(solution)/shard_map/ppermute | solution.py:352
  36.8 3.8 %collective-permute-done.8 = f16[8,32,128]{2,1,0:T(8,128)(2,1)S(1)} collective-permute-done((f16[8,32,128]{2,1,0:T(8,128)(2,1)S(1)}, f16[8,32,128]{2,1,0:T(8,128)(2,1)S(1)}, u32[]{:S(2)}, u32[]{:S(2)}) %collective-permute-start.8) | collective-permute-done | bytes 65568 | tf_op jit(solution)/shard_map/ppermute | solution.py:352
  40.7 0.1 pad_maximum_fusion
  40.8 0.7 collective-permute-start.11
  41.5 3.0 %collective-permute-start.10 = (f16[4,3,32,128]{3,2,1,0:T(8,128)(2,1)S(1)}, f16[4,3,32,128]{3,2,1,0:T(8,128)(2,1)S(1)}, u32[]{:S(2)}, u32[]{:S(2)}) collective-permute-start(f16[4,3,32,128]{3,2,1,0:T(8,128)(2,1)S(1)} %get-tuple-element.33), channel_id=1, source_target_pairs={{1,8},{8,1},{3,10},{10,3},{5,12},{12,5},{7,14},{14,7},{9,16},{16,9... | collective-permute-start | bytes 294920 | tf_op jit(solution)/shard_map/ppermute | solution.py:373
  44.6 5.8 %shard_map.67 = (f32[4,5,32,128]{3,2,1,0:T(8,128)S(1)}, f32[4,2,128,128]{3,2,1,0:T(8,128)S(1)}, f32[4,2,128,128]{3,2,1,0:T(8,128)S(1)}) custom-call(s32[3]{0:T(128)S(1)} %copy-done.3, f32[4,12]{1,0:T(4,128)S(1)} %concatenate.21.coef, f32[4,8,32,128]{3,2,1,0:T(8,128)S(1)} %get-tuple-element.36.current, f32[4,3,32,128]{3,2,1,0:T(8,128)S(1)} %convert_element_type.16.across, ...), custom_call_target="tpu_custom_call" | custom-call | flops 34406400 | bytes 1048576 | tf_op jit(solution)/shard_map/pallas_call | solution.py:282
  50.4 3.3 %shard_map.68 = f32[4,3,32,128]{3,2,1,0:T(8,128)S(1)} custom-call(s32[3]{0:T(128)S(1)} %copy-done.3, f32[4,12]{1,0:T(4,128)S(1)} %concatenate.21.coef, f32[4,8,32,128]{3,2,1,0:T(8,128)S(1)} %get-tuple-element.36.current, f32[4,3,32,128]{3,2,1,0:T(8,128)S(1)} %convert_element_type.15.beyond, f32[16,128,128]{2,1,0:T(8,128)S(1)} %copy-done, ...), custom_call_target="tpu_custom_call" | custom-call | flops 14745600 | bytes 1048576 | tf_op jit(solution)/shard_map/pallas_call | solution.py:282
  53.8 0.1 fusion.16
  53.8 1.6 %collective-permute-start.14 = (f16[8,32,128]{2,1,0:T(8,128)(2,1)S(1)}, f16[8,32,128]{2,1,0:T(8,128)(2,1)S(1)}, u32[]{:S(2)}, u32[]{:S(2)}) collective-permute-start(f16[8,32,128]{2,1,0:T(8,128)(2,1)S(1)} %get-tuple-element.31), channel_id=1, source_target_pairs={{0,6},{1,7},{2,4},{3,5},{4,2},{5,3},{6,0},{7,1},{8,14},{9,15},{10,... | collective-permute-start | bytes 196616 | tf_op jit(solution)/shard_map/ppermute | solution.py:345
  55.4 2.0 %collective-permute-start.12 = (f16[8,32,128]{2,1,0:T(8,128)(2,1)S(1)}, f16[8,32,128]{2,1,0:T(8,128)(2,1)S(1)}, u32[]{:S(2)}, u32[]{:S(2)}) collective-permute-start(f16[8,32,128]{2,1,0:T(8,128)(2,1)S(1)} %get-tuple-element.30), channel_id=1, source_target_pairs={{0,2},{1,3},{2,0},{3,1},{4,6},{5,7},{6,4},{7,5},{8,10},{9,11},{10,... | collective-permute-start | bytes 196616 | tf_op jit(solution)/shard_map/ppermute | solution.py:345
  57.4 1.4 %collective-permute-done.14 = f16[8,32,128]{2,1,0:T(8,128)(2,1)S(1)} collective-permute-done((f16[8,32,128]{2,1,0:T(8,128)(2,1)S(1)}, f16[8,32,128]{2,1,0:T(8,128)(2,1)S(1)}, u32[]{:S(2)}, u32[]{:S(2)}) %collective-permute-start.14) | collective-permute-done | bytes 65568 | tf_op jit(solution)/shard_map/ppermute | solution.py:345
  58.8 3.7 %collective-permute-done.13 = f16[8,32,128]{2,1,0:T(8,128)(2,1)S(1)} collective-permute-done((f16[8,32,128]{2,1,0:T(8,128)(2,1)S(1)}, f16[8,32,128]{2,1,0:T(8,128)(2,1)S(1)}, u32[]{:S(2)}, u32[]{:S(2)}) %collective-permute-start.13) | collective-permute-done | bytes 65568 | tf_op jit(solution)/shard_map/ppermute | solution.py:345
  62.6 1.6 %collective-permute-start.17 = (f16[8,32,128]{2,1,0:T(8,128)(2,1)S(1)}, f16[8,32,128]{2,1,0:T(8,128)(2,1)S(1)}, u32[]{:S(2)}, u32[]{:S(2)}) collective-permute-start(f16[8,32,128]{2,1,0:T(8,128)(2,1)S(1)} %fusion.14), channel_id=1, source_target_pairs={{6,0},{7,1},{4,2},{5,3},{2,4},{3,5},{0,6},{1,7},{14,8},{15,9},{12,... | collective-permute-start | bytes 196616 | tf_op jit(solution)/shard_map/ppermute | solution.py:352
  64.1 2.0 %collective-permute-start.15 = (f16[8,32,128]{2,1,0:T(8,128)(2,1)S(1)}, f16[8,32,128]{2,1,0:T(8,128)(2,1)S(1)}, u32[]{:S(2)}, u32[]{:S(2)}) collective-permute-start(f16[8,32,128]{2,1,0:T(8,128)(2,1)S(1)} %fusion.14), channel_id=1, source_target_pairs={{2,0},{3,1},{0,2},{1,3},{6,4},{7,5},{4,6},{5,7},{10,8},{11,9},{8,1... | collective-permute-start | bytes 196616 | tf_op jit(solution)/shard_map/ppermute | solution.py:352
  66.2 1.4 %collective-permute-done.17 = f16[8,32,128]{2,1,0:T(8,128)(2,1)S(1)} collective-permute-done((f16[8,32,128]{2,1,0:T(8,128)(2,1)S(1)}, f16[8,32,128]{2,1,0:T(8,128)(2,1)S(1)}, u32[]{:S(2)}, u32[]{:S(2)}) %collective-permute-start.17) | collective-permute-done | bytes 65568 | tf_op jit(solution)/shard_map/ppermute | solution.py:352
  67.6 3.7 %collective-permute-done.16 = f16[8,32,128]{2,1,0:T(8,128)(2,1)S(1)} collective-permute-done((f16[8,32,128]{2,1,0:T(8,128)(2,1)S(1)}, f16[8,32,128]{2,1,0:T(8,128)(2,1)S(1)}, u32[]{:S(2)}, u32[]{:S(2)}) %collective-permute-start.16) | collective-permute-done | bytes 65568 | tf_op jit(solution)/shard_map/ppermute | solution.py:352
  71.3 0.1 pad_maximum_fusion.1
  71.3 0.6 collective-permute-start.18
  71.9 1.2 %collective-permute-done.18 = f16[4,8,32,128]{3,2,1,0:T(8,128)(2,1)S(1)} collective-permute-done((f16[4,8,32,128]{3,2,1,0:T(8,128)(2,1)S(1)}, f16[4,8,32,128]{3,2,1,0:T(8,128)(2,1)S(1)}, u32[]{:S(2)}, u32[]{:S(2)}) %collective-permute-start.18) | collective-permute-done | bytes 262176 | tf_op jit(solution)/shard_map/ppermute | solution.py:391
  73.1 0.2 broadcast_select_fusion
  73.3 0.1 rev.3
  73.3 0.2 fusion.3
  73.5 1.1 %maximum_convert_fusion = f32[16,128,128]{2,1,0:T(8,128)} fusion(f16[16,32,128]{2,1,0:T(8,128)(2,1)S(1)} %get-tuple-element.27, f16[16,32,128]{2,1,0:T(8,128)(2,1)S(1)} %get-tuple-element.26, f16[16,32,128]{2,1,0:T(8,128)(2,1)S(1)} %get-tuple-element.25, f16[16,32,128]{2,1,0:T(8,128)(2,1)S(1)} %get-tuple-element.24), kind=kLoop, calls=%fused_computation.8 | loop fusion | flops 1048576 | bytes 1572864 | tf_op jit(solution)/shard_map/convert_element_type | solution.py:399
  (38 shorter events, 0.3 us)
Async XLA Ops:
  0.0 11.6 %collective-permute-start.1 = (bf16[2,16,128,128]{3,2,1,0:T(8,128)(2,1)}, bf16[2,16,128,128]{3,2,1,0:T(8,128)(2,1)S(1)}, u32[]{:S(2)}, u32[]{:S(2)}) collective-permute-start(bf16[2,16,128,128]{3,2,1,0:T(8,128)(2,1)} %reward.9), channel_id=1, source_target_pairs={{0,1},{1,0},{2,3},{3,2},{4,5},{5,4},{6,7},{7,6},{8,9},{9,8},{10,11... | collective-permute-start | bytes 3145736 | tf_op jit(solution)/shard_map/ppermute | solution.py:303
  0.7 10.0 %collective-permute-start = (s32[2]{0:T(128)}, s32[2]{0:T(128)S(1)}, u32[]{:S(2)}, u32[]{:S(2)}) collective-permute-start(s32[2]{0:T(128)} %param.9), channel_id=1, source_target_pairs={{0,1},{1,0},{2,3},{3,2},{4,5},{5,4},{6,7},{7,6},{8,9},{9,8},{10,11... | collective-permute-start | bytes 32 | tf_op jit(solution)/shard_map/ppermute | solution.py:302
  1.3 10.3 %copy-start = (f32[16,128,128]{2,1,0:T(8,128)S(1)}, f32[16,128,128]{2,1,0:T(8,128)}, u32[]{:S(2)}) copy-start(f32[16,128,128]{2,1,0:T(8,128)} %speed.9) | copy-start | bytes 3145732
  1.3 10.3 %copy-start.1 = (bf16[2,16,128,128]{3,2,1,0:T(8,128)(2,1)S(1)}, bf16[2,16,128,128]{3,2,1,0:T(8,128)(2,1)}, u32[]{:S(2)}) copy-start(bf16[2,16,128,128]{3,2,1,0:T(8,128)(2,1)} %reward.9) | copy-start | bytes 3145732
  4.0 6.6 %copy-start.6 = (s32[2]{0:T(128)S(1)}, s32[2]{0:T(128)}, u32[]{:S(2)}) copy-start(s32[2]{0:T(128)} %param.9) | copy-start | bytes 28
  4.0 15.1 %collective-permute-start.2 = (bf16[9,128,128]{2,1,0:T(8,128)(2,1)}, bf16[9,128,128]{2,1,0:T(8,128)(2,1)S(1)}, u32[]{:S(2)}, u32[]{:S(2)}) collective-permute-start(bf16[9,128,128]{2,1,0:T(8,128)(2,1)} %get-tuple-element.13), channel_id=1, source_target_pairs={{1,8},{8,1},{3,10},{10,3},{5,12},{12,5},{7,14},{14,7},{9,16},{16,9... | collective-permute-start | bytes 884744 | tf_op jit(solution)/shard_map/ppermute | solution.py:320
  7.6 3.3 %copy-start.5 = (f32[16,3]{0,1:T(4,128)S(1)}, f32[16,3]{0,1:T(4,128)}, u32[]{:S(2)}) copy-start(f32[16,3]{0,1:T(4,128)} %param.10) | copy-start | bytes 580
  7.6 3.3 %copy-start.4 = (f32[16,3]{0,1:T(4,128)S(1)}, f32[16,3]{0,1:T(4,128)}, u32[]{:S(2)}) copy-start(f32[16,3]{0,1:T(4,128)} %param.11) | copy-start | bytes 580
  7.6 11.5 %collective-permute-start.3 = (bf16[4,128,128]{2,1,0:T(8,128)(2,1)}, bf16[4,128,128]{2,1,0:T(8,128)(2,1)}, u32[]{:S(2)}, u32[]{:S(2)}) collective-permute-start(bf16[4,128,128]{2,1,0:T(8,128)(2,1)} %get-tuple-element.14), channel_id=1, source_target_pairs={{0,8},{9,1},{2,10},{11,3},{4,12},{13,5},{6,14},{15,7},{8,16},{17,9... | collective-permute-start | bytes 393224 | tf_op jit(solution)/shard_map/ppermute | solution.py:321
  11.5 0.6 copy-start.3
  12.1 1.2 %copy-start.2 = (f32[16,128,128]{2,1,0:T(8,128)S(1)}, f32[16,128,128]{2,1,0:T(8,128)}, u32[]{:S(2)}) copy-start(f32[16,128,128]{2,1,0:T(8,128)} %value.5) | copy-start | bytes 3145732
  22.6 5.6 %collective-permute-start.6 = (f16[8,32,128]{2,1,0:T(8,128)(2,1)S(1)}, f16[8,32,128]{2,1,0:T(8,128)(2,1)S(1)}, u32[]{:S(2)}, u32[]{:S(2)}) collective-permute-start(f16[8,32,128]{2,1,0:T(8,128)(2,1)S(1)} %get-tuple-element.38), channel_id=1, source_target_pairs={{0,6},{1,7},{2,4},{3,5},{4,2},{5,3},{6,0},{7,1},{8,14},{9,15},{10,... | collective-permute-start | bytes 196616 | tf_op jit(solution)/shard_map/ppermute | solution.py:345
  26.0 5.7 %collective-permute-start.5 = (f16[8,32,128]{2,1,0:T(8,128)(2,1)S(1)}, f16[8,32,128]{2,1,0:T(8,128)(2,1)S(1)}, u32[]{:S(2)}, u32[]{:S(2)}) collective-permute-start(f16[8,32,128]{2,1,0:T(8,128)(2,1)S(1)} %get-tuple-element.39), channel_id=1, source_target_pairs={{0,4},{1,5},{2,6},{3,7},{4,0},{5,1},{6,2},{7,3},{8,12},{9,13},{10,... | collective-permute-start | bytes 196616 | tf_op jit(solution)/shard_map/ppermute | solution.py:345
  26.0 5.7 %collective-permute-start.4 = (f16[8,32,128]{2,1,0:T(8,128)(2,1)S(1)}, f16[8,32,128]{2,1,0:T(8,128)(2,1)S(1)}, u32[]{:S(2)}, u32[]{:S(2)}) collective-permute-start(f16[8,32,128]{2,1,0:T(8,128)(2,1)S(1)} %get-tuple-element.37), channel_id=1, source_target_pairs={{0,2},{1,3},{2,0},{3,1},{4,6},{5,7},{6,4},{7,5},{8,10},{9,11},{10,... | collective-permute-start | bytes 196616 | tf_op jit(solution)/shard_map/ppermute | solution.py:345
  31.7 5.1 %collective-permute-start.9 = (f16[8,32,128]{2,1,0:T(8,128)(2,1)S(1)}, f16[8,32,128]{2,1,0:T(8,128)(2,1)S(1)}, u32[]{:S(2)}, u32[]{:S(2)}) collective-permute-start(f16[8,32,128]{2,1,0:T(8,128)(2,1)S(1)} %fusion.23), channel_id=1, source_target_pairs={{6,0},{7,1},{4,2},{5,3},{2,4},{3,5},{0,6},{1,7},{14,8},{15,9},{12,... | collective-permute-start | bytes 196616 | tf_op jit(solution)/shard_map/ppermute | solution.py:352
  34.0 6.7 %collective-permute-start.8 = (f16[8,32,128]{2,1,0:T(8,128)(2,1)S(1)}, f16[8,32,128]{2,1,0:T(8,128)(2,1)S(1)}, u32[]{:S(2)}, u32[]{:S(2)}) collective-permute-start(f16[8,32,128]{2,1,0:T(8,128)(2,1)S(1)} %fusion.23), channel_id=1, source_target_pairs={{4,0},{5,1},{6,2},{7,3},{0,4},{1,5},{2,6},{3,7},{12,8},{13,9},{14,... | collective-permute-start | bytes 196616 | tf_op jit(solution)/shard_map/ppermute | solution.py:352
  34.0 6.7 %collective-permute-start.7 = (f16[8,32,128]{2,1,0:T(8,128)(2,1)S(1)}, f16[8,32,128]{2,1,0:T(8,128)(2,1)S(1)}, u32[]{:S(2)}, u32[]{:S(2)}) collective-permute-start(f16[8,32,128]{2,1,0:T(8,128)(2,1)S(1)} %fusion.23), channel_id=1, source_target_pairs={{2,0},{3,1},{0,2},{1,3},{6,4},{7,5},{4,6},{5,7},{10,8},{11,9},{8,1... | collective-permute-start | bytes 196616 | tf_op jit(solution)/shard_map/ppermute | solution.py:352
  40.8 3.7 %collective-permute-start.11 = (f16[4,3,32,128]{3,2,1,0:T(8,128)(2,1)S(1)}, f16[4,3,32,128]{3,2,1,0:T(8,128)(2,1)S(1)}, u32[]{:S(2)}, u32[]{:S(2)}) collective-permute-start(f16[4,3,32,128]{3,2,1,0:T(8,128)(2,1)S(1)} %get-tuple-element.34), channel_id=1, source_target_pairs={{0,1},{1,0},{2,3},{3,2},{4,5},{5,4},{6,7},{7,6},{8,9},{9,8},{10,11... | collective-permute-start | bytes 294920 | tf_op jit(solution)/shard_map/ppermute | solution.py:372
  41.5 8.8 %collective-permute-start.10 = (f16[4,3,32,128]{3,2,1,0:T(8,128)(2,1)S(1)}, f16[4,3,32,128]{3,2,1,0:T(8,128)(2,1)S(1)}, u32[]{:S(2)}, u32[]{:S(2)}) collective-permute-start(f16[4,3,32,128]{3,2,1,0:T(8,128)(2,1)S(1)} %get-tuple-element.33), channel_id=1, source_target_pairs={{1,8},{8,1},{3,10},{10,3},{5,12},{12,5},{7,14},{14,7},{9,16},{16,9... | collective-permute-start | bytes 294920 | tf_op jit(solution)/shard_map/ppermute | solution.py:373
  53.8 5.0 %collective-permute-start.14 = (f16[8,32,128]{2,1,0:T(8,128)(2,1)S(1)}, f16[8,32,128]{2,1,0:T(8,128)(2,1)S(1)}, u32[]{:S(2)}, u32[]{:S(2)}) collective-permute-start(f16[8,32,128]{2,1,0:T(8,128)(2,1)S(1)} %get-tuple-element.31), channel_id=1, source_target_pairs={{0,6},{1,7},{2,4},{3,5},{4,2},{5,3},{6,0},{7,1},{8,14},{9,15},{10,... | collective-permute-start | bytes 196616 | tf_op jit(solution)/shard_map/ppermute | solution.py:345
  55.4 7.1 %collective-permute-start.13 = (f16[8,32,128]{2,1,0:T(8,128)(2,1)S(1)}, f16[8,32,128]{2,1,0:T(8,128)(2,1)S(1)}, u32[]{:S(2)}, u32[]{:S(2)}) collective-permute-start(f16[8,32,128]{2,1,0:T(8,128)(2,1)S(1)} %get-tuple-element.32), channel_id=1, source_target_pairs={{0,4},{1,5},{2,6},{3,7},{4,0},{5,1},{6,2},{7,3},{8,12},{9,13},{10,... | collective-permute-start | bytes 196616 | tf_op jit(solution)/shard_map/ppermute | solution.py:345
  55.4 7.1 %collective-permute-start.12 = (f16[8,32,128]{2,1,0:T(8,128)(2,1)S(1)}, f16[8,32,128]{2,1,0:T(8,128)(2,1)S(1)}, u32[]{:S(2)}, u32[]{:S(2)}) collective-permute-start(f16[8,32,128]{2,1,0:T(8,128)(2,1)S(1)} %get-tuple-element.30), channel_id=1, source_target_pairs={{0,2},{1,3},{2,0},{3,1},{4,6},{5,7},{6,4},{7,5},{8,10},{9,11},{10,... | collective-permute-start | bytes 196616 | tf_op jit(solution)/shard_map/ppermute | solution.py:345
  62.6 5.0 %collective-permute-start.17 = (f16[8,32,128]{2,1,0:T(8,128)(2,1)S(1)}, f16[8,32,128]{2,1,0:T(8,128)(2,1)S(1)}, u32[]{:S(2)}, u32[]{:S(2)}) collective-permute-start(f16[8,32,128]{2,1,0:T(8,128)(2,1)S(1)} %fusion.14), channel_id=1, source_target_pairs={{6,0},{7,1},{4,2},{5,3},{2,4},{3,5},{0,6},{1,7},{14,8},{15,9},{12,... | collective-permute-start | bytes 196616 | tf_op jit(solution)/shard_map/ppermute | solution.py:352
  64.1 7.1 %collective-permute-start.16 = (f16[8,32,128]{2,1,0:T(8,128)(2,1)S(1)}, f16[8,32,128]{2,1,0:T(8,128)(2,1)S(1)}, u32[]{:S(2)}, u32[]{:S(2)}) collective-permute-start(f16[8,32,128]{2,1,0:T(8,128)(2,1)S(1)} %fusion.14), channel_id=1, source_target_pairs={{4,0},{5,1},{6,2},{7,3},{0,4},{1,5},{2,6},{3,7},{12,8},{13,9},{14,... | collective-permute-start | bytes 196616 | tf_op jit(solution)/shard_map/ppermute | solution.py:352
  64.1 7.1 %collective-permute-start.15 = (f16[8,32,128]{2,1,0:T(8,128)(2,1)S(1)}, f16[8,32,128]{2,1,0:T(8,128)(2,1)S(1)}, u32[]{:S(2)}, u32[]{:S(2)}) collective-permute-start(f16[8,32,128]{2,1,0:T(8,128)(2,1)S(1)} %fusion.14), channel_id=1, source_target_pairs={{2,0},{3,1},{0,2},{1,3},{6,4},{7,5},{4,6},{5,7},{10,8},{11,9},{8,1... | collective-permute-start | bytes 196616 | tf_op jit(solution)/shard_map/ppermute | solution.py:352
  71.3 1.7 %collective-permute-start.18 = (f16[4,8,32,128]{3,2,1,0:T(8,128)(2,1)S(1)}, f16[4,8,32,128]{3,2,1,0:T(8,128)(2,1)S(1)}, u32[]{:S(2)}, u32[]{:S(2)}) collective-permute-start(f16[4,8,32,128]{3,2,1,0:T(8,128)(2,1)S(1)} %pad_maximum_fusion.1), channel_id=1, source_target_pairs={{0,1},{1,0},{2,3},{3,2},{4,5},{5,4},{6,7},{7,6},{8,9},{9,8},{10,11... | collective-permute-start | bytes 786440 | tf_op jit(solution)/shard_map/ppermute | solution.py:391

commit v4 on v3

v4 whole, which is shorter than its diff:
```python
import functools

import jax
import jax.numpy as jnp
from jax import lax
from jax.experimental import pallas as pl
from jax.experimental.pallas import tpu as pltpu
from jax.sharding import PartitionSpec as P

SUBSTEPS = 3
PAD = 8
LOWEST = -3.0e38


def mate(chip, step, chips):
    if chips & (chips - 1) == 0:
        return chip ^ step
    return (chip + step) % chips


def mate_step(chip, other, chips):
    if chips & (chips - 1) == 0:
        return chip ^ other
    return (other - chip) % chips


def where_am_i():
    slab, member = lax.axis_index("slab"), lax.axis_index("ctrl")
    upper = (member + slab) % 2
    end = jnp.where(upper == 0, 0, lax.axis_size("slab") - 1)
    return member // 2, upper, jnp.where(slab == end, 0, 1)


def coefficients(sets, ctrl):
    own_set, other_set, drift_sets, diffusion_sets = sets
    own = own_set.shape[0]
    kind = jnp.where(ctrl < own, own_set[jnp.minimum(ctrl, own - 1)], other_set[jnp.maximum(ctrl - own, 0)])
    rates = [diffusion_sets[kind, dim] for dim in range(3)]
    drifts = [drift_sets[kind, dim] for dim in range(3)]
    sizes = [jnp.maximum(drift, -drift) for drift in drifts]
    return rates, sizes, 1.0 - 2.0 * (rates[0] + rates[1] + rates[2]), sizes[0] + sizes[1] + sizes[2], drifts


def stencil(coef, src, row, speed, reward, winds):
    ny = src.shape[1] - 2 * PAD
    lines = pl.ds(PAD, ny)
    center = src[row, lines, :]
    y_ahead = src[row, pl.ds(PAD + 1, ny), :]
    y_behind = src[row, pl.ds(PAD - 1, ny), :]
    x_sum = src[row + 1, lines, :] + src[row - 1, lines, :]
    x_wind = src[row + winds[0], lines, :]
    nz = center.shape[1]
    lane = lax.broadcasted_iota(jnp.int32, center.shape, 1)
    z_ahead = jnp.where(lane == nz - 1, 0.0, pltpu.roll(center, nz - 1, 1))
    z_behind = jnp.where(lane == 0, 0.0, pltpu.roll(center, 1, 1))
    y_wind = jnp.where(winds[1], y_ahead, y_behind)
    z_wind = jnp.where(winds[2], z_ahead, z_behind)
    rates, sizes, weight, size, _ = coef
    still = reward + weight * center + rates[0] * x_sum
    still = still + rates[1] * (y_ahead + y_behind) + rates[2] * (z_ahead + z_behind)
    wind = sizes[0] * x_wind + sizes[1] * y_wind + sizes[2] * z_wind
    return still + speed * (wind - size * center)


def winds_of(place, drifts):
    step = jnp.where(drifts[0] > 0.0, 1, -1)
    return jnp.where(place[1] == 0, step, -step), drifts[1] > 0.0, drifts[2] > 0.0


def put_max(place, out, index, new):
    chips, width = out.shape[0], out.shape[2]
    for shard in range(chips):
        spot = mate_step(place[0], shard, chips)
        out[spot, index] = jnp.maximum(out[spot, index], new[shard * width : (shard + 1) * width])


def start_max(out):
    for shard in range(out.shape[0]):
        for row in range(out.shape[1]):
            out[shard, row] = jnp.full(out.shape[2:], LOWEST, out.dtype)


def clear_pads(field, ny):
    zero = jnp.zeros((PAD, field.shape[2]), field.dtype)
    for row in range(field.shape[0]):
        field[row, 0:PAD, :] = zero
        field[row, PAD + ny : 2 * PAD + ny, :] = zero


def lay_rows(place, speed, reward, other, speed_rows, reward_rows):
    own, cells = reward.shape[:2]
    for q in range(speed_rows.shape[0]):
        real = jnp.where(place[1] == 0, q, cells - 1 - q)
        speed_rows[q] = speed[real]
        for ctrl in range(own):
            reward_rows[ctrl, q] = reward[ctrl, real].astype(jnp.float32)
            reward_rows[own + ctrl, q] = other[ctrl, real].astype(jnp.float32)


def lay_lower(edge, edge_other, lower_rows):
    mine = edge_other.shape[0]
    for row in range(mine):
        lower_rows[row] = edge[edge.shape[0] - mine + row]
        lower_rows[mine + row] = edge_other[row]


def spread(place, pieces, index, field, row):
    chips, width = pieces.shape[0], pieces.shape[2]
    for shard in range(chips):
        piece = pieces[mate_step(place[0], shard, chips), index]
        field[row, pl.ds(PAD + shard * width, width), :] = piece.astype(field.dtype)


def early_march(place, sets, half, block, speed_rows, reward_rows, out, keeps, fields):
    ny = block.shape[1] - 2 * PAD
    start_max(out)

    def one(ctrl, carry):
        coef = coefficients(sets, ctrl)
        winds = winds_of(place, coef[4])
        source = block
        for substep in range(SUBSTEPS):
            for q in range(1 + substep, half + SUBSTEPS - 1 - substep):
                new = stencil(coef, source, q, speed_rows[q], reward_rows[ctrl, q], winds)
                if substep == SUBSTEPS - 1:
                    put_max(place, out, q - SUBSTEPS, new)
                    continue
                fields[substep][q, pl.ds(PAD, ny), :] = new
                if q < substep + 3:
                    keeps[substep][ctrl, q - substep - 1] = new
            if substep < SUBSTEPS - 1:
                source = fields[substep]
        return carry

    lax.fori_loop(0, reward_rows.shape[0], one, 0)


def rest_march(place, sets, edge, lower_rows, block, speed_rows, reward_rows, out, keeps, fields):
    ny = block.shape[1] - 2 * PAD
    margin = SUBSTEPS - 1
    inside = place[2].astype(jnp.float32)
    start_max(out)

    def one(ctrl, carry):
        coef = coefficients(sets, ctrl)
        winds = winds_of(place, coef[4])
        source = block
        for substep in range(SUBSTEPS):
            for q in range(substep + 1 - SUBSTEPS, 1 + substep):
                if q < 0:
                    speed = edge[SUBSTEPS - 1 - q].astype(jnp.float32)
                    reward = lower_rows[ctrl * margin - 1 - q].astype(jnp.float32)
                else:
                    speed, reward = speed_rows[q], reward_rows[ctrl, q]
                new = stencil(coef, source, q + SUBSTEPS, speed, reward, winds)
                if substep == SUBSTEPS - 1:
                    put_max(place, out, q, new)
                    continue
                if q < 0:
                    new = new * inside
                fields[substep][q + SUBSTEPS, pl.ds(PAD, ny), :] = new
            if substep < SUBSTEPS - 1:
                source = fields[substep]
                for kept in range(2):
                    row = 1 + substep + kept + SUBSTEPS
                    source[row, pl.ds(PAD, ny), :] = keeps[substep][ctrl, kept]
        return carry

    lax.fori_loop(0, reward_rows.shape[0], one, 0)


def pack_kernel(value, speed, reward, edge, far, block, speed_rows, value_sem, speed_sem, near_sem, far_sem):
    place = where_am_i()
    cells, ny = value.shape[:2]
    own = reward.shape[0]
    margin = SUBSTEPS - 1
    copies, later = [], []
    for row in range(SUBSTEPS):
        near = jnp.where(place[1] == 0, row, cells - 1 - row)
        away = jnp.where(place[1] == 0, cells - 1 - row, row)
        copies.append(pltpu.make_async_copy(value.at[near], block.at[row, pl.ds(PAD, ny)], value_sem.at[row]))
        if row < margin:
            copies.append(pltpu.make_async_copy(speed.at[near], speed_rows.at[row], speed_sem.at[row]))
            for ctrl in range(own):
                spot = ctrl * margin + row
                place_near = edge.at[SUBSTEPS + margin + spot]
                later.append(pltpu.make_async_copy(reward.at[ctrl, near], place_near, near_sem.at[spot]))
                later.append(pltpu.make_async_copy(reward.at[ctrl, away], far.at[spot], far_sem.at[spot]))
    for row in range(SUBSTEPS, block.shape[0]):
        real = jnp.where(place[1] == 0, row, cells - 1 - row)
        later.append(pltpu.make_async_copy(value.at[real], block.at[row, pl.ds(PAD, ny)], value_sem.at[row]))
    for copy in copies + later:
        copy.start()
    clear_pads(block, ny)
    for copy in copies:
        copy.wait()
    for row in range(SUBSTEPS):
        edge[row] = block[row, pl.ds(PAD, ny), :].astype(edge.dtype)
    for row in range(margin):
        edge[SUBSTEPS + row] = speed_rows[row].astype(edge.dtype)
    for copy in later:
        copy.wait()


def early_first(own_set, other_set, drift_sets, diffusion_sets, block, speed, reward, other, out, *refs, half):
    keeps, (speed_rows, reward_rows), fields = refs[:2], refs[2:4], refs[4:]
    place = where_am_i()
    for field in fields:
        clear_pads(field, speed.shape[1])
    lay_rows(place, speed, reward, other, speed_rows, reward_rows)
    sets = own_set, other_set, drift_sets, diffusion_sets
    early_march(place, sets, half, block, speed_rows, reward_rows, out, keeps, fields)


def rest_first(own_set, other_set, drift_sets, diffusion_sets, first, speed_rows, reward_rows, edge, *refs, half):
    edge_other, keeps, out, fields, block, lower_rows = refs[0], refs[1:3], refs[3], refs[4:6], refs[6], refs[7]
    place = where_am_i()
    ny = speed_rows.shape[1]
    for field in (block, *fields):
        clear_pads(field, ny)
    for row in range(SUBSTEPS):
        block[SUBSTEPS - 1 - row, pl.ds(PAD, ny), :] = edge[row].astype(jnp.float32)
    for row in range(2):
        block[SUBSTEPS + row] = first[row]
    lay_lower(edge, edge_other, lower_rows)
    sets = own_set, other_set, drift_sets, diffusion_sets
    rest_march(place, sets, edge, lower_rows, block, speed_rows, reward_rows, out, keeps, fields)


def early_later(own_set, other_set, drift_sets, diffusion_sets, current, across, speed_rows, reward_rows, out, *refs, half):
    keeps, fields, block = refs[:2], refs[2:4], refs[4]
    place = where_am_i()
    for field in (block, *fields):
        clear_pads(field, speed_rows.shape[1])
    for q in range(half):
        spread(place, current, q, block, q)
    for row in range(SUBSTEPS):
        spread(place, across, SUBSTEPS - 1 - row, block, half + row)
    early_march(place, (own_set, other_set, drift_sets, diffusion_sets), half, block, speed_rows, reward_rows, out, keeps, fields)


def rest_later(own_set, other_set, drift_sets, diffusion_sets, current, beyond, speed_rows, reward_rows, edge, *refs, half):
    edge_other, keeps, out, fields, block, lower_rows = refs[0], refs[1:3], refs[3], refs[4:6], refs[6], refs[7]
    place = where_am_i()
    for field in (block, *fields):
        clear_pads(field, speed_rows.shape[1])
    for row in range(SUBSTEPS):
        spread(place, beyond, row, block, SUBSTEPS - 1 - row)
    for row in range(2):
        spread(place, current, row, block, SUBSTEPS + row)
    lay_lower(edge, edge_other, lower_rows)
    sets = own_set, other_set, drift_sets, diffusion_sets
    rest_march(place, sets, edge, lower_rows, block, speed_rows, reward_rows, out, keeps, fields)


def body(value, speed, reward, ctrl_set, drift_sets, diffusion_sets):
    own, cells, ny, nz = reward.shape
    count = 2 * own
    slabs, members = lax.axis_size("slab"), lax.axis_size("ctrl")
    chips, half = members // 2, cells // 2
    width = ny // chips
    chip, upper, _ = where_am_i()
    margin = SUBSTEPS - 1
    narrow, wire = jnp.bfloat16, jnp.float16
    both = ("slab", "ctrl")

    def device(s, z, c):
        return s * members + 2 * z + c

    partners = [(i, i ^ 1) for i in range(members)]

    facing, beside = [], []
    for s in range(slabs - 1):
        for z in range(chips):
            c = (s + 1) % 2
            facing += [(device(s, z, c), device(s + 1, z, c)), (device(s + 1, z, c), device(s, z, c))]
            beside += [(device(s, z, 1 - c), device(s + 1, z, c)), (device(s + 1, z, 1 - c), device(s, z, c))]

    whole = pl.BlockSpec(memory_space=pltpu.VMEM)
    scalars = pl.BlockSpec(memory_space=pltpu.SMEM)
    def shape(*dims):
        return jax.ShapeDtypeStruct(dims, jnp.float32)

    def call(kernel, rows, marched, arrays, outs):
        field = pltpu.VMEM((rows, ny + 2 * PAD, nz), jnp.float32)
        scratch = [field] * (2 if kernel is early_first else 3)
        if kernel in (rest_first, rest_later):
            scratch.append(pltpu.VMEM((count * margin, ny, nz), narrow))
        return pl.pallas_call(
            functools.partial(kernel, half=half),
            out_shape=outs,
            in_specs=[scalars] * 4 + [whole] * len(arrays),
            out_specs=jax.tree.map(lambda _: whole, outs),
            scratch_shapes=scratch,
            compiler_params=pltpu.CompilerParams(vmem_limit_bytes=32 * 2**20),
            cost_estimate=pl.CostEstimate(
                flops=25 * count * marched * ny * nz, bytes_accessed=12 * count * marched * ny * nz, transcendentals=0
            ),
        )(ctrl_set, other_set, drift_sets, diffusion_sets, *arrays)

    keeps = [shape(count, 2, ny, nz)] * (SUBSTEPS - 1)

    rows, given = half + SUBSTEPS, half + margin
    other_set = lax.ppermute(ctrl_set, "ctrl", partners)
    other = lax.ppermute(reward, "ctrl", partners)
    anywhere = pl.BlockSpec(memory_space=pl.ANY)
    dma = pltpu.SemaphoreType.DMA
    packed, far, block = pl.pallas_call(
        pack_kernel,
        out_shape=[
            pltpu.VMEM((SUBSTEPS + margin + own * margin, ny, nz), narrow),
            pltpu.VMEM((own * margin, ny, nz), narrow),
            pltpu.VMEM((rows, ny + 2 * PAD, nz), jnp.float32),
        ],
        in_specs=[anywhere] * 3,
        out_specs=[whole] * 3,
        scratch_shapes=[
            pltpu.VMEM((margin, ny, nz), jnp.float32),
            dma((rows,)),
            dma((margin,)),
            dma((own * margin,)),
            dma((own * margin,)),
        ],
    )(value, speed, reward)
    packed, far, other_set = lax.optimization_barrier((packed, far, other_set))
    edge = lax.ppermute(packed, both, facing)
    edge_other = lax.ppermute(far, both, beside)

    def reduce(best):
        parts = best.astype(wire)
        mine = parts[0]
        for step in range(chips - 1, 0, -1):
            pairs = [(2 * z + c, 2 * mate(z, step, chips) + c) for z in range(chips) for c in range(2)]
            mine = jnp.maximum(mine, lax.ppermute(parts[step], "ctrl", pairs))
        return mine

    def gather(mine):
        pieces = []
        for step in range(chips - 1, 0, -1):
            pairs = [(2 * mate(z, step, chips) + c, 2 * z + c) for z in range(chips) for c in range(2)]
            pieces.append(lax.ppermute(mine, "ctrl", pairs))
        return jnp.stack([mine, *pieces[::-1]])

    steps = sum(half + SUBSTEPS - 2 - 2 * k for k in range(SUBSTEPS))
    early_out = [shape(chips, half - SUBSTEPS, width, nz)] + keeps
    rest_out = shape(chips, SUBSTEPS, width, nz)
    rest_rows, rest_steps = 2 * SUBSTEPS + 2, SUBSTEPS * SUBSTEPS

    best, keep_a, keep_b, speed_rows, reward_rows = call(
        early_first,
        rows,
        steps,
        (block, speed, reward, other),
        early_out + [shape(given, ny, nz), shape(count, given, ny, nz)],
    )
    laid, edges = (speed_rows, reward_rows), (edge, edge_other)
    best_rest = call(rest_first, rest_rows, rest_steps, (block, *laid, *edges, keep_a, keep_b), rest_out)
    pieces = gather(reduce(jnp.concatenate([best_rest, best], axis=1)))

    across = lax.ppermute(pieces[:, -SUBSTEPS:], "ctrl", partners)
    beyond = lax.ppermute(pieces[:, :SUBSTEPS].astype(narrow), both, facing)
    current = pieces.astype(jnp.float32)
    best, *kept = call(early_later, rows, steps, (current, across.astype(jnp.float32), *laid), early_out)
    best_rest = call(
        rest_later, rest_rows, rest_steps, (current, beyond, *laid, *edges, *kept), rest_out
    )
    pieces = gather(reduce(jnp.concatenate([best_rest, best], axis=1)))

    from_partner = lax.ppermute(pieces, "ctrl", partners)
    low_half = jnp.where(upper == 0, pieces, from_partner)
    high_half = jnp.where(upper == 0, from_partner, pieces)[:, ::-1]
    slab_pieces = jnp.concatenate([low_half, high_half], axis=1)
    ordered = [
        lax.dynamic_index_in_dim(slab_pieces, mate_step(chip, shard, chips), 0, keepdims=False)
        for shard in range(chips)
    ]
    return jnp.concatenate(ordered, axis=1).astype(jnp.float32)


def solution(mesh):
    in_specs = (
        P("slab", None, None),
        P("slab", None, None),
        P("ctrl", "slab", None, None),
        P("ctrl"),
        P(),
        P(),
    )
    out_specs = P("slab", None, None)
    return jax.shard_map(body, mesh=mesh, in_specs=in_specs, out_specs=out_specs, check_vma=False)
```

time: 74.9 us -> 71.8 us (0.959)
  starting transfers between devices: 26.1 us -> 29 us
  waiting for transfers between devices: 22 us -> 19.6 us
  local copies, waits for them, and re-layouts: 2.33 us -> 0.95 us
  Pallas kernels: 20.9 us -> 19.8 us
  other arithmetic: 2.97 us -> 1.99 us
    ppermute x6, waiting for transfers between devices: 10.4 us -> 7.81 us  [gather(): pieces.append(lax.ppermute(mine, 'ctrl', pairs))]
    ppermute x1, starting transfers between devices: 0.72 us -> 2.64 us  [body(): across = lax.ppermute(pieces[:, -SUBSTEPS:], 'ctrl', partners)]
    ppermute x1, starting transfers between devices: 0.56 us -> 2.12 us  [body(): from_partner = lax.ppermute(pieces, 'ctrl', partners)]
    pallas_call x1, Pallas kernels: 2.75 us -> 1.46 us  [body(): pl.pallas_call(pack_kernel, out_shape=[pltpu.VMEM((SUBSTEPS + margin + ow...]
    unnamed x14, local copies, waits for them, and re-layouts: 1.75 us -> 0.89 us
  transfers between devices with their start and end apart: 19 -> 19, of which waited for: 9 -> 9; matrix products, arithmetic and copies ran while one was open for 2% -> 0% of each run, Pallas kernels for 19% -> 19%
where the time goes in v4:
time: 71.8 us; the launch traced here: 71.6 us
  starting transfers between devices  29 us (40%)
  Pallas kernels  19.8 us (28%)
  waiting for transfers between devices  19.6 us (27%)
  other arithmetic  1.99 us (3%)
  local copies, waits for them, and re-layouts  0.95 us (1%)
    pallas_call x4, Pallas kernels, call(): pl.pallas_call(functools.partial(kernel, half=half), out_shape=outs, in_s...  18.3 us
    ppermute x6, waiting for transfers between devices, reduce(): mine = jnp.maximum(mine, lax.ppermute(parts[step], 'ctrl', pairs))  10.6 us
    ppermute x6, waiting for transfers between devices, gather(): pieces.append(lax.ppermute(mine, 'ctrl', pairs))  7.81 us
    ppermute x6, starting transfers between devices, reduce(): mine = jnp.maximum(mine, lax.ppermute(parts[step], 'ctrl', pairs))  7.36 us
    ppermute x6, starting transfers between devices, gather(): pieces.append(lax.ppermute(mine, 'ctrl', pairs))  7.22 us
    ppermute x1, starting transfers between devices, body(): edge_other = lax.ppermute(far, both, beside)  3.73 us
    ppermute x1, starting transfers between devices, body(): edge = lax.ppermute(packed, both, facing)  3.11 us
    ppermute x1, starting transfers between devices, body(): across = lax.ppermute(pieces[:, -SUBSTEPS:], 'ctrl', partners)  2.64 us
  transfers between devices with their start and end apart: 19, of which 9 were waited for; matrix products, arithmetic and copies ran while one was open for 0% of the time, Pallas kernels for 19%

profile of v4, /device:TPU:5, one launch (start us, length us, event | category | flops | bytes accessed | tf_op | source)
XLA Modules:
  0.0 71.6 jit_solution(2405134694323957093)
XLA Ops:
  0.0 0.7 %collective-permute-start.1 = (bf16[2,16,128,128]{3,2,1,0:T(8,128)(2,1)}, bf16[2,16,128,128]{3,2,1,0:T(8,128)(2,1)}, u32[]{:S(2)}, u32[]{:S(2)}) collective-permute-start(bf16[2,16,128,128]{3,2,1,0:T(8,128)(2,1)} %reward.3), channel_id=1, source_target_pairs={{0,1},{1,0},{2,3},{3,2},{4,5},{5,4},{6,7},{7,6},{8,9},{9,8},{10,11... | collective-permute-start | bytes 3145736 | tf_op jit(solution)/shard_map/ppermute | solution.py:305
  0.8 0.1 collective-permute-start
  0.9 1.5 %shard_map.64 = (bf16[9,128,128]{2,1,0:T(8,128)(2,1)S(1)}, bf16[4,128,128]{2,1,0:T(8,128)(2,1)S(1)}, f32[11,144,128]{2,1,0:T(8,128)S(1)}) custom-call(f32[16,128,128]{2,1,0:T(8,128)} %value.1, f32[16,128,128]{2,1,0:T(8,128)} %speed.3, bf16[2,16,128,128]{3,2,1,0:T(8,128)(2,1)} %reward.3), custom_call_target="tpu_custom_call" | custom-call | tf_op jit(solution)/shard_map/pallas_call | solution.py:308
  2.3 0.0 copy-start.3
  2.3 0.7 copy-done.3
  3.0 3.1 %collective-permute-start.2 = (bf16[9,128,128]{2,1,0:T(8,128)(2,1)}, bf16[9,128,128]{2,1,0:T(8,128)(2,1)S(1)}, u32[]{:S(2)}, u32[]{:S(2)}) collective-permute-start(bf16[9,128,128]{2,1,0:T(8,128)(2,1)} %copy-done.3), channel_id=1, source_target_pairs={{1,9},{9,1},{3,11},{11,3},{5,13},{13,5},{7,15},{15,7},{8,16},{16,8... | collective-permute-start | bytes 884744 | tf_op jit(solution)/shard_map/ppermute | solution.py:326
  6.2 3.7 %collective-permute-start.3 = (bf16[4,128,128]{2,1,0:T(8,128)(2,1)S(1)}, bf16[4,128,128]{2,1,0:T(8,128)(2,1)S(1)}, u32[]{:S(2)}, u32[]{:S(2)}) collective-permute-start(bf16[4,128,128]{2,1,0:T(8,128)(2,1)S(1)} %get-tuple-element.26), channel_id=1, source_target_pairs={{0,9},{8,1},{2,11},{10,3},{4,13},{12,5},{6,15},{14,7},{9,16},{17,8... | collective-permute-start | bytes 393224 | tf_op jit(solution)/shard_map/ppermute | solution.py:327
  9.9 0.1 copy.13.drift_sets
  10.0 0.1 copy.14.diffusion_sets
  10.1 6.2 %shard_map.65 = (f32[4,5,32,128]{3,2,1,0:T(8,128)S(1)}, f32[4,2,128,128]{3,2,1,0:T(8,128)S(1)}, f32[4,2,128,128]{3,2,1,0:T(8,128)S(1)}, f32[10,128,128]{2,1,0:T(8,128)S(1)}, f32[4,10,128,128]{3,2,1,0:T(8,128)S(1)}) custom-call(s32[2]{0:T(128)S(1)} %copy-done.2, s32[2]{0:T(128)S(1)} %collective-permute-done.other_set, f32[16,3]{1,0:T(8,128)S(1)} %copy.13.drift_sets, ...), custom_call_target="tpu_custom_call" | custom-call | flops 34406400 | bytes 16515072 | tf_op jit(solution)/shard_map/pallas_call | solution.py:289
  16.3 0.0 collective-permute-done.3.refs_0_
  16.3 0.0 collective-permute-done.2.edge
  16.4 3.1 %shard_map.66 = f32[4,3,32,128]{3,2,1,0:T(8,128)S(1)} custom-call(s32[2]{0:T(128)S(1)} %copy-done.2, s32[2]{0:T(128)S(1)} %collective-permute-done.other_set, f32[16,3]{1,0:T(8,128)S(1)} %copy.13.drift_sets, f32[16,3]{1,0:T(8,128)S(1)} %copy.14.diffusion_sets, f32[11,144,128]{2,1,0:T(8,128)S(1)} %get-tuple-element.22.block.first, ...), custom_call_target="tpu_custom_call" | custom-call | flops 14745600 | bytes 7077888 | tf_op jit(solution)/shard_map/pallas_call | solution.py:289
  19.6 0.1 fusion.25
  19.6 3.4 %collective-permute-start.4 = (f16[8,32,128]{2,1,0:T(8,128)(2,1)S(1)}, f16[8,32,128]{2,1,0:T(8,128)(2,1)S(1)}, u32[]{:S(2)}, u32[]{:S(2)}) collective-permute-start(f16[8,32,128]{2,1,0:T(8,128)(2,1)S(1)} %get-tuple-element.46), channel_id=1, source_target_pairs={{0,6},{1,7},{2,4},{3,5},{4,2},{5,3},{6,0},{7,1},{8,14},{9,15},{10,... | collective-permute-start | bytes 196616 | tf_op jit(solution)/shard_map/ppermute | solution.py:334
  23.0 0.4 collective-permute-start.6
  23.4 2.0 %collective-permute-done.4 = f16[8,32,128]{2,1,0:T(8,128)(2,1)S(1)} collective-permute-done((f16[8,32,128]{2,1,0:T(8,128)(2,1)S(1)}, f16[8,32,128]{2,1,0:T(8,128)(2,1)S(1)}, u32[]{:S(2)}, u32[]{:S(2)}) %collective-permute-start.4) | collective-permute-done | bytes 65568 | tf_op jit(solution)/shard_map/ppermute | solution.py:334
  25.4 3.2 %collective-permute-done.5 = f16[8,32,128]{2,1,0:T(8,128)(2,1)S(1)} collective-permute-done((f16[8,32,128]{2,1,0:T(8,128)(2,1)S(1)}, f16[8,32,128]{2,1,0:T(8,128)(2,1)S(1)}, u32[]{:S(2)}, u32[]{:S(2)}) %collective-permute-start.5) | collective-permute-done | bytes 65568 | tf_op jit(solution)/shard_map/ppermute | solution.py:334
  28.7 1.0 %collective-permute-start.7 = (f16[8,32,128]{2,1,0:T(8,128)(2,1)S(1)}, f16[8,32,128]{2,1,0:T(8,128)(2,1)S(1)}, u32[]{:S(2)}, u32[]{:S(2)}) collective-permute-start(f16[8,32,128]{2,1,0:T(8,128)(2,1)S(1)} %fusion.23), channel_id=1, source_target_pairs={{2,0},{3,1},{0,2},{1,3},{6,4},{7,5},{4,6},{5,7},{10,8},{11,9},{8,1... | collective-permute-start | bytes 196616 | tf_op jit(solution)/shard_map/ppermute | solution.py:341
  29.7 1.6 %collective-permute-start.8 = (f16[8,32,128]{2,1,0:T(8,128)(2,1)S(1)}, f16[8,32,128]{2,1,0:T(8,128)(2,1)S(1)}, u32[]{:S(2)}, u32[]{:S(2)}) collective-permute-start(f16[8,32,128]{2,1,0:T(8,128)(2,1)S(1)} %fusion.23), channel_id=1, source_target_pairs={{4,0},{5,1},{6,2},{7,3},{0,4},{1,5},{2,6},{3,7},{12,8},{13,9},{14,... | collective-permute-start | bytes 196616 | tf_op jit(solution)/shard_map/ppermute | solution.py:341
  31.3 1.0 %collective-permute-start.9 = (f16[8,32,128]{2,1,0:T(8,128)(2,1)S(1)}, f16[8,32,128]{2,1,0:T(8,128)(2,1)S(1)}, u32[]{:S(2)}, u32[]{:S(2)}) collective-permute-start(f16[8,32,128]{2,1,0:T(8,128)(2,1)S(1)} %fusion.23), channel_id=1, source_target_pairs={{6,0},{7,1},{4,2},{5,3},{2,4},{3,5},{0,6},{1,7},{14,8},{15,9},{12,... | collective-permute-start | bytes 196616 | tf_op jit(solution)/shard_map/ppermute | solution.py:341
  32.3 1.9 %collective-permute-done.8 = f16[8,32,128]{2,1,0:T(8,128)(2,1)S(1)} collective-permute-done((f16[8,32,128]{2,1,0:T(8,128)(2,1)S(1)}, f16[8,32,128]{2,1,0:T(8,128)(2,1)S(1)}, u32[]{:S(2)}, u32[]{:S(2)}) %collective-permute-start.8) | collective-permute-done | bytes 65568 | tf_op jit(solution)/shard_map/ppermute | solution.py:341
  34.1 2.0 %collective-permute-done.9 = f16[8,32,128]{2,1,0:T(8,128)(2,1)S(1)} collective-permute-done((f16[8,32,128]{2,1,0:T(8,128)(2,1)S(1)}, f16[8,32,128]{2,1,0:T(8,128)(2,1)S(1)}, u32[]{:S(2)}, u32[]{:S(2)}) %collective-permute-start.9) | collective-permute-done | bytes 65568 | tf_op jit(solution)/shard_map/ppermute | solution.py:341
  36.2 0.1 pad_maximum_fusion
  36.3 2.6 %collective-permute-start.11 = (f16[4,3,32,128]{3,2,1,0:T(8,128)(2,1)S(1)}, f16[4,3,32,128]{3,2,1,0:T(8,128)(2,1)S(1)}, u32[]{:S(2)}, u32[]{:S(2)}) collective-permute-start(f16[4,3,32,128]{3,2,1,0:T(8,128)(2,1)S(1)} %get-tuple-element.43), channel_id=1, source_target_pairs={{0,1},{1,0},{2,3},{3,2},{4,5},{5,4},{6,7},{7,6},{8,9},{9,8},{10,11... | collective-permute-start | bytes 294920 | tf_op jit(solution)/shard_map/ppermute | solution.py:360
  39.0 2.0 %collective-permute-start.10 = (bf16[4,3,32,128]{3,2,1,0:T(8,128)(2,1)S(1)}, bf16[4,3,32,128]{3,2,1,0:T(8,128)(2,1)S(1)}, u32[]{:S(2)}, u32[]{:S(2)}) collective-permute-start(bf16[4,3,32,128]{3,2,1,0:T(8,128)(2,1)S(1)} %get-tuple-element.42), channel_id=1, source_target_pairs={{1,9},{9,1},{3,11},{11,3},{5,13},{13,5},{7,15},{15,7},{8,16},{16,8... | collective-permute-start | bytes 294920 | tf_op jit(solution)/shard_map/ppermute | solution.py:361
  41.0 5.7 %shard_map.67 = (f32[4,5,32,128]{3,2,1,0:T(8,128)S(1)}, f32[4,2,128,128]{3,2,1,0:T(8,128)S(1)}, f32[4,2,128,128]{3,2,1,0:T(8,128)S(1)}) custom-call(s32[2]{0:T(128)S(1)} %copy-done.2, s32[2]{0:T(128)S(1)} %collective-permute-done.other_set, f32[16,3]{1,0:T(8,128)S(1)} %copy.13.drift_sets, f32[16,3]{1,0:T(8,128)S(1)} %copy.14.diffusion_sets, ...), custom_call_target="tpu_custom_call" | custom-call | flops 34406400 | bytes 16515072 | tf_op jit(solution)/shard_map/pallas_call | solution.py:289
  46.8 3.2 %shard_map.68 = f32[4,3,32,128]{3,2,1,0:T(8,128)S(1)} custom-call(s32[2]{0:T(128)S(1)} %copy-done.2, s32[2]{0:T(128)S(1)} %collective-permute-done.other_set, f32[16,3]{1,0:T(8,128)S(1)} %copy.13.drift_sets, f32[16,3]{1,0:T(8,128)S(1)} %copy.14.diffusion_sets, f32[4,8,32,128]{3,2,1,0:T(8,128)S(1)} %get-tuple-element.45.current, ...), custom_call_target="tpu_custom_call" | custom-call | flops 14745600 | bytes 7077888 | tf_op jit(solution)/shard_map/pallas_call | solution.py:289
  50.1 0.1 fusion.16
  50.1 2.0 %collective-permute-start.12 = (f16[8,32,128]{2,1,0:T(8,128)(2,1)S(1)}, f16[8,32,128]{2,1,0:T(8,128)(2,1)S(1)}, u32[]{:S(2)}, u32[]{:S(2)}) collective-permute-start(f16[8,32,128]{2,1,0:T(8,128)(2,1)S(1)} %get-tuple-element.39), channel_id=1, source_target_pairs={{0,6},{1,7},{2,4},{3,5},{4,2},{5,3},{6,0},{7,1},{8,14},{9,15},{10,... | collective-permute-start | bytes 196616 | tf_op jit(solution)/shard_map/ppermute | solution.py:334
  52.1 0.6 collective-permute-start.13
  52.7 1.0 %collective-permute-start.14 = (f16[8,32,128]{2,1,0:T(8,128)(2,1)S(1)}, f16[8,32,128]{2,1,0:T(8,128)(2,1)S(1)}, u32[]{:S(2)}, u32[]{:S(2)}) collective-permute-start(f16[8,32,128]{2,1,0:T(8,128)(2,1)S(1)} %get-tuple-element.40), channel_id=1, source_target_pairs={{0,2},{1,3},{2,0},{3,1},{4,6},{5,7},{6,4},{7,5},{8,10},{9,11},{10,... | collective-permute-start | bytes 196616 | tf_op jit(solution)/shard_map/ppermute | solution.py:334
  53.7 1.5 %collective-permute-done.12 = f16[8,32,128]{2,1,0:T(8,128)(2,1)S(1)} collective-permute-done((f16[8,32,128]{2,1,0:T(8,128)(2,1)S(1)}, f16[8,32,128]{2,1,0:T(8,128)(2,1)S(1)}, u32[]{:S(2)}, u32[]{:S(2)}) %collective-permute-start.12) | collective-permute-done | bytes 65568 | tf_op jit(solution)/shard_map/ppermute | solution.py:334
  55.2 3.9 %collective-permute-done.13 = f16[8,32,128]{2,1,0:T(8,128)(2,1)S(1)} collective-permute-done((f16[8,32,128]{2,1,0:T(8,128)(2,1)S(1)}, f16[8,32,128]{2,1,0:T(8,128)(2,1)S(1)}, u32[]{:S(2)}, u32[]{:S(2)}) %collective-permute-start.13) | collective-permute-done | bytes 65568 | tf_op jit(solution)/shard_map/ppermute | solution.py:334
  59.1 0.0 collective-permute-done.14
  59.2 0.1 collective-permute-start.15
  59.2 2.0 %collective-permute-start.16 = (f16[8,32,128]{2,1,0:T(8,128)(2,1)S(1)}, f16[8,32,128]{2,1,0:T(8,128)(2,1)S(1)}, u32[]{:S(2)}, u32[]{:S(2)}) collective-permute-start(f16[8,32,128]{2,1,0:T(8,128)(2,1)S(1)} %fusion.14), channel_id=1, source_target_pairs={{4,0},{5,1},{6,2},{7,3},{0,4},{1,5},{2,6},{3,7},{12,8},{13,9},{14,... | collective-permute-start | bytes 196616 | tf_op jit(solution)/shard_map/ppermute | solution.py:341
  61.3 1.5 %collective-permute-start.17 = (f16[8,32,128]{2,1,0:T(8,128)(2,1)S(1)}, f16[8,32,128]{2,1,0:T(8,128)(2,1)S(1)}, u32[]{:S(2)}, u32[]{:S(2)}) collective-permute-start(f16[8,32,128]{2,1,0:T(8,128)(2,1)S(1)} %fusion.14), channel_id=1, source_target_pairs={{6,0},{7,1},{4,2},{5,3},{2,4},{3,5},{0,6},{1,7},{14,8},{15,9},{12,... | collective-permute-start | bytes 196616 | tf_op jit(solution)/shard_map/ppermute | solution.py:341
  62.8 0.0 collective-permute-done.15
  62.8 0.6 collective-permute-done.16
  63.4 3.3 %collective-permute-done.17 = f16[8,32,128]{2,1,0:T(8,128)(2,1)S(1)} collective-permute-done((f16[8,32,128]{2,1,0:T(8,128)(2,1)S(1)}, f16[8,32,128]{2,1,0:T(8,128)(2,1)S(1)}, u32[]{:S(2)}, u32[]{:S(2)}) %collective-permute-start.17) | collective-permute-done | bytes 65568 | tf_op jit(solution)/shard_map/ppermute | solution.py:341
  66.7 0.1 pad_maximum_fusion.1
  66.8 2.1 %collective-permute-start.18 = (f16[4,8,32,128]{3,2,1,0:T(8,128)(2,1)S(1)}, f16[4,8,32,128]{3,2,1,0:T(8,128)(2,1)S(1)}, u32[]{:S(2)}, u32[]{:S(2)}) collective-permute-start(f16[4,8,32,128]{3,2,1,0:T(8,128)(2,1)S(1)} %pad_maximum_fusion.1), channel_id=1, source_target_pairs={{0,1},{1,0},{2,3},{3,2},{4,5},{5,4},{6,7},{7,6},{8,9},{9,8},{10,11... | collective-permute-start | bytes 786440 | tf_op jit(solution)/shard_map/ppermute | solution.py:369
  68.9 1.2 %collective-permute-done.18 = f16[4,8,32,128]{3,2,1,0:T(8,128)(2,1)S(1)} collective-permute-done((f16[4,8,32,128]{3,2,1,0:T(8,128)(2,1)S(1)}, f16[4,8,32,128]{3,2,1,0:T(8,128)(2,1)S(1)}, u32[]{:S(2)}, u32[]{:S(2)}) %collective-permute-start.18) | collective-permute-done | bytes 262176 | tf_op jit(solution)/shard_map/ppermute | solution.py:369
  70.1 0.2 broadcast_select_fusion
  70.3 0.1 rev.3
  70.3 0.2 fusion.3
  70.5 1.1 %maximum_convert_fusion = f32[16,128,128]{2,1,0:T(8,128)} fusion(f16[16,32,128]{2,1,0:T(8,128)(2,1)S(1)} %get-tuple-element.36, f16[16,32,128]{2,1,0:T(8,128)(2,1)S(1)} %get-tuple-element.35, f16[16,32,128]{2,1,0:T(8,128)(2,1)S(1)} %get-tuple-element.34, f16[16,32,128]{2,1,0:T(8,128)(2,1)S(1)} %get-tuple-element.33), kind=kLoop, calls=%fused_computation.8 | loop fusion | flops 1048576 | bytes 1572864 | tf_op jit(solution)/shard_map/convert_element_type | solution.py:377
  (25 shorter events, 0.3 us)
Async XLA Ops:
  0.0 10.1 %copy-start.1 = (bf16[2,16,128,128]{3,2,1,0:T(8,128)(2,1)S(1)}, bf16[2,16,128,128]{3,2,1,0:T(8,128)(2,1)}, u32[]{:S(2)}) copy-start(bf16[2,16,128,128]{3,2,1,0:T(8,128)(2,1)} %reward.3) | copy-start | bytes 3145732
  0.0 10.1 %copy-start.2 = (s32[2]{0:T(128)S(1)}, s32[2]{0:T(128)}, u32[]{:S(2)}) copy-start(s32[2]{0:T(128)} %own_set.7) | copy-start | bytes 28
  0.0 10.1 %copy-start = (f32[16,128,128]{2,1,0:T(8,128)S(1)}, f32[16,128,128]{2,1,0:T(8,128)}, u32[]{:S(2)}) copy-start(f32[16,128,128]{2,1,0:T(8,128)} %speed.3) | copy-start | bytes 3145732
  0.0 9.9 %copy-start.4 = (f32[16,3]{0,1:T(4,128)S(1)}, f32[16,3]{0,1:T(4,128)}, u32[]{:S(2)}) copy-start(f32[16,3]{0,1:T(4,128)} %param.10) | copy-start | bytes 580
  0.0 10.0 %copy-start.5 = (f32[16,3]{0,1:T(4,128)S(1)}, f32[16,3]{0,1:T(4,128)}, u32[]{:S(2)}) copy-start(f32[16,3]{0,1:T(4,128)} %param.11) | copy-start | bytes 580
  0.0 10.0 %collective-permute-start.1 = (bf16[2,16,128,128]{3,2,1,0:T(8,128)(2,1)}, bf16[2,16,128,128]{3,2,1,0:T(8,128)(2,1)}, u32[]{:S(2)}, u32[]{:S(2)}) collective-permute-start(bf16[2,16,128,128]{3,2,1,0:T(8,128)(2,1)} %reward.3), channel_id=1, source_target_pairs={{0,1},{1,0},{2,3},{3,2},{4,5},{5,4},{6,7},{7,6},{8,9},{9,8},{10,11... | collective-permute-start | bytes 3145736 | tf_op jit(solution)/shard_map/ppermute | solution.py:305
  0.8 2.3 %collective-permute-start = (s32[2]{0:T(128)}, s32[2]{0:T(128)S(1)}, u32[]{:S(2)}, u32[]{:S(2)}) collective-permute-start(s32[2]{0:T(128)} %own_set.7), channel_id=1, source_target_pairs={{0,1},{1,0},{2,3},{3,2},{4,5},{5,4},{6,7},{7,6},{8,9},{9,8},{10,11... | collective-permute-start | bytes 32 | tf_op jit(solution)/shard_map/ppermute | solution.py:304
  2.3 0.7 %copy-start.3 = (bf16[9,128,128]{2,1,0:T(8,128)(2,1)}, bf16[9,128,128]{2,1,0:T(8,128)(2,1)S(1)}, u32[]{:S(2)}) copy-start(bf16[9,128,128]{2,1,0:T(8,128)(2,1)S(1)} %get-tuple-element.25) | copy-start | bytes 884740
  3.0 13.3 %collective-permute-start.2 = (bf16[9,128,128]{2,1,0:T(8,128)(2,1)}, bf16[9,128,128]{2,1,0:T(8,128)(2,1)S(1)}, u32[]{:S(2)}, u32[]{:S(2)}) collective-permute-start(bf16[9,128,128]{2,1,0:T(8,128)(2,1)} %copy-done.3), channel_id=1, source_target_pairs={{1,9},{9,1},{3,11},{11,3},{5,13},{13,5},{7,15},{15,7},{8,16},{16,8... | collective-permute-start | bytes 884744 | tf_op jit(solution)/shard_map/ppermute | solution.py:326
  6.2 10.2 %collective-permute-start.3 = (bf16[4,128,128]{2,1,0:T(8,128)(2,1)S(1)}, bf16[4,128,128]{2,1,0:T(8,128)(2,1)S(1)}, u32[]{:S(2)}, u32[]{:S(2)}) collective-permute-start(bf16[4,128,128]{2,1,0:T(8,128)(2,1)S(1)} %get-tuple-element.26), channel_id=1, source_target_pairs={{0,9},{8,1},{2,11},{10,3},{4,13},{12,5},{6,15},{14,7},{9,16},{17,8... | collective-permute-start | bytes 393224 | tf_op jit(solution)/shard_map/ppermute | solution.py:327
  19.6 5.8 %collective-permute-start.4 = (f16[8,32,128]{2,1,0:T(8,128)(2,1)S(1)}, f16[8,32,128]{2,1,0:T(8,128)(2,1)S(1)}, u32[]{:S(2)}, u32[]{:S(2)}) collective-permute-start(f16[8,32,128]{2,1,0:T(8,128)(2,1)S(1)} %get-tuple-element.46), channel_id=1, source_target_pairs={{0,6},{1,7},{2,4},{3,5},{4,2},{5,3},{6,0},{7,1},{8,14},{9,15},{10,... | collective-permute-start | bytes 196616 | tf_op jit(solution)/shard_map/ppermute | solution.py:334
  23.0 5.6 %collective-permute-start.5 = (f16[8,32,128]{2,1,0:T(8,128)(2,1)S(1)}, f16[8,32,128]{2,1,0:T(8,128)(2,1)S(1)}, u32[]{:S(2)}, u32[]{:S(2)}) collective-permute-start(f16[8,32,128]{2,1,0:T(8,128)(2,1)S(1)} %get-tuple-element.48), channel_id=1, source_target_pairs={{0,4},{1,5},{2,6},{3,7},{4,0},{5,1},{6,2},{7,3},{8,12},{9,13},{10,... | collective-permute-start | bytes 196616 | tf_op jit(solution)/shard_map/ppermute | solution.py:334
  23.0 5.6 %collective-permute-start.6 = (f16[8,32,128]{2,1,0:T(8,128)(2,1)S(1)}, f16[8,32,128]{2,1,0:T(8,128)(2,1)S(1)}, u32[]{:S(2)}, u32[]{:S(2)}) collective-permute-start(f16[8,32,128]{2,1,0:T(8,128)(2,1)S(1)} %get-tuple-element.47), channel_id=1, source_target_pairs={{0,2},{1,3},{2,0},{3,1},{4,6},{5,7},{6,4},{7,5},{8,10},{9,11},{10,... | collective-permute-start | bytes 196616 | tf_op jit(solution)/shard_map/ppermute | solution.py:334
  28.7 3.6 %collective-permute-start.7 = (f16[8,32,128]{2,1,0:T(8,128)(2,1)S(1)}, f16[8,32,128]{2,1,0:T(8,128)(2,1)S(1)}, u32[]{:S(2)}, u32[]{:S(2)}) collective-permute-start(f16[8,32,128]{2,1,0:T(8,128)(2,1)S(1)} %fusion.23), channel_id=1, source_target_pairs={{2,0},{3,1},{0,2},{1,3},{6,4},{7,5},{4,6},{5,7},{10,8},{11,9},{8,1... | collective-permute-start | bytes 196616 | tf_op jit(solution)/shard_map/ppermute | solution.py:341
  29.7 4.5 %collective-permute-start.8 = (f16[8,32,128]{2,1,0:T(8,128)(2,1)S(1)}, f16[8,32,128]{2,1,0:T(8,128)(2,1)S(1)}, u32[]{:S(2)}, u32[]{:S(2)}) collective-permute-start(f16[8,32,128]{2,1,0:T(8,128)(2,1)S(1)} %fusion.23), channel_id=1, source_target_pairs={{4,0},{5,1},{6,2},{7,3},{0,4},{1,5},{2,6},{3,7},{12,8},{13,9},{14,... | collective-permute-start | bytes 196616 | tf_op jit(solution)/shard_map/ppermute | solution.py:341
  31.3 4.9 %collective-permute-start.9 = (f16[8,32,128]{2,1,0:T(8,128)(2,1)S(1)}, f16[8,32,128]{2,1,0:T(8,128)(2,1)S(1)}, u32[]{:S(2)}, u32[]{:S(2)}) collective-permute-start(f16[8,32,128]{2,1,0:T(8,128)(2,1)S(1)} %fusion.23), channel_id=1, source_target_pairs={{6,0},{7,1},{4,2},{5,3},{2,4},{3,5},{0,6},{1,7},{14,8},{15,9},{12,... | collective-permute-start | bytes 196616 | tf_op jit(solution)/shard_map/ppermute | solution.py:341
  36.3 4.7 %collective-permute-start.11 = (f16[4,3,32,128]{3,2,1,0:T(8,128)(2,1)S(1)}, f16[4,3,32,128]{3,2,1,0:T(8,128)(2,1)S(1)}, u32[]{:S(2)}, u32[]{:S(2)}) collective-permute-start(f16[4,3,32,128]{3,2,1,0:T(8,128)(2,1)S(1)} %get-tuple-element.43), channel_id=1, source_target_pairs={{0,1},{1,0},{2,3},{3,2},{4,5},{5,4},{6,7},{7,6},{8,9},{9,8},{10,11... | collective-permute-start | bytes 294920 | tf_op jit(solution)/shard_map/ppermute | solution.py:360
  39.0 7.8 %collective-permute-start.10 = (bf16[4,3,32,128]{3,2,1,0:T(8,128)(2,1)S(1)}, bf16[4,3,32,128]{3,2,1,0:T(8,128)(2,1)S(1)}, u32[]{:S(2)}, u32[]{:S(2)}) collective-permute-start(bf16[4,3,32,128]{3,2,1,0:T(8,128)(2,1)S(1)} %get-tuple-element.42), channel_id=1, source_target_pairs={{1,9},{9,1},{3,11},{11,3},{5,13},{13,5},{7,15},{15,7},{8,16},{16,8... | collective-permute-start | bytes 294920 | tf_op jit(solution)/shard_map/ppermute | solution.py:361
  50.1 5.1 %collective-permute-start.12 = (f16[8,32,128]{2,1,0:T(8,128)(2,1)S(1)}, f16[8,32,128]{2,1,0:T(8,128)(2,1)S(1)}, u32[]{:S(2)}, u32[]{:S(2)}) collective-permute-start(f16[8,32,128]{2,1,0:T(8,128)(2,1)S(1)} %get-tuple-element.39), channel_id=1, source_target_pairs={{0,6},{1,7},{2,4},{3,5},{4,2},{5,3},{6,0},{7,1},{8,14},{9,15},{10,... | collective-permute-start | bytes 196616 | tf_op jit(solution)/shard_map/ppermute | solution.py:334
  52.1 7.0 %collective-permute-start.13 = (f16[8,32,128]{2,1,0:T(8,128)(2,1)S(1)}, f16[8,32,128]{2,1,0:T(8,128)(2,1)S(1)}, u32[]{:S(2)}, u32[]{:S(2)}) collective-permute-start(f16[8,32,128]{2,1,0:T(8,128)(2,1)S(1)} %get-tuple-element.41), channel_id=1, source_target_pairs={{0,4},{1,5},{2,6},{3,7},{4,0},{5,1},{6,2},{7,3},{8,12},{9,13},{10,... | collective-permute-start | bytes 196616 | tf_op jit(solution)/shard_map/ppermute | solution.py:334
  52.7 6.4 %collective-permute-start.14 = (f16[8,32,128]{2,1,0:T(8,128)(2,1)S(1)}, f16[8,32,128]{2,1,0:T(8,128)(2,1)S(1)}, u32[]{:S(2)}, u32[]{:S(2)}) collective-permute-start(f16[8,32,128]{2,1,0:T(8,128)(2,1)S(1)} %get-tuple-element.40), channel_id=1, source_target_pairs={{0,2},{1,3},{2,0},{3,1},{4,6},{5,7},{6,4},{7,5},{8,10},{9,11},{10,... | collective-permute-start | bytes 196616 | tf_op jit(solution)/shard_map/ppermute | solution.py:334
  59.2 3.6 %collective-permute-start.15 = (f16[8,32,128]{2,1,0:T(8,128)(2,1)S(1)}, f16[8,32,128]{2,1,0:T(8,128)(2,1)S(1)}, u32[]{:S(2)}, u32[]{:S(2)}) collective-permute-start(f16[8,32,128]{2,1,0:T(8,128)(2,1)S(1)} %fusion.14), channel_id=1, source_target_pairs={{2,0},{3,1},{0,2},{1,3},{6,4},{7,5},{4,6},{5,7},{10,8},{11,9},{8,1... | collective-permute-start | bytes 196616 | tf_op jit(solution)/shard_map/ppermute | solution.py:341
  59.2 4.1 %collective-permute-start.16 = (f16[8,32,128]{2,1,0:T(8,128)(2,1)S(1)}, f16[8,32,128]{2,1,0:T(8,128)(2,1)S(1)}, u32[]{:S(2)}, u32[]{:S(2)}) collective-permute-start(f16[8,32,128]{2,1,0:T(8,128)(2,1)S(1)} %fusion.14), channel_id=1, source_target_pairs={{4,0},{5,1},{6,2},{7,3},{0,4},{1,5},{2,6},{3,7},{12,8},{13,9},{14,... | collective-permute-start | bytes 196616 | tf_op jit(solution)/shard_map/ppermute | solution.py:341
  61.3 5.4 %collective-permute-start.17 = (f16[8,32,128]{2,1,0:T(8,128)(2,1)S(1)}, f16[8,32,128]{2,1,0:T(8,128)(2,1)S(1)}, u32[]{:S(2)}, u32[]{:S(2)}) collective-permute-start(f16[8,32,128]{2,1,0:T(8,128)(2,1)S(1)} %fusion.14), channel_id=1, source_target_pairs={{6,0},{7,1},{4,2},{5,3},{2,4},{3,5},{0,6},{1,7},{14,8},{15,9},{12,... | collective-permute-start | bytes 196616 | tf_op jit(solution)/shard_map/ppermute | solution.py:341
  66.8 3.3 %collective-permute-start.18 = (f16[4,8,32,128]{3,2,1,0:T(8,128)(2,1)S(1)}, f16[4,8,32,128]{3,2,1,0:T(8,128)(2,1)S(1)}, u32[]{:S(2)}, u32[]{:S(2)}) collective-permute-start(f16[4,8,32,128]{3,2,1,0:T(8,128)(2,1)S(1)} %pad_maximum_fusion.1), channel_id=1, source_target_pairs={{0,1},{1,0},{2,3},{3,2},{4,5},{5,4},{6,7},{7,6},{8,9},{9,8},{10,11... | collective-permute-start | bytes 786440 | tf_op jit(solution)/shard_map/ppermute | solution.py:369

commit v5 on v4

--- a/solution.py
+++ b/solution.py
@@ -9,6 +9,7 @@
 
 SUBSTEPS = 3
 PAD = 8
+CHUNK = 32
 LOWEST = -3.0e38
 
 
@@ -41,37 +42,56 @@
     return rates, sizes, 1.0 - 2.0 * (rates[0] + rates[1] + rates[2]), sizes[0] + sizes[1] + sizes[2], drifts
 
 
-def stencil(coef, src, row, speed, reward, winds):
-    ny = src.shape[1] - 2 * PAD
-    lines = pl.ds(PAD, ny)
-    center = src[row, lines, :]
-    y_ahead = src[row, pl.ds(PAD + 1, ny), :]
-    y_behind = src[row, pl.ds(PAD - 1, ny), :]
-    x_sum = src[row + 1, lines, :] + src[row - 1, lines, :]
-    x_wind = src[row + winds[0], lines, :]
+def taps(src, rows, first, size):
+    lines = pl.ds(PAD + first, size)
+    behind, center = src[rows[0] - 1, lines, :], src[rows[0], lines, :]
     nz = center.shape[1]
     lane = lax.broadcasted_iota(jnp.int32, center.shape, 1)
-    z_ahead = jnp.where(lane == nz - 1, 0.0, pltpu.roll(center, nz - 1, 1))
-    z_behind = jnp.where(lane == 0, 0.0, pltpu.roll(center, 1, 1))
-    y_wind = jnp.where(winds[1], y_ahead, y_behind)
-    z_wind = jnp.where(winds[2], z_ahead, z_behind)
+    for row in rows:
+        ahead = src[row + 1, lines, :]
+        y_ahead = src[row, pl.ds(PAD + first + 1, size), :]
+        y_behind = src[row, pl.ds(PAD + first - 1, size), :]
+        z_ahead = jnp.where(lane == nz - 1, 0.0, pltpu.roll(center, nz - 1, 1))
+        z_behind = jnp.where(lane == 0, 0.0, pltpu.roll(center, 1, 1))
+        yield row, center, ((ahead, behind), (y_ahead, y_behind), (z_ahead, z_behind))
+        behind, center = center, ahead
+
+
+def blend(coef, ups, center, sides, sums, speed, reward):
     rates, sizes, weight, size, _ = coef
-    still = reward + weight * center + rates[0] * x_sum
-    still = still + rates[1] * (y_ahead + y_behind) + rates[2] * (z_ahead + z_behind)
-    wind = sizes[0] * x_wind + sizes[1] * y_wind + sizes[2] * z_wind
+    winds = [jnp.where(up, *side) for up, side in zip(ups, sides)]
+    still = reward + weight * center + rates[0] * sums[0]
+    still = still + rates[1] * sums[1] + rates[2] * sums[2]
+    wind = sizes[0] * winds[0] + sizes[1] * winds[1] + sizes[2] * winds[2]
     return still + speed * (wind - size * center)
 
 
+def sweep(place, sets, ctrls, src, rows, speed, reward, store):
+    ny = src.shape[1] - 2 * PAD
+    coefs = [coefficients(sets, ctrl) for ctrl in ctrls]
+    ups = [winds_of(place, coef[4]) for coef in coefs]
+    size = min(ny, CHUNK)
+    for first in range(0, ny, size):
+        spot = pl.ds(first, size)
+        for row, center, sides in taps(src, rows, first, size):
+            sums = [ahead + behind for ahead, behind in sides]
+            pace = speed(row, spot)
+            for ctrl, coef, up in zip(ctrls, coefs, ups):
+                store(ctrl, row, first, size, blend(coef, up, center, sides, sums, pace, reward(ctrl, row, spot)))
+
+
 def winds_of(place, drifts):
-    step = jnp.where(drifts[0] > 0.0, 1, -1)
-    return jnp.where(place[1] == 0, step, -step), drifts[1] > 0.0, drifts[2] > 0.0
-
-
-def put_max(place, out, index, new):
+    x_up = jnp.where(place[1] == 0, drifts[0], -drifts[0]) > 0.0
+    return x_up, drifts[1] > 0.0, drifts[2] > 0.0
+
+
+def put_max(place, out, index, first, new):
     chips, width = out.shape[0], out.shape[2]
-    for shard in range(chips):
-        spot = mate_step(place[0], shard, chips)
-        out[spot, index] = jnp.maximum(out[spot, index], new[shard * width : (shard + 1) * width])
+    size = min(width, new.shape[0])
+    for part in range(0, new.shape[0], size):
+        spot = mate_step(place[0], (first + part) // width, chips)
+        lines = pl.ds((first + part) % width, size)
+        out[spot, index, lines, :] = jnp.maximum(out[spot, index, lines, :], new[part : part + size])
 
 
 def start_max(out):
@@ -81,6 +101,10 @@
 
 
 def clear_pads(field, ny):
+    if len(field.shape) > 3:
+        for part in range(field.shape[0]):
+            clear_pads(field.at[part], ny)
+        return
     zero = jnp.zeros((PAD, field.shape[2]), field.dtype)
     for row in range(field.shape[0]):
         field[row, 0:PAD, :] = zero
@@ -112,61 +136,89 @@
 
 
 def early_march(place, sets, half, block, speed_rows, reward_rows, out, keeps, fields):
-    ny = block.shape[1] - 2 * PAD
+    count = reward_rows.shape[0]
     start_max(out)
 
+    def speed(q, spot):
+        return speed_rows[q, spot, :]
+
+    def reward(ctrl, q, spot):
+        return reward_rows[ctrl, q, spot, :]
+
+    def keep(substep, ctrl, q, first, size, new):
+        if q < substep + 3:
+            keeps[substep][ctrl, q - substep - 1, pl.ds(first, size), :] = new
+
+    def store(ctrl, q, first, size, new):
+        fields[0][ctrl, q, pl.ds(PAD + first, size), :] = new
+        keep(0, ctrl, q, first, size, new)
+
+    sweep(place, sets, range(count), block, range(1, half + SUBSTEPS - 1), speed, reward, store)
+
     def one(ctrl, carry):
-        coef = coefficients(sets, ctrl)
-        winds = winds_of(place, coef[4])
-        source = block
-        for substep in range(SUBSTEPS):
-            for q in range(1 + substep, half + SUBSTEPS - 1 - substep):
-                new = stencil(coef, source, q, speed_rows[q], reward_rows[ctrl, q], winds)
-                if substep == SUBSTEPS - 1:
-                    put_max(place, out, q - SUBSTEPS, new)
-                    continue
-                fields[substep][q, pl.ds(PAD, ny), :] = new
-                if q < substep + 3:
-                    keeps[substep][ctrl, q - substep - 1] = new
-            if substep < SUBSTEPS - 1:
-                source = fields[substep]
+        source = fields[0].at[ctrl]
+        for substep in range(1, SUBSTEPS):
+            last = substep == SUBSTEPS - 1
+
+            def store(ctrl, q, first, size, new, substep=substep, last=last):
+                if last:
+                    put_max(place, out, q - SUBSTEPS, first, new)
+                    return
+                fields[substep][q, pl.ds(PAD + first, size), :] = new
+                keep(substep, ctrl, q, first, size, new)
+
+            rows = range(1 + substep, half + SUBSTEPS - 1 - substep)
+            sweep(place, sets, [ctrl], source, rows, speed, reward, store)
+            source = None if last else fields[substep]
         return carry
 
-    lax.fori_loop(0, reward_rows.shape[0], one, 0)
+    lax.fori_loop(0, count, one, 0)
 
 
 def rest_march(place, sets, edge, lower_rows, block, speed_rows, reward_rows, out, keeps, fields):
     ny = block.shape[1] - 2 * PAD
+    count = reward_rows.shape[0]
     margin = SUBSTEPS - 1
     inside = place[2].astype(jnp.float32)
     start_max(out)
 
+    def speed(row, spot):
+        q = row - SUBSTEPS
+        if q < 0:
+            return edge[SUBSTEPS - 1 - q, spot, :].astype(jnp.float32)
+        return speed_rows[q, spot, :]
+
+    def reward(ctrl, row, spot):
+        q = row - SUBSTEPS
+        if q < 0:
+            return lower_rows[ctrl * margin - 1 - q, spot, :].astype(jnp.float32)
+        return reward_rows[ctrl, q, spot, :]
+
+    def store(ctrl, row, first, size, new):
+        fields[0][ctrl, row, pl.ds(PAD + first, size), :] = new * inside if row < SUBSTEPS else new
+
+    sweep(place, sets, range(count), block, range(1, SUBSTEPS + 1), speed, reward, store)
+
     def one(ctrl, carry):
-        coef = coefficients(sets, ctrl)
-        winds = winds_of(place, coef[4])
-        source = block
-        for substep in range(SUBSTEPS):
-            for q in range(substep + 1 - SUBSTEPS, 1 + substep):
-                if q < 0:
-                    speed = edge[SUBSTEPS - 1 - q].astype(jnp.float32)
-                    reward = lower_rows[ctrl * margin - 1 - q].astype(jnp.float32)
-                else:
-                    speed, reward = speed_rows[q], reward_rows[ctrl, q]
-                new = stencil(coef, source, q + SUBSTEPS, speed, reward, winds)
-                if substep == SUBSTEPS - 1:
-                    put_max(place, out, q, new)
-                    continue
-                if q < 0:
-                    new = new * inside
-                fields[substep][q + SUBSTEPS, pl.ds(PAD, ny), :] = new
-            if substep < SUBSTEPS - 1:
-                source = fields[substep]
-                for kept in range(2):
-                    row = 1 + substep + kept + SUBSTEPS
-                    source[row, pl.ds(PAD, ny), :] = keeps[substep][ctrl, kept]
+        source = fields[0].at[ctrl]
+        for substep in range(1, SUBSTEPS):
+            last = substep == SUBSTEPS - 1
+            for kept in range(2):
+                source[substep + kept + SUBSTEPS, pl.ds(PAD, ny), :] = keeps[substep - 1][ctrl, kept]
+
+            def store(ctrl, row, first, size, new, substep=substep, last=last):
+                if last:
+                    put_max(place, out, row - SUBSTEPS, first, new)
+                    return
+                new = new * inside if row < SUBSTEPS else new
+                fields[substep][row, pl.ds(PAD + first, size), :] = new
+
+            rows = range(1 + substep, SUBSTEPS + 1 + substep)
+            sweep(place, sets, [ctrl], source, rows, speed, reward, store)
+            source = None if last else fields[substep]
         return carry
 
-    lax.fori_loop(0, reward_rows.shape[0], one, 0)
+    lax.fori_loop(0, count, one, 0)
 
 
 def pack_kernel(value, speed, reward, edge, far, block, speed_rows, value_sem, speed_sem, near_sem, far_sem):
@@ -283,7 +335,9 @@
 
     def call(kernel, rows, marched, arrays, outs):
         field = pltpu.VMEM((rows, ny + 2 * PAD, nz), jnp.float32)
-        scratch = [field] * (2 if kernel is early_first else 3)
+        scratch = [pltpu.VMEM((count, rows, ny + 2 * PAD, nz), jnp.float32)] + [field] * (SUBSTEPS - 2)
+        if kernel is not early_first:
+            scratch.append(field)
         if kernel in (rest_first, rest_later):
             scratch.append(pltpu.VMEM((count * margin, ny, nz), narrow))
         return pl.pallas_call(
@@ -292,7 +346,7 @@
             in_specs=[scalars] * 4 + [whole] * len(arrays),
             out_specs=jax.tree.map(lambda _: whole, outs),
             scratch_shapes=scratch,
-            compiler_params=pltpu.CompilerParams(vmem_limit_bytes=32 * 2**20),
+            compiler_params=pltpu.CompilerParams(vmem_limit_bytes=16 * 2**20),
             cost_estimate=pl.CostEstimate(
                 flops=25 * count * marched * ny * nz, bytes_accessed=12 * count * marched * ny * nz, transcendentals=0
             ),

time: 71.8 us -> 70.7 us (0.985)
  Pallas kernels: 19.8 us -> 18.6 us
    ppermute x6, waiting for transfers between devices: 7.81 us -> 9.18 us  [gather(): pieces.append(lax.ppermute(mine, 'ctrl', pairs))]
    ppermute x6, waiting for transfers between devices: 10.6 us -> 9.33 us  [reduce(): mine = jnp.maximum(mine, lax.ppermute(parts[step], 'ctrl', pairs))]
    pallas_call x4, Pallas kernels: 18.3 us -> 17.1 us  [call(): pl.pallas_call(functools.partial(kernel, half=half), out_shape=outs, in_s...]
  transfers between devices with their start and end apart: 19 -> 19, of which waited for: 9 -> 9; matrix products, arithmetic and copies ran while one was open for 0% -> 0% of each run, Pallas kernels for 19% -> 18%
where the time goes in v5:
time: 70.7 us; the launch traced here: 70.5 us
  starting transfers between devices  29 us (41%)
  waiting for transfers between devices  19.7 us (28%)
  Pallas kernels  18.6 us (26%)
  other arithmetic  1.99 us (3%)
  local copies, waits for them, and re-layouts  0.95 us (1%)
    pallas_call x4, Pallas kernels, call(): pl.pallas_call(functools.partial(kernel, half=half), out_shape=outs, in_s...  17.1 us
    ppermute x6, waiting for transfers between devices, reduce(): mine = jnp.maximum(mine, lax.ppermute(parts[step], 'ctrl', pairs))  9.33 us
    ppermute x6, waiting for transfers between devices, gather(): pieces.append(lax.ppermute(mine, 'ctrl', pairs))  9.18 us
    ppermute x6, starting transfers between devices, reduce(): mine = jnp.maximum(mine, lax.ppermute(parts[step], 'ctrl', pairs))  7.36 us
    ppermute x6, starting transfers between devices, gather(): pieces.append(lax.ppermute(mine, 'ctrl', pairs))  7.22 us
    ppermute x1, starting transfers between devices, body(): edge_other = lax.ppermute(far, both, beside)  3.73 us
    ppermute x1, starting transfers between devices, body(): edge = lax.ppermute(packed, both, facing)  3.11 us
    ppermute x1, starting transfers between devices, body(): across = lax.ppermute(pieces[:, -SUBSTEPS:], 'ctrl', partners)  2.61 us
  transfers between devices with their start and end apart: 19, of which 9 were waited for; matrix products, arithmetic and copies ran while one was open for 0% of the time, Pallas kernels for 18%

profile of v5, /device:TPU:5, one launch (start us, length us, event | category | flops | bytes accessed | tf_op | source)
XLA Modules:
  0.0 70.5 jit_solution(2242701710901593875)
XLA Ops:
  0.0 0.7 %collective-permute-start.1 = (bf16[2,16,128,128]{3,2,1,0:T(8,128)(2,1)}, bf16[2,16,128,128]{3,2,1,0:T(8,128)(2,1)}, u32[]{:S(2)}, u32[]{:S(2)}) collective-permute-start(bf16[2,16,128,128]{3,2,1,0:T(8,128)(2,1)} %reward.3), channel_id=1, source_target_pairs={{0,1},{1,0},{2,3},{3,2},{4,5},{5,4},{6,7},{7,6},{8,9},{9,8},{10,11... | collective-permute-start | bytes 3145736 | tf_op jit(solution)/shard_map/ppermute | solution.py:359
  0.8 0.1 collective-permute-start
  0.9 1.5 %shard_map.64 = (bf16[9,128,128]{2,1,0:T(8,128)(2,1)S(1)}, bf16[4,128,128]{2,1,0:T(8,128)(2,1)S(1)}, f32[11,144,128]{2,1,0:T(8,128)S(1)}) custom-call(f32[16,128,128]{2,1,0:T(8,128)} %value.1, f32[16,128,128]{2,1,0:T(8,128)} %speed.3, bf16[2,16,128,128]{3,2,1,0:T(8,128)(2,1)} %reward.3), custom_call_target="tpu_custom_call" | custom-call | tf_op jit(solution)/shard_map/pallas_call | solution.py:362
  2.3 0.0 copy-start.3
  2.3 0.7 copy-done.3
  3.0 3.1 %collective-permute-start.2 = (bf16[9,128,128]{2,1,0:T(8,128)(2,1)}, bf16[9,128,128]{2,1,0:T(8,128)(2,1)S(1)}, u32[]{:S(2)}, u32[]{:S(2)}) collective-permute-start(bf16[9,128,128]{2,1,0:T(8,128)(2,1)} %copy-done.3), channel_id=1, source_target_pairs={{1,9},{9,1},{3,11},{11,3},{5,13},{13,5},{7,15},{15,7},{8,16},{16,8... | collective-permute-start | bytes 884744 | tf_op jit(solution)/shard_map/ppermute | solution.py:380
  6.2 3.7 %collective-permute-start.3 = (bf16[4,128,128]{2,1,0:T(8,128)(2,1)S(1)}, bf16[4,128,128]{2,1,0:T(8,128)(2,1)S(1)}, u32[]{:S(2)}, u32[]{:S(2)}) collective-permute-start(bf16[4,128,128]{2,1,0:T(8,128)(2,1)S(1)} %get-tuple-element.26), channel_id=1, source_target_pairs={{0,9},{8,1},{2,11},{10,3},{4,13},{12,5},{6,15},{14,7},{9,16},{17,8... | collective-permute-start | bytes 393224 | tf_op jit(solution)/shard_map/ppermute | solution.py:381
  9.9 0.1 copy.13.drift_sets
  10.0 0.1 copy.14.diffusion_sets
  10.1 0.0 collective-permute-done.1.other
  10.1 5.9 %shard_map.65 = (f32[4,5,32,128]{3,2,1,0:T(8,128)S(1)}, f32[4,2,128,128]{3,2,1,0:T(8,128)S(1)}, f32[4,2,128,128]{3,2,1,0:T(8,128)S(1)}, f32[10,128,128]{2,1,0:T(8,128)S(1)}, f32[4,10,128,128]{3,2,1,0:T(8,128)S(1)}) custom-call(s32[2]{0:T(128)S(1)} %copy-done.2, s32[2]{0:T(128)S(1)} %collective-permute-done.other_set, f32[16,3]{1,0:T(8,128)S(1)} %copy.13.drift_sets, ...), custom_call_target="tpu_custom_call" | custom-call | flops 34406400 | bytes 16515072 | tf_op jit(solution)/shard_map/pallas_call | solution.py:343
  16.0 0.0 collective-permute-done.3.refs_0_
  16.0 2.9 %shard_map.66 = f32[4,3,32,128]{3,2,1,0:T(8,128)S(1)} custom-call(s32[2]{0:T(128)S(1)} %copy-done.2, s32[2]{0:T(128)S(1)} %collective-permute-done.other_set, f32[16,3]{1,0:T(8,128)S(1)} %copy.13.drift_sets, f32[16,3]{1,0:T(8,128)S(1)} %copy.14.diffusion_sets, f32[11,144,128]{2,1,0:T(8,128)S(1)} %get-tuple-element.22.block.first, ...), custom_call_target="tpu_custom_call" | custom-call | flops 14745600 | bytes 7077888 | tf_op jit(solution)/shard_map/pallas_call | solution.py:343
  19.0 0.1 fusion.25
  19.0 3.4 %collective-permute-start.4 = (f16[8,32,128]{2,1,0:T(8,128)(2,1)S(1)}, f16[8,32,128]{2,1,0:T(8,128)(2,1)S(1)}, u32[]{:S(2)}, u32[]{:S(2)}) collective-permute-start(f16[8,32,128]{2,1,0:T(8,128)(2,1)S(1)} %get-tuple-element.46), channel_id=1, source_target_pairs={{0,6},{1,7},{2,4},{3,5},{4,2},{5,3},{6,0},{7,1},{8,14},{9,15},{10,... | collective-permute-start | bytes 196616 | tf_op jit(solution)/shard_map/ppermute | solution.py:388
  22.4 0.4 collective-permute-start.6
  22.8 1.4 %collective-permute-done.4 = f16[8,32,128]{2,1,0:T(8,128)(2,1)S(1)} collective-permute-done((f16[8,32,128]{2,1,0:T(8,128)(2,1)S(1)}, f16[8,32,128]{2,1,0:T(8,128)(2,1)S(1)}, u32[]{:S(2)}, u32[]{:S(2)}) %collective-permute-start.4) | collective-permute-done | bytes 65568 | tf_op jit(solution)/shard_map/ppermute | solution.py:388
  24.2 4.0 %collective-permute-done.5 = f16[8,32,128]{2,1,0:T(8,128)(2,1)S(1)} collective-permute-done((f16[8,32,128]{2,1,0:T(8,128)(2,1)S(1)}, f16[8,32,128]{2,1,0:T(8,128)(2,1)S(1)}, u32[]{:S(2)}, u32[]{:S(2)}) %collective-permute-start.5) | collective-permute-done | bytes 65568 | tf_op jit(solution)/shard_map/ppermute | solution.py:388
  28.1 0.0 collective-permute-done.6
  28.2 0.2 collective-permute-start.7
  28.4 1.9 %collective-permute-start.8 = (f16[8,32,128]{2,1,0:T(8,128)(2,1)S(1)}, f16[8,32,128]{2,1,0:T(8,128)(2,1)S(1)}, u32[]{:S(2)}, u32[]{:S(2)}) collective-permute-start(f16[8,32,128]{2,1,0:T(8,128)(2,1)S(1)} %fusion.23), channel_id=1, source_target_pairs={{4,0},{5,1},{6,2},{7,3},{0,4},{1,5},{2,6},{3,7},{12,8},{13,9},{14,... | collective-permute-start | bytes 196616 | tf_op jit(solution)/shard_map/ppermute | solution.py:395
  30.4 1.5 %collective-permute-start.9 = (f16[8,32,128]{2,1,0:T(8,128)(2,1)S(1)}, f16[8,32,128]{2,1,0:T(8,128)(2,1)S(1)}, u32[]{:S(2)}, u32[]{:S(2)}) collective-permute-start(f16[8,32,128]{2,1,0:T(8,128)(2,1)S(1)} %fusion.23), channel_id=1, source_target_pairs={{6,0},{7,1},{4,2},{5,3},{2,4},{3,5},{0,6},{1,7},{14,8},{15,9},{12,... | collective-permute-start | bytes 196616 | tf_op jit(solution)/shard_map/ppermute | solution.py:395
  31.8 0.0 collective-permute-done.7
  31.8 0.7 collective-permute-done.8
  32.5 3.2 %collective-permute-done.9 = f16[8,32,128]{2,1,0:T(8,128)(2,1)S(1)} collective-permute-done((f16[8,32,128]{2,1,0:T(8,128)(2,1)S(1)}, f16[8,32,128]{2,1,0:T(8,128)(2,1)S(1)}, u32[]{:S(2)}, u32[]{:S(2)}) %collective-permute-start.9) | collective-permute-done | bytes 65568 | tf_op jit(solution)/shard_map/ppermute | solution.py:395
  35.7 0.1 pad_maximum_fusion
  35.9 2.6 %collective-permute-start.11 = (f16[4,3,32,128]{3,2,1,0:T(8,128)(2,1)S(1)}, f16[4,3,32,128]{3,2,1,0:T(8,128)(2,1)S(1)}, u32[]{:S(2)}, u32[]{:S(2)}) collective-permute-start(f16[4,3,32,128]{3,2,1,0:T(8,128)(2,1)S(1)} %get-tuple-element.43), channel_id=1, source_target_pairs={{0,1},{1,0},{2,3},{3,2},{4,5},{5,4},{6,7},{7,6},{8,9},{9,8},{10,11... | collective-permute-start | bytes 294920 | tf_op jit(solution)/shard_map/ppermute | solution.py:414
  38.5 1.9 %collective-permute-start.10 = (bf16[4,3,32,128]{3,2,1,0:T(8,128)(2,1)S(1)}, bf16[4,3,32,128]{3,2,1,0:T(8,128)(2,1)S(1)}, u32[]{:S(2)}, u32[]{:S(2)}) collective-permute-start(bf16[4,3,32,128]{3,2,1,0:T(8,128)(2,1)S(1)} %get-tuple-element.42), channel_id=1, source_target_pairs={{1,9},{9,1},{3,11},{11,3},{5,13},{13,5},{7,15},{15,7},{8,16},{16,8... | collective-permute-start | bytes 294920 | tf_op jit(solution)/shard_map/ppermute | solution.py:415
  40.4 5.4 %shard_map.67 = (f32[4,5,32,128]{3,2,1,0:T(8,128)S(1)}, f32[4,2,128,128]{3,2,1,0:T(8,128)S(1)}, f32[4,2,128,128]{3,2,1,0:T(8,128)S(1)}) custom-call(s32[2]{0:T(128)S(1)} %copy-done.2, s32[2]{0:T(128)S(1)} %collective-permute-done.other_set, f32[16,3]{1,0:T(8,128)S(1)} %copy.13.drift_sets, f32[16,3]{1,0:T(8,128)S(1)} %copy.14.diffusion_sets, ...), custom_call_target="tpu_custom_call" | custom-call | flops 34406400 | bytes 16515072 | tf_op jit(solution)/shard_map/pallas_call | solution.py:343
  45.9 2.9 %shard_map.68 = f32[4,3,32,128]{3,2,1,0:T(8,128)S(1)} custom-call(s32[2]{0:T(128)S(1)} %copy-done.2, s32[2]{0:T(128)S(1)} %collective-permute-done.other_set, f32[16,3]{1,0:T(8,128)S(1)} %copy.13.drift_sets, f32[16,3]{1,0:T(8,128)S(1)} %copy.14.diffusion_sets, f32[4,8,32,128]{3,2,1,0:T(8,128)S(1)} %get-tuple-element.45.current, ...), custom_call_target="tpu_custom_call" | custom-call | flops 14745600 | bytes 7077888 | tf_op jit(solution)/shard_map/pallas_call | solution.py:343
  48.9 0.1 fusion.16
  48.9 1.7 %collective-permute-start.12 = (f16[8,32,128]{2,1,0:T(8,128)(2,1)S(1)}, f16[8,32,128]{2,1,0:T(8,128)(2,1)S(1)}, u32[]{:S(2)}, u32[]{:S(2)}) collective-permute-start(f16[8,32,128]{2,1,0:T(8,128)(2,1)S(1)} %get-tuple-element.39), channel_id=1, source_target_pairs={{0,6},{1,7},{2,4},{3,5},{4,2},{5,3},{6,0},{7,1},{8,14},{9,15},{10,... | collective-permute-start | bytes 196616 | tf_op jit(solution)/shard_map/ppermute | solution.py:388
  50.6 0.9 %collective-permute-start.13 = (f16[8,32,128]{2,1,0:T(8,128)(2,1)S(1)}, f16[8,32,128]{2,1,0:T(8,128)(2,1)S(1)}, u32[]{:S(2)}, u32[]{:S(2)}) collective-permute-start(f16[8,32,128]{2,1,0:T(8,128)(2,1)S(1)} %get-tuple-element.41), channel_id=1, source_target_pairs={{0,4},{1,5},{2,6},{3,7},{4,0},{5,1},{6,2},{7,3},{8,12},{9,13},{10,... | collective-permute-start | bytes 196616 | tf_op jit(solution)/shard_map/ppermute | solution.py:388
  51.5 1.0 %collective-permute-start.14 = (f16[8,32,128]{2,1,0:T(8,128)(2,1)S(1)}, f16[8,32,128]{2,1,0:T(8,128)(2,1)S(1)}, u32[]{:S(2)}, u32[]{:S(2)}) collective-permute-start(f16[8,32,128]{2,1,0:T(8,128)(2,1)S(1)} %get-tuple-element.40), channel_id=1, source_target_pairs={{0,2},{1,3},{2,0},{3,1},{4,6},{5,7},{6,4},{7,5},{8,10},{9,11},{10,... | collective-permute-start | bytes 196616 | tf_op jit(solution)/shard_map/ppermute | solution.py:388
  52.5 1.5 %collective-permute-done.12 = f16[8,32,128]{2,1,0:T(8,128)(2,1)S(1)} collective-permute-done((f16[8,32,128]{2,1,0:T(8,128)(2,1)S(1)}, f16[8,32,128]{2,1,0:T(8,128)(2,1)S(1)}, u32[]{:S(2)}, u32[]{:S(2)}) %collective-permute-start.12) | collective-permute-done | bytes 65568 | tf_op jit(solution)/shard_map/ppermute | solution.py:388
  54.0 2.5 %collective-permute-done.13 = f16[8,32,128]{2,1,0:T(8,128)(2,1)S(1)} collective-permute-done((f16[8,32,128]{2,1,0:T(8,128)(2,1)S(1)}, f16[8,32,128]{2,1,0:T(8,128)(2,1)S(1)}, u32[]{:S(2)}, u32[]{:S(2)}) %collective-permute-start.13) | collective-permute-done | bytes 65568 | tf_op jit(solution)/shard_map/ppermute | solution.py:388
  56.6 0.3 collective-permute-start.15
  56.9 3.2 %collective-permute-start.16 = (f16[8,32,128]{2,1,0:T(8,128)(2,1)S(1)}, f16[8,32,128]{2,1,0:T(8,128)(2,1)S(1)}, u32[]{:S(2)}, u32[]{:S(2)}) collective-permute-start(f16[8,32,128]{2,1,0:T(8,128)(2,1)S(1)} %fusion.14), channel_id=1, source_target_pairs={{4,0},{5,1},{6,2},{7,3},{0,4},{1,5},{2,6},{3,7},{12,8},{13,9},{14,... | collective-permute-start | bytes 196616 | tf_op jit(solution)/shard_map/ppermute | solution.py:395
  60.1 0.1 collective-permute-start.17
  60.2 2.3 %collective-permute-done.16 = f16[8,32,128]{2,1,0:T(8,128)(2,1)S(1)} collective-permute-done((f16[8,32,128]{2,1,0:T(8,128)(2,1)S(1)}, f16[8,32,128]{2,1,0:T(8,128)(2,1)S(1)}, u32[]{:S(2)}, u32[]{:S(2)}) %collective-permute-start.16) | collective-permute-done | bytes 65568 | tf_op jit(solution)/shard_map/ppermute | solution.py:395
  62.5 3.0 %collective-permute-done.17 = f16[8,32,128]{2,1,0:T(8,128)(2,1)S(1)} collective-permute-done((f16[8,32,128]{2,1,0:T(8,128)(2,1)S(1)}, f16[8,32,128]{2,1,0:T(8,128)(2,1)S(1)}, u32[]{:S(2)}, u32[]{:S(2)}) %collective-permute-start.17) | collective-permute-done | bytes 65568 | tf_op jit(solution)/shard_map/ppermute | solution.py:395
  65.5 0.1 pad_maximum_fusion.1
  65.6 2.3 %collective-permute-start.18 = (f16[4,8,32,128]{3,2,1,0:T(8,128)(2,1)S(1)}, f16[4,8,32,128]{3,2,1,0:T(8,128)(2,1)S(1)}, u32[]{:S(2)}, u32[]{:S(2)}) collective-permute-start(f16[4,8,32,128]{3,2,1,0:T(8,128)(2,1)S(1)} %pad_maximum_fusion.1), channel_id=1, source_target_pairs={{0,1},{1,0},{2,3},{3,2},{4,5},{5,4},{6,7},{7,6},{8,9},{9,8},{10,11... | collective-permute-start | bytes 786440 | tf_op jit(solution)/shard_map/ppermute | solution.py:423
  67.8 1.2 %collective-permute-done.18 = f16[4,8,32,128]{3,2,1,0:T(8,128)(2,1)S(1)} collective-permute-done((f16[4,8,32,128]{3,2,1,0:T(8,128)(2,1)S(1)}, f16[4,8,32,128]{3,2,1,0:T(8,128)(2,1)S(1)}, u32[]{:S(2)}, u32[]{:S(2)}) %collective-permute-start.18) | collective-permute-done | bytes 262176 | tf_op jit(solution)/shard_map/ppermute | solution.py:423
  69.0 0.2 broadcast_select_fusion
  69.2 0.1 rev.3
  69.2 0.2 fusion.3
  69.4 1.1 %maximum_convert_fusion = f32[16,128,128]{2,1,0:T(8,128)} fusion(f16[16,32,128]{2,1,0:T(8,128)(2,1)S(1)} %get-tuple-element.36, f16[16,32,128]{2,1,0:T(8,128)(2,1)S(1)} %get-tuple-element.35, f16[16,32,128]{2,1,0:T(8,128)(2,1)S(1)} %get-tuple-element.34, f16[16,32,128]{2,1,0:T(8,128)(2,1)S(1)} %get-tuple-element.33), kind=kLoop, calls=%fused_computation.8 | loop fusion | flops 1048576 | bytes 1572864 | tf_op jit(solution)/shard_map/convert_element_type | solution.py:431
  (25 shorter events, 0.3 us)
Async XLA Ops:
  0.0 10.1 %copy-start.1 = (bf16[2,16,128,128]{3,2,1,0:T(8,128)(2,1)S(1)}, bf16[2,16,128,128]{3,2,1,0:T(8,128)(2,1)}, u32[]{:S(2)}) copy-start(bf16[2,16,128,128]{3,2,1,0:T(8,128)(2,1)} %reward.3) | copy-start | bytes 3145732
  0.0 10.1 %copy-start.2 = (s32[2]{0:T(128)S(1)}, s32[2]{0:T(128)}, u32[]{:S(2)}) copy-start(s32[2]{0:T(128)} %own_set.7) | copy-start | bytes 28
  0.0 10.1 %copy-start = (f32[16,128,128]{2,1,0:T(8,128)S(1)}, f32[16,128,128]{2,1,0:T(8,128)}, u32[]{:S(2)}) copy-start(f32[16,128,128]{2,1,0:T(8,128)} %speed.3) | copy-start | bytes 3145732
  0.0 9.9 %copy-start.4 = (f32[16,3]{0,1:T(4,128)S(1)}, f32[16,3]{0,1:T(4,128)}, u32[]{:S(2)}) copy-start(f32[16,3]{0,1:T(4,128)} %param.10) | copy-start | bytes 580
  0.0 10.0 %copy-start.5 = (f32[16,3]{0,1:T(4,128)S(1)}, f32[16,3]{0,1:T(4,128)}, u32[]{:S(2)}) copy-start(f32[16,3]{0,1:T(4,128)} %param.11) | copy-start | bytes 580
  0.0 10.0 %collective-permute-start.1 = (bf16[2,16,128,128]{3,2,1,0:T(8,128)(2,1)}, bf16[2,16,128,128]{3,2,1,0:T(8,128)(2,1)}, u32[]{:S(2)}, u32[]{:S(2)}) collective-permute-start(bf16[2,16,128,128]{3,2,1,0:T(8,128)(2,1)} %reward.3), channel_id=1, source_target_pairs={{0,1},{1,0},{2,3},{3,2},{4,5},{5,4},{6,7},{7,6},{8,9},{9,8},{10,11... | collective-permute-start | bytes 3145736 | tf_op jit(solution)/shard_map/ppermute | solution.py:359
  0.8 2.3 %collective-permute-start = (s32[2]{0:T(128)}, s32[2]{0:T(128)S(1)}, u32[]{:S(2)}, u32[]{:S(2)}) collective-permute-start(s32[2]{0:T(128)} %own_set.7), channel_id=1, source_target_pairs={{0,1},{1,0},{2,3},{3,2},{4,5},{5,4},{6,7},{7,6},{8,9},{9,8},{10,11... | collective-permute-start | bytes 32 | tf_op jit(solution)/shard_map/ppermute | solution.py:358
  2.3 0.7 %copy-start.3 = (bf16[9,128,128]{2,1,0:T(8,128)(2,1)}, bf16[9,128,128]{2,1,0:T(8,128)(2,1)S(1)}, u32[]{:S(2)}) copy-start(bf16[9,128,128]{2,1,0:T(8,128)(2,1)S(1)} %get-tuple-element.25) | copy-start | bytes 884740
  3.0 13.0 %collective-permute-start.2 = (bf16[9,128,128]{2,1,0:T(8,128)(2,1)}, bf16[9,128,128]{2,1,0:T(8,128)(2,1)S(1)}, u32[]{:S(2)}, u32[]{:S(2)}) collective-permute-start(bf16[9,128,128]{2,1,0:T(8,128)(2,1)} %copy-done.3), channel_id=1, source_target_pairs={{1,9},{9,1},{3,11},{11,3},{5,13},{13,5},{7,15},{15,7},{8,16},{16,8... | collective-permute-start | bytes 884744 | tf_op jit(solution)/shard_map/ppermute | solution.py:380
  6.2 9.8 %collective-permute-start.3 = (bf16[4,128,128]{2,1,0:T(8,128)(2,1)S(1)}, bf16[4,128,128]{2,1,0:T(8,128)(2,1)S(1)}, u32[]{:S(2)}, u32[]{:S(2)}) collective-permute-start(bf16[4,128,128]{2,1,0:T(8,128)(2,1)S(1)} %get-tuple-element.26), channel_id=1, source_target_pairs={{0,9},{8,1},{2,11},{10,3},{4,13},{12,5},{6,15},{14,7},{9,16},{17,8... | collective-permute-start | bytes 393224 | tf_op jit(solution)/shard_map/ppermute | solution.py:381
  19.0 5.1 %collective-permute-start.4 = (f16[8,32,128]{2,1,0:T(8,128)(2,1)S(1)}, f16[8,32,128]{2,1,0:T(8,128)(2,1)S(1)}, u32[]{:S(2)}, u32[]{:S(2)}) collective-permute-start(f16[8,32,128]{2,1,0:T(8,128)(2,1)S(1)} %get-tuple-element.46), channel_id=1, source_target_pairs={{0,6},{1,7},{2,4},{3,5},{4,2},{5,3},{6,0},{7,1},{8,14},{9,15},{10,... | collective-permute-start | bytes 196616 | tf_op jit(solution)/shard_map/ppermute | solution.py:388
  22.4 5.7 %collective-permute-start.5 = (f16[8,32,128]{2,1,0:T(8,128)(2,1)S(1)}, f16[8,32,128]{2,1,0:T(8,128)(2,1)S(1)}, u32[]{:S(2)}, u32[]{:S(2)}) collective-permute-start(f16[8,32,128]{2,1,0:T(8,128)(2,1)S(1)} %get-tuple-element.48), channel_id=1, source_target_pairs={{0,4},{1,5},{2,6},{3,7},{4,0},{5,1},{6,2},{7,3},{8,12},{9,13},{10,... | collective-permute-start | bytes 196616 | tf_op jit(solution)/shard_map/ppermute | solution.py:388
  22.4 5.7 %collective-permute-start.6 = (f16[8,32,128]{2,1,0:T(8,128)(2,1)S(1)}, f16[8,32,128]{2,1,0:T(8,128)(2,1)S(1)}, u32[]{:S(2)}, u32[]{:S(2)}) collective-permute-start(f16[8,32,128]{2,1,0:T(8,128)(2,1)S(1)} %get-tuple-element.47), channel_id=1, source_target_pairs={{0,2},{1,3},{2,0},{3,1},{4,6},{5,7},{6,4},{7,5},{8,10},{9,11},{10,... | collective-permute-start | bytes 196616 | tf_op jit(solution)/shard_map/ppermute | solution.py:388
  28.2 3.6 %collective-permute-start.7 = (f16[8,32,128]{2,1,0:T(8,128)(2,1)S(1)}, f16[8,32,128]{2,1,0:T(8,128)(2,1)S(1)}, u32[]{:S(2)}, u32[]{:S(2)}) collective-permute-start(f16[8,32,128]{2,1,0:T(8,128)(2,1)S(1)} %fusion.23), channel_id=1, source_target_pairs={{2,0},{3,1},{0,2},{1,3},{6,4},{7,5},{4,6},{5,7},{10,8},{11,9},{8,1... | collective-permute-start | bytes 196616 | tf_op jit(solution)/shard_map/ppermute | solution.py:395
  28.4 4.1 %collective-permute-start.8 = (f16[8,32,128]{2,1,0:T(8,128)(2,1)S(1)}, f16[8,32,128]{2,1,0:T(8,128)(2,1)S(1)}, u32[]{:S(2)}, u32[]{:S(2)}) collective-permute-start(f16[8,32,128]{2,1,0:T(8,128)(2,1)S(1)} %fusion.23), channel_id=1, source_target_pairs={{4,0},{5,1},{6,2},{7,3},{0,4},{1,5},{2,6},{3,7},{12,8},{13,9},{14,... | collective-permute-start | bytes 196616 | tf_op jit(solution)/shard_map/ppermute | solution.py:395
  30.4 5.4 %collective-permute-start.9 = (f16[8,32,128]{2,1,0:T(8,128)(2,1)S(1)}, f16[8,32,128]{2,1,0:T(8,128)(2,1)S(1)}, u32[]{:S(2)}, u32[]{:S(2)}) collective-permute-start(f16[8,32,128]{2,1,0:T(8,128)(2,1)S(1)} %fusion.23), channel_id=1, source_target_pairs={{6,0},{7,1},{4,2},{5,3},{2,4},{3,5},{0,6},{1,7},{14,8},{15,9},{12,... | collective-permute-start | bytes 196616 | tf_op jit(solution)/shard_map/ppermute | solution.py:395
  35.9 4.5 %collective-permute-start.11 = (f16[4,3,32,128]{3,2,1,0:T(8,128)(2,1)S(1)}, f16[4,3,32,128]{3,2,1,0:T(8,128)(2,1)S(1)}, u32[]{:S(2)}, u32[]{:S(2)}) collective-permute-start(f16[4,3,32,128]{3,2,1,0:T(8,128)(2,1)S(1)} %get-tuple-element.43), channel_id=1, source_target_pairs={{0,1},{1,0},{2,3},{3,2},{4,5},{5,4},{6,7},{7,6},{8,9},{9,8},{10,11... | collective-permute-start | bytes 294920 | tf_op jit(solution)/shard_map/ppermute | solution.py:414
  38.5 7.4 %collective-permute-start.10 = (bf16[4,3,32,128]{3,2,1,0:T(8,128)(2,1)S(1)}, bf16[4,3,32,128]{3,2,1,0:T(8,128)(2,1)S(1)}, u32[]{:S(2)}, u32[]{:S(2)}) collective-permute-start(bf16[4,3,32,128]{3,2,1,0:T(8,128)(2,1)S(1)} %get-tuple-element.42), channel_id=1, source_target_pairs={{1,9},{9,1},{3,11},{11,3},{5,13},{13,5},{7,15},{15,7},{8,16},{16,8... | collective-permute-start | bytes 294920 | tf_op jit(solution)/shard_map/ppermute | solution.py:415
  48.9 5.1 %collective-permute-start.12 = (f16[8,32,128]{2,1,0:T(8,128)(2,1)S(1)}, f16[8,32,128]{2,1,0:T(8,128)(2,1)S(1)}, u32[]{:S(2)}, u32[]{:S(2)}) collective-permute-start(f16[8,32,128]{2,1,0:T(8,128)(2,1)S(1)} %get-tuple-element.39), channel_id=1, source_target_pairs={{0,6},{1,7},{2,4},{3,5},{4,2},{5,3},{6,0},{7,1},{8,14},{9,15},{10,... | collective-permute-start | bytes 196616 | tf_op jit(solution)/shard_map/ppermute | solution.py:388
  50.6 5.9 %collective-permute-start.13 = (f16[8,32,128]{2,1,0:T(8,128)(2,1)S(1)}, f16[8,32,128]{2,1,0:T(8,128)(2,1)S(1)}, u32[]{:S(2)}, u32[]{:S(2)}) collective-permute-start(f16[8,32,128]{2,1,0:T(8,128)(2,1)S(1)} %get-tuple-element.41), channel_id=1, source_target_pairs={{0,4},{1,5},{2,6},{3,7},{4,0},{5,1},{6,2},{7,3},{8,12},{9,13},{10,... | collective-permute-start | bytes 196616 | tf_op jit(solution)/shard_map/ppermute | solution.py:388
  51.5 5.0 %collective-permute-start.14 = (f16[8,32,128]{2,1,0:T(8,128)(2,1)S(1)}, f16[8,32,128]{2,1,0:T(8,128)(2,1)S(1)}, u32[]{:S(2)}, u32[]{:S(2)}) collective-permute-start(f16[8,32,128]{2,1,0:T(8,128)(2,1)S(1)} %get-tuple-element.40), channel_id=1, source_target_pairs={{0,2},{1,3},{2,0},{3,1},{4,6},{5,7},{6,4},{7,5},{8,10},{9,11},{10,... | collective-permute-start | bytes 196616 | tf_op jit(solution)/shard_map/ppermute | solution.py:388
  56.6 3.6 %collective-permute-start.15 = (f16[8,32,128]{2,1,0:T(8,128)(2,1)S(1)}, f16[8,32,128]{2,1,0:T(8,128)(2,1)S(1)}, u32[]{:S(2)}, u32[]{:S(2)}) collective-permute-start(f16[8,32,128]{2,1,0:T(8,128)(2,1)S(1)} %fusion.14), channel_id=1, source_target_pairs={{2,0},{3,1},{0,2},{1,3},{6,4},{7,5},{4,6},{5,7},{10,8},{11,9},{8,1... | collective-permute-start | bytes 196616 | tf_op jit(solution)/shard_map/ppermute | solution.py:395
  56.9 5.6 %collective-permute-start.16 = (f16[8,32,128]{2,1,0:T(8,128)(2,1)S(1)}, f16[8,32,128]{2,1,0:T(8,128)(2,1)S(1)}, u32[]{:S(2)}, u32[]{:S(2)}) collective-permute-start(f16[8,32,128]{2,1,0:T(8,128)(2,1)S(1)} %fusion.14), channel_id=1, source_target_pairs={{4,0},{5,1},{6,2},{7,3},{0,4},{1,5},{2,6},{3,7},{12,8},{13,9},{14,... | collective-permute-start | bytes 196616 | tf_op jit(solution)/shard_map/ppermute | solution.py:395
  60.1 5.4 %collective-permute-start.17 = (f16[8,32,128]{2,1,0:T(8,128)(2,1)S(1)}, f16[8,32,128]{2,1,0:T(8,128)(2,1)S(1)}, u32[]{:S(2)}, u32[]{:S(2)}) collective-permute-start(f16[8,32,128]{2,1,0:T(8,128)(2,1)S(1)} %fusion.14), channel_id=1, source_target_pairs={{6,0},{7,1},{4,2},{5,3},{2,4},{3,5},{0,6},{1,7},{14,8},{15,9},{12,... | collective-permute-start | bytes 196616 | tf_op jit(solution)/shard_map/ppermute | solution.py:395
  65.6 3.4 %collective-permute-start.18 = (f16[4,8,32,128]{3,2,1,0:T(8,128)(2,1)S(1)}, f16[4,8,32,128]{3,2,1,0:T(8,128)(2,1)S(1)}, u32[]{:S(2)}, u32[]{:S(2)}) collective-permute-start(f16[4,8,32,128]{3,2,1,0:T(8,128)(2,1)S(1)} %pad_maximum_fusion.1), channel_id=1, source_target_pairs={{0,1},{1,0},{2,3},{3,2},{4,5},{5,4},{6,7},{7,6},{8,9},{9,8},{10,11... | collective-permute-start | bytes 786440 | tf_op jit(solution)/shard_map/ppermute | solution.py:423

commit v6 on v5

--- a/solution.py
+++ b/solution.py
@@ -32,12 +32,9 @@
     return member // 2, upper, jnp.where(slab == end, 0, 1)
 
 
-def coefficients(sets, ctrl):
-    own_set, other_set, drift_sets, diffusion_sets = sets
-    own = own_set.shape[0]
-    kind = jnp.where(ctrl < own, own_set[jnp.minimum(ctrl, own - 1)], other_set[jnp.maximum(ctrl - own, 0)])
-    rates = [diffusion_sets[kind, dim] for dim in range(3)]
-    drifts = [drift_sets[kind, dim] for dim in range(3)]
+def coefficients(coef, ctrl):
+    rates = [coef[ctrl, dim] for dim in range(3)]
+    drifts = [coef[ctrl, 3 + dim] for dim in range(3)]
     sizes = [jnp.maximum(drift, -drift) for drift in drifts]
     return rates, sizes, 1.0 - 2.0 * (rates[0] + rates[1] + rates[2]), sizes[0] + sizes[1] + sizes[2], drifts
 
@@ -66,18 +63,18 @@
     return still + speed * (wind - size * center)
 
 
-def sweep(place, sets, ctrls, src, rows, speed, reward, store):
+def sweep(place, coef, ctrls, src, rows, speed, reward, store):
     ny = src.shape[1] - 2 * PAD
-    coefs = [coefficients(sets, ctrl) for ctrl in ctrls]
-    ups = [winds_of(place, coef[4]) for coef in coefs]
+    coefs = [coefficients(coef, ctrl) for ctrl in ctrls]
+    ups = [winds_of(place, own_coef[4]) for own_coef in coefs]
     size = min(ny, CHUNK)
     for first in range(0, ny, size):
         spot = pl.ds(first, size)
         for row, center, sides in taps(src, rows, first, size):
             sums = [ahead + behind for ahead, behind in sides]
             pace = speed(row, spot)
-            for ctrl, coef, up in zip(ctrls, coefs, ups):
-                store(ctrl, row, first, size, blend(coef, up, center, sides, sums, pace, reward(ctrl, row, spot)))
+            for ctrl, own_coef, up in zip(ctrls, coefs, ups):
+                store(ctrl, row, first, size, blend(own_coef, up, center, sides, sums, pace, reward(ctrl, row, spot)))
 
 
 def winds_of(place, drifts):
@@ -135,7 +132,7 @@
         field[row, pl.ds(PAD + shard * width, width), :] = piece.astype(field.dtype)
 
 
-def early_march(place, sets, half, block, speed_rows, reward_rows, out, keeps, fields):
+def early_march(place, coef, half, block, speed_rows, reward_rows, out, keeps, fields):
     count = reward_rows.shape[0]
     start_max(out)
 
@@ -153,7 +150,7 @@
         fields[0][ctrl, q, pl.ds(PAD + first, size), :] = new
         keep(0, ctrl, q, first, size, new)
 
-    sweep(place, sets, range(count), block, range(1, half + SUBSTEPS - 1), speed, reward, store)
+    sweep(place, coef, range(count), block, range(1, half + SUBSTEPS - 1), speed, reward, store)
 
     def one(ctrl, carry):
         source = fields[0].at[ctrl]
@@ -168,14 +165,14 @@
                 keep(substep, ctrl, q, first, size, new)
 
             rows = range(1 + substep, half + SUBSTEPS - 1 - substep)
-            sweep(place, sets, [ctrl], source, rows, speed, reward, store)
+            sweep(place, coef, [ctrl], source, rows, speed, reward, store)
             source = None if last else fields[substep]
         return carry
 
     lax.fori_loop(0, count, one, 0)
 
 
-def rest_march(place, sets, edge, lower_rows, block, speed_rows, reward_rows, out, keeps, fields):
+def rest_march(place, coef, edge, lower_rows, block, speed_rows, reward_rows, out, keeps, fields):
     ny = block.shape[1] - 2 * PAD
     count = reward_rows.shape[0]
     margin = SUBSTEPS - 1
@@ -197,7 +194,7 @@
     def store(ctrl, row, first, size, new):
         fields[0][ctrl, row, pl.ds(PAD + first, size), :] = new * inside if row < SUBSTEPS else new
 
-    sweep(place, sets, range(count), block, range(1, SUBSTEPS + 1), speed, reward, store)
+    sweep(place, coef, range(count), block, range(1, SUBSTEPS + 1), speed, reward, store)
 
     def one(ctrl, carry):
         source = fields[0].at[ctrl]
@@ -214,7 +211,7 @@
                 fields[substep][row, pl.ds(PAD + first, size), :] = new
 
             rows = range(1 + substep, SUBSTEPS + 1 + substep)
-            sweep(place, sets, [ctrl], source, rows, speed, reward, store)
+            sweep(place, coef, [ctrl], source, rows, speed, reward, store)
             source = None if last else fields[substep]
         return carry
 
@@ -254,17 +251,16 @@
         copy.wait()
 
 
-def early_first(own_set, other_set, drift_sets, diffusion_sets, block, speed, reward, other, out, *refs, half):
+def early_first(coef, block, speed, reward, other, out, *refs, half):
     keeps, (speed_rows, reward_rows), fields = refs[:2], refs[2:4], refs[4:]
     place = where_am_i()
     for field in fields:
         clear_pads(field, speed.shape[1])
     lay_rows(place, speed, reward, other, speed_rows, reward_rows)
-    sets = own_set, other_set, drift_sets, diffusion_sets
-    early_march(place, sets, half, block, speed_rows, reward_rows, out, keeps, fields)
-
-
-def rest_first(own_set, other_set, drift_sets, diffusion_sets, first, speed_rows, reward_rows, edge, *refs, half):
+    early_march(place, coef, half, block, speed_rows, reward_rows, out, keeps, fields)
+
+
+def rest_first(coef, first, speed_rows, reward_rows, edge, *refs, half):
     edge_other, keeps, out, fields, block, lower_rows = refs[0], refs[1:3], refs[3], refs[4:6], refs[6], refs[7]
     place = where_am_i()
     ny = speed_rows.shape[1]
@@ -275,11 +271,10 @@
     for row in range(2):
         block[SUBSTEPS + row] = first[row]
     lay_lower(edge, edge_other, lower_rows)
-    sets = own_set, other_set, drift_sets, diffusion_sets
-    rest_march(place, sets, edge, lower_rows, block, speed_rows, reward_rows, out, keeps, fields)
-
-
-def early_later(own_set, other_set, drift_sets, diffusion_sets, current, across, speed_rows, reward_rows, out, *refs, half):
+    rest_march(place, coef, edge, lower_rows, block, speed_rows, reward_rows, out, keeps, fields)
+
+
+def early_later(coef, current, across, speed_rows, reward_rows, out, *refs, half):
     keeps, fields, block = refs[:2], refs[2:4], refs[4]
     place = where_am_i()
     for field in (block, *fields):
@@ -288,10 +283,10 @@
         spread(place, current, q, block, q)
     for row in range(SUBSTEPS):
         spread(place, across, SUBSTEPS - 1 - row, block, half + row)
-    early_march(place, (own_set, other_set, drift_sets, diffusion_sets), half, block, speed_rows, reward_rows, out, keeps, fields)
-
-
-def rest_later(own_set, other_set, drift_sets, diffusion_sets, current, beyond, speed_rows, reward_rows, edge, *refs, half):
+    early_march(place, coef, half, block, speed_rows, reward_rows, out, keeps, fields)
+
+
+def rest_later(coef, current, beyond, speed_rows, reward_rows, edge, *refs, half):
     edge_other, keeps, out, fields, block, lower_rows = refs[0], refs[1:3], refs[3], refs[4:6], refs[6], refs[7]
     place = where_am_i()
     for field in (block, *fields):
@@ -301,8 +296,7 @@
     for row in range(2):
         spread(place, current, row, block, SUBSTEPS + row)
     lay_lower(edge, edge_other, lower_rows)
-    sets = own_set, other_set, drift_sets, diffusion_sets
-    rest_march(place, sets, edge, lower_rows, block, speed_rows, reward_rows, out, keeps, fields)
+    rest_march(place, coef, edge, lower_rows, block, speed_rows, reward_rows, out, keeps, fields)
 
 
 def body(value, speed, reward, ctrl_set, drift_sets, diffusion_sets):
@@ -343,14 +337,14 @@
         return pl.pallas_call(
             functools.partial(kernel, half=half),
             out_shape=outs,
-            in_specs=[scalars] * 4 + [whole] * len(arrays),
+            in_specs=[scalars] + [whole] * len(arrays),
             out_specs=jax.tree.map(lambda _: whole, outs),
             scratch_shapes=scratch,
             compiler_params=pltpu.CompilerParams(vmem_limit_bytes=16 * 2**20),
             cost_estimate=pl.CostEstimate(
                 flops=25 * count * marched * ny * nz, bytes_accessed=12 * count * marched * ny * nz, transcendentals=0
             ),
-        )(ctrl_set, other_set, drift_sets, diffusion_sets, *arrays)
+        )(coef, *arrays)
 
     keeps = [shape(count, 2, ny, nz)] * (SUBSTEPS - 1)
 
@@ -380,6 +374,11 @@
     edge = lax.ppermute(packed, both, facing)
     edge_other = lax.ppermute(far, both, beside)
 
+    sets = jnp.concatenate([ctrl_set, other_set])
+    picked = sets[:, None] == jnp.arange(drift_sets.shape[0], dtype=jnp.int32)[None, :]
+    pairs = jnp.concatenate([diffusion_sets, drift_sets], axis=1)
+    coef = jnp.sum(jnp.where(picked[:, :, None], pairs[None], 0.0), axis=1)
+
     def reduce(best):
         parts = best.astype(wire)
         mine = parts[0]
@@ -421,14 +420,17 @@
     pieces = gather(reduce(jnp.concatenate([best_rest, best], axis=1)))
 
     from_partner = lax.ppermute(pieces, "ctrl", partners)
-    low_half = jnp.where(upper == 0, pieces, from_partner)
-    high_half = jnp.where(upper == 0, from_partner, pieces)[:, ::-1]
-    slab_pieces = jnp.concatenate([low_half, high_half], axis=1)
-    ordered = [
-        lax.dynamic_index_in_dim(slab_pieces, mate_step(chip, shard, chips), 0, keepdims=False)
-        for shard in range(chips)
-    ]
-    return jnp.concatenate(ordered, axis=1).astype(jnp.float32)
+
+    def in_order(parts, flipped):
+        ordered = [
+            lax.dynamic_index_in_dim(parts, mate_step(chip, shard, chips), 0, keepdims=False) for shard in range(chips)
+        ]
+        block_rows = jnp.concatenate(ordered, axis=1)
+        return jnp.where(flipped, block_rows[::-1], block_rows).astype(jnp.float32)
+
+    result = jnp.zeros((cells, ny, nz), jnp.float32)
+    result = lax.dynamic_update_slice_in_dim(result, in_order(pieces, upper == 1), upper * half, axis=0)
+    return lax.dynamic_update_slice_in_dim(result, in_order(from_partner, upper == 0), (1 - upper) * half, axis=0)
 
 
 def solution(mesh):

time: 70.7 us -> 70 us (0.990)
    ppermute x6, waiting for transfers between devices: 9.33 us -> 10.8 us  [reduce(): mine = jnp.maximum(mine, lax.ppermute(parts[step], 'ctrl', pairs))]
    ppermute x6, waiting for transfers between devices: 9.18 us -> 7.76 us  [gather(): pieces.append(lax.ppermute(mine, 'ctrl', pairs))]
    convert_element_type x1 -> x0, other arithmetic: 1.11 us -> none  [body(): return jnp.concatenate(ordered, axis=1).astype(jnp.float32)]
    dynamic_update_slice x0 -> x2, other arithmetic: none -> 0.88 us  [the longest x1 0.84 us: body(): lax.dynamic_update_slice_in_dim(result, in_order(from_partner, upper == 0...]
  transfers between devices with their start and end apart: 19 -> 19, of which waited for: 9 -> 9; matrix products, arithmetic and copies ran while one was open for 0% -> 1% of each run, Pallas kernels for 18% -> 18%
where the time goes in v6:
time: 70 us; the launch traced here: 69.8 us
  starting transfers between devices  28.9 us (41%)
  waiting for transfers between devices  19.4 us (28%)
  Pallas kernels  18.2 us (26%)
  other arithmetic  1.87 us (3%)
  local copies, waits for them, and re-layouts  1.03 us (1%)
    pallas_call x4, Pallas kernels, call(): pl.pallas_call(functools.partial(kernel, half=half), out_shape=outs, in_s...  16.8 us
    ppermute x6, waiting for transfers between devices, reduce(): mine = jnp.maximum(mine, lax.ppermute(parts[step], 'ctrl', pairs))  10.8 us
    ppermute x6, waiting for transfers between devices, gather(): pieces.append(lax.ppermute(mine, 'ctrl', pairs))  7.76 us
    ppermute x6, starting transfers between devices, reduce(): mine = jnp.maximum(mine, lax.ppermute(parts[step], 'ctrl', pairs))  7.36 us
    ppermute x6, starting transfers between devices, gather(): pieces.append(lax.ppermute(mine, 'ctrl', pairs))  7.22 us
    ppermute x1, starting transfers between devices, body(): edge_other = lax.ppermute(far, both, beside)  3.73 us
    ppermute x1, starting transfers between devices, body(): edge = lax.ppermute(packed, both, facing)  3.12 us
    ppermute x1, starting transfers between devices, body(): across = lax.ppermute(pieces[:, -SUBSTEPS:], 'ctrl', partners)  2.64 us
  transfers between devices with their start and end apart: 19, of which 9 were waited for; matrix products, arithmetic and copies ran while one was open for 1% of the time, Pallas kernels for 18%

profile of v6, /device:TPU:5, one launch (start us, length us, event | category | flops | bytes accessed | tf_op | source)
XLA Modules:
  0.0 69.8 jit_solution(1136662479851173771)
XLA Ops:
  0.0 0.7 %collective-permute-start.1 = (bf16[2,16,128,128]{3,2,1,0:T(8,128)(2,1)}, bf16[2,16,128,128]{3,2,1,0:T(8,128)(2,1)}, u32[]{:S(2)}, u32[]{:S(2)}) collective-permute-start(bf16[2,16,128,128]{3,2,1,0:T(8,128)(2,1)} %reward.3), channel_id=1, source_target_pairs={{0,1},{1,0},{2,3},{3,2},{4,5},{5,4},{6,7},{7,6},{8,9},{9,8},{10,11... | collective-permute-start | bytes 3145736 | tf_op jit(solution)/shard_map/ppermute | solution.py:353
  0.8 0.1 collective-permute-start
  0.9 1.5 %shard_map.64 = (bf16[9,128,128]{2,1,0:T(8,128)(2,1)S(1)}, bf16[4,128,128]{2,1,0:T(8,128)(2,1)S(1)}, f32[11,144,128]{2,1,0:T(8,128)S(1)}) custom-call(f32[16,128,128]{2,1,0:T(8,128)} %value.1, f32[16,128,128]{2,1,0:T(8,128)} %speed.3, bf16[2,16,128,128]{3,2,1,0:T(8,128)(2,1)} %reward.3), custom_call_target="tpu_custom_call" | custom-call | tf_op jit(solution)/shard_map/pallas_call | solution.py:356
  2.3 0.0 copy-start.2
  2.3 0.7 %copy-done.2 = bf16[9,128,128]{2,1,0:T(8,128)(2,1)} copy-done((bf16[9,128,128]{2,1,0:T(8,128)(2,1)}, bf16[9,128,128]{2,1,0:T(8,128)(2,1)S(1)}, u32[]{:S(2)}) %copy-start.2) | copy-done | bytes 294936
  3.1 3.1 %collective-permute-start.2 = (bf16[9,128,128]{2,1,0:T(8,128)(2,1)}, bf16[9,128,128]{2,1,0:T(8,128)(2,1)S(1)}, u32[]{:S(2)}, u32[]{:S(2)}) collective-permute-start(bf16[9,128,128]{2,1,0:T(8,128)(2,1)} %copy-done.2), channel_id=1, source_target_pairs={{1,9},{9,1},{3,11},{11,3},{5,13},{13,5},{7,15},{15,7},{8,16},{16,8... | collective-permute-start | bytes 884744 | tf_op jit(solution)/shard_map/ppermute | solution.py:374
  6.2 3.7 %collective-permute-start.3 = (bf16[4,128,128]{2,1,0:T(8,128)(2,1)S(1)}, bf16[4,128,128]{2,1,0:T(8,128)(2,1)S(1)}, u32[]{:S(2)}, u32[]{:S(2)}) collective-permute-start(bf16[4,128,128]{2,1,0:T(8,128)(2,1)S(1)} %get-tuple-element.26), channel_id=1, source_target_pairs={{0,9},{8,1},{2,11},{10,3},{4,13},{12,5},{6,15},{14,7},{9,16},{17,8... | collective-permute-start | bytes 393224 | tf_op jit(solution)/shard_map/ppermute | solution.py:375
  9.9 0.1 pad_add_fusion
  10.0 0.1 iota_compare_fusion
  10.1 0.1 select_reduce_fusion
  10.2 0.1 copy.11.coef
  10.3 6.1 %shard_map.65 = (f32[4,5,32,128]{3,2,1,0:T(8,128)S(1)}, f32[4,2,128,128]{3,2,1,0:T(8,128)S(1)}, f32[4,2,128,128]{3,2,1,0:T(8,128)S(1)}, f32[10,128,128]{2,1,0:T(8,128)S(1)}, f32[4,10,128,128]{3,2,1,0:T(8,128)S(1)}) custom-call(f32[4,6]{1,0:T(4,128)S(1)} %copy.11.coef, f32[11,144,128]{2,1,0:T(8,128)S(1)} %get-tuple-element.22.block.first, ...), custom_call_target="tpu_custom_call" | custom-call | flops 34406400 | bytes 16515072 | tf_op jit(solution)/shard_map/pallas_call | solution.py:337
  16.4 2.7 %shard_map.66 = f32[4,3,32,128]{3,2,1,0:T(8,128)S(1)} custom-call(f32[4,6]{1,0:T(4,128)S(1)} %copy.11.coef, f32[11,144,128]{2,1,0:T(8,128)S(1)} %get-tuple-element.22.block.first, f32[10,128,128]{2,1,0:T(8,128)S(1)} %get-tuple-element.23.speed_rows, f32[4,10,128,128]{3,2,1,0:T(8,128)S(1)} %get-tuple-element.24.reward_rows, ...), custom_call_target="tpu_custom_call" | custom-call | flops 14745600 | bytes 7077888 | tf_op jit(solution)/shard_map/pallas_call | solution.py:337
  19.1 0.1 fusion.17
  19.2 3.4 %collective-permute-start.4 = (f16[8,32,128]{2,1,0:T(8,128)(2,1)S(1)}, f16[8,32,128]{2,1,0:T(8,128)(2,1)S(1)}, u32[]{:S(2)}, u32[]{:S(2)}) collective-permute-start(f16[8,32,128]{2,1,0:T(8,128)(2,1)S(1)} %get-tuple-element.48), channel_id=1, source_target_pairs={{0,6},{1,7},{2,4},{3,5},{4,2},{5,3},{6,0},{7,1},{8,14},{9,15},{10,... | collective-permute-start | bytes 196616 | tf_op jit(solution)/shard_map/ppermute | solution.py:387
  22.6 0.4 collective-permute-start.6
  23.0 2.0 %collective-permute-done.4 = f16[8,32,128]{2,1,0:T(8,128)(2,1)S(1)} collective-permute-done((f16[8,32,128]{2,1,0:T(8,128)(2,1)S(1)}, f16[8,32,128]{2,1,0:T(8,128)(2,1)S(1)}, u32[]{:S(2)}, u32[]{:S(2)}) %collective-permute-start.4) | collective-permute-done | bytes 65568 | tf_op jit(solution)/shard_map/ppermute | solution.py:387
  24.9 3.2 %collective-permute-done.5 = f16[8,32,128]{2,1,0:T(8,128)(2,1)S(1)} collective-permute-done((f16[8,32,128]{2,1,0:T(8,128)(2,1)S(1)}, f16[8,32,128]{2,1,0:T(8,128)(2,1)S(1)}, u32[]{:S(2)}, u32[]{:S(2)}) %collective-permute-start.5) | collective-permute-done | bytes 65568 | tf_op jit(solution)/shard_map/ppermute | solution.py:387
  28.2 1.0 %collective-permute-start.7 = (f16[8,32,128]{2,1,0:T(8,128)(2,1)S(1)}, f16[8,32,128]{2,1,0:T(8,128)(2,1)S(1)}, u32[]{:S(2)}, u32[]{:S(2)}) collective-permute-start(f16[8,32,128]{2,1,0:T(8,128)(2,1)S(1)} %fusion.15), channel_id=1, source_target_pairs={{2,0},{3,1},{0,2},{1,3},{6,4},{7,5},{4,6},{5,7},{10,8},{11,9},{8,1... | collective-permute-start | bytes 196616 | tf_op jit(solution)/shard_map/ppermute | solution.py:394
  29.2 1.6 %collective-permute-start.8 = (f16[8,32,128]{2,1,0:T(8,128)(2,1)S(1)}, f16[8,32,128]{2,1,0:T(8,128)(2,1)S(1)}, u32[]{:S(2)}, u32[]{:S(2)}) collective-permute-start(f16[8,32,128]{2,1,0:T(8,128)(2,1)S(1)} %fusion.15), channel_id=1, source_target_pairs={{4,0},{5,1},{6,2},{7,3},{0,4},{1,5},{2,6},{3,7},{12,8},{13,9},{14,... | collective-permute-start | bytes 196616 | tf_op jit(solution)/shard_map/ppermute | solution.py:394
  30.8 1.0 %collective-permute-start.9 = (f16[8,32,128]{2,1,0:T(8,128)(2,1)S(1)}, f16[8,32,128]{2,1,0:T(8,128)(2,1)S(1)}, u32[]{:S(2)}, u32[]{:S(2)}) collective-permute-start(f16[8,32,128]{2,1,0:T(8,128)(2,1)S(1)} %fusion.15), channel_id=1, source_target_pairs={{6,0},{7,1},{4,2},{5,3},{2,4},{3,5},{0,6},{1,7},{14,8},{15,9},{12,... | collective-permute-start | bytes 196616 | tf_op jit(solution)/shard_map/ppermute | solution.py:394
  31.8 1.9 %collective-permute-done.8 = f16[8,32,128]{2,1,0:T(8,128)(2,1)S(1)} collective-permute-done((f16[8,32,128]{2,1,0:T(8,128)(2,1)S(1)}, f16[8,32,128]{2,1,0:T(8,128)(2,1)S(1)}, u32[]{:S(2)}, u32[]{:S(2)}) %collective-permute-start.8) | collective-permute-done | bytes 65568 | tf_op jit(solution)/shard_map/ppermute | solution.py:394
  33.7 2.1 %collective-permute-done.9 = f16[8,32,128]{2,1,0:T(8,128)(2,1)S(1)} collective-permute-done((f16[8,32,128]{2,1,0:T(8,128)(2,1)S(1)}, f16[8,32,128]{2,1,0:T(8,128)(2,1)S(1)}, u32[]{:S(2)}, u32[]{:S(2)}) %collective-permute-start.9) | collective-permute-done | bytes 65568 | tf_op jit(solution)/shard_map/ppermute | solution.py:394
  35.8 0.1 pad_maximum_fusion
  35.9 2.6 %collective-permute-start.11 = (f16[4,3,32,128]{3,2,1,0:T(8,128)(2,1)S(1)}, f16[4,3,32,128]{3,2,1,0:T(8,128)(2,1)S(1)}, u32[]{:S(2)}, u32[]{:S(2)}) collective-permute-start(f16[4,3,32,128]{3,2,1,0:T(8,128)(2,1)S(1)} %get-tuple-element.45), channel_id=1, source_target_pairs={{0,1},{1,0},{2,3},{3,2},{4,5},{5,4},{6,7},{7,6},{8,9},{9,8},{10,11... | collective-permute-start | bytes 294920 | tf_op jit(solution)/shard_map/ppermute | solution.py:413
  38.6 2.0 %collective-permute-start.10 = (bf16[4,3,32,128]{3,2,1,0:T(8,128)(2,1)S(1)}, bf16[4,3,32,128]{3,2,1,0:T(8,128)(2,1)S(1)}, u32[]{:S(2)}, u32[]{:S(2)}) collective-permute-start(bf16[4,3,32,128]{3,2,1,0:T(8,128)(2,1)S(1)} %get-tuple-element.44), channel_id=1, source_target_pairs={{1,9},{9,1},{3,11},{11,3},{5,13},{13,5},{7,15},{15,7},{8,16},{16,8... | collective-permute-start | bytes 294920 | tf_op jit(solution)/shard_map/ppermute | solution.py:414
  40.6 5.3 %shard_map.67 = (f32[4,5,32,128]{3,2,1,0:T(8,128)S(1)}, f32[4,2,128,128]{3,2,1,0:T(8,128)S(1)}, f32[4,2,128,128]{3,2,1,0:T(8,128)S(1)}) custom-call(f32[4,6]{1,0:T(4,128)S(1)} %copy.11.coef, f32[4,8,32,128]{3,2,1,0:T(8,128)S(1)} %get-tuple-element.47.current, f32[4,3,32,128]{3,2,1,0:T(8,128)S(1)} %convert_element_type.19.across, ...), custom_call_target="tpu_custom_call" | custom-call | flops 34406400 | bytes 16515072 | tf_op jit(solution)/shard_map/pallas_call | solution.py:337
  45.9 2.7 %shard_map.68 = f32[4,3,32,128]{3,2,1,0:T(8,128)S(1)} custom-call(f32[4,6]{1,0:T(4,128)S(1)} %copy.11.coef, f32[4,8,32,128]{3,2,1,0:T(8,128)S(1)} %get-tuple-element.47.current, bf16[4,3,32,128]{3,2,1,0:T(8,128)(2,1)S(1)} %collective-permute-done.10.beyond, f32[10,128,128]{2,1,0:T(8,128)S(1)} %get-tuple-element.23.speed_rows, ...), custom_call_target="tpu_custom_call" | custom-call | flops 14745600 | bytes 7077888 | tf_op jit(solution)/shard_map/pallas_call | solution.py:337
  48.7 0.1 fusion.8
  48.7 2.0 %collective-permute-start.12 = (f16[8,32,128]{2,1,0:T(8,128)(2,1)S(1)}, f16[8,32,128]{2,1,0:T(8,128)(2,1)S(1)}, u32[]{:S(2)}, u32[]{:S(2)}) collective-permute-start(f16[8,32,128]{2,1,0:T(8,128)(2,1)S(1)} %get-tuple-element.41), channel_id=1, source_target_pairs={{0,6},{1,7},{2,4},{3,5},{4,2},{5,3},{6,0},{7,1},{8,14},{9,15},{10,... | collective-permute-start | bytes 196616 | tf_op jit(solution)/shard_map/ppermute | solution.py:387
  50.7 0.6 collective-permute-start.13
  51.3 1.0 %collective-permute-start.14 = (f16[8,32,128]{2,1,0:T(8,128)(2,1)S(1)}, f16[8,32,128]{2,1,0:T(8,128)(2,1)S(1)}, u32[]{:S(2)}, u32[]{:S(2)}) collective-permute-start(f16[8,32,128]{2,1,0:T(8,128)(2,1)S(1)} %get-tuple-element.42), channel_id=1, source_target_pairs={{0,2},{1,3},{2,0},{3,1},{4,6},{5,7},{6,4},{7,5},{8,10},{9,11},{10,... | collective-permute-start | bytes 196616 | tf_op jit(solution)/shard_map/ppermute | solution.py:387
  52.3 1.5 %collective-permute-done.12 = f16[8,32,128]{2,1,0:T(8,128)(2,1)S(1)} collective-permute-done((f16[8,32,128]{2,1,0:T(8,128)(2,1)S(1)}, f16[8,32,128]{2,1,0:T(8,128)(2,1)S(1)}, u32[]{:S(2)}, u32[]{:S(2)}) %collective-permute-start.12) | collective-permute-done | bytes 65568 | tf_op jit(solution)/shard_map/ppermute | solution.py:387
  53.8 4.1 %collective-permute-done.13 = f16[8,32,128]{2,1,0:T(8,128)(2,1)S(1)} collective-permute-done((f16[8,32,128]{2,1,0:T(8,128)(2,1)S(1)}, f16[8,32,128]{2,1,0:T(8,128)(2,1)S(1)}, u32[]{:S(2)}, u32[]{:S(2)}) %collective-permute-start.13) | collective-permute-done | bytes 65568 | tf_op jit(solution)/shard_map/ppermute | solution.py:387
  58.0 0.1 collective-permute-start.15
  58.1 1.8 %collective-permute-start.16 = (f16[8,32,128]{2,1,0:T(8,128)(2,1)S(1)}, f16[8,32,128]{2,1,0:T(8,128)(2,1)S(1)}, u32[]{:S(2)}, u32[]{:S(2)}) collective-permute-start(f16[8,32,128]{2,1,0:T(8,128)(2,1)S(1)} %fusion.6), channel_id=1, source_target_pairs={{4,0},{5,1},{6,2},{7,3},{0,4},{1,5},{2,6},{3,7},{12,8},{13,9},{14,... | collective-permute-start | bytes 196616 | tf_op jit(solution)/shard_map/ppermute | solution.py:394
  59.9 1.7 %collective-permute-start.17 = (f16[8,32,128]{2,1,0:T(8,128)(2,1)S(1)}, f16[8,32,128]{2,1,0:T(8,128)(2,1)S(1)}, u32[]{:S(2)}, u32[]{:S(2)}) collective-permute-start(f16[8,32,128]{2,1,0:T(8,128)(2,1)S(1)} %fusion.6), channel_id=1, source_target_pairs={{6,0},{7,1},{4,2},{5,3},{2,4},{3,5},{0,6},{1,7},{14,8},{15,9},{12,... | collective-permute-start | bytes 196616 | tf_op jit(solution)/shard_map/ppermute | solution.py:394
  61.6 0.6 collective-permute-done.16
  62.2 3.2 %collective-permute-done.17 = f16[8,32,128]{2,1,0:T(8,128)(2,1)S(1)} collective-permute-done((f16[8,32,128]{2,1,0:T(8,128)(2,1)S(1)}, f16[8,32,128]{2,1,0:T(8,128)(2,1)S(1)}, u32[]{:S(2)}, u32[]{:S(2)}) %collective-permute-start.17) | collective-permute-done | bytes 65568 | tf_op jit(solution)/shard_map/ppermute | solution.py:394
  65.5 0.1 pad_maximum_fusion.1
  65.6 2.0 %collective-permute-start.18 = (f16[4,8,32,128]{3,2,1,0:T(8,128)(2,1)S(1)}, f16[4,8,32,128]{3,2,1,0:T(8,128)(2,1)S(1)}, u32[]{:S(2)}, u32[]{:S(2)}) collective-permute-start(f16[4,8,32,128]{3,2,1,0:T(8,128)(2,1)S(1)} %pad_maximum_fusion.1), channel_id=1, source_target_pairs={{0,1},{1,0},{2,3},{3,2},{4,5},{5,4},{6,7},{7,6},{8,9},{9,8},{10,11... | collective-permute-start | bytes 786440 | tf_op jit(solution)/shard_map/ppermute | solution.py:422
  67.6 0.1 dynamic-slice_bitcast_fusion.7
  67.7 0.1 pad_maximum_fusion.2
  67.8 0.1 broadcast_in_dim.27
  67.9 0.8 %collective-permute-done.18 = f16[4,8,32,128]{3,2,1,0:T(8,128)(2,1)S(1)} collective-permute-done((f16[4,8,32,128]{3,2,1,0:T(8,128)(2,1)S(1)}, f16[4,8,32,128]{3,2,1,0:T(8,128)(2,1)S(1)}, u32[]{:S(2)}, u32[]{:S(2)}) %collective-permute-start.18) | collective-permute-done | bytes 262176 | tf_op jit(solution)/shard_map/ppermute | solution.py:422
  68.8 0.1 dynamic-slice_bitcast_fusion.3
  68.8 0.1 pad_maximum_fusion.3
  68.9 0.8 %convert_dynamic-update-slice_fusion = f32[16,128,128]{2,1,0:T(8,128)} fusion(f32[16,128,128]{2,1,0:T(8,128)} %copy-done.3, s32[]{:T(128)S(6)} %select_n.64, f16[8,128,128]{2,1,0:T(8,128)(2,1)S(1)} %pad_maximum_fusion.3, pred[]{:T(512)S(6)} %eq.29), kind=kLoop, calls=%fused_computation | loop fusion | flops 262144 | bytes 786437 | tf_op jit(solution)/shard_map/dynamic_update_slice | solution.py:433
  (33 shorter events, 0.3 us)
Async XLA Ops:
  0.0 10.3 %copy-start.1 = (bf16[2,16,128,128]{3,2,1,0:T(8,128)(2,1)S(1)}, bf16[2,16,128,128]{3,2,1,0:T(8,128)(2,1)}, u32[]{:S(2)}) copy-start(bf16[2,16,128,128]{3,2,1,0:T(8,128)(2,1)} %reward.3) | copy-start | bytes 3145732
  0.0 9.9 %copy-start.6 = (s32[2]{0:T(128)S(1)}, s32[2]{0:T(128)}, u32[]{:S(2)}) copy-start(s32[2]{0:T(128)} %param.9) | copy-start | bytes 28
  0.0 10.3 %copy-start = (f32[16,128,128]{2,1,0:T(8,128)S(1)}, f32[16,128,128]{2,1,0:T(8,128)}, u32[]{:S(2)}) copy-start(f32[16,128,128]{2,1,0:T(8,128)} %speed.3) | copy-start | bytes 3145732
  0.0 3.0 %copy-start.4 = (f32[16,3]{0,1:T(4,128)S(1)}, f32[16,3]{0,1:T(4,128)}, u32[]{:S(2)}) copy-start(f32[16,3]{0,1:T(4,128)} %param.10) | copy-start | bytes 580
  0.0 3.0 %copy-start.5 = (f32[16,3]{0,1:T(4,128)S(1)}, f32[16,3]{0,1:T(4,128)}, u32[]{:S(2)}) copy-start(f32[16,3]{0,1:T(4,128)} %param.11) | copy-start | bytes 580
  0.0 10.2 %collective-permute-start.1 = (bf16[2,16,128,128]{3,2,1,0:T(8,128)(2,1)}, bf16[2,16,128,128]{3,2,1,0:T(8,128)(2,1)}, u32[]{:S(2)}, u32[]{:S(2)}) collective-permute-start(bf16[2,16,128,128]{3,2,1,0:T(8,128)(2,1)} %reward.3), channel_id=1, source_target_pairs={{0,1},{1,0},{2,3},{3,2},{4,5},{5,4},{6,7},{7,6},{8,9},{9,8},{10,11... | collective-permute-start | bytes 3145736 | tf_op jit(solution)/shard_map/ppermute | solution.py:353
  0.8 2.3 %collective-permute-start = (s32[2]{0:T(128)}, s32[2]{0:T(128)S(1)}, u32[]{:S(2)}, u32[]{:S(2)}) collective-permute-start(s32[2]{0:T(128)} %param.9), channel_id=1, source_target_pairs={{0,1},{1,0},{2,3},{3,2},{4,5},{5,4},{6,7},{7,6},{8,9},{9,8},{10,11... | collective-permute-start | bytes 32 | tf_op jit(solution)/shard_map/ppermute | solution.py:352
  2.3 0.7 %copy-start.2 = (bf16[9,128,128]{2,1,0:T(8,128)(2,1)}, bf16[9,128,128]{2,1,0:T(8,128)(2,1)S(1)}, u32[]{:S(2)}) copy-start(bf16[9,128,128]{2,1,0:T(8,128)(2,1)S(1)} %get-tuple-element.25) | copy-start | bytes 884740
  3.1 13.3 %collective-permute-start.2 = (bf16[9,128,128]{2,1,0:T(8,128)(2,1)}, bf16[9,128,128]{2,1,0:T(8,128)(2,1)S(1)}, u32[]{:S(2)}, u32[]{:S(2)}) collective-permute-start(bf16[9,128,128]{2,1,0:T(8,128)(2,1)} %copy-done.2), channel_id=1, source_target_pairs={{1,9},{9,1},{3,11},{11,3},{5,13},{13,5},{7,15},{15,7},{8,16},{16,8... | collective-permute-start | bytes 884744 | tf_op jit(solution)/shard_map/ppermute | solution.py:374
  6.2 10.1 %collective-permute-start.3 = (bf16[4,128,128]{2,1,0:T(8,128)(2,1)S(1)}, bf16[4,128,128]{2,1,0:T(8,128)(2,1)S(1)}, u32[]{:S(2)}, u32[]{:S(2)}) collective-permute-start(bf16[4,128,128]{2,1,0:T(8,128)(2,1)S(1)} %get-tuple-element.26), channel_id=1, source_target_pairs={{0,9},{8,1},{2,11},{10,3},{4,13},{12,5},{6,15},{14,7},{9,16},{17,8... | collective-permute-start | bytes 393224 | tf_op jit(solution)/shard_map/ppermute | solution.py:375
  19.2 5.7 %collective-permute-start.4 = (f16[8,32,128]{2,1,0:T(8,128)(2,1)S(1)}, f16[8,32,128]{2,1,0:T(8,128)(2,1)S(1)}, u32[]{:S(2)}, u32[]{:S(2)}) collective-permute-start(f16[8,32,128]{2,1,0:T(8,128)(2,1)S(1)} %get-tuple-element.48), channel_id=1, source_target_pairs={{0,6},{1,7},{2,4},{3,5},{4,2},{5,3},{6,0},{7,1},{8,14},{9,15},{10,... | collective-permute-start | bytes 196616 | tf_op jit(solution)/shard_map/ppermute | solution.py:387
  22.6 5.6 %collective-permute-start.5 = (f16[8,32,128]{2,1,0:T(8,128)(2,1)S(1)}, f16[8,32,128]{2,1,0:T(8,128)(2,1)S(1)}, u32[]{:S(2)}, u32[]{:S(2)}) collective-permute-start(f16[8,32,128]{2,1,0:T(8,128)(2,1)S(1)} %get-tuple-element.50), channel_id=1, source_target_pairs={{0,4},{1,5},{2,6},{3,7},{4,0},{5,1},{6,2},{7,3},{8,12},{9,13},{10,... | collective-permute-start | bytes 196616 | tf_op jit(solution)/shard_map/ppermute | solution.py:387
  22.6 5.6 %collective-permute-start.6 = (f16[8,32,128]{2,1,0:T(8,128)(2,1)S(1)}, f16[8,32,128]{2,1,0:T(8,128)(2,1)S(1)}, u32[]{:S(2)}, u32[]{:S(2)}) collective-permute-start(f16[8,32,128]{2,1,0:T(8,128)(2,1)S(1)} %get-tuple-element.49), channel_id=1, source_target_pairs={{0,2},{1,3},{2,0},{3,1},{4,6},{5,7},{6,4},{7,5},{8,10},{9,11},{10,... | collective-permute-start | bytes 196616 | tf_op jit(solution)/shard_map/ppermute | solution.py:387
  28.2 3.6 %collective-permute-start.7 = (f16[8,32,128]{2,1,0:T(8,128)(2,1)S(1)}, f16[8,32,128]{2,1,0:T(8,128)(2,1)S(1)}, u32[]{:S(2)}, u32[]{:S(2)}) collective-permute-start(f16[8,32,128]{2,1,0:T(8,128)(2,1)S(1)} %fusion.15), channel_id=1, source_target_pairs={{2,0},{3,1},{0,2},{1,3},{6,4},{7,5},{4,6},{5,7},{10,8},{11,9},{8,1... | collective-permute-start | bytes 196616 | tf_op jit(solution)/shard_map/ppermute | solution.py:394
  29.2 4.5 %collective-permute-start.8 = (f16[8,32,128]{2,1,0:T(8,128)(2,1)S(1)}, f16[8,32,128]{2,1,0:T(8,128)(2,1)S(1)}, u32[]{:S(2)}, u32[]{:S(2)}) collective-permute-start(f16[8,32,128]{2,1,0:T(8,128)(2,1)S(1)} %fusion.15), channel_id=1, source_target_pairs={{4,0},{5,1},{6,2},{7,3},{0,4},{1,5},{2,6},{3,7},{12,8},{13,9},{14,... | collective-permute-start | bytes 196616 | tf_op jit(solution)/shard_map/ppermute | solution.py:394
  30.8 4.9 %collective-permute-start.9 = (f16[8,32,128]{2,1,0:T(8,128)(2,1)S(1)}, f16[8,32,128]{2,1,0:T(8,128)(2,1)S(1)}, u32[]{:S(2)}, u32[]{:S(2)}) collective-permute-start(f16[8,32,128]{2,1,0:T(8,128)(2,1)S(1)} %fusion.15), channel_id=1, source_target_pairs={{6,0},{7,1},{4,2},{5,3},{2,4},{3,5},{0,6},{1,7},{14,8},{15,9},{12,... | collective-permute-start | bytes 196616 | tf_op jit(solution)/shard_map/ppermute | solution.py:394
  35.9 4.6 %collective-permute-start.11 = (f16[4,3,32,128]{3,2,1,0:T(8,128)(2,1)S(1)}, f16[4,3,32,128]{3,2,1,0:T(8,128)(2,1)S(1)}, u32[]{:S(2)}, u32[]{:S(2)}) collective-permute-start(f16[4,3,32,128]{3,2,1,0:T(8,128)(2,1)S(1)} %get-tuple-element.45), channel_id=1, source_target_pairs={{0,1},{1,0},{2,3},{3,2},{4,5},{5,4},{6,7},{7,6},{8,9},{9,8},{10,11... | collective-permute-start | bytes 294920 | tf_op jit(solution)/shard_map/ppermute | solution.py:413
  38.6 7.3 %collective-permute-start.10 = (bf16[4,3,32,128]{3,2,1,0:T(8,128)(2,1)S(1)}, bf16[4,3,32,128]{3,2,1,0:T(8,128)(2,1)S(1)}, u32[]{:S(2)}, u32[]{:S(2)}) collective-permute-start(bf16[4,3,32,128]{3,2,1,0:T(8,128)(2,1)S(1)} %get-tuple-element.44), channel_id=1, source_target_pairs={{1,9},{9,1},{3,11},{11,3},{5,13},{13,5},{7,15},{15,7},{8,16},{16,8... | collective-permute-start | bytes 294920 | tf_op jit(solution)/shard_map/ppermute | solution.py:414
  48.7 5.1 %collective-permute-start.12 = (f16[8,32,128]{2,1,0:T(8,128)(2,1)S(1)}, f16[8,32,128]{2,1,0:T(8,128)(2,1)S(1)}, u32[]{:S(2)}, u32[]{:S(2)}) collective-permute-start(f16[8,32,128]{2,1,0:T(8,128)(2,1)S(1)} %get-tuple-element.41), channel_id=1, source_target_pairs={{0,6},{1,7},{2,4},{3,5},{4,2},{5,3},{6,0},{7,1},{8,14},{9,15},{10,... | collective-permute-start | bytes 196616 | tf_op jit(solution)/shard_map/ppermute | solution.py:387
  50.7 7.2 %collective-permute-start.13 = (f16[8,32,128]{2,1,0:T(8,128)(2,1)S(1)}, f16[8,32,128]{2,1,0:T(8,128)(2,1)S(1)}, u32[]{:S(2)}, u32[]{:S(2)}) collective-permute-start(f16[8,32,128]{2,1,0:T(8,128)(2,1)S(1)} %get-tuple-element.43), channel_id=1, source_target_pairs={{0,4},{1,5},{2,6},{3,7},{4,0},{5,1},{6,2},{7,3},{8,12},{9,13},{10,... | collective-permute-start | bytes 196616 | tf_op jit(solution)/shard_map/ppermute | solution.py:387
  51.3 6.6 %collective-permute-start.14 = (f16[8,32,128]{2,1,0:T(8,128)(2,1)S(1)}, f16[8,32,128]{2,1,0:T(8,128)(2,1)S(1)}, u32[]{:S(2)}, u32[]{:S(2)}) collective-permute-start(f16[8,32,128]{2,1,0:T(8,128)(2,1)S(1)} %get-tuple-element.42), channel_id=1, source_target_pairs={{0,2},{1,3},{2,0},{3,1},{4,6},{5,7},{6,4},{7,5},{8,10},{9,11},{10,... | collective-permute-start | bytes 196616 | tf_op jit(solution)/shard_map/ppermute | solution.py:387
  58.0 3.6 %collective-permute-start.15 = (f16[8,32,128]{2,1,0:T(8,128)(2,1)S(1)}, f16[8,32,128]{2,1,0:T(8,128)(2,1)S(1)}, u32[]{:S(2)}, u32[]{:S(2)}) collective-permute-start(f16[8,32,128]{2,1,0:T(8,128)(2,1)S(1)} %fusion.6), channel_id=1, source_target_pairs={{2,0},{3,1},{0,2},{1,3},{6,4},{7,5},{4,6},{5,7},{10,8},{11,9},{8,1... | collective-permute-start | bytes 196616 | tf_op jit(solution)/shard_map/ppermute | solution.py:394
  58.1 4.1 %collective-permute-start.16 = (f16[8,32,128]{2,1,0:T(8,128)(2,1)S(1)}, f16[8,32,128]{2,1,0:T(8,128)(2,1)S(1)}, u32[]{:S(2)}, u32[]{:S(2)}) collective-permute-start(f16[8,32,128]{2,1,0:T(8,128)(2,1)S(1)} %fusion.6), channel_id=1, source_target_pairs={{4,0},{5,1},{6,2},{7,3},{0,4},{1,5},{2,6},{3,7},{12,8},{13,9},{14,... | collective-permute-start | bytes 196616 | tf_op jit(solution)/shard_map/ppermute | solution.py:394
  59.9 5.5 %collective-permute-start.17 = (f16[8,32,128]{2,1,0:T(8,128)(2,1)S(1)}, f16[8,32,128]{2,1,0:T(8,128)(2,1)S(1)}, u32[]{:S(2)}, u32[]{:S(2)}) collective-permute-start(f16[8,32,128]{2,1,0:T(8,128)(2,1)S(1)} %fusion.6), channel_id=1, source_target_pairs={{6,0},{7,1},{4,2},{5,3},{2,4},{3,5},{0,6},{1,7},{14,8},{15,9},{12,... | collective-permute-start | bytes 196616 | tf_op jit(solution)/shard_map/ppermute | solution.py:394
  65.6 3.2 %collective-permute-start.18 = (f16[4,8,32,128]{3,2,1,0:T(8,128)(2,1)S(1)}, f16[4,8,32,128]{3,2,1,0:T(8,128)(2,1)S(1)}, u32[]{:S(2)}, u32[]{:S(2)}) collective-permute-start(f16[4,8,32,128]{3,2,1,0:T(8,128)(2,1)S(1)} %pad_maximum_fusion.1), channel_id=1, source_target_pairs={{0,1},{1,0},{2,3},{3,2},{4,5},{5,4},{6,7},{7,6},{8,9},{9,8},{10,11... | collective-permute-start | bytes 786440 | tf_op jit(solution)/shard_map/ppermute | solution.py:422
  67.9 1.0 %copy-start.3 = (f32[16,128,128]{2,1,0:T(8,128)}, f32[16,128,128]{2,1,0:T(8,128)S(1)}, u32[]{:S(2)}) copy-start(f32[16,128,128]{2,1,0:T(8,128)S(1)} %convert_dynamic-update-slice_fusion.1) | copy-start | bytes 3145732

commit v7 on v6

--- a/solution.py
+++ b/solution.py
@@ -11,6 +11,7 @@
 PAD = 8
 CHUNK = 32
 LOWEST = -3.0e38
+WIRE_SCALE = 4096.0
 
 
 def mate(chip, step, chips):
@@ -324,6 +325,7 @@
 
     whole = pl.BlockSpec(memory_space=pltpu.VMEM)
     scalars = pl.BlockSpec(memory_space=pltpu.SMEM)
+
     def shape(*dims):
         return jax.ShapeDtypeStruct(dims, jnp.float32)
 
@@ -379,8 +381,11 @@
     pairs = jnp.concatenate([diffusion_sets, drift_sets], axis=1)
     coef = jnp.sum(jnp.where(picked[:, :, None], pairs[None], 0.0), axis=1)
 
+    def from_wire(values):
+        return values.astype(jnp.float32) * (1.0 / WIRE_SCALE)
+
     def reduce(best):
-        parts = best.astype(wire)
+        parts = (best * WIRE_SCALE).astype(wire)
         mine = parts[0]
         for step in range(chips - 1, 0, -1):
             pairs = [(2 * z + c, 2 * mate(z, step, chips) + c) for z in range(chips) for c in range(2)]
@@ -411,9 +416,9 @@
     pieces = gather(reduce(jnp.concatenate([best_rest, best], axis=1)))
 
     across = lax.ppermute(pieces[:, -SUBSTEPS:], "ctrl", partners)
-    beyond = lax.ppermute(pieces[:, :SUBSTEPS].astype(narrow), both, facing)
-    current = pieces.astype(jnp.float32)
-    best, *kept = call(early_later, rows, steps, (current, across.astype(jnp.float32), *laid), early_out)
+    beyond = lax.ppermute(from_wire(pieces[:, :SUBSTEPS]).astype(narrow), both, facing)
+    current = from_wire(pieces)
+    best, *kept = call(early_later, rows, steps, (current, from_wire(across), *laid), early_out)
     best_rest = call(
         rest_later, rest_rows, rest_steps, (current, beyond, *laid, *edges, *kept), rest_out
     )
@@ -426,7 +431,7 @@
             lax.dynamic_index_in_dim(parts, mate_step(chip, shard, chips), 0, keepdims=False) for shard in range(chips)
         ]
         block_rows = jnp.concatenate(ordered, axis=1)
-        return jnp.where(flipped, block_rows[::-1], block_rows).astype(jnp.float32)
+        return from_wire(jnp.where(flipped, block_rows[::-1], block_rows))
 
     result = jnp.zeros((cells, ny, nz), jnp.float32)
     result = lax.dynamic_update_slice_in_dim(result, in_order(pieces, upper == 1), upper * half, axis=0)

time: 70 us -> 70.1 us (level)
  no operation moved by 1% of the time
where the time goes in v7:
time: 70.1 us; the launch traced here: 69.9 us
  starting transfers between devices  29 us (41%)
  waiting for transfers between devices  19.3 us (28%)
  Pallas kernels  18.2 us (26%)
  other arithmetic  1.88 us (3%)
  local copies, waits for them, and re-layouts  1.14 us (2%)
    pallas_call x4, Pallas kernels, call(): pl.pallas_call(functools.partial(kernel, half=half), out_shape=outs, in_s...  16.8 us
    ppermute x6, waiting for transfers between devices, reduce(): mine = jnp.maximum(mine, lax.ppermute(parts[step], 'ctrl', pairs))  10.6 us
    ppermute x6, waiting for transfers between devices, gather(): pieces.append(lax.ppermute(mine, 'ctrl', pairs))  7.85 us
    ppermute x6, starting transfers between devices, reduce(): mine = jnp.maximum(mine, lax.ppermute(parts[step], 'ctrl', pairs))  7.36 us
    ppermute x6, starting transfers between devices, gather(): pieces.append(lax.ppermute(mine, 'ctrl', pairs))  7.22 us
    ppermute x1, starting transfers between devices, body(): edge_other = lax.ppermute(far, both, beside)  3.73 us
    ppermute x1, starting transfers between devices, body(): edge = lax.ppermute(packed, both, facing)  3.12 us
    ppermute x1, starting transfers between devices, body(): across = lax.ppermute(pieces[:, -SUBSTEPS:], 'ctrl', partners)  2.64 us
  transfers between devices with their start and end apart: 19, of which 9 were waited for; matrix products, arithmetic and copies ran while one was open for 1% of the time, Pallas kernels for 18%

profile of v7, /device:TPU:5, one launch (start us, length us, event | category | flops | bytes accessed | tf_op | source)
XLA Modules:
  0.0 69.9 jit_solution(14089437798076771828)
XLA Ops:
  0.0 0.7 %collective-permute-start.1 = (bf16[2,16,128,128]{3,2,1,0:T(8,128)(2,1)}, bf16[2,16,128,128]{3,2,1,0:T(8,128)(2,1)}, u32[]{:S(2)}, u32[]{:S(2)}) collective-permute-start(bf16[2,16,128,128]{3,2,1,0:T(8,128)(2,1)} %reward.3), channel_id=1, source_target_pairs={{0,1},{1,0},{2,3},{3,2},{4,5},{5,4},{6,7},{7,6},{8,9},{9,8},{10,11... | collective-permute-start | bytes 3145736 | tf_op jit(solution)/shard_map/ppermute | solution.py:355
  0.8 0.1 collective-permute-start
  0.9 1.5 %shard_map.64 = (bf16[9,128,128]{2,1,0:T(8,128)(2,1)S(1)}, bf16[4,128,128]{2,1,0:T(8,128)(2,1)S(1)}, f32[11,144,128]{2,1,0:T(8,128)S(1)}) custom-call(f32[16,128,128]{2,1,0:T(8,128)} %value.1, f32[16,128,128]{2,1,0:T(8,128)} %speed.3, bf16[2,16,128,128]{3,2,1,0:T(8,128)(2,1)} %reward.3), custom_call_target="tpu_custom_call" | custom-call | tf_op jit(solution)/shard_map/pallas_call | solution.py:358
  2.3 0.7 %copy-done.2 = bf16[9,128,128]{2,1,0:T(8,128)(2,1)} copy-done((bf16[9,128,128]{2,1,0:T(8,128)(2,1)}, bf16[9,128,128]{2,1,0:T(8,128)(2,1)S(1)}, u32[]{:S(2)}) %copy-start.2) | copy-done | bytes 294936
  3.1 3.1 %collective-permute-start.2 = (bf16[9,128,128]{2,1,0:T(8,128)(2,1)}, bf16[9,128,128]{2,1,0:T(8,128)(2,1)S(1)}, u32[]{:S(2)}, u32[]{:S(2)}) collective-permute-start(bf16[9,128,128]{2,1,0:T(8,128)(2,1)} %copy-done.2), channel_id=1, source_target_pairs={{1,9},{9,1},{3,11},{11,3},{5,13},{13,5},{7,15},{15,7},{8,16},{16,8... | collective-permute-start | bytes 884744 | tf_op jit(solution)/shard_map/ppermute | solution.py:376
  6.2 3.7 %collective-permute-start.3 = (bf16[4,128,128]{2,1,0:T(8,128)(2,1)S(1)}, bf16[4,128,128]{2,1,0:T(8,128)(2,1)S(1)}, u32[]{:S(2)}, u32[]{:S(2)}) collective-permute-start(bf16[4,128,128]{2,1,0:T(8,128)(2,1)S(1)} %get-tuple-element.26), channel_id=1, source_target_pairs={{0,9},{8,1},{2,11},{10,3},{4,13},{12,5},{6,15},{14,7},{9,16},{17,8... | collective-permute-start | bytes 393224 | tf_op jit(solution)/shard_map/ppermute | solution.py:377
  9.9 0.1 pad_add_fusion
  10.0 0.1 iota_compare_fusion
  10.1 0.1 select_reduce_fusion
  10.2 0.1 copy.11.coef
  10.3 6.1 %shard_map.65 = (f32[4,5,32,128]{3,2,1,0:T(8,128)S(1)}, f32[4,2,128,128]{3,2,1,0:T(8,128)S(1)}, f32[4,2,128,128]{3,2,1,0:T(8,128)S(1)}, f32[10,128,128]{2,1,0:T(8,128)S(1)}, f32[4,10,128,128]{3,2,1,0:T(8,128)S(1)}) custom-call(f32[4,6]{1,0:T(4,128)S(1)} %copy.11.coef, f32[11,144,128]{2,1,0:T(8,128)S(1)} %get-tuple-element.22.block.first, ...), custom_call_target="tpu_custom_call" | custom-call | flops 34406400 | bytes 16515072 | tf_op jit(solution)/shard_map/pallas_call | solution.py:339
  16.4 2.7 %shard_map.66 = f32[4,3,32,128]{3,2,1,0:T(8,128)S(1)} custom-call(f32[4,6]{1,0:T(4,128)S(1)} %copy.11.coef, f32[11,144,128]{2,1,0:T(8,128)S(1)} %get-tuple-element.22.block.first, f32[10,128,128]{2,1,0:T(8,128)S(1)} %get-tuple-element.23.speed_rows, f32[4,10,128,128]{3,2,1,0:T(8,128)S(1)} %get-tuple-element.24.reward_rows, ...), custom_call_target="tpu_custom_call" | custom-call | flops 14745600 | bytes 7077888 | tf_op jit(solution)/shard_map/pallas_call | solution.py:339
  19.1 0.1 fusion
  19.2 3.4 %collective-permute-start.4 = (f16[8,32,128]{2,1,0:T(8,128)(2,1)S(1)}, f16[8,32,128]{2,1,0:T(8,128)(2,1)S(1)}, u32[]{:S(2)}, u32[]{:S(2)}) collective-permute-start(f16[8,32,128]{2,1,0:T(8,128)(2,1)S(1)} %get-tuple-element.44), channel_id=1, source_target_pairs={{0,6},{1,7},{2,4},{3,5},{4,2},{5,3},{6,0},{7,1},{8,14},{9,15},{10,... | collective-permute-start | bytes 196616 | tf_op jit(solution)/shard_map/ppermute | solution.py:392
  22.6 0.4 collective-permute-start.6
  22.9 2.0 %collective-permute-done.4 = f16[8,32,128]{2,1,0:T(8,128)(2,1)S(1)} collective-permute-done((f16[8,32,128]{2,1,0:T(8,128)(2,1)S(1)}, f16[8,32,128]{2,1,0:T(8,128)(2,1)S(1)}, u32[]{:S(2)}, u32[]{:S(2)}) %collective-permute-start.4) | collective-permute-done | bytes 65568 | tf_op jit(solution)/shard_map/ppermute | solution.py:392
  24.9 3.2 %collective-permute-done.5 = f16[8,32,128]{2,1,0:T(8,128)(2,1)S(1)} collective-permute-done((f16[8,32,128]{2,1,0:T(8,128)(2,1)S(1)}, f16[8,32,128]{2,1,0:T(8,128)(2,1)S(1)}, u32[]{:S(2)}, u32[]{:S(2)}) %collective-permute-start.5) | collective-permute-done | bytes 65568 | tf_op jit(solution)/shard_map/ppermute | solution.py:392
  28.2 1.0 %collective-permute-start.7 = (f16[8,32,128]{2,1,0:T(8,128)(2,1)S(1)}, f16[8,32,128]{2,1,0:T(8,128)(2,1)S(1)}, u32[]{:S(2)}, u32[]{:S(2)}) collective-permute-start(f16[8,32,128]{2,1,0:T(8,128)(2,1)S(1)} %fusion.7), channel_id=1, source_target_pairs={{2,0},{3,1},{0,2},{1,3},{6,4},{7,5},{4,6},{5,7},{10,8},{11,9},{8,1... | collective-permute-start | bytes 196616 | tf_op jit(solution)/shard_map/ppermute | solution.py:399
  29.2 1.6 %collective-permute-start.8 = (f16[8,32,128]{2,1,0:T(8,128)(2,1)S(1)}, f16[8,32,128]{2,1,0:T(8,128)(2,1)S(1)}, u32[]{:S(2)}, u32[]{:S(2)}) collective-permute-start(f16[8,32,128]{2,1,0:T(8,128)(2,1)S(1)} %fusion.7), channel_id=1, source_target_pairs={{4,0},{5,1},{6,2},{7,3},{0,4},{1,5},{2,6},{3,7},{12,8},{13,9},{14,... | collective-permute-start | bytes 196616 | tf_op jit(solution)/shard_map/ppermute | solution.py:399
  30.8 1.0 %collective-permute-start.9 = (f16[8,32,128]{2,1,0:T(8,128)(2,1)S(1)}, f16[8,32,128]{2,1,0:T(8,128)(2,1)S(1)}, u32[]{:S(2)}, u32[]{:S(2)}) collective-permute-start(f16[8,32,128]{2,1,0:T(8,128)(2,1)S(1)} %fusion.7), channel_id=1, source_target_pairs={{6,0},{7,1},{4,2},{5,3},{2,4},{3,5},{0,6},{1,7},{14,8},{15,9},{12,... | collective-permute-start | bytes 196616 | tf_op jit(solution)/shard_map/ppermute | solution.py:399
  31.8 1.9 %collective-permute-done.8 = f16[8,32,128]{2,1,0:T(8,128)(2,1)S(1)} collective-permute-done((f16[8,32,128]{2,1,0:T(8,128)(2,1)S(1)}, f16[8,32,128]{2,1,0:T(8,128)(2,1)S(1)}, u32[]{:S(2)}, u32[]{:S(2)}) %collective-permute-start.8) | collective-permute-done | bytes 65568 | tf_op jit(solution)/shard_map/ppermute | solution.py:399
  33.7 2.1 %collective-permute-done.9 = f16[8,32,128]{2,1,0:T(8,128)(2,1)S(1)} collective-permute-done((f16[8,32,128]{2,1,0:T(8,128)(2,1)S(1)}, f16[8,32,128]{2,1,0:T(8,128)(2,1)S(1)}, u32[]{:S(2)}, u32[]{:S(2)}) %collective-permute-start.9) | collective-permute-done | bytes 65568 | tf_op jit(solution)/shard_map/ppermute | solution.py:399
  35.8 0.1 pad_maximum_fusion
  35.9 2.6 %collective-permute-start.11 = (f16[4,3,32,128]{3,2,1,0:T(8,128)(2,1)S(1)}, f16[4,3,32,128]{3,2,1,0:T(8,128)(2,1)S(1)}, u32[]{:S(2)}, u32[]{:S(2)}) collective-permute-start(f16[4,3,32,128]{3,2,1,0:T(8,128)(2,1)S(1)} %slice.45), channel_id=1, source_target_pairs={{0,1},{1,0},{2,3},{3,2},{4,5},{5,4},{6,7},{7,6},{8,9},{9,8},{10,11... | collective-permute-start | bytes 294920 | tf_op jit(solution)/shard_map/ppermute | solution.py:418
  38.6 2.0 %collective-permute-start.10 = (bf16[4,3,32,128]{3,2,1,0:T(8,128)(2,1)S(1)}, bf16[4,3,32,128]{3,2,1,0:T(8,128)(2,1)S(1)}, u32[]{:S(2)}, u32[]{:S(2)}) collective-permute-start(bf16[4,3,32,128]{3,2,1,0:T(8,128)(2,1)S(1)} %multiply_convert_fusion), channel_id=1, source_target_pairs={{1,9},{9,1},{3,11},{11,3},{5,13},{13,5},{7,15},{15,7},{8,16},{16,8... | collective-permute-start | bytes 294920 | tf_op jit(solution)/shard_map/ppermute | solution.py:419
  40.5 0.1 convert_multiply_fusion.current
  40.7 5.3 %shard_map.67 = (f32[4,5,32,128]{3,2,1,0:T(8,128)S(1)}, f32[4,2,128,128]{3,2,1,0:T(8,128)S(1)}, f32[4,2,128,128]{3,2,1,0:T(8,128)S(1)}) custom-call(f32[4,6]{1,0:T(4,128)S(1)} %copy.11.coef, f32[4,8,32,128]{3,2,1,0:T(8,128)S(1)} %convert_multiply_fusion.current, f32[4,3,32,128]{3,2,1,0:T(8,128)S(1)} %convert_multiply_fusion.1.across, ...), custom_call_target="tpu_custom_call" | custom-call | flops 34406400 | bytes 16515072 | tf_op jit(solution)/shard_map/pallas_call | solution.py:339
  46.0 2.7 %shard_map.68 = f32[4,3,32,128]{3,2,1,0:T(8,128)S(1)} custom-call(f32[4,6]{1,0:T(4,128)S(1)} %copy.11.coef, f32[4,8,32,128]{3,2,1,0:T(8,128)S(1)} %convert_multiply_fusion.current, bf16[4,3,32,128]{3,2,1,0:T(8,128)(2,1)S(1)} %collective-permute-done.10.beyond, f32[10,128,128]{2,1,0:T(8,128)S(1)} %get-tuple-element.23.speed_rows, ...), custom_call_target="tpu_custom_call" | custom-call | flops 14745600 | bytes 7077888 | tf_op jit(solution)/shard_map/pallas_call | solution.py:339
  48.7 0.1 fusion.1
  48.8 2.0 %collective-permute-start.12 = (f16[8,32,128]{2,1,0:T(8,128)(2,1)S(1)}, f16[8,32,128]{2,1,0:T(8,128)(2,1)S(1)}, u32[]{:S(2)}, u32[]{:S(2)}) collective-permute-start(f16[8,32,128]{2,1,0:T(8,128)(2,1)S(1)} %get-tuple-element.41), channel_id=1, source_target_pairs={{0,6},{1,7},{2,4},{3,5},{4,2},{5,3},{6,0},{7,1},{8,14},{9,15},{10,... | collective-permute-start | bytes 196616 | tf_op jit(solution)/shard_map/ppermute | solution.py:392
  50.8 0.6 collective-permute-start.13
  51.4 1.0 %collective-permute-start.14 = (f16[8,32,128]{2,1,0:T(8,128)(2,1)S(1)}, f16[8,32,128]{2,1,0:T(8,128)(2,1)S(1)}, u32[]{:S(2)}, u32[]{:S(2)}) collective-permute-start(f16[8,32,128]{2,1,0:T(8,128)(2,1)S(1)} %get-tuple-element.42), channel_id=1, source_target_pairs={{0,2},{1,3},{2,0},{3,1},{4,6},{5,7},{6,4},{7,5},{8,10},{9,11},{10,... | collective-permute-start | bytes 196616 | tf_op jit(solution)/shard_map/ppermute | solution.py:392
  52.4 1.5 %collective-permute-done.12 = f16[8,32,128]{2,1,0:T(8,128)(2,1)S(1)} collective-permute-done((f16[8,32,128]{2,1,0:T(8,128)(2,1)S(1)}, f16[8,32,128]{2,1,0:T(8,128)(2,1)S(1)}, u32[]{:S(2)}, u32[]{:S(2)}) %collective-permute-start.12) | collective-permute-done | bytes 65568 | tf_op jit(solution)/shard_map/ppermute | solution.py:392
  53.9 4.0 %collective-permute-done.13 = f16[8,32,128]{2,1,0:T(8,128)(2,1)S(1)} collective-permute-done((f16[8,32,128]{2,1,0:T(8,128)(2,1)S(1)}, f16[8,32,128]{2,1,0:T(8,128)(2,1)S(1)}, u32[]{:S(2)}, u32[]{:S(2)}) %collective-permute-start.13) | collective-permute-done | bytes 65568 | tf_op jit(solution)/shard_map/ppermute | solution.py:392
  57.9 0.1 collective-permute-start.15
  58.0 2.0 %collective-permute-start.16 = (f16[8,32,128]{2,1,0:T(8,128)(2,1)S(1)}, f16[8,32,128]{2,1,0:T(8,128)(2,1)S(1)}, u32[]{:S(2)}, u32[]{:S(2)}) collective-permute-start(f16[8,32,128]{2,1,0:T(8,128)(2,1)S(1)} %fusion.4), channel_id=1, source_target_pairs={{4,0},{5,1},{6,2},{7,3},{0,4},{1,5},{2,6},{3,7},{12,8},{13,9},{14,... | collective-permute-start | bytes 196616 | tf_op jit(solution)/shard_map/ppermute | solution.py:399
  60.0 1.5 %collective-permute-start.17 = (f16[8,32,128]{2,1,0:T(8,128)(2,1)S(1)}, f16[8,32,128]{2,1,0:T(8,128)(2,1)S(1)}, u32[]{:S(2)}, u32[]{:S(2)}) collective-permute-start(f16[8,32,128]{2,1,0:T(8,128)(2,1)S(1)} %fusion.4), channel_id=1, source_target_pairs={{6,0},{7,1},{4,2},{5,3},{2,4},{3,5},{0,6},{1,7},{14,8},{15,9},{12,... | collective-permute-start | bytes 196616 | tf_op jit(solution)/shard_map/ppermute | solution.py:399
  61.5 0.6 collective-permute-done.16
  62.1 3.3 %collective-permute-done.17 = f16[8,32,128]{2,1,0:T(8,128)(2,1)S(1)} collective-permute-done((f16[8,32,128]{2,1,0:T(8,128)(2,1)S(1)}, f16[8,32,128]{2,1,0:T(8,128)(2,1)S(1)}, u32[]{:S(2)}, u32[]{:S(2)}) %collective-permute-start.17) | collective-permute-done | bytes 65568 | tf_op jit(solution)/shard_map/ppermute | solution.py:399
  65.5 0.1 pad_maximum_fusion.1
  65.5 2.1 %collective-permute-start.18 = (f16[4,8,32,128]{3,2,1,0:T(8,128)(2,1)S(1)}, f16[4,8,32,128]{3,2,1,0:T(8,128)(2,1)S(1)}, u32[]{:S(2)}, u32[]{:S(2)}) collective-permute-start(f16[4,8,32,128]{3,2,1,0:T(8,128)(2,1)S(1)} %pad_maximum_fusion.1), channel_id=1, source_target_pairs={{0,1},{1,0},{2,3},{3,2},{4,5},{5,4},{6,7},{7,6},{8,9},{9,8},{10,11... | collective-permute-start | bytes 786440 | tf_op jit(solution)/shard_map/ppermute | solution.py:427
  67.7 0.1 dynamic-slice_bitcast_fusion.7
  67.7 0.1 pad_maximum_fusion.2
  67.8 0.1 broadcast_in_dim.27
  68.0 0.1 multiply_dynamic-update-slice_fusion.1
  68.0 0.8 %collective-permute-done.18 = f16[4,8,32,128]{3,2,1,0:T(8,128)(2,1)S(1)} collective-permute-done((f16[4,8,32,128]{3,2,1,0:T(8,128)(2,1)S(1)}, f16[4,8,32,128]{3,2,1,0:T(8,128)(2,1)S(1)}, u32[]{:S(2)}, u32[]{:S(2)}) %collective-permute-start.18) | collective-permute-done | bytes 262176 | tf_op jit(solution)/shard_map/ppermute | solution.py:427
  68.9 0.1 pad_maximum_fusion.3
  69.0 0.9 %multiply_dynamic-update-slice_fusion = f32[16,128,128]{2,1,0:T(8,128)} fusion(f32[16,128,128]{2,1,0:T(8,128)} %copy-done.3, s32[]{:T(128)S(6)} %select_n.64, f16[8,128,128]{2,1,0:T(8,128)(2,1)S(1)} %pad_maximum_fusion.3, pred[]{:T(512)S(6)} %eq.29), kind=kLoop, calls=%fused_computation.4 | loop fusion | flops 393216 | bytes 786437 | tf_op jit(solution)/shard_map/dynamic_update_slice | solution.py:438
  (33 shorter events, 0.4 us)
Async XLA Ops:
  0.0 10.3 %copy-start.1 = (bf16[2,16,128,128]{3,2,1,0:T(8,128)(2,1)S(1)}, bf16[2,16,128,128]{3,2,1,0:T(8,128)(2,1)}, u32[]{:S(2)}) copy-start(bf16[2,16,128,128]{3,2,1,0:T(8,128)(2,1)} %reward.3) | copy-start | bytes 3145732
  0.0 9.9 %copy-start.6 = (s32[2]{0:T(128)S(1)}, s32[2]{0:T(128)}, u32[]{:S(2)}) copy-start(s32[2]{0:T(128)} %param.9) | copy-start | bytes 28
  0.0 10.3 %copy-start = (f32[16,128,128]{2,1,0:T(8,128)S(1)}, f32[16,128,128]{2,1,0:T(8,128)}, u32[]{:S(2)}) copy-start(f32[16,128,128]{2,1,0:T(8,128)} %speed.3) | copy-start | bytes 3145732
  0.0 3.0 %copy-start.4 = (f32[16,3]{0,1:T(4,128)S(1)}, f32[16,3]{0,1:T(4,128)}, u32[]{:S(2)}) copy-start(f32[16,3]{0,1:T(4,128)} %param.10) | copy-start | bytes 580
  0.0 3.0 %copy-start.5 = (f32[16,3]{0,1:T(4,128)S(1)}, f32[16,3]{0,1:T(4,128)}, u32[]{:S(2)}) copy-start(f32[16,3]{0,1:T(4,128)} %param.11) | copy-start | bytes 580
  0.0 10.2 %collective-permute-start.1 = (bf16[2,16,128,128]{3,2,1,0:T(8,128)(2,1)}, bf16[2,16,128,128]{3,2,1,0:T(8,128)(2,1)}, u32[]{:S(2)}, u32[]{:S(2)}) collective-permute-start(bf16[2,16,128,128]{3,2,1,0:T(8,128)(2,1)} %reward.3), channel_id=1, source_target_pairs={{0,1},{1,0},{2,3},{3,2},{4,5},{5,4},{6,7},{7,6},{8,9},{9,8},{10,11... | collective-permute-start | bytes 3145736 | tf_op jit(solution)/shard_map/ppermute | solution.py:355
  0.8 2.3 %collective-permute-start = (s32[2]{0:T(128)}, s32[2]{0:T(128)S(1)}, u32[]{:S(2)}, u32[]{:S(2)}) collective-permute-start(s32[2]{0:T(128)} %param.9), channel_id=1, source_target_pairs={{0,1},{1,0},{2,3},{3,2},{4,5},{5,4},{6,7},{7,6},{8,9},{9,8},{10,11... | collective-permute-start | bytes 32 | tf_op jit(solution)/shard_map/ppermute | solution.py:354
  2.3 0.7 %copy-start.2 = (bf16[9,128,128]{2,1,0:T(8,128)(2,1)}, bf16[9,128,128]{2,1,0:T(8,128)(2,1)S(1)}, u32[]{:S(2)}) copy-start(bf16[9,128,128]{2,1,0:T(8,128)(2,1)S(1)} %get-tuple-element.25) | copy-start | bytes 884740
  3.1 13.3 %collective-permute-start.2 = (bf16[9,128,128]{2,1,0:T(8,128)(2,1)}, bf16[9,128,128]{2,1,0:T(8,128)(2,1)S(1)}, u32[]{:S(2)}, u32[]{:S(2)}) collective-permute-start(bf16[9,128,128]{2,1,0:T(8,128)(2,1)} %copy-done.2), channel_id=1, source_target_pairs={{1,9},{9,1},{3,11},{11,3},{5,13},{13,5},{7,15},{15,7},{8,16},{16,8... | collective-permute-start | bytes 884744 | tf_op jit(solution)/shard_map/ppermute | solution.py:376
  6.2 10.1 %collective-permute-start.3 = (bf16[4,128,128]{2,1,0:T(8,128)(2,1)S(1)}, bf16[4,128,128]{2,1,0:T(8,128)(2,1)S(1)}, u32[]{:S(2)}, u32[]{:S(2)}) collective-permute-start(bf16[4,128,128]{2,1,0:T(8,128)(2,1)S(1)} %get-tuple-element.26), channel_id=1, source_target_pairs={{0,9},{8,1},{2,11},{10,3},{4,13},{12,5},{6,15},{14,7},{9,16},{17,8... | collective-permute-start | bytes 393224 | tf_op jit(solution)/shard_map/ppermute | solution.py:377
  19.2 5.7 %collective-permute-start.4 = (f16[8,32,128]{2,1,0:T(8,128)(2,1)S(1)}, f16[8,32,128]{2,1,0:T(8,128)(2,1)S(1)}, u32[]{:S(2)}, u32[]{:S(2)}) collective-permute-start(f16[8,32,128]{2,1,0:T(8,128)(2,1)S(1)} %get-tuple-element.44), channel_id=1, source_target_pairs={{0,6},{1,7},{2,4},{3,5},{4,2},{5,3},{6,0},{7,1},{8,14},{9,15},{10,... | collective-permute-start | bytes 196616 | tf_op jit(solution)/shard_map/ppermute | solution.py:392
  22.6 5.6 %collective-permute-start.5 = (f16[8,32,128]{2,1,0:T(8,128)(2,1)S(1)}, f16[8,32,128]{2,1,0:T(8,128)(2,1)S(1)}, u32[]{:S(2)}, u32[]{:S(2)}) collective-permute-start(f16[8,32,128]{2,1,0:T(8,128)(2,1)S(1)} %get-tuple-element.46), channel_id=1, source_target_pairs={{0,4},{1,5},{2,6},{3,7},{4,0},{5,1},{6,2},{7,3},{8,12},{9,13},{10,... | collective-permute-start | bytes 196616 | tf_op jit(solution)/shard_map/ppermute | solution.py:392
  22.6 5.6 %collective-permute-start.6 = (f16[8,32,128]{2,1,0:T(8,128)(2,1)S(1)}, f16[8,32,128]{2,1,0:T(8,128)(2,1)S(1)}, u32[]{:S(2)}, u32[]{:S(2)}) collective-permute-start(f16[8,32,128]{2,1,0:T(8,128)(2,1)S(1)} %get-tuple-element.45), channel_id=1, source_target_pairs={{0,2},{1,3},{2,0},{3,1},{4,6},{5,7},{6,4},{7,5},{8,10},{9,11},{10,... | collective-permute-start | bytes 196616 | tf_op jit(solution)/shard_map/ppermute | solution.py:392
  28.2 3.6 %collective-permute-start.7 = (f16[8,32,128]{2,1,0:T(8,128)(2,1)S(1)}, f16[8,32,128]{2,1,0:T(8,128)(2,1)S(1)}, u32[]{:S(2)}, u32[]{:S(2)}) collective-permute-start(f16[8,32,128]{2,1,0:T(8,128)(2,1)S(1)} %fusion.7), channel_id=1, source_target_pairs={{2,0},{3,1},{0,2},{1,3},{6,4},{7,5},{4,6},{5,7},{10,8},{11,9},{8,1... | collective-permute-start | bytes 196616 | tf_op jit(solution)/shard_map/ppermute | solution.py:399
  29.2 4.5 %collective-permute-start.8 = (f16[8,32,128]{2,1,0:T(8,128)(2,1)S(1)}, f16[8,32,128]{2,1,0:T(8,128)(2,1)S(1)}, u32[]{:S(2)}, u32[]{:S(2)}) collective-permute-start(f16[8,32,128]{2,1,0:T(8,128)(2,1)S(1)} %fusion.7), channel_id=1, source_target_pairs={{4,0},{5,1},{6,2},{7,3},{0,4},{1,5},{2,6},{3,7},{12,8},{13,9},{14,... | collective-permute-start | bytes 196616 | tf_op jit(solution)/shard_map/ppermute | solution.py:399
  30.8 4.9 %collective-permute-start.9 = (f16[8,32,128]{2,1,0:T(8,128)(2,1)S(1)}, f16[8,32,128]{2,1,0:T(8,128)(2,1)S(1)}, u32[]{:S(2)}, u32[]{:S(2)}) collective-permute-start(f16[8,32,128]{2,1,0:T(8,128)(2,1)S(1)} %fusion.7), channel_id=1, source_target_pairs={{6,0},{7,1},{4,2},{5,3},{2,4},{3,5},{0,6},{1,7},{14,8},{15,9},{12,... | collective-permute-start | bytes 196616 | tf_op jit(solution)/shard_map/ppermute | solution.py:399
  35.9 4.7 %collective-permute-start.11 = (f16[4,3,32,128]{3,2,1,0:T(8,128)(2,1)S(1)}, f16[4,3,32,128]{3,2,1,0:T(8,128)(2,1)S(1)}, u32[]{:S(2)}, u32[]{:S(2)}) collective-permute-start(f16[4,3,32,128]{3,2,1,0:T(8,128)(2,1)S(1)} %slice.45), channel_id=1, source_target_pairs={{0,1},{1,0},{2,3},{3,2},{4,5},{5,4},{6,7},{7,6},{8,9},{9,8},{10,11... | collective-permute-start | bytes 294920 | tf_op jit(solution)/shard_map/ppermute | solution.py:418
  38.6 7.4 %collective-permute-start.10 = (bf16[4,3,32,128]{3,2,1,0:T(8,128)(2,1)S(1)}, bf16[4,3,32,128]{3,2,1,0:T(8,128)(2,1)S(1)}, u32[]{:S(2)}, u32[]{:S(2)}) collective-permute-start(bf16[4,3,32,128]{3,2,1,0:T(8,128)(2,1)S(1)} %multiply_convert_fusion), channel_id=1, source_target_pairs={{1,9},{9,1},{3,11},{11,3},{5,13},{13,5},{7,15},{15,7},{8,16},{16,8... | collective-permute-start | bytes 294920 | tf_op jit(solution)/shard_map/ppermute | solution.py:419
  48.8 5.1 %collective-permute-start.12 = (f16[8,32,128]{2,1,0:T(8,128)(2,1)S(1)}, f16[8,32,128]{2,1,0:T(8,128)(2,1)S(1)}, u32[]{:S(2)}, u32[]{:S(2)}) collective-permute-start(f16[8,32,128]{2,1,0:T(8,128)(2,1)S(1)} %get-tuple-element.41), channel_id=1, source_target_pairs={{0,6},{1,7},{2,4},{3,5},{4,2},{5,3},{6,0},{7,1},{8,14},{9,15},{10,... | collective-permute-start | bytes 196616 | tf_op jit(solution)/shard_map/ppermute | solution.py:392
  50.8 7.1 %collective-permute-start.13 = (f16[8,32,128]{2,1,0:T(8,128)(2,1)S(1)}, f16[8,32,128]{2,1,0:T(8,128)(2,1)S(1)}, u32[]{:S(2)}, u32[]{:S(2)}) collective-permute-start(f16[8,32,128]{2,1,0:T(8,128)(2,1)S(1)} %get-tuple-element.43), channel_id=1, source_target_pairs={{0,4},{1,5},{2,6},{3,7},{4,0},{5,1},{6,2},{7,3},{8,12},{9,13},{10,... | collective-permute-start | bytes 196616 | tf_op jit(solution)/shard_map/ppermute | solution.py:392
  51.4 6.4 %collective-permute-start.14 = (f16[8,32,128]{2,1,0:T(8,128)(2,1)S(1)}, f16[8,32,128]{2,1,0:T(8,128)(2,1)S(1)}, u32[]{:S(2)}, u32[]{:S(2)}) collective-permute-start(f16[8,32,128]{2,1,0:T(8,128)(2,1)S(1)} %get-tuple-element.42), channel_id=1, source_target_pairs={{0,2},{1,3},{2,0},{3,1},{4,6},{5,7},{6,4},{7,5},{8,10},{9,11},{10,... | collective-permute-start | bytes 196616 | tf_op jit(solution)/shard_map/ppermute | solution.py:392
  57.9 3.6 %collective-permute-start.15 = (f16[8,32,128]{2,1,0:T(8,128)(2,1)S(1)}, f16[8,32,128]{2,1,0:T(8,128)(2,1)S(1)}, u32[]{:S(2)}, u32[]{:S(2)}) collective-permute-start(f16[8,32,128]{2,1,0:T(8,128)(2,1)S(1)} %fusion.4), channel_id=1, source_target_pairs={{2,0},{3,1},{0,2},{1,3},{6,4},{7,5},{4,6},{5,7},{10,8},{11,9},{8,1... | collective-permute-start | bytes 196616 | tf_op jit(solution)/shard_map/ppermute | solution.py:399
  58.0 4.1 %collective-permute-start.16 = (f16[8,32,128]{2,1,0:T(8,128)(2,1)S(1)}, f16[8,32,128]{2,1,0:T(8,128)(2,1)S(1)}, u32[]{:S(2)}, u32[]{:S(2)}) collective-permute-start(f16[8,32,128]{2,1,0:T(8,128)(2,1)S(1)} %fusion.4), channel_id=1, source_target_pairs={{4,0},{5,1},{6,2},{7,3},{0,4},{1,5},{2,6},{3,7},{12,8},{13,9},{14,... | collective-permute-start | bytes 196616 | tf_op jit(solution)/shard_map/ppermute | solution.py:399
  60.0 5.4 %collective-permute-start.17 = (f16[8,32,128]{2,1,0:T(8,128)(2,1)S(1)}, f16[8,32,128]{2,1,0:T(8,128)(2,1)S(1)}, u32[]{:S(2)}, u32[]{:S(2)}) collective-permute-start(f16[8,32,128]{2,1,0:T(8,128)(2,1)S(1)} %fusion.4), channel_id=1, source_target_pairs={{6,0},{7,1},{4,2},{5,3},{2,4},{3,5},{0,6},{1,7},{14,8},{15,9},{12,... | collective-permute-start | bytes 196616 | tf_op jit(solution)/shard_map/ppermute | solution.py:399
  65.5 3.3 %collective-permute-start.18 = (f16[4,8,32,128]{3,2,1,0:T(8,128)(2,1)S(1)}, f16[4,8,32,128]{3,2,1,0:T(8,128)(2,1)S(1)}, u32[]{:S(2)}, u32[]{:S(2)}) collective-permute-start(f16[4,8,32,128]{3,2,1,0:T(8,128)(2,1)S(1)} %pad_maximum_fusion.1), channel_id=1, source_target_pairs={{0,1},{1,0},{2,3},{3,2},{4,5},{5,4},{6,7},{7,6},{8,9},{9,8},{10,11... | collective-permute-start | bytes 786440 | tf_op jit(solution)/shard_map/ppermute | solution.py:427
  68.0 1.0 %copy-start.3 = (f32[16,128,128]{2,1,0:T(8,128)}, f32[16,128,128]{2,1,0:T(8,128)S(1)}, u32[]{:S(2)}) copy-start(f32[16,128,128]{2,1,0:T(8,128)S(1)} %multiply_dynamic-update-slice_fusion.1) | copy-start | bytes 3145732

commit v8 on v7

--- a/solution.py
+++ b/solution.py
@@ -173,12 +173,10 @@
     lax.fori_loop(0, count, one, 0)
 
 
-def rest_march(place, coef, edge, lower_rows, block, speed_rows, reward_rows, out, keeps, fields):
+def rest_march(place, coef, ctrls, edge, lower_rows, block, speed_rows, reward_rows, out, keeps, fields):
     ny = block.shape[1] - 2 * PAD
-    count = reward_rows.shape[0]
     margin = SUBSTEPS - 1
     inside = place[2].astype(jnp.float32)
-    start_max(out)
 
     def speed(row, spot):
         q = row - SUBSTEPS
@@ -189,13 +187,13 @@
     def reward(ctrl, row, spot):
         q = row - SUBSTEPS
         if q < 0:
-            return lower_rows[ctrl * margin - 1 - q, spot, :].astype(jnp.float32)
+            return lower_rows[(ctrl - ctrls[0]) * margin - 1 - q, spot, :].astype(jnp.float32)
         return reward_rows[ctrl, q, spot, :]
 
     def store(ctrl, row, first, size, new):
         fields[0][ctrl, row, pl.ds(PAD + first, size), :] = new * inside if row < SUBSTEPS else new
 
-    sweep(place, coef, range(count), block, range(1, SUBSTEPS + 1), speed, reward, store)
+    sweep(place, coef, ctrls, block, range(1, SUBSTEPS + 1), speed, reward, store)
 
     def one(ctrl, carry):
         source = fields[0].at[ctrl]
@@ -216,7 +214,7 @@
             source = None if last else fields[substep]
         return carry
 
-    lax.fori_loop(0, count, one, 0)
+    lax.fori_loop(ctrls[0], ctrls[-1] + 1, one, 0)
 
 
 def pack_kernel(value, speed, reward, edge, far, block, speed_rows, value_sem, speed_sem, near_sem, far_sem):
@@ -262,17 +260,26 @@
 
 
 def rest_first(coef, first, speed_rows, reward_rows, edge, *refs, half):
-    edge_other, keeps, out, fields, block, lower_rows = refs[0], refs[1:3], refs[3], refs[4:6], refs[6], refs[7]
+    *others, keep_a, keep_b, out, field_a, field_b, block = refs
     place = where_am_i()
     ny = speed_rows.shape[1]
-    for field in (block, *fields):
+    own = reward_rows.shape[0] // 2
+    for field in (field_a.at[pl.ds(own if others else 0, own)], field_b, block):
         clear_pads(field, ny)
     for row in range(SUBSTEPS):
         block[SUBSTEPS - 1 - row, pl.ds(PAD, ny), :] = edge[row].astype(jnp.float32)
     for row in range(2):
         block[SUBSTEPS + row] = first[row]
-    lay_lower(edge, edge_other, lower_rows)
-    rest_march(place, coef, edge, lower_rows, block, speed_rows, reward_rows, out, keeps, fields)
+    if others:
+        lower_rows, best = others
+        ctrls = range(own, 2 * own)
+        for shard in range(out.shape[0]):
+            out[shard] = best[shard]
+    else:
+        lower_rows, ctrls = edge.at[pl.ds(2 * SUBSTEPS - 1, own * (SUBSTEPS - 1))], range(own)
+        start_max(out)
+    keeps, fields = (keep_a, keep_b), (field_a, field_b)
+    rest_march(place, coef, ctrls, edge, lower_rows, block, speed_rows, reward_rows, out, keeps, fields)
 
 
 def early_later(coef, current, across, speed_rows, reward_rows, out, *refs, half):
@@ -297,7 +304,9 @@
     for row in range(2):
         spread(place, current, row, block, SUBSTEPS + row)
     lay_lower(edge, edge_other, lower_rows)
-    rest_march(place, coef, edge, lower_rows, block, speed_rows, reward_rows, out, keeps, fields)
+    start_max(out)
+    ctrls = range(reward_rows.shape[0])
+    rest_march(place, coef, ctrls, edge, lower_rows, block, speed_rows, reward_rows, out, keeps, fields)
 
 
 def body(value, speed, reward, ctrl_set, drift_sets, diffusion_sets):
@@ -334,7 +343,7 @@
         scratch = [pltpu.VMEM((count, rows, ny + 2 * PAD, nz), jnp.float32)] + [field] * (SUBSTEPS - 2)
         if kernel is not early_first:
             scratch.append(field)
-        if kernel in (rest_first, rest_later):
+        if kernel is rest_later:
             scratch.append(pltpu.VMEM((count * margin, ny, nz), narrow))
         return pl.pallas_call(
             functools.partial(kernel, half=half),
@@ -384,20 +393,30 @@
     def from_wire(values):
         return values.astype(jnp.float32) * (1.0 / WIRE_SCALE)
 
-    def reduce(best):
+    falling = list(range(chips - 1, 0, -1))
+    turned = falling[1:-1] + falling[:1] + falling[-1:]
+    odd_core = lax.axis_index("ctrl") % 2
+
+    def reduce(best, orders):
         parts = (best * WIRE_SCALE).astype(wire)
         mine = parts[0]
-        for step in range(chips - 1, 0, -1):
-            pairs = [(2 * z + c, 2 * mate(z, step, chips) + c) for z in range(chips) for c in range(2)]
-            mine = jnp.maximum(mine, lax.ppermute(parts[step], "ctrl", pairs))
+        for steps_of in zip(*orders):
+            pairs = [(2 * z + c, 2 * mate(z, steps_of[c], chips) + c) for z in range(chips) for c in range(2)]
+            same = steps_of[0] == steps_of[1]
+            part = parts[steps_of[0]] if same else jnp.where(odd_core == 0, parts[steps_of[0]], parts[steps_of[1]])
+            mine = jnp.maximum(mine, lax.ppermute(part, "ctrl", pairs))
         return mine
 
-    def gather(mine):
-        pieces = []
-        for step in range(chips - 1, 0, -1):
-            pairs = [(2 * mate(z, step, chips) + c, 2 * z + c) for z in range(chips) for c in range(2)]
-            pieces.append(lax.ppermute(mine, "ctrl", pairs))
-        return jnp.stack([mine, *pieces[::-1]])
+    def gather(mine, orders):
+        got = []
+        for steps_of in zip(*orders):
+            pairs = [(2 * mate(z, steps_of[c], chips) + c, 2 * z + c) for z in range(chips) for c in range(2)]
+            got.append(lax.ppermute(mine, "ctrl", pairs))
+        pieces = [mine]
+        for step in range(1, chips):
+            even, odd = got[orders[0].index(step)], got[orders[1].index(step)]
+            pieces.append(even if even is odd else jnp.where(odd_core == 0, even, odd))
+        return jnp.stack(pieces)
 
     steps = sum(half + SUBSTEPS - 2 - 2 * k for k in range(SUBSTEPS))
     early_out = [shape(chips, half - SUBSTEPS, width, nz)] + keeps
@@ -412,8 +431,10 @@
         early_out + [shape(given, ny, nz), shape(count, given, ny, nz)],
     )
     laid, edges = (speed_rows, reward_rows), (edge, edge_other)
-    best_rest = call(rest_first, rest_rows, rest_steps, (block, *laid, *edges, keep_a, keep_b), rest_out)
-    pieces = gather(reduce(jnp.concatenate([best_rest, best], axis=1)))
+    best_rest = call(rest_first, rest_rows, rest_steps // 2, (block, *laid, edge, keep_a, keep_b), rest_out)
+    more = (block, *laid, *edges, best_rest, keep_a, keep_b)
+    best_rest = call(rest_first, rest_rows, rest_steps // 2, more, rest_out)
+    pieces = gather(reduce(jnp.concatenate([best_rest, best], axis=1), (falling, turned)), (falling, turned))
 
     across = lax.ppermute(pieces[:, -SUBSTEPS:], "ctrl", partners)
     beyond = lax.ppermute(from_wire(pieces[:, :SUBSTEPS]).astype(narrow), both, facing)
@@ -422,7 +443,7 @@
     best_rest = call(
         rest_later, rest_rows, rest_steps, (current, beyond, *laid, *edges, *kept), rest_out
     )
-    pieces = gather(reduce(jnp.concatenate([best_rest, best], axis=1)))
+    pieces = gather(reduce(jnp.concatenate([best_rest, best], axis=1), (falling, turned)), (falling, turned))
 
     from_partner = lax.ppermute(pieces, "ctrl", partners)
 

time: 70.1 us -> 69.7 us (level)
  starting transfers between devices: 29 us -> 28.1 us
    ppermute x1, starting transfers between devices: 2.64 us -> 1.17 us  [body(): across = lax.ppermute(pieces[:, -SUBSTEPS:], 'ctrl', partners)]
    ppermute x1, starting transfers between devices: 2.14 us -> 3.28 us  [body(): from_partner = lax.ppermute(pieces, 'ctrl', partners)]
    ppermute x12, waiting for transfers between devices: 18.5 us -> 17.8 us  [the longest x6 9.02 us: reduce(): mine = jnp.maximum(mine, lax.ppermute(part, 'ctrl', pairs))]
    pallas_call x4 -> x5, Pallas kernels: 16.8 us -> 17.4 us  [call(): pl.pallas_call(functools.partial(kernel, half=half), out_shape=outs, in_s...]
  transfers between devices with their start and end apart: 19 -> 19, of which waited for: 9 -> 10; matrix products, arithmetic and copies ran while one was open for 1% -> 1% of each run, Pallas kernels for 18% -> 21%
where the time goes in v8:
time: 69.7 us; the launch traced here: 69 us
  starting transfers between devices  28.1 us (40%)
  Pallas kernels  18.9 us (27%)
  waiting for transfers between devices  18.6 us (27%)
  other arithmetic  2.07 us (3%)
  local copies, waits for them, and re-layouts  1.06 us (2%)
    pallas_call x5, Pallas kernels, call(): pl.pallas_call(functools.partial(kernel, half=half), out_shape=outs, in_s...  17.4 us
    ppermute x6, waiting for transfers between devices, reduce(): mine = jnp.maximum(mine, lax.ppermute(part, 'ctrl', pairs))  9.02 us
    ppermute x6, waiting for transfers between devices, gather(): got.append(lax.ppermute(mine, 'ctrl', pairs))  8.75 us
    ppermute x6, starting transfers between devices, gather(): got.append(lax.ppermute(mine, 'ctrl', pairs))  7.63 us
    ppermute x6, starting transfers between devices, reduce(): mine = jnp.maximum(mine, lax.ppermute(part, 'ctrl', pairs))  6.43 us
    ppermute x1, starting transfers between devices, body(): edge_other = lax.ppermute(far, both, beside)  3.73 us
    ppermute x1, starting transfers between devices, body(): from_partner = lax.ppermute(pieces, 'ctrl', partners)  3.28 us
    ppermute x1, starting transfers between devices, body(): edge = lax.ppermute(packed, both, facing)  3.12 us
  transfers between devices with their start and end apart: 19, of which 10 were waited for; matrix products, arithmetic and copies ran while one was open for 1% of the time, Pallas kernels for 21%

profile of v8, /device:TPU:5, one launch (start us, length us, event | category | flops | bytes accessed | tf_op | source)
XLA Modules:
  0.0 69.0 jit_solution(3254498744665678714)
XLA Ops:
  0.0 0.7 %collective-permute-start.1 = (bf16[2,16,128,128]{3,2,1,0:T(8,128)(2,1)}, bf16[2,16,128,128]{3,2,1,0:T(8,128)(2,1)}, u32[]{:S(2)}, u32[]{:S(2)}) collective-permute-start(bf16[2,16,128,128]{3,2,1,0:T(8,128)(2,1)} %reward.3), channel_id=1, source_target_pairs={{0,1},{1,0},{2,3},{3,2},{4,5},{5,4},{6,7},{7,6},{8,9},{9,8},{10,11... | collective-permute-start | bytes 3145736 | tf_op jit(solution)/shard_map/ppermute | solution.py:364
  0.8 0.1 collective-permute-start
  0.9 1.5 %shard_map.64 = (bf16[9,128,128]{2,1,0:T(8,128)(2,1)S(1)}, bf16[4,128,128]{2,1,0:T(8,128)(2,1)S(1)}, f32[11,144,128]{2,1,0:T(8,128)S(1)}) custom-call(f32[16,128,128]{2,1,0:T(8,128)} %value.1, f32[16,128,128]{2,1,0:T(8,128)} %speed.3, bf16[2,16,128,128]{3,2,1,0:T(8,128)(2,1)} %reward.3), custom_call_target="tpu_custom_call" | custom-call | tf_op jit(solution)/shard_map/pallas_call | solution.py:367
  2.3 0.7 %copy-done.2 = bf16[9,128,128]{2,1,0:T(8,128)(2,1)} copy-done((bf16[9,128,128]{2,1,0:T(8,128)(2,1)}, bf16[9,128,128]{2,1,0:T(8,128)(2,1)S(1)}, u32[]{:S(2)}) %copy-start.2) | copy-done | bytes 294936
  3.1 3.1 %collective-permute-start.2 = (bf16[9,128,128]{2,1,0:T(8,128)(2,1)}, bf16[9,128,128]{2,1,0:T(8,128)(2,1)S(1)}, u32[]{:S(2)}, u32[]{:S(2)}) collective-permute-start(bf16[9,128,128]{2,1,0:T(8,128)(2,1)} %copy-done.2), channel_id=1, source_target_pairs={{1,9},{9,1},{3,11},{11,3},{5,13},{13,5},{7,15},{15,7},{8,16},{16,8... | collective-permute-start | bytes 884744 | tf_op jit(solution)/shard_map/ppermute | solution.py:385
  6.2 3.7 %collective-permute-start.3 = (bf16[4,128,128]{2,1,0:T(8,128)(2,1)S(1)}, bf16[4,128,128]{2,1,0:T(8,128)(2,1)S(1)}, u32[]{:S(2)}, u32[]{:S(2)}) collective-permute-start(bf16[4,128,128]{2,1,0:T(8,128)(2,1)S(1)} %get-tuple-element.26), channel_id=1, source_target_pairs={{0,9},{8,1},{2,11},{10,3},{4,13},{12,5},{6,15},{14,7},{9,16},{17,8... | collective-permute-start | bytes 393224 | tf_op jit(solution)/shard_map/ppermute | solution.py:386
  9.9 0.1 pad_add_fusion
  10.0 0.1 iota_compare_fusion
  10.1 0.1 select_reduce_fusion
  10.2 0.1 copy.12.coef
  10.3 6.1 %shard_map.65 = (f32[4,5,32,128]{3,2,1,0:T(8,128)S(1)}, f32[4,2,128,128]{3,2,1,0:T(8,128)S(1)}, f32[4,2,128,128]{3,2,1,0:T(8,128)S(1)}, f32[10,128,128]{2,1,0:T(8,128)S(1)}, f32[4,10,128,128]{3,2,1,0:T(8,128)S(1)}) custom-call(f32[4,6]{1,0:T(4,128)S(1)} %copy.12.coef, f32[11,144,128]{2,1,0:T(8,128)S(1)} %get-tuple-element.22.block.first, ...), custom_call_target="tpu_custom_call" | custom-call | flops 34406400 | bytes 16515072 | tf_op jit(solution)/shard_map/pallas_call | solution.py:348
  16.3 1.7 %shard_map.66.refs_1_ = f32[4,3,32,128]{3,2,1,0:T(8,128)S(1)} custom-call(f32[4,6]{1,0:T(4,128)S(1)} %copy.12.coef, f32[11,144,128]{2,1,0:T(8,128)S(1)} %get-tuple-element.22.block.first, f32[10,128,128]{2,1,0:T(8,128)S(1)} %get-tuple-element.23.speed_rows, f32[4,10,128,128]{3,2,1,0:T(8,128)S(1)} %get-tuple-element.24.reward_rows, ...), custom_call_target="tpu_custom_call" | custom-call | flops 6553600 | bytes 3145728 | tf_op jit(solution)/shard_map/pallas_call | solution.py:348
  18.0 1.7 %shard_map.67 = f32[4,3,32,128]{3,2,1,0:T(8,128)S(1)} custom-call(f32[4,6]{1,0:T(4,128)S(1)} %copy.12.coef, f32[11,144,128]{2,1,0:T(8,128)S(1)} %get-tuple-element.22.block.first, f32[10,128,128]{2,1,0:T(8,128)S(1)} %get-tuple-element.23.speed_rows, f32[4,10,128,128]{3,2,1,0:T(8,128)S(1)} %get-tuple-element.24.reward_rows, ...), custom_call_target="tpu_custom_call" | custom-call | flops 6553600 | bytes 3145728 | tf_op jit(solution)/shard_map/pallas_call | solution.py:348
  19.7 0.1 fusion
  19.9 2.4 %collective-permute-start.4 = (f16[8,32,128]{2,1,0:T(8,128)(2,1)S(1)}, f16[8,32,128]{2,1,0:T(8,128)(2,1)S(1)}, u32[]{:S(2)}, u32[]{:S(2)}) collective-permute-start(f16[8,32,128]{2,1,0:T(8,128)(2,1)S(1)} %get-tuple-element.44), channel_id=1, source_target_pairs={{0,6},{1,5},{2,4},{3,7},{4,2},{5,1},{6,0},{7,3},{8,14},{9,13},{10,... | collective-permute-start | bytes 196616 | tf_op jit(solution)/shard_map/ppermute | solution.py:407
  22.2 1.1 %collective-permute-start.5 = (f16[8,32,128]{2,1,0:T(8,128)(2,1)S(1)}, f16[8,32,128]{2,1,0:T(8,128)(2,1)S(1)}, u32[]{:S(2)}, u32[]{:S(2)}) collective-permute-start(f16[8,32,128]{2,1,0:T(8,128)(2,1)S(1)} %get-tuple-element.46), channel_id=1, source_target_pairs={{0,4},{1,7},{2,6},{3,5},{4,0},{5,3},{6,2},{7,1},{8,12},{9,15},{10,... | collective-permute-start | bytes 196616 | tf_op jit(solution)/shard_map/ppermute | solution.py:407
  23.3 0.2 collective-permute-start.6
  23.5 3.8 %collective-permute-done.4 = f16[8,32,128]{2,1,0:T(8,128)(2,1)S(1)} collective-permute-done((f16[8,32,128]{2,1,0:T(8,128)(2,1)S(1)}, f16[8,32,128]{2,1,0:T(8,128)(2,1)S(1)}, u32[]{:S(2)}, u32[]{:S(2)}) %collective-permute-start.4) | collective-permute-done | bytes 65568 | tf_op jit(solution)/shard_map/ppermute | solution.py:407
  27.4 0.8 %collective-permute-done.6 = f16[8,32,128]{2,1,0:T(8,128)(2,1)S(1)} collective-permute-done((f16[8,32,128]{2,1,0:T(8,128)(2,1)S(1)}, f16[8,32,128]{2,1,0:T(8,128)(2,1)S(1)}, u32[]{:S(2)}, u32[]{:S(2)}) %collective-permute-start.6) | collective-permute-done | bytes 65568 | tf_op jit(solution)/shard_map/ppermute | solution.py:407
  28.2 3.6 %collective-permute-start.8 = (f16[8,32,128]{2,1,0:T(8,128)(2,1)S(1)}, f16[8,32,128]{2,1,0:T(8,128)(2,1)S(1)}, u32[]{:S(2)}, u32[]{:S(2)}) collective-permute-start(f16[8,32,128]{2,1,0:T(8,128)(2,1)S(1)} %fusion.7), channel_id=1, source_target_pairs={{4,0},{7,1},{6,2},{5,3},{0,4},{3,5},{2,6},{1,7},{12,8},{15,9},{14,... | collective-permute-start | bytes 196616 | tf_op jit(solution)/shard_map/ppermute | solution.py:414
  31.8 0.4 collective-permute-start.7
  32.1 1.3 %collective-permute-done.8 = f16[8,32,128]{2,1,0:T(8,128)(2,1)S(1)} collective-permute-done((f16[8,32,128]{2,1,0:T(8,128)(2,1)S(1)}, f16[8,32,128]{2,1,0:T(8,128)(2,1)S(1)}, u32[]{:S(2)}, u32[]{:S(2)}) %collective-permute-start.8) | collective-permute-done | bytes 65568 | tf_op jit(solution)/shard_map/ppermute | solution.py:414
  33.4 3.8 %collective-permute-done.9 = f16[8,32,128]{2,1,0:T(8,128)(2,1)S(1)} collective-permute-done((f16[8,32,128]{2,1,0:T(8,128)(2,1)S(1)}, f16[8,32,128]{2,1,0:T(8,128)(2,1)S(1)}, u32[]{:S(2)}, u32[]{:S(2)}) %collective-permute-start.9) | collective-permute-done | bytes 65568 | tf_op jit(solution)/shard_map/ppermute | solution.py:414
  37.2 0.1 pad_maximum_fusion
  37.4 1.2 %collective-permute-start.11 = (f16[4,3,32,128]{3,2,1,0:T(8,128)(2,1)S(1)}, f16[4,3,32,128]{3,2,1,0:T(8,128)(2,1)S(1)}, u32[]{:S(2)}, u32[]{:S(2)}) collective-permute-start(f16[4,3,32,128]{3,2,1,0:T(8,128)(2,1)S(1)} %slice.49), channel_id=1, source_target_pairs={{0,1},{1,0},{2,3},{3,2},{4,5},{5,4},{6,7},{7,6},{8,9},{9,8},{10,11... | collective-permute-start | bytes 294920 | tf_op jit(solution)/shard_map/ppermute | solution.py:439
  38.6 1.9 %collective-permute-start.10 = (bf16[4,3,32,128]{3,2,1,0:T(8,128)(2,1)S(1)}, bf16[4,3,32,128]{3,2,1,0:T(8,128)(2,1)S(1)}, u32[]{:S(2)}, u32[]{:S(2)}) collective-permute-start(bf16[4,3,32,128]{3,2,1,0:T(8,128)(2,1)S(1)} %multiply_convert_fusion), channel_id=1, source_target_pairs={{1,9},{9,1},{3,11},{11,3},{5,13},{13,5},{7,15},{15,7},{8,16},{16,8... | collective-permute-start | bytes 294920 | tf_op jit(solution)/shard_map/ppermute | solution.py:440
  40.5 0.1 convert_multiply_fusion.current
  40.6 5.3 %shard_map.68 = (f32[4,5,32,128]{3,2,1,0:T(8,128)S(1)}, f32[4,2,128,128]{3,2,1,0:T(8,128)S(1)}, f32[4,2,128,128]{3,2,1,0:T(8,128)S(1)}) custom-call(f32[4,6]{1,0:T(4,128)S(1)} %copy.12.coef, f32[4,8,32,128]{3,2,1,0:T(8,128)S(1)} %convert_multiply_fusion.current, f32[4,3,32,128]{3,2,1,0:T(8,128)S(1)} %convert_multiply_fusion.1.across, ...), custom_call_target="tpu_custom_call" | custom-call | flops 34406400 | bytes 16515072 | tf_op jit(solution)/shard_map/pallas_call | solution.py:348
  45.9 2.7 %shard_map.69 = f32[4,3,32,128]{3,2,1,0:T(8,128)S(1)} custom-call(f32[4,6]{1,0:T(4,128)S(1)} %copy.12.coef, f32[4,8,32,128]{3,2,1,0:T(8,128)S(1)} %convert_multiply_fusion.current, bf16[4,3,32,128]{3,2,1,0:T(8,128)(2,1)S(1)} %collective-permute-done.10.beyond, f32[10,128,128]{2,1,0:T(8,128)S(1)} %get-tuple-element.23.speed_rows, ...), custom_call_target="tpu_custom_call" | custom-call | flops 14745600 | bytes 7077888 | tf_op jit(solution)/shard_map/pallas_call | solution.py:348
  48.6 0.1 fusion.1
  48.8 1.6 %collective-permute-start.12 = (f16[8,32,128]{2,1,0:T(8,128)(2,1)S(1)}, f16[8,32,128]{2,1,0:T(8,128)(2,1)S(1)}, u32[]{:S(2)}, u32[]{:S(2)}) collective-permute-start(f16[8,32,128]{2,1,0:T(8,128)(2,1)S(1)} %get-tuple-element.41), channel_id=1, source_target_pairs={{0,6},{1,5},{2,4},{3,7},{4,2},{5,1},{6,0},{7,3},{8,14},{9,13},{10,... | collective-permute-start | bytes 196616 | tf_op jit(solution)/shard_map/ppermute | solution.py:407
  50.4 0.9 %collective-permute-start.13 = (f16[8,32,128]{2,1,0:T(8,128)(2,1)S(1)}, f16[8,32,128]{2,1,0:T(8,128)(2,1)S(1)}, u32[]{:S(2)}, u32[]{:S(2)}) collective-permute-start(f16[8,32,128]{2,1,0:T(8,128)(2,1)S(1)} %get-tuple-element.43), channel_id=1, source_target_pairs={{0,4},{1,7},{2,6},{3,5},{4,0},{5,3},{6,2},{7,1},{8,12},{9,15},{10,... | collective-permute-start | bytes 196616 | tf_op jit(solution)/shard_map/ppermute | solution.py:407
  51.3 0.2 collective-permute-start.14
  51.5 2.2 %collective-permute-done.12 = f16[8,32,128]{2,1,0:T(8,128)(2,1)S(1)} collective-permute-done((f16[8,32,128]{2,1,0:T(8,128)(2,1)S(1)}, f16[8,32,128]{2,1,0:T(8,128)(2,1)S(1)}, u32[]{:S(2)}, u32[]{:S(2)}) %collective-permute-start.12) | collective-permute-done | bytes 65568 | tf_op jit(solution)/shard_map/ppermute | solution.py:407
  53.7 2.2 %collective-permute-done.13 = f16[8,32,128]{2,1,0:T(8,128)(2,1)S(1)} collective-permute-done((f16[8,32,128]{2,1,0:T(8,128)(2,1)S(1)}, f16[8,32,128]{2,1,0:T(8,128)(2,1)S(1)}, u32[]{:S(2)}, u32[]{:S(2)}) %collective-permute-start.13) | collective-permute-done | bytes 65568 | tf_op jit(solution)/shard_map/ppermute | solution.py:407
  56.0 1.8 %collective-permute-start.16 = (f16[8,32,128]{2,1,0:T(8,128)(2,1)S(1)}, f16[8,32,128]{2,1,0:T(8,128)(2,1)S(1)}, u32[]{:S(2)}, u32[]{:S(2)}) collective-permute-start(f16[8,32,128]{2,1,0:T(8,128)(2,1)S(1)} %fusion.4), channel_id=1, source_target_pairs={{4,0},{7,1},{6,2},{5,3},{0,4},{3,5},{2,6},{1,7},{12,8},{15,9},{14,... | collective-permute-start | bytes 196616 | tf_op jit(solution)/shard_map/ppermute | solution.py:414
  57.8 1.7 %collective-permute-start.17 = (f16[8,32,128]{2,1,0:T(8,128)(2,1)S(1)}, f16[8,32,128]{2,1,0:T(8,128)(2,1)S(1)}, u32[]{:S(2)}, u32[]{:S(2)}) collective-permute-start(f16[8,32,128]{2,1,0:T(8,128)(2,1)S(1)} %fusion.4), channel_id=1, source_target_pairs={{6,0},{5,1},{4,2},{7,3},{2,4},{1,5},{0,6},{3,7},{14,8},{13,9},{12,... | collective-permute-start | bytes 196616 | tf_op jit(solution)/shard_map/ppermute | solution.py:414
  59.5 0.2 collective-permute-start.15
  59.7 1.4 %collective-permute-done.16 = f16[8,32,128]{2,1,0:T(8,128)(2,1)S(1)} collective-permute-done((f16[8,32,128]{2,1,0:T(8,128)(2,1)S(1)}, f16[8,32,128]{2,1,0:T(8,128)(2,1)S(1)}, u32[]{:S(2)}, u32[]{:S(2)}) %collective-permute-start.16) | collective-permute-done | bytes 65568 | tf_op jit(solution)/shard_map/ppermute | solution.py:414
  61.1 1.4 %collective-permute-done.17 = f16[8,32,128]{2,1,0:T(8,128)(2,1)S(1)} collective-permute-done((f16[8,32,128]{2,1,0:T(8,128)(2,1)S(1)}, f16[8,32,128]{2,1,0:T(8,128)(2,1)S(1)}, u32[]{:S(2)}, u32[]{:S(2)}) %collective-permute-start.17) | collective-permute-done | bytes 65568 | tf_op jit(solution)/shard_map/ppermute | solution.py:414
  62.5 0.9 %collective-permute-done.15 = f16[8,32,128]{2,1,0:T(8,128)(2,1)S(1)} collective-permute-done((f16[8,32,128]{2,1,0:T(8,128)(2,1)S(1)}, f16[8,32,128]{2,1,0:T(8,128)(2,1)S(1)}, u32[]{:S(2)}, u32[]{:S(2)}) %collective-permute-start.15) | collective-permute-done | bytes 65568 | tf_op jit(solution)/shard_map/ppermute | solution.py:414
  63.4 0.1 pad_maximum_fusion.1
  63.5 3.3 %collective-permute-start.18 = (f16[4,8,32,128]{3,2,1,0:T(8,128)(2,1)S(1)}, f16[4,8,32,128]{3,2,1,0:T(8,128)(2,1)S(1)}, u32[]{:S(2)}, u32[]{:S(2)}) collective-permute-start(f16[4,8,32,128]{3,2,1,0:T(8,128)(2,1)S(1)} %pad_maximum_fusion.1), channel_id=1, source_target_pairs={{0,1},{1,0},{2,3},{3,2},{4,5},{5,4},{6,7},{7,6},{8,9},{9,8},{10,11... | collective-permute-start | bytes 786440 | tf_op jit(solution)/shard_map/ppermute | solution.py:448
  66.9 0.1 pad_maximum_fusion.2
  67.0 0.1 broadcast_in_dim.27
  67.2 0.8 %collective-permute-done.18 = f16[4,8,32,128]{3,2,1,0:T(8,128)(2,1)S(1)} collective-permute-done((f16[4,8,32,128]{3,2,1,0:T(8,128)(2,1)S(1)}, f16[4,8,32,128]{3,2,1,0:T(8,128)(2,1)S(1)}, u32[]{:S(2)}, u32[]{:S(2)}) %collective-permute-start.18) | collective-permute-done | bytes 262176 | tf_op jit(solution)/shard_map/ppermute | solution.py:448
  68.0 0.1 pad_maximum_fusion.3
  68.2 0.9 %multiply_dynamic-update-slice_fusion = f32[16,128,128]{2,1,0:T(8,128)} fusion(f32[16,128,128]{2,1,0:T(8,128)} %copy-done.3, s32[]{:T(128)S(6)} %select_n.133, f16[8,128,128]{2,1,0:T(8,128)(2,1)S(1)} %pad_maximum_fusion.3, pred[]{:T(512)S(6)} %eq.41), kind=kLoop, calls=%fused_computation.4 | loop fusion | flops 393216 | bytes 786437 | tf_op jit(solution)/shard_map/dynamic_update_slice | solution.py:459
  (36 shorter events, 0.6 us)
Async XLA Ops:
  0.0 10.3 %copy-start.1 = (bf16[2,16,128,128]{3,2,1,0:T(8,128)(2,1)S(1)}, bf16[2,16,128,128]{3,2,1,0:T(8,128)(2,1)}, u32[]{:S(2)}) copy-start(bf16[2,16,128,128]{3,2,1,0:T(8,128)(2,1)} %reward.3) | copy-start | bytes 3145732
  0.0 9.9 %copy-start.6 = (s32[2]{0:T(128)S(1)}, s32[2]{0:T(128)}, u32[]{:S(2)}) copy-start(s32[2]{0:T(128)} %param.9) | copy-start | bytes 28
  0.0 10.3 %copy-start = (f32[16,128,128]{2,1,0:T(8,128)S(1)}, f32[16,128,128]{2,1,0:T(8,128)}, u32[]{:S(2)}) copy-start(f32[16,128,128]{2,1,0:T(8,128)} %speed.3) | copy-start | bytes 3145732
  0.0 3.0 %copy-start.4 = (f32[16,3]{0,1:T(4,128)S(1)}, f32[16,3]{0,1:T(4,128)}, u32[]{:S(2)}) copy-start(f32[16,3]{0,1:T(4,128)} %param.10) | copy-start | bytes 580
  0.0 3.0 %copy-start.5 = (f32[16,3]{0,1:T(4,128)S(1)}, f32[16,3]{0,1:T(4,128)}, u32[]{:S(2)}) copy-start(f32[16,3]{0,1:T(4,128)} %param.11) | copy-start | bytes 580
  0.0 10.2 %collective-permute-start.1 = (bf16[2,16,128,128]{3,2,1,0:T(8,128)(2,1)}, bf16[2,16,128,128]{3,2,1,0:T(8,128)(2,1)}, u32[]{:S(2)}, u32[]{:S(2)}) collective-permute-start(bf16[2,16,128,128]{3,2,1,0:T(8,128)(2,1)} %reward.3), channel_id=1, source_target_pairs={{0,1},{1,0},{2,3},{3,2},{4,5},{5,4},{6,7},{7,6},{8,9},{9,8},{10,11... | collective-permute-start | bytes 3145736 | tf_op jit(solution)/shard_map/ppermute | solution.py:364
  0.8 2.3 %collective-permute-start = (s32[2]{0:T(128)}, s32[2]{0:T(128)S(1)}, u32[]{:S(2)}, u32[]{:S(2)}) collective-permute-start(s32[2]{0:T(128)} %param.9), channel_id=1, source_target_pairs={{0,1},{1,0},{2,3},{3,2},{4,5},{5,4},{6,7},{7,6},{8,9},{9,8},{10,11... | collective-permute-start | bytes 32 | tf_op jit(solution)/shard_map/ppermute | solution.py:363
  2.3 0.7 %copy-start.2 = (bf16[9,128,128]{2,1,0:T(8,128)(2,1)}, bf16[9,128,128]{2,1,0:T(8,128)(2,1)S(1)}, u32[]{:S(2)}) copy-start(bf16[9,128,128]{2,1,0:T(8,128)(2,1)S(1)} %get-tuple-element.25) | copy-start | bytes 884740
  3.1 13.3 %collective-permute-start.2 = (bf16[9,128,128]{2,1,0:T(8,128)(2,1)}, bf16[9,128,128]{2,1,0:T(8,128)(2,1)S(1)}, u32[]{:S(2)}, u32[]{:S(2)}) collective-permute-start(bf16[9,128,128]{2,1,0:T(8,128)(2,1)} %copy-done.2), channel_id=1, source_target_pairs={{1,9},{9,1},{3,11},{11,3},{5,13},{13,5},{7,15},{15,7},{8,16},{16,8... | collective-permute-start | bytes 884744 | tf_op jit(solution)/shard_map/ppermute | solution.py:385
  6.2 11.8 %collective-permute-start.3 = (bf16[4,128,128]{2,1,0:T(8,128)(2,1)S(1)}, bf16[4,128,128]{2,1,0:T(8,128)(2,1)S(1)}, u32[]{:S(2)}, u32[]{:S(2)}) collective-permute-start(bf16[4,128,128]{2,1,0:T(8,128)(2,1)S(1)} %get-tuple-element.26), channel_id=1, source_target_pairs={{0,9},{8,1},{2,11},{10,3},{4,13},{12,5},{6,15},{14,7},{9,16},{17,8... | collective-permute-start | bytes 393224 | tf_op jit(solution)/shard_map/ppermute | solution.py:386
  19.9 7.5 %collective-permute-start.4 = (f16[8,32,128]{2,1,0:T(8,128)(2,1)S(1)}, f16[8,32,128]{2,1,0:T(8,128)(2,1)S(1)}, u32[]{:S(2)}, u32[]{:S(2)}) collective-permute-start(f16[8,32,128]{2,1,0:T(8,128)(2,1)S(1)} %get-tuple-element.44), channel_id=1, source_target_pairs={{0,6},{1,5},{2,4},{3,7},{4,2},{5,1},{6,0},{7,3},{8,14},{9,13},{10,... | collective-permute-start | bytes 196616 | tf_op jit(solution)/shard_map/ppermute | solution.py:407
  22.2 5.1 %collective-permute-start.5 = (f16[8,32,128]{2,1,0:T(8,128)(2,1)S(1)}, f16[8,32,128]{2,1,0:T(8,128)(2,1)S(1)}, u32[]{:S(2)}, u32[]{:S(2)}) collective-permute-start(f16[8,32,128]{2,1,0:T(8,128)(2,1)S(1)} %get-tuple-element.46), channel_id=1, source_target_pairs={{0,4},{1,7},{2,6},{3,5},{4,0},{5,3},{6,2},{7,1},{8,12},{9,15},{10,... | collective-permute-start | bytes 196616 | tf_op jit(solution)/shard_map/ppermute | solution.py:407
  23.3 4.8 %collective-permute-start.6 = (f16[8,32,128]{2,1,0:T(8,128)(2,1)S(1)}, f16[8,32,128]{2,1,0:T(8,128)(2,1)S(1)}, u32[]{:S(2)}, u32[]{:S(2)}) collective-permute-start(f16[8,32,128]{2,1,0:T(8,128)(2,1)S(1)} %get-tuple-element.45), channel_id=1, source_target_pairs={{0,2},{1,3},{2,0},{3,1},{4,6},{5,7},{6,4},{7,5},{8,10},{9,11},{10,... | collective-permute-start | bytes 196616 | tf_op jit(solution)/shard_map/ppermute | solution.py:407
  28.2 5.2 %collective-permute-start.8 = (f16[8,32,128]{2,1,0:T(8,128)(2,1)S(1)}, f16[8,32,128]{2,1,0:T(8,128)(2,1)S(1)}, u32[]{:S(2)}, u32[]{:S(2)}) collective-permute-start(f16[8,32,128]{2,1,0:T(8,128)(2,1)S(1)} %fusion.7), channel_id=1, source_target_pairs={{4,0},{7,1},{6,2},{5,3},{0,4},{3,5},{2,6},{1,7},{12,8},{15,9},{14,... | collective-permute-start | bytes 196616 | tf_op jit(solution)/shard_map/ppermute | solution.py:414
  31.8 5.4 %collective-permute-start.9 = (f16[8,32,128]{2,1,0:T(8,128)(2,1)S(1)}, f16[8,32,128]{2,1,0:T(8,128)(2,1)S(1)}, u32[]{:S(2)}, u32[]{:S(2)}) collective-permute-start(f16[8,32,128]{2,1,0:T(8,128)(2,1)S(1)} %fusion.7), channel_id=1, source_target_pairs={{6,0},{5,1},{4,2},{7,3},{2,4},{1,5},{0,6},{3,7},{14,8},{13,9},{12,... | collective-permute-start | bytes 196616 | tf_op jit(solution)/shard_map/ppermute | solution.py:414
  31.8 5.5 %collective-permute-start.7 = (f16[8,32,128]{2,1,0:T(8,128)(2,1)S(1)}, f16[8,32,128]{2,1,0:T(8,128)(2,1)S(1)}, u32[]{:S(2)}, u32[]{:S(2)}) collective-permute-start(f16[8,32,128]{2,1,0:T(8,128)(2,1)S(1)} %fusion.7), channel_id=1, source_target_pairs={{2,0},{3,1},{0,2},{1,3},{6,4},{7,5},{4,6},{5,7},{10,8},{11,9},{8,1... | collective-permute-start | bytes 196616 | tf_op jit(solution)/shard_map/ppermute | solution.py:414
  37.4 3.2 %collective-permute-start.11 = (f16[4,3,32,128]{3,2,1,0:T(8,128)(2,1)S(1)}, f16[4,3,32,128]{3,2,1,0:T(8,128)(2,1)S(1)}, u32[]{:S(2)}, u32[]{:S(2)}) collective-permute-start(f16[4,3,32,128]{3,2,1,0:T(8,128)(2,1)S(1)} %slice.49), channel_id=1, source_target_pairs={{0,1},{1,0},{2,3},{3,2},{4,5},{5,4},{6,7},{7,6},{8,9},{9,8},{10,11... | collective-permute-start | bytes 294920 | tf_op jit(solution)/shard_map/ppermute | solution.py:439
  38.6 7.3 %collective-permute-start.10 = (bf16[4,3,32,128]{3,2,1,0:T(8,128)(2,1)S(1)}, bf16[4,3,32,128]{3,2,1,0:T(8,128)(2,1)S(1)}, u32[]{:S(2)}, u32[]{:S(2)}) collective-permute-start(bf16[4,3,32,128]{3,2,1,0:T(8,128)(2,1)S(1)} %multiply_convert_fusion), channel_id=1, source_target_pairs={{1,9},{9,1},{3,11},{11,3},{5,13},{13,5},{7,15},{15,7},{8,16},{16,8... | collective-permute-start | bytes 294920 | tf_op jit(solution)/shard_map/ppermute | solution.py:440
  48.8 5.0 %collective-permute-start.12 = (f16[8,32,128]{2,1,0:T(8,128)(2,1)S(1)}, f16[8,32,128]{2,1,0:T(8,128)(2,1)S(1)}, u32[]{:S(2)}, u32[]{:S(2)}) collective-permute-start(f16[8,32,128]{2,1,0:T(8,128)(2,1)S(1)} %get-tuple-element.41), channel_id=1, source_target_pairs={{0,6},{1,5},{2,4},{3,7},{4,2},{5,1},{6,0},{7,3},{8,14},{9,13},{10,... | collective-permute-start | bytes 196616 | tf_op jit(solution)/shard_map/ppermute | solution.py:407
  50.4 5.6 %collective-permute-start.13 = (f16[8,32,128]{2,1,0:T(8,128)(2,1)S(1)}, f16[8,32,128]{2,1,0:T(8,128)(2,1)S(1)}, u32[]{:S(2)}, u32[]{:S(2)}) collective-permute-start(f16[8,32,128]{2,1,0:T(8,128)(2,1)S(1)} %get-tuple-element.43), channel_id=1, source_target_pairs={{0,4},{1,7},{2,6},{3,5},{4,0},{5,3},{6,2},{7,1},{8,12},{9,15},{10,... | collective-permute-start | bytes 196616 | tf_op jit(solution)/shard_map/ppermute | solution.py:407
  51.3 4.6 %collective-permute-start.14 = (f16[8,32,128]{2,1,0:T(8,128)(2,1)S(1)}, f16[8,32,128]{2,1,0:T(8,128)(2,1)S(1)}, u32[]{:S(2)}, u32[]{:S(2)}) collective-permute-start(f16[8,32,128]{2,1,0:T(8,128)(2,1)S(1)} %get-tuple-element.42), channel_id=1, source_target_pairs={{0,2},{1,3},{2,0},{3,1},{4,6},{5,7},{6,4},{7,5},{8,10},{9,11},{10,... | collective-permute-start | bytes 196616 | tf_op jit(solution)/shard_map/ppermute | solution.py:407
  56.0 5.0 %collective-permute-start.16 = (f16[8,32,128]{2,1,0:T(8,128)(2,1)S(1)}, f16[8,32,128]{2,1,0:T(8,128)(2,1)S(1)}, u32[]{:S(2)}, u32[]{:S(2)}) collective-permute-start(f16[8,32,128]{2,1,0:T(8,128)(2,1)S(1)} %fusion.4), channel_id=1, source_target_pairs={{4,0},{7,1},{6,2},{5,3},{0,4},{3,5},{2,6},{1,7},{12,8},{15,9},{14,... | collective-permute-start | bytes 196616 | tf_op jit(solution)/shard_map/ppermute | solution.py:414
  57.8 4.7 %collective-permute-start.17 = (f16[8,32,128]{2,1,0:T(8,128)(2,1)S(1)}, f16[8,32,128]{2,1,0:T(8,128)(2,1)S(1)}, u32[]{:S(2)}, u32[]{:S(2)}) collective-permute-start(f16[8,32,128]{2,1,0:T(8,128)(2,1)S(1)} %fusion.4), channel_id=1, source_target_pairs={{6,0},{5,1},{4,2},{7,3},{2,4},{1,5},{0,6},{3,7},{14,8},{13,9},{12,... | collective-permute-start | bytes 196616 | tf_op jit(solution)/shard_map/ppermute | solution.py:414
  59.5 3.9 %collective-permute-start.15 = (f16[8,32,128]{2,1,0:T(8,128)(2,1)S(1)}, f16[8,32,128]{2,1,0:T(8,128)(2,1)S(1)}, u32[]{:S(2)}, u32[]{:S(2)}) collective-permute-start(f16[8,32,128]{2,1,0:T(8,128)(2,1)S(1)} %fusion.4), channel_id=1, source_target_pairs={{2,0},{3,1},{0,2},{1,3},{6,4},{7,5},{4,6},{5,7},{10,8},{11,9},{8,1... | collective-permute-start | bytes 196616 | tf_op jit(solution)/shard_map/ppermute | solution.py:414
  63.5 4.4 %collective-permute-start.18 = (f16[4,8,32,128]{3,2,1,0:T(8,128)(2,1)S(1)}, f16[4,8,32,128]{3,2,1,0:T(8,128)(2,1)S(1)}, u32[]{:S(2)}, u32[]{:S(2)}) collective-permute-start(f16[4,8,32,128]{3,2,1,0:T(8,128)(2,1)S(1)} %pad_maximum_fusion.1), channel_id=1, source_target_pairs={{0,1},{1,0},{2,3},{3,2},{4,5},{5,4},{6,7},{7,6},{8,9},{9,8},{10,11... | collective-permute-start | bytes 786440 | tf_op jit(solution)/shard_map/ppermute | solution.py:448
  67.2 1.0 %copy-start.3 = (f32[16,128,128]{2,1,0:T(8,128)}, f32[16,128,128]{2,1,0:T(8,128)S(1)}, u32[]{:S(2)}) copy-start(f32[16,128,128]{2,1,0:T(8,128)S(1)} %multiply_dynamic-update-slice_fusion.1) | copy-start | bytes 3145732

commit v9 on v8

--- a/solution.py
+++ b/solution.py
@@ -9,7 +9,7 @@
 
 SUBSTEPS = 3
 PAD = 8
-CHUNK = 32
+CHUNK = 16
 LOWEST = -3.0e38
 WIRE_SCALE = 4096.0
 

time: 69.7 us -> 69.5 us (level)
    ppermute x1, starting transfers between devices: 3.28 us -> 2.48 us  [body(): from_partner = lax.ppermute(pieces, 'ctrl', partners)]
    ppermute x6, waiting for transfers between devices: 8.75 us -> 9.49 us  [gather(): got.append(lax.ppermute(mine, 'ctrl', pairs))]
where the time goes in v9:
time: 69.5 us; the launch traced here: 69 us
  starting transfers between devices  27.6 us (40%)
  waiting for transfers between devices  19.2 us (28%)
  Pallas kernels  18.7 us (27%)
  other arithmetic  2.08 us (3%)
  local copies, waits for them, and re-layouts  1.06 us (2%)
    pallas_call x5, Pallas kernels, call(): pl.pallas_call(functools.partial(kernel, half=half), out_shape=outs, in_s...  17.2 us
    ppermute x6, waiting for transfers between devices, gather(): got.append(lax.ppermute(mine, 'ctrl', pairs))  9.49 us
    ppermute x6, waiting for transfers between devices, reduce(): mine = jnp.maximum(mine, lax.ppermute(part, 'ctrl', pairs))  8.91 us
    ppermute x6, starting transfers between devices, gather(): got.append(lax.ppermute(mine, 'ctrl', pairs))  7.8 us
    ppermute x6, starting transfers between devices, reduce(): mine = jnp.maximum(mine, lax.ppermute(part, 'ctrl', pairs))  6.46 us
    ppermute x1, starting transfers between devices, body(): edge_other = lax.ppermute(far, both, beside)  3.73 us
    ppermute x1, starting transfers between devices, body(): edge = lax.ppermute(packed, both, facing)  3.12 us
    ppermute x1, starting transfers between devices, body(): from_partner = lax.ppermute(pieces, 'ctrl', partners)  2.48 us
  transfers between devices with their start and end apart: 19, of which 10 were waited for; matrix products, arithmetic and copies ran while one was open for 1% of the time, Pallas kernels for 21%

profile of v9, /device:TPU:5, one launch (start us, length us, event | category | flops | bytes accessed | tf_op | source)
XLA Modules:
  0.0 69.0 jit_solution(17034305673773807890)
XLA Ops:
  0.0 0.7 %collective-permute-start.1 = (bf16[2,16,128,128]{3,2,1,0:T(8,128)(2,1)}, bf16[2,16,128,128]{3,2,1,0:T(8,128)(2,1)}, u32[]{:S(2)}, u32[]{:S(2)}) collective-permute-start(bf16[2,16,128,128]{3,2,1,0:T(8,128)(2,1)} %reward.3), channel_id=1, source_target_pairs={{0,1},{1,0},{2,3},{3,2},{4,5},{5,4},{6,7},{7,6},{8,9},{9,8},{10,11... | collective-permute-start | bytes 3145736 | tf_op jit(solution)/shard_map/ppermute | solution.py:364
  0.8 0.1 collective-permute-start
  0.9 1.5 %shard_map.64 = (bf16[9,128,128]{2,1,0:T(8,128)(2,1)S(1)}, bf16[4,128,128]{2,1,0:T(8,128)(2,1)S(1)}, f32[11,144,128]{2,1,0:T(8,128)S(1)}) custom-call(f32[16,128,128]{2,1,0:T(8,128)} %value.1, f32[16,128,128]{2,1,0:T(8,128)} %speed.3, bf16[2,16,128,128]{3,2,1,0:T(8,128)(2,1)} %reward.3), custom_call_target="tpu_custom_call" | custom-call | tf_op jit(solution)/shard_map/pallas_call | solution.py:367
  2.3 0.7 %copy-done.2 = bf16[9,128,128]{2,1,0:T(8,128)(2,1)} copy-done((bf16[9,128,128]{2,1,0:T(8,128)(2,1)}, bf16[9,128,128]{2,1,0:T(8,128)(2,1)S(1)}, u32[]{:S(2)}) %copy-start.2) | copy-done | bytes 294936
  3.1 3.1 %collective-permute-start.2 = (bf16[9,128,128]{2,1,0:T(8,128)(2,1)}, bf16[9,128,128]{2,1,0:T(8,128)(2,1)S(1)}, u32[]{:S(2)}, u32[]{:S(2)}) collective-permute-start(bf16[9,128,128]{2,1,0:T(8,128)(2,1)} %copy-done.2), channel_id=1, source_target_pairs={{1,9},{9,1},{3,11},{11,3},{5,13},{13,5},{7,15},{15,7},{8,16},{16,8... | collective-permute-start | bytes 884744 | tf_op jit(solution)/shard_map/ppermute | solution.py:385
  6.2 3.7 %collective-permute-start.3 = (bf16[4,128,128]{2,1,0:T(8,128)(2,1)S(1)}, bf16[4,128,128]{2,1,0:T(8,128)(2,1)S(1)}, u32[]{:S(2)}, u32[]{:S(2)}) collective-permute-start(bf16[4,128,128]{2,1,0:T(8,128)(2,1)S(1)} %get-tuple-element.26), channel_id=1, source_target_pairs={{0,9},{8,1},{2,11},{10,3},{4,13},{12,5},{6,15},{14,7},{9,16},{17,8... | collective-permute-start | bytes 393224 | tf_op jit(solution)/shard_map/ppermute | solution.py:386
  9.9 0.1 pad_add_fusion
  10.0 0.1 iota_compare_fusion
  10.1 0.1 select_reduce_fusion
  10.2 0.1 copy.12.coef
  10.3 6.0 %shard_map.65 = (f32[4,5,32,128]{3,2,1,0:T(8,128)S(1)}, f32[4,2,128,128]{3,2,1,0:T(8,128)S(1)}, f32[4,2,128,128]{3,2,1,0:T(8,128)S(1)}, f32[10,128,128]{2,1,0:T(8,128)S(1)}, f32[4,10,128,128]{3,2,1,0:T(8,128)S(1)}) custom-call(f32[4,6]{1,0:T(4,128)S(1)} %copy.12.coef, f32[11,144,128]{2,1,0:T(8,128)S(1)} %get-tuple-element.22.block.first, ...), custom_call_target="tpu_custom_call" | custom-call | flops 34406400 | bytes 16515072 | tf_op jit(solution)/shard_map/pallas_call | solution.py:348
  16.3 1.7 %shard_map.66.refs_1_ = f32[4,3,32,128]{3,2,1,0:T(8,128)S(1)} custom-call(f32[4,6]{1,0:T(4,128)S(1)} %copy.12.coef, f32[11,144,128]{2,1,0:T(8,128)S(1)} %get-tuple-element.22.block.first, f32[10,128,128]{2,1,0:T(8,128)S(1)} %get-tuple-element.23.speed_rows, f32[4,10,128,128]{3,2,1,0:T(8,128)S(1)} %get-tuple-element.24.reward_rows, ...), custom_call_target="tpu_custom_call" | custom-call | flops 6553600 | bytes 3145728 | tf_op jit(solution)/shard_map/pallas_call | solution.py:348
  17.9 1.7 %shard_map.67 = f32[4,3,32,128]{3,2,1,0:T(8,128)S(1)} custom-call(f32[4,6]{1,0:T(4,128)S(1)} %copy.12.coef, f32[11,144,128]{2,1,0:T(8,128)S(1)} %get-tuple-element.22.block.first, f32[10,128,128]{2,1,0:T(8,128)S(1)} %get-tuple-element.23.speed_rows, f32[4,10,128,128]{3,2,1,0:T(8,128)S(1)} %get-tuple-element.24.reward_rows, ...), custom_call_target="tpu_custom_call" | custom-call | flops 6553600 | bytes 3145728 | tf_op jit(solution)/shard_map/pallas_call | solution.py:348
  19.6 0.1 fusion
  19.8 2.4 %collective-permute-start.4 = (f16[8,32,128]{2,1,0:T(8,128)(2,1)S(1)}, f16[8,32,128]{2,1,0:T(8,128)(2,1)S(1)}, u32[]{:S(2)}, u32[]{:S(2)}) collective-permute-start(f16[8,32,128]{2,1,0:T(8,128)(2,1)S(1)} %get-tuple-element.44), channel_id=1, source_target_pairs={{0,6},{1,5},{2,4},{3,7},{4,2},{5,1},{6,0},{7,3},{8,14},{9,13},{10,... | collective-permute-start | bytes 196616 | tf_op jit(solution)/shard_map/ppermute | solution.py:407
  22.1 1.1 %collective-permute-start.5 = (f16[8,32,128]{2,1,0:T(8,128)(2,1)S(1)}, f16[8,32,128]{2,1,0:T(8,128)(2,1)S(1)}, u32[]{:S(2)}, u32[]{:S(2)}) collective-permute-start(f16[8,32,128]{2,1,0:T(8,128)(2,1)S(1)} %get-tuple-element.46), channel_id=1, source_target_pairs={{0,4},{1,7},{2,6},{3,5},{4,0},{5,3},{6,2},{7,1},{8,12},{9,15},{10,... | collective-permute-start | bytes 196616 | tf_op jit(solution)/shard_map/ppermute | solution.py:407
  23.2 0.2 collective-permute-start.6
  23.4 2.3 %collective-permute-done.4 = f16[8,32,128]{2,1,0:T(8,128)(2,1)S(1)} collective-permute-done((f16[8,32,128]{2,1,0:T(8,128)(2,1)S(1)}, f16[8,32,128]{2,1,0:T(8,128)(2,1)S(1)}, u32[]{:S(2)}, u32[]{:S(2)}) %collective-permute-start.4) | collective-permute-done | bytes 65568 | tf_op jit(solution)/shard_map/ppermute | solution.py:407
  25.7 1.7 %collective-permute-done.5 = f16[8,32,128]{2,1,0:T(8,128)(2,1)S(1)} collective-permute-done((f16[8,32,128]{2,1,0:T(8,128)(2,1)S(1)}, f16[8,32,128]{2,1,0:T(8,128)(2,1)S(1)}, u32[]{:S(2)}, u32[]{:S(2)}) %collective-permute-start.5) | collective-permute-done | bytes 65568 | tf_op jit(solution)/shard_map/ppermute | solution.py:407
  27.4 0.4 collective-permute-done.6
  27.8 3.8 %collective-permute-start.8 = (f16[8,32,128]{2,1,0:T(8,128)(2,1)S(1)}, f16[8,32,128]{2,1,0:T(8,128)(2,1)S(1)}, u32[]{:S(2)}, u32[]{:S(2)}) collective-permute-start(f16[8,32,128]{2,1,0:T(8,128)(2,1)S(1)} %fusion.7), channel_id=1, source_target_pairs={{4,0},{7,1},{6,2},{5,3},{0,4},{3,5},{2,6},{1,7},{12,8},{15,9},{14,... | collective-permute-start | bytes 196616 | tf_op jit(solution)/shard_map/ppermute | solution.py:414
  31.7 0.4 collective-permute-start.7
  32.0 1.3 %collective-permute-done.8 = f16[8,32,128]{2,1,0:T(8,128)(2,1)S(1)} collective-permute-done((f16[8,32,128]{2,1,0:T(8,128)(2,1)S(1)}, f16[8,32,128]{2,1,0:T(8,128)(2,1)S(1)}, u32[]{:S(2)}, u32[]{:S(2)}) %collective-permute-start.8) | collective-permute-done | bytes 65568 | tf_op jit(solution)/shard_map/ppermute | solution.py:414
  33.3 3.8 %collective-permute-done.9 = f16[8,32,128]{2,1,0:T(8,128)(2,1)S(1)} collective-permute-done((f16[8,32,128]{2,1,0:T(8,128)(2,1)S(1)}, f16[8,32,128]{2,1,0:T(8,128)(2,1)S(1)}, u32[]{:S(2)}, u32[]{:S(2)}) %collective-permute-start.9) | collective-permute-done | bytes 65568 | tf_op jit(solution)/shard_map/ppermute | solution.py:414
  37.1 0.1 pad_maximum_fusion
  37.3 1.2 %collective-permute-start.11 = (f16[4,3,32,128]{3,2,1,0:T(8,128)(2,1)S(1)}, f16[4,3,32,128]{3,2,1,0:T(8,128)(2,1)S(1)}, u32[]{:S(2)}, u32[]{:S(2)}) collective-permute-start(f16[4,3,32,128]{3,2,1,0:T(8,128)(2,1)S(1)} %slice.49), channel_id=1, source_target_pairs={{0,1},{1,0},{2,3},{3,2},{4,5},{5,4},{6,7},{7,6},{8,9},{9,8},{10,11... | collective-permute-start | bytes 294920 | tf_op jit(solution)/shard_map/ppermute | solution.py:439
  38.5 2.0 %collective-permute-start.10 = (bf16[4,3,32,128]{3,2,1,0:T(8,128)(2,1)S(1)}, bf16[4,3,32,128]{3,2,1,0:T(8,128)(2,1)S(1)}, u32[]{:S(2)}, u32[]{:S(2)}) collective-permute-start(bf16[4,3,32,128]{3,2,1,0:T(8,128)(2,1)S(1)} %multiply_convert_fusion), channel_id=1, source_target_pairs={{1,9},{9,1},{3,11},{11,3},{5,13},{13,5},{7,15},{15,7},{8,16},{16,8... | collective-permute-start | bytes 294920 | tf_op jit(solution)/shard_map/ppermute | solution.py:440
  40.5 0.1 convert_multiply_fusion.current
  40.6 5.2 %shard_map.68 = (f32[4,5,32,128]{3,2,1,0:T(8,128)S(1)}, f32[4,2,128,128]{3,2,1,0:T(8,128)S(1)}, f32[4,2,128,128]{3,2,1,0:T(8,128)S(1)}) custom-call(f32[4,6]{1,0:T(4,128)S(1)} %copy.12.coef, f32[4,8,32,128]{3,2,1,0:T(8,128)S(1)} %convert_multiply_fusion.current, f32[4,3,32,128]{3,2,1,0:T(8,128)S(1)} %convert_multiply_fusion.1.across, ...), custom_call_target="tpu_custom_call" | custom-call | flops 34406400 | bytes 16515072 | tf_op jit(solution)/shard_map/pallas_call | solution.py:348
  45.8 2.7 %shard_map.69 = f32[4,3,32,128]{3,2,1,0:T(8,128)S(1)} custom-call(f32[4,6]{1,0:T(4,128)S(1)} %copy.12.coef, f32[4,8,32,128]{3,2,1,0:T(8,128)S(1)} %convert_multiply_fusion.current, bf16[4,3,32,128]{3,2,1,0:T(8,128)(2,1)S(1)} %collective-permute-done.10.beyond, f32[10,128,128]{2,1,0:T(8,128)S(1)} %get-tuple-element.23.speed_rows, ...), custom_call_target="tpu_custom_call" | custom-call | flops 14745600 | bytes 7077888 | tf_op jit(solution)/shard_map/pallas_call | solution.py:348
  48.6 0.1 fusion.1
  48.7 1.7 %collective-permute-start.12 = (f16[8,32,128]{2,1,0:T(8,128)(2,1)S(1)}, f16[8,32,128]{2,1,0:T(8,128)(2,1)S(1)}, u32[]{:S(2)}, u32[]{:S(2)}) collective-permute-start(f16[8,32,128]{2,1,0:T(8,128)(2,1)S(1)} %get-tuple-element.41), channel_id=1, source_target_pairs={{0,6},{1,5},{2,4},{3,7},{4,2},{5,1},{6,0},{7,3},{8,14},{9,13},{10,... | collective-permute-start | bytes 196616 | tf_op jit(solution)/shard_map/ppermute | solution.py:407
  50.3 0.9 %collective-permute-start.13 = (f16[8,32,128]{2,1,0:T(8,128)(2,1)S(1)}, f16[8,32,128]{2,1,0:T(8,128)(2,1)S(1)}, u32[]{:S(2)}, u32[]{:S(2)}) collective-permute-start(f16[8,32,128]{2,1,0:T(8,128)(2,1)S(1)} %get-tuple-element.43), channel_id=1, source_target_pairs={{0,4},{1,7},{2,6},{3,5},{4,0},{5,3},{6,2},{7,1},{8,12},{9,15},{10,... | collective-permute-start | bytes 196616 | tf_op jit(solution)/shard_map/ppermute | solution.py:407
  51.3 0.2 collective-permute-start.14
  51.5 2.3 %collective-permute-done.12 = f16[8,32,128]{2,1,0:T(8,128)(2,1)S(1)} collective-permute-done((f16[8,32,128]{2,1,0:T(8,128)(2,1)S(1)}, f16[8,32,128]{2,1,0:T(8,128)(2,1)S(1)}, u32[]{:S(2)}, u32[]{:S(2)}) %collective-permute-start.12) | collective-permute-done | bytes 65568 | tf_op jit(solution)/shard_map/ppermute | solution.py:407
  53.8 2.3 %collective-permute-done.13 = f16[8,32,128]{2,1,0:T(8,128)(2,1)S(1)} collective-permute-done((f16[8,32,128]{2,1,0:T(8,128)(2,1)S(1)}, f16[8,32,128]{2,1,0:T(8,128)(2,1)S(1)}, u32[]{:S(2)}, u32[]{:S(2)}) %collective-permute-start.13) | collective-permute-done | bytes 65568 | tf_op jit(solution)/shard_map/ppermute | solution.py:407
  56.1 1.6 %collective-permute-start.16 = (f16[8,32,128]{2,1,0:T(8,128)(2,1)S(1)}, f16[8,32,128]{2,1,0:T(8,128)(2,1)S(1)}, u32[]{:S(2)}, u32[]{:S(2)}) collective-permute-start(f16[8,32,128]{2,1,0:T(8,128)(2,1)S(1)} %fusion.4), channel_id=1, source_target_pairs={{4,0},{7,1},{6,2},{5,3},{0,4},{3,5},{2,6},{1,7},{12,8},{15,9},{14,... | collective-permute-start | bytes 196616 | tf_op jit(solution)/shard_map/ppermute | solution.py:414
  57.7 1.7 %collective-permute-start.17 = (f16[8,32,128]{2,1,0:T(8,128)(2,1)S(1)}, f16[8,32,128]{2,1,0:T(8,128)(2,1)S(1)}, u32[]{:S(2)}, u32[]{:S(2)}) collective-permute-start(f16[8,32,128]{2,1,0:T(8,128)(2,1)S(1)} %fusion.4), channel_id=1, source_target_pairs={{6,0},{5,1},{4,2},{7,3},{2,4},{1,5},{0,6},{3,7},{14,8},{13,9},{12,... | collective-permute-start | bytes 196616 | tf_op jit(solution)/shard_map/ppermute | solution.py:414
  59.4 0.3 collective-permute-start.15
  59.7 1.5 %collective-permute-done.16 = f16[8,32,128]{2,1,0:T(8,128)(2,1)S(1)} collective-permute-done((f16[8,32,128]{2,1,0:T(8,128)(2,1)S(1)}, f16[8,32,128]{2,1,0:T(8,128)(2,1)S(1)}, u32[]{:S(2)}, u32[]{:S(2)}) %collective-permute-start.16) | collective-permute-done | bytes 65568 | tf_op jit(solution)/shard_map/ppermute | solution.py:414
  61.2 3.0 %collective-permute-done.17 = f16[8,32,128]{2,1,0:T(8,128)(2,1)S(1)} collective-permute-done((f16[8,32,128]{2,1,0:T(8,128)(2,1)S(1)}, f16[8,32,128]{2,1,0:T(8,128)(2,1)S(1)}, u32[]{:S(2)}, u32[]{:S(2)}) %collective-permute-start.17) | collective-permute-done | bytes 65568 | tf_op jit(solution)/shard_map/ppermute | solution.py:414
  64.2 0.1 pad_maximum_fusion.1
  64.3 2.5 %collective-permute-start.18 = (f16[4,8,32,128]{3,2,1,0:T(8,128)(2,1)S(1)}, f16[4,8,32,128]{3,2,1,0:T(8,128)(2,1)S(1)}, u32[]{:S(2)}, u32[]{:S(2)}) collective-permute-start(f16[4,8,32,128]{3,2,1,0:T(8,128)(2,1)S(1)} %pad_maximum_fusion.1), channel_id=1, source_target_pairs={{0,1},{1,0},{2,3},{3,2},{4,5},{5,4},{6,7},{7,6},{8,9},{9,8},{10,11... | collective-permute-start | bytes 786440 | tf_op jit(solution)/shard_map/ppermute | solution.py:448
  66.8 0.1 pad_maximum_fusion.2
  66.9 0.1 broadcast_in_dim.27
  67.1 0.8 %collective-permute-done.18 = f16[4,8,32,128]{3,2,1,0:T(8,128)(2,1)S(1)} collective-permute-done((f16[4,8,32,128]{3,2,1,0:T(8,128)(2,1)S(1)}, f16[4,8,32,128]{3,2,1,0:T(8,128)(2,1)S(1)}, u32[]{:S(2)}, u32[]{:S(2)}) %collective-permute-start.18) | collective-permute-done | bytes 262176 | tf_op jit(solution)/shard_map/ppermute | solution.py:448
  68.0 0.1 pad_maximum_fusion.3
  68.1 0.9 %multiply_dynamic-update-slice_fusion = f32[16,128,128]{2,1,0:T(8,128)} fusion(f32[16,128,128]{2,1,0:T(8,128)} %copy-done.3, s32[]{:T(128)S(6)} %select_n.133, f16[8,128,128]{2,1,0:T(8,128)(2,1)S(1)} %pad_maximum_fusion.3, pred[]{:T(512)S(6)} %eq.41), kind=kLoop, calls=%fused_computation.4 | loop fusion | flops 393216 | bytes 786437 | tf_op jit(solution)/shard_map/dynamic_update_slice | solution.py:459
  (36 shorter events, 0.6 us)
Async XLA Ops:
  0.0 10.3 %copy-start.1 = (bf16[2,16,128,128]{3,2,1,0:T(8,128)(2,1)S(1)}, bf16[2,16,128,128]{3,2,1,0:T(8,128)(2,1)}, u32[]{:S(2)}) copy-start(bf16[2,16,128,128]{3,2,1,0:T(8,128)(2,1)} %reward.3) | copy-start | bytes 3145732
  0.0 9.9 %copy-start.6 = (s32[2]{0:T(128)S(1)}, s32[2]{0:T(128)}, u32[]{:S(2)}) copy-start(s32[2]{0:T(128)} %param.9) | copy-start | bytes 28
  0.0 10.3 %copy-start = (f32[16,128,128]{2,1,0:T(8,128)S(1)}, f32[16,128,128]{2,1,0:T(8,128)}, u32[]{:S(2)}) copy-start(f32[16,128,128]{2,1,0:T(8,128)} %speed.3) | copy-start | bytes 3145732
  0.0 3.0 %copy-start.4 = (f32[16,3]{0,1:T(4,128)S(1)}, f32[16,3]{0,1:T(4,128)}, u32[]{:S(2)}) copy-start(f32[16,3]{0,1:T(4,128)} %param.10) | copy-start | bytes 580
  0.0 3.0 %copy-start.5 = (f32[16,3]{0,1:T(4,128)S(1)}, f32[16,3]{0,1:T(4,128)}, u32[]{:S(2)}) copy-start(f32[16,3]{0,1:T(4,128)} %param.11) | copy-start | bytes 580
  0.0 10.2 %collective-permute-start.1 = (bf16[2,16,128,128]{3,2,1,0:T(8,128)(2,1)}, bf16[2,16,128,128]{3,2,1,0:T(8,128)(2,1)}, u32[]{:S(2)}, u32[]{:S(2)}) collective-permute-start(bf16[2,16,128,128]{3,2,1,0:T(8,128)(2,1)} %reward.3), channel_id=1, source_target_pairs={{0,1},{1,0},{2,3},{3,2},{4,5},{5,4},{6,7},{7,6},{8,9},{9,8},{10,11... | collective-permute-start | bytes 3145736 | tf_op jit(solution)/shard_map/ppermute | solution.py:364
  0.8 2.3 %collective-permute-start = (s32[2]{0:T(128)}, s32[2]{0:T(128)S(1)}, u32[]{:S(2)}, u32[]{:S(2)}) collective-permute-start(s32[2]{0:T(128)} %param.9), channel_id=1, source_target_pairs={{0,1},{1,0},{2,3},{3,2},{4,5},{5,4},{6,7},{7,6},{8,9},{9,8},{10,11... | collective-permute-start | bytes 32 | tf_op jit(solution)/shard_map/ppermute | solution.py:363
  2.3 0.7 %copy-start.2 = (bf16[9,128,128]{2,1,0:T(8,128)(2,1)}, bf16[9,128,128]{2,1,0:T(8,128)(2,1)S(1)}, u32[]{:S(2)}) copy-start(bf16[9,128,128]{2,1,0:T(8,128)(2,1)S(1)} %get-tuple-element.25) | copy-start | bytes 884740
  3.1 13.2 %collective-permute-start.2 = (bf16[9,128,128]{2,1,0:T(8,128)(2,1)}, bf16[9,128,128]{2,1,0:T(8,128)(2,1)S(1)}, u32[]{:S(2)}, u32[]{:S(2)}) collective-permute-start(bf16[9,128,128]{2,1,0:T(8,128)(2,1)} %copy-done.2), channel_id=1, source_target_pairs={{1,9},{9,1},{3,11},{11,3},{5,13},{13,5},{7,15},{15,7},{8,16},{16,8... | collective-permute-start | bytes 884744 | tf_op jit(solution)/shard_map/ppermute | solution.py:385
  6.2 11.8 %collective-permute-start.3 = (bf16[4,128,128]{2,1,0:T(8,128)(2,1)S(1)}, bf16[4,128,128]{2,1,0:T(8,128)(2,1)S(1)}, u32[]{:S(2)}, u32[]{:S(2)}) collective-permute-start(bf16[4,128,128]{2,1,0:T(8,128)(2,1)S(1)} %get-tuple-element.26), channel_id=1, source_target_pairs={{0,9},{8,1},{2,11},{10,3},{4,13},{12,5},{6,15},{14,7},{9,16},{17,8... | collective-permute-start | bytes 393224 | tf_op jit(solution)/shard_map/ppermute | solution.py:386
  19.8 5.9 %collective-permute-start.4 = (f16[8,32,128]{2,1,0:T(8,128)(2,1)S(1)}, f16[8,32,128]{2,1,0:T(8,128)(2,1)S(1)}, u32[]{:S(2)}, u32[]{:S(2)}) collective-permute-start(f16[8,32,128]{2,1,0:T(8,128)(2,1)S(1)} %get-tuple-element.44), channel_id=1, source_target_pairs={{0,6},{1,5},{2,4},{3,7},{4,2},{5,1},{6,0},{7,3},{8,14},{9,13},{10,... | collective-permute-start | bytes 196616 | tf_op jit(solution)/shard_map/ppermute | solution.py:407
  22.1 5.2 %collective-permute-start.5 = (f16[8,32,128]{2,1,0:T(8,128)(2,1)S(1)}, f16[8,32,128]{2,1,0:T(8,128)(2,1)S(1)}, u32[]{:S(2)}, u32[]{:S(2)}) collective-permute-start(f16[8,32,128]{2,1,0:T(8,128)(2,1)S(1)} %get-tuple-element.46), channel_id=1, source_target_pairs={{0,4},{1,7},{2,6},{3,5},{4,0},{5,3},{6,2},{7,1},{8,12},{9,15},{10,... | collective-permute-start | bytes 196616 | tf_op jit(solution)/shard_map/ppermute | solution.py:407
  23.2 4.5 %collective-permute-start.6 = (f16[8,32,128]{2,1,0:T(8,128)(2,1)S(1)}, f16[8,32,128]{2,1,0:T(8,128)(2,1)S(1)}, u32[]{:S(2)}, u32[]{:S(2)}) collective-permute-start(f16[8,32,128]{2,1,0:T(8,128)(2,1)S(1)} %get-tuple-element.45), channel_id=1, source_target_pairs={{0,2},{1,3},{2,0},{3,1},{4,6},{5,7},{6,4},{7,5},{8,10},{9,11},{10,... | collective-permute-start | bytes 196616 | tf_op jit(solution)/shard_map/ppermute | solution.py:407
  27.8 5.5 %collective-permute-start.8 = (f16[8,32,128]{2,1,0:T(8,128)(2,1)S(1)}, f16[8,32,128]{2,1,0:T(8,128)(2,1)S(1)}, u32[]{:S(2)}, u32[]{:S(2)}) collective-permute-start(f16[8,32,128]{2,1,0:T(8,128)(2,1)S(1)} %fusion.7), channel_id=1, source_target_pairs={{4,0},{7,1},{6,2},{5,3},{0,4},{3,5},{2,6},{1,7},{12,8},{15,9},{14,... | collective-permute-start | bytes 196616 | tf_op jit(solution)/shard_map/ppermute | solution.py:414
  31.7 5.4 %collective-permute-start.9 = (f16[8,32,128]{2,1,0:T(8,128)(2,1)S(1)}, f16[8,32,128]{2,1,0:T(8,128)(2,1)S(1)}, u32[]{:S(2)}, u32[]{:S(2)}) collective-permute-start(f16[8,32,128]{2,1,0:T(8,128)(2,1)S(1)} %fusion.7), channel_id=1, source_target_pairs={{6,0},{5,1},{4,2},{7,3},{2,4},{1,5},{0,6},{3,7},{14,8},{13,9},{12,... | collective-permute-start | bytes 196616 | tf_op jit(solution)/shard_map/ppermute | solution.py:414
  31.7 5.5 %collective-permute-start.7 = (f16[8,32,128]{2,1,0:T(8,128)(2,1)S(1)}, f16[8,32,128]{2,1,0:T(8,128)(2,1)S(1)}, u32[]{:S(2)}, u32[]{:S(2)}) collective-permute-start(f16[8,32,128]{2,1,0:T(8,128)(2,1)S(1)} %fusion.7), channel_id=1, source_target_pairs={{2,0},{3,1},{0,2},{1,3},{6,4},{7,5},{4,6},{5,7},{10,8},{11,9},{8,1... | collective-permute-start | bytes 196616 | tf_op jit(solution)/shard_map/ppermute | solution.py:414
  37.3 3.3 %collective-permute-start.11 = (f16[4,3,32,128]{3,2,1,0:T(8,128)(2,1)S(1)}, f16[4,3,32,128]{3,2,1,0:T(8,128)(2,1)S(1)}, u32[]{:S(2)}, u32[]{:S(2)}) collective-permute-start(f16[4,3,32,128]{3,2,1,0:T(8,128)(2,1)S(1)} %slice.49), channel_id=1, source_target_pairs={{0,1},{1,0},{2,3},{3,2},{4,5},{5,4},{6,7},{7,6},{8,9},{9,8},{10,11... | collective-permute-start | bytes 294920 | tf_op jit(solution)/shard_map/ppermute | solution.py:439
  38.5 7.3 %collective-permute-start.10 = (bf16[4,3,32,128]{3,2,1,0:T(8,128)(2,1)S(1)}, bf16[4,3,32,128]{3,2,1,0:T(8,128)(2,1)S(1)}, u32[]{:S(2)}, u32[]{:S(2)}) collective-permute-start(bf16[4,3,32,128]{3,2,1,0:T(8,128)(2,1)S(1)} %multiply_convert_fusion), channel_id=1, source_target_pairs={{1,9},{9,1},{3,11},{11,3},{5,13},{13,5},{7,15},{15,7},{8,16},{16,8... | collective-permute-start | bytes 294920 | tf_op jit(solution)/shard_map/ppermute | solution.py:440
  48.7 5.1 %collective-permute-start.12 = (f16[8,32,128]{2,1,0:T(8,128)(2,1)S(1)}, f16[8,32,128]{2,1,0:T(8,128)(2,1)S(1)}, u32[]{:S(2)}, u32[]{:S(2)}) collective-permute-start(f16[8,32,128]{2,1,0:T(8,128)(2,1)S(1)} %get-tuple-element.41), channel_id=1, source_target_pairs={{0,6},{1,5},{2,4},{3,7},{4,2},{5,1},{6,0},{7,3},{8,14},{9,13},{10,... | collective-permute-start | bytes 196616 | tf_op jit(solution)/shard_map/ppermute | solution.py:407
  50.3 5.7 %collective-permute-start.13 = (f16[8,32,128]{2,1,0:T(8,128)(2,1)S(1)}, f16[8,32,128]{2,1,0:T(8,128)(2,1)S(1)}, u32[]{:S(2)}, u32[]{:S(2)}) collective-permute-start(f16[8,32,128]{2,1,0:T(8,128)(2,1)S(1)} %get-tuple-element.43), channel_id=1, source_target_pairs={{0,4},{1,7},{2,6},{3,5},{4,0},{5,3},{6,2},{7,1},{8,12},{9,15},{10,... | collective-permute-start | bytes 196616 | tf_op jit(solution)/shard_map/ppermute | solution.py:407
  51.3 4.8 %collective-permute-start.14 = (f16[8,32,128]{2,1,0:T(8,128)(2,1)S(1)}, f16[8,32,128]{2,1,0:T(8,128)(2,1)S(1)}, u32[]{:S(2)}, u32[]{:S(2)}) collective-permute-start(f16[8,32,128]{2,1,0:T(8,128)(2,1)S(1)} %get-tuple-element.42), channel_id=1, source_target_pairs={{0,2},{1,3},{2,0},{3,1},{4,6},{5,7},{6,4},{7,5},{8,10},{9,11},{10,... | collective-permute-start | bytes 196616 | tf_op jit(solution)/shard_map/ppermute | solution.py:407
  56.1 5.1 %collective-permute-start.16 = (f16[8,32,128]{2,1,0:T(8,128)(2,1)S(1)}, f16[8,32,128]{2,1,0:T(8,128)(2,1)S(1)}, u32[]{:S(2)}, u32[]{:S(2)}) collective-permute-start(f16[8,32,128]{2,1,0:T(8,128)(2,1)S(1)} %fusion.4), channel_id=1, source_target_pairs={{4,0},{7,1},{6,2},{5,3},{0,4},{3,5},{2,6},{1,7},{12,8},{15,9},{14,... | collective-permute-start | bytes 196616 | tf_op jit(solution)/shard_map/ppermute | solution.py:414
  57.7 6.4 %collective-permute-start.17 = (f16[8,32,128]{2,1,0:T(8,128)(2,1)S(1)}, f16[8,32,128]{2,1,0:T(8,128)(2,1)S(1)}, u32[]{:S(2)}, u32[]{:S(2)}) collective-permute-start(f16[8,32,128]{2,1,0:T(8,128)(2,1)S(1)} %fusion.4), channel_id=1, source_target_pairs={{6,0},{5,1},{4,2},{7,3},{2,4},{1,5},{0,6},{3,7},{14,8},{13,9},{12,... | collective-permute-start | bytes 196616 | tf_op jit(solution)/shard_map/ppermute | solution.py:414
  59.4 4.8 %collective-permute-start.15 = (f16[8,32,128]{2,1,0:T(8,128)(2,1)S(1)}, f16[8,32,128]{2,1,0:T(8,128)(2,1)S(1)}, u32[]{:S(2)}, u32[]{:S(2)}) collective-permute-start(f16[8,32,128]{2,1,0:T(8,128)(2,1)S(1)} %fusion.4), channel_id=1, source_target_pairs={{2,0},{3,1},{0,2},{1,3},{6,4},{7,5},{4,6},{5,7},{10,8},{11,9},{8,1... | collective-permute-start | bytes 196616 | tf_op jit(solution)/shard_map/ppermute | solution.py:414
  64.3 3.6 %collective-permute-start.18 = (f16[4,8,32,128]{3,2,1,0:T(8,128)(2,1)S(1)}, f16[4,8,32,128]{3,2,1,0:T(8,128)(2,1)S(1)}, u32[]{:S(2)}, u32[]{:S(2)}) collective-permute-start(f16[4,8,32,128]{3,2,1,0:T(8,128)(2,1)S(1)} %pad_maximum_fusion.1), channel_id=1, source_target_pairs={{0,1},{1,0},{2,3},{3,2},{4,5},{5,4},{6,7},{7,6},{8,9},{9,8},{10,11... | collective-permute-start | bytes 786440 | tf_op jit(solution)/shard_map/ppermute | solution.py:448
  67.1 1.0 %copy-start.3 = (f32[16,128,128]{2,1,0:T(8,128)}, f32[16,128,128]{2,1,0:T(8,128)S(1)}, u32[]{:S(2)}) copy-start(f32[16,128,128]{2,1,0:T(8,128)S(1)} %multiply_dynamic-update-slice_fusion.1) | copy-start | bytes 3145732
